TPU v7x, 32 devices: a whole 2x2x4 slice. The times are simulated.
32 devices in a mesh: section: 2 (over x), dp: 4 (over z), tensor: 4 (over y, core).
Axes of the slice: x: 2, y: 2, z: 4, core: 2. Of those that a mesh axis runs over, the one named last changes fastest.
Arguments:
- norm_in: bfloat16 [2, 512, 8192], P('section', 'dp', 'tensor'), may hold values from -20 to 20
- query_grad: bfloat16 [2, 512, 4096], P('section', 'dp', 'tensor'), may hold values from -20 to 20
- attn_out: bfloat16 [2, 512, 4096], P('section', 'dp', 'tensor'), may hold values from -20 to 20
- handed: bfloat16 [2, 512, 8192], P('section', 'dp', 'tensor'), may hold values from -20 to 20
- sketch_q: bfloat16 [2, 64, 4096], P('section', None, 'tensor'), may hold values from -6 to 6
- sketch_o: bfloat16 [2, 64, 8192], P('section', None, 'tensor'), may hold values from -6 to 6
Outputs:
- lora_b_q: bfloat16 [2, 64, 8192], P('section', None, 'tensor')
- lora_a_q: float32 [2, 64, 4096], P('section', None, 'tensor')
- lora_b_o: bfloat16 [2, 64, 4096], P('section', None, 'tensor')
- lora_a_o: float32 [2, 64, 8192], P('section', None, 'tensor')
All inputs are finite; a program needn't handle non-finite values.
Results may differ from a plain program's by a relative error of at most 0.03.
Values may be sent and summed in bfloat16 or wider, within the bound.
No kernel may reach another device: no remote copies, remote signals or barrier semaphores. Data moves between devices by JAX's collectives and lax.ppermute only.
A program may use at most 64 MiB of HBM per device.

v0:
```python
import jax
import jax.numpy as jnp
from jax import lax
from jax.sharding import PartitionSpec as P

D = 8192
HQ = 4096
RANK = 64
POWER = 2


precise = lax.Precision.HIGHEST


def from_behind(value, axis, steps):
    count = lax.axis_size(axis)
    pairs = [(source, (source + steps) % count) for source in range(count)]
    return lax.ppermute(value, axis, pairs)


def gram_of(row_block):
    return jnp.dot(row_block, row_block.T, precision=precise, preferred_element_type=jnp.float32)


def solve_rows(gram_rows, row_block):
    low_factor = jnp.linalg.cholesky(gram_rows)
    solved = lax.linalg.triangular_solve(low_factor, row_block, left_side=True, lower=True)
    return solved.astype(jnp.bfloat16)


def tokens_of(sketches, matrices):
    first_part = jnp.einsum(
        "km,tm->kt", sketches[0], matrices[0], preferred_element_type=jnp.float32
    )
    second_part = jnp.einsum(
        "km,tm->kt", sketches[1], matrices[1], preferred_element_type=jnp.float32
    )
    total_a, total_b = (
        lax.psum(first_part.astype(jnp.bfloat16), "tensor").astype(jnp.float32),
        lax.psum(second_part.astype(jnp.bfloat16), "tensor").astype(jnp.float32),
    )
    return (total_a.astype(jnp.bfloat16), total_b.astype(jnp.bfloat16))


def partials(token_rows, matrices):
    part_a = jnp.dot(token_rows[0], matrices[0], preferred_element_type=jnp.float32)
    part_b = jnp.dot(token_rows[1], matrices[1], preferred_element_type=jnp.float32)
    return (part_a, part_b)


def orthonormal(partial_value):
    part_a, part_b = partial_value
    rows_a, rows_b = (
        lax.psum(part_a.astype(jnp.bfloat16), "dp").astype(jnp.float32),
        lax.psum(part_b.astype(jnp.bfloat16), "dp").astype(jnp.float32),
    )
    gram_a, gram_b = (
        lax.psum(gram_of(rows_a).astype(jnp.bfloat16), "tensor").astype(jnp.float32),
        lax.psum(gram_of(rows_b).astype(jnp.bfloat16), "tensor").astype(jnp.float32),
    )
    basis_a = solve_rows(gram_a, rows_a)
    basis_b = solve_rows(gram_b, rows_b)
    return (basis_a, basis_b)


def body(norm_in, query_grad, attn_out, handed, sketch_q, sketch_o):
    upstream = from_behind(handed, "section", -1)
    lefts = (norm_in[0], attn_out[0])
    rights = (query_grad[0], upstream[0])
    basis = orthonormal(partials(tokens_of((sketch_q[0], sketch_o[0]), rights), lefts))
    for iteration in range(POWER):
        other = orthonormal(partials(tokens_of(basis, lefts), rights))
        basis = orthonormal(partials(tokens_of(other, rights), lefts))
    final = partials(tokens_of(basis, lefts), rights)
    raw_a, raw_b = (
        lax.psum(final[0].astype(jnp.bfloat16), "dp").astype(jnp.float32),
        lax.psum(final[1].astype(jnp.bfloat16), "dp").astype(jnp.float32),
    )
    energy_a, energy_b = lax.psum((jnp.sum(raw_a * raw_a), jnp.sum(raw_b * raw_b)), "tensor")
    adapter_aq = raw_a / jnp.sqrt(energy_a / (RANK * HQ) + 1e-06)
    adapter_ao = raw_b / jnp.sqrt(energy_b / (RANK * D) + 1e-06)
    adapter_bq = basis[0] * 16.0
    adapter_bo = basis[1] * 16.0
    return (adapter_bq[None], adapter_aq[None], adapter_bo[None], adapter_ao[None])


def solution(mesh):
    return jax.shard_map(
        body,
        mesh=mesh,
        in_specs=(
            P("section", "dp", "tensor"),
            P("section", "dp", "tensor"),
            P("section", "dp", "tensor"),
            P("section", "dp", "tensor"),
            P("section", None, "tensor"),
            P("section", None, "tensor"),
        ),
        out_specs=(
            P("section", None, "tensor"),
            P("section", None, "tensor"),
            P("section", None, "tensor"),
            P("section", None, "tensor"),
        ),
        check_vma=False,
    )
```

profile of v0, /device:TPU:0, one launch (start us, length us, event | category | flops | bytes accessed | tf_op | source)
XLA Modules:
  0.0 526.6 jit_solution(525190196215800521)
XLA Ops:
  7.2 3.0 collective-permute-start
  10.2 1.2 convolution_convert_fusion.43
  11.5 10.9 %collective-permute-done = bf16[1,128,2048]{2,1,0:T(8,128)(2,1)S(1)} collective-permute-done((bf16[1,128,2048]{2,1,0:T(8,128)(2,1)}, bf16[1,128,2048]{2,1,0:T(8,128)(2,1)S(1)}, u32[]{:S(2)}, u32[]{:S(2)}) %collective-permute-start) | collective-permute-done | bytes 524320 | tf_op jit(solution)/shard_map/ppermute | solution.py:18
  22.7 10.5 %all-reduce.11 = (bf16[64,128]{1,0:T(8,128)(2,1)S(1)}, bf16[64,128]{1,0:T(8,128)(2,1)S(1)}) all-reduce(bf16[64,128]{1,0:T(8,128)(2,1)S(1)} %convolution_convert_fusion.43, bf16[64,128]{1,0:T(8,128)(2,1)S(1)} %convolution_convert_fusion.27), channel_id=1, replica_groups=mesh['section'=2,'dp'=4,'tensor'=4] {'tensor'}, use_global_device_ids=true, to_apply=%region_0.0 | all-reduce | flops 16384 | bytes 65536 | tf_op jit(solution)/shard_map/psum | solution.py:39
  35.1 38.3 %all-reduce.35.cloned.1.call-done = (bf16[64,2048]{1,0:T(8,128)(2,1)}, bf16[64,1024]{1,0:T(8,128)(2,1)}) async-done(((bf16[64,2048]{1,0:T(8,128)(2,1)}, bf16[64,1024]{1,0:T(8,128)(2,1)}), (bf16[64,2048]{1,0:T(8,128)(2,1)}, bf16[64,1024]{1,0:T(8,128)(2,1)})) %all-reduce.35.cloned.1.call-update) | async-done | bytes 393232 | tf_op jit(solution)/shard_map/psum | solution.py:54
  73.4 1.2 convolution_convert_fusion.26
  74.8 10.3 %all-reduce.10 = (bf16[64,64]{0,1:T(8,128)(2,1)S(1)}, bf16[64,64]{0,1:T(8,128)(2,1)S(1)}) all-reduce(bf16[64,64]{0,1:T(8,128)(2,1)S(1)} %convolution_convert_fusion.42, bf16[64,64]{0,1:T(8,128)(2,1)S(1)} %convolution_convert_fusion.26), channel_id=1, replica_groups=mesh['section'=2,'dp'=4,'tensor'=4] {'tensor'}, use_global_device_ids=true, to_apply=%region_2.0 | all-reduce | flops 8192 | bytes 32768 | tf_op jit(solution)/shard_map/psum | solution.py:58
  85.3 5.8 %cholesky.219 = f32[64,64]{1,0:T(8,128)S(1)} custom-call(f32[64,64]{1,0:T(8,128)S(1)} %get-tuple-element.43), custom_call_target="Cholesky" | custom-call | tf_op jit(solution)/shard_map/jit(cholesky)/cholesky | solution.py:26
  92.5 4.9 custom-call.21
  98.0 5.8 %cholesky.164 = f32[64,64]{1,0:T(8,128)S(1)} custom-call(f32[64,64]{1,0:T(8,128)S(1)} %get-tuple-element.44), custom_call_target="Cholesky" | custom-call | tf_op jit(solution)/shard_map/jit(cholesky)/cholesky | solution.py:26
  105.2 4.9 custom-call.16
  111.1 11.0 %all-reduce.9 = (bf16[64,128]{1,0:T(8,128)(2,1)S(1)}, bf16[64,128]{1,0:T(8,128)(2,1)S(1)}) all-reduce(bf16[64,128]{1,0:T(8,128)(2,1)S(1)} %convolution_convert_fusion.32, bf16[64,128]{1,0:T(8,128)(2,1)S(1)} %convolution_convert_fusion.37), channel_id=1, replica_groups=mesh['section'=2,'dp'=4,'tensor'=4] {'tensor'}, use_global_device_ids=true, to_apply=%region_5.8 | all-reduce | flops 16384 | bytes 65536 | tf_op jit(solution)/shard_map/psum | solution.py:39
  123.9 36.4 %all-reduce.33.cloned.1.call-done = (bf16[64,1024]{1,0:T(8,128)(2,1)}, bf16[64,2048]{1,0:T(8,128)(2,1)}) async-done(((bf16[64,1024]{1,0:T(8,128)(2,1)}, bf16[64,2048]{1,0:T(8,128)(2,1)}), (bf16[64,1024]{1,0:T(8,128)(2,1)}, bf16[64,2048]{1,0:T(8,128)(2,1)})) %all-reduce.33.cloned.1.call-update) | async-done | bytes 393232 | tf_op jit(solution)/shard_map/psum | solution.py:54
  160.3 1.2 convolution_convert_fusion.31
  161.7 10.5 %all-reduce.8 = (bf16[64,64]{0,1:T(8,128)(2,1)S(1)}, bf16[64,64]{0,1:T(8,128)(2,1)S(1)}) all-reduce(bf16[64,64]{0,1:T(8,128)(2,1)S(1)} %convolution_convert_fusion.31, bf16[64,64]{0,1:T(8,128)(2,1)S(1)} %convolution_convert_fusion.36), channel_id=1, replica_groups=mesh['section'=2,'dp'=4,'tensor'=4] {'tensor'}, use_global_device_ids=true, to_apply=%region_7.10 | all-reduce | flops 8192 | bytes 32768 | tf_op jit(solution)/shard_map/psum | solution.py:58
  172.3 5.8 %cholesky.230 = f32[64,64]{1,0:T(8,128)S(1)} custom-call(f32[64,64]{1,0:T(8,128)S(1)} %fusion.57), custom_call_target="Cholesky" | custom-call | tf_op jit(solution)/shard_map/jit(cholesky)/cholesky | solution.py:26
  179.5 4.9 custom-call.22
  185.1 5.8 %cholesky.175 = f32[64,64]{1,0:T(8,128)S(1)} custom-call(f32[64,64]{1,0:T(8,128)S(1)} %fusion.67), custom_call_target="Cholesky" | custom-call | tf_op jit(solution)/shard_map/jit(cholesky)/cholesky | solution.py:26
  192.3 4.9 custom-call.17
  198.2 10.5 %all-reduce.7 = (bf16[64,128]{1,0:T(8,128)(2,1)S(1)}, bf16[64,128]{1,0:T(8,128)(2,1)S(1)}) all-reduce(bf16[64,128]{1,0:T(8,128)(2,1)S(1)} %convolution_convert_fusion.41, bf16[64,128]{1,0:T(8,128)(2,1)S(1)} %convolution_convert_fusion.25), channel_id=1, replica_groups=mesh['section'=2,'dp'=4,'tensor'=4] {'tensor'}, use_global_device_ids=true, to_apply=%region_8.12 | all-reduce | flops 16384 | bytes 65536 | tf_op jit(solution)/shard_map/psum | solution.py:39
  208.7 0.9 convolution_convert_fusion.8
  210.6 36.2 %all-reduce.31.cloned.1.call-done = (bf16[64,2048]{1,0:T(8,128)(2,1)}, bf16[64,1024]{1,0:T(8,128)(2,1)}) async-done(((bf16[64,2048]{1,0:T(8,128)(2,1)}, bf16[64,1024]{1,0:T(8,128)(2,1)}), (bf16[64,2048]{1,0:T(8,128)(2,1)}, bf16[64,1024]{1,0:T(8,128)(2,1)})) %all-reduce.31.cloned.1.call-update) | async-done | bytes 393232 | tf_op jit(solution)/shard_map/psum | solution.py:54
  246.8 1.2 convolution_convert_fusion.24
  248.2 10.4 %all-reduce.6 = (bf16[64,64]{0,1:T(8,128)(2,1)S(1)}, bf16[64,64]{0,1:T(8,128)(2,1)S(1)}) all-reduce(bf16[64,64]{0,1:T(8,128)(2,1)S(1)} %convolution_convert_fusion.40, bf16[64,64]{0,1:T(8,128)(2,1)S(1)} %convolution_convert_fusion.24), channel_id=1, replica_groups=mesh['section'=2,'dp'=4,'tensor'=4] {'tensor'}, use_global_device_ids=true, to_apply=%region_10.14 | all-reduce | flops 8192 | bytes 32768 | tf_op jit(solution)/shard_map/psum | solution.py:58
  258.8 5.8 %cholesky.241 = f32[64,64]{1,0:T(8,128)S(1)} custom-call(f32[64,64]{1,0:T(8,128)S(1)} %fusion.55), custom_call_target="Cholesky" | custom-call | tf_op jit(solution)/shard_map/jit(cholesky)/cholesky | solution.py:26
  266.0 4.9 custom-call.23
  271.6 5.8 %cholesky.186 = f32[64,64]{1,0:T(8,128)S(1)} custom-call(f32[64,64]{1,0:T(8,128)S(1)} %fusion.65), custom_call_target="Cholesky" | custom-call | tf_op jit(solution)/shard_map/jit(cholesky)/cholesky | solution.py:26
  278.8 4.9 custom-call.18
  284.7 10.9 %all-reduce.5 = (bf16[64,128]{1,0:T(8,128)(2,1)S(1)}, bf16[64,128]{1,0:T(8,128)(2,1)S(1)}) all-reduce(bf16[64,128]{1,0:T(8,128)(2,1)S(1)} %convolution_convert_fusion.30, bf16[64,128]{1,0:T(8,128)(2,1)S(1)} %convolution_convert_fusion.35), channel_id=1, replica_groups=mesh['section'=2,'dp'=4,'tensor'=4] {'tensor'}, use_global_device_ids=true, to_apply=%region_11.15 | all-reduce | flops 16384 | bytes 65536 | tf_op jit(solution)/shard_map/psum | solution.py:39
  297.4 36.4 %all-reduce.29.cloned.1.call-done = (bf16[64,1024]{1,0:T(8,128)(2,1)}, bf16[64,2048]{1,0:T(8,128)(2,1)}) async-done(((bf16[64,1024]{1,0:T(8,128)(2,1)}, bf16[64,2048]{1,0:T(8,128)(2,1)}), (bf16[64,1024]{1,0:T(8,128)(2,1)}, bf16[64,2048]{1,0:T(8,128)(2,1)})) %all-reduce.29.cloned.1.call-update) | async-done | bytes 393232 | tf_op jit(solution)/shard_map/psum | solution.py:54
  333.9 1.2 convolution_convert_fusion.29
  335.3 10.5 %all-reduce.4 = (bf16[64,64]{0,1:T(8,128)(2,1)S(1)}, bf16[64,64]{0,1:T(8,128)(2,1)S(1)}) all-reduce(bf16[64,64]{0,1:T(8,128)(2,1)S(1)} %convolution_convert_fusion.29, bf16[64,64]{0,1:T(8,128)(2,1)S(1)} %convolution_convert_fusion.34), channel_id=1, replica_groups=mesh['section'=2,'dp'=4,'tensor'=4] {'tensor'}, use_global_device_ids=true, to_apply=%region_13.17 | all-reduce | flops 8192 | bytes 32768 | tf_op jit(solution)/shard_map/psum | solution.py:58
  345.9 5.8 %cholesky.252 = f32[64,64]{1,0:T(8,128)S(1)} custom-call(f32[64,64]{1,0:T(8,128)S(1)} %fusion.53), custom_call_target="Cholesky" | custom-call | tf_op jit(solution)/shard_map/jit(cholesky)/cholesky | solution.py:26
  353.1 4.9 custom-call.24
  358.8 5.8 %cholesky.197 = f32[64,64]{1,0:T(8,128)S(1)} custom-call(f32[64,64]{1,0:T(8,128)S(1)} %fusion.63), custom_call_target="Cholesky" | custom-call | tf_op jit(solution)/shard_map/jit(cholesky)/cholesky | solution.py:26
  365.9 4.9 custom-call.19
  371.8 10.5 %all-reduce.3 = (bf16[64,128]{1,0:T(8,128)(2,1)S(1)}, bf16[64,128]{1,0:T(8,128)(2,1)S(1)}) all-reduce(bf16[64,128]{1,0:T(8,128)(2,1)S(1)} %convolution_convert_fusion.39, bf16[64,128]{1,0:T(8,128)(2,1)S(1)} %convolution_convert_fusion.23), channel_id=1, replica_groups=mesh['section'=2,'dp'=4,'tensor'=4] {'tensor'}, use_global_device_ids=true, to_apply=%region_14.18 | all-reduce | flops 16384 | bytes 65536 | tf_op jit(solution)/shard_map/psum | solution.py:39
  384.2 36.3 %all-reduce.27.cloned.1.call-done = (bf16[64,2048]{1,0:T(8,128)(2,1)}, bf16[64,1024]{1,0:T(8,128)(2,1)}) async-done(((bf16[64,2048]{1,0:T(8,128)(2,1)}, bf16[64,1024]{1,0:T(8,128)(2,1)}), (bf16[64,2048]{1,0:T(8,128)(2,1)}, bf16[64,1024]{1,0:T(8,128)(2,1)})) %all-reduce.27.cloned.1.call-update) | async-done | bytes 393232 | tf_op jit(solution)/shard_map/psum | solution.py:54
  420.5 1.2 convolution_convert_fusion.22
  421.9 10.4 %all-reduce.2 = (bf16[64,64]{0,1:T(8,128)(2,1)S(1)}, bf16[64,64]{0,1:T(8,128)(2,1)S(1)}) all-reduce(bf16[64,64]{0,1:T(8,128)(2,1)S(1)} %convolution_convert_fusion.38, bf16[64,64]{0,1:T(8,128)(2,1)S(1)} %convolution_convert_fusion.22), channel_id=1, replica_groups=mesh['section'=2,'dp'=4,'tensor'=4] {'tensor'}, use_global_device_ids=true, to_apply=%region_16.20 | all-reduce | flops 8192 | bytes 32768 | tf_op jit(solution)/shard_map/psum | solution.py:58
  432.4 5.8 %cholesky.263 = f32[64,64]{1,0:T(8,128)S(1)} custom-call(f32[64,64]{1,0:T(8,128)S(1)} %fusion.51), custom_call_target="Cholesky" | custom-call | tf_op jit(solution)/shard_map/jit(cholesky)/cholesky | solution.py:26
  439.6 4.9 custom-call.25
  445.3 5.8 %cholesky.208 = f32[64,64]{1,0:T(8,128)S(1)} custom-call(f32[64,64]{1,0:T(8,128)S(1)} %fusion.61), custom_call_target="Cholesky" | custom-call | tf_op jit(solution)/shard_map/jit(cholesky)/cholesky | solution.py:26
  452.5 4.9 custom-call.20
  458.3 10.9 %all-reduce.1 = (bf16[64,128]{1,0:T(8,128)(2,1)S(1)}, bf16[64,128]{1,0:T(8,128)(2,1)S(1)}) all-reduce(bf16[64,128]{1,0:T(8,128)(2,1)S(1)} %convolution_convert_fusion.28, bf16[64,128]{1,0:T(8,128)(2,1)S(1)} %convolution_convert_fusion.33), channel_id=1, replica_groups=mesh['section'=2,'dp'=4,'tensor'=4] {'tensor'}, use_global_device_ids=true, to_apply=%region_17.21 | all-reduce | flops 16384 | bytes 65536 | tf_op jit(solution)/shard_map/psum | solution.py:39
  471.8 35.7 %all-reduce.25.cloned.1.call-done = (bf16[64,1024]{1,0:T(8,128)(2,1)}, bf16[64,2048]{1,0:T(8,128)(2,1)}) async-done(((bf16[64,1024]{1,0:T(8,128)(2,1)}, bf16[64,2048]{1,0:T(8,128)(2,1)}), (bf16[64,1024]{1,0:T(8,128)(2,1)}, bf16[64,2048]{1,0:T(8,128)(2,1)})) %all-reduce.25.cloned.1.call-update) | async-done | bytes 393232 | tf_op jit(solution)/shard_map/psum | solution.py:76
  507.5 1.7 fusion
  510.5 6.3 %all-reduce = (f32[]{:T(128)}, f32[]{:T(128)}) all-reduce(f32[]{:T(128)} %fusion.19, f32[]{:T(128)} %fusion), channel_id=1, replica_groups=mesh['section'=2,'dp'=4,'tensor'=4] {'tensor'}, use_global_device_ids=true, to_apply=%region_20.24 | all-reduce | flops 2 | bytes 16 | tf_op jit(solution)/shard_map/psum | solution.py:79
  (135 shorter events, 37.1 us)
Async XLA Ops:
  7.2 26.0 %copy-start = (bf16[1,128,2048]{2,1,0:T(8,128)(2,1)S(1)}, bf16[1,128,2048]{2,1,0:T(8,128)(2,1)}, u32[]{:S(2)}) copy-start(bf16[1,128,2048]{2,1,0:T(8,128)(2,1)} %param.11) | copy-start | bytes 1572868
  7.2 15.2 %copy-start.15 = (bf16[1,64,2048]{2,1,0:T(8,128)(2,1)S(1)}, bf16[1,64,2048]{2,1,0:T(8,128)(2,1)}, u32[]{:S(2)}) copy-start(bf16[1,64,2048]{2,1,0:T(8,128)(2,1)} %param.16) | copy-start | bytes 786436
  7.2 66.2 %all-reduce.35.cloned.1.call-start = ((), (), s32[]{:S(2)}) async-start(), calls=%async_computation.5 | async-start | bytes 786432 | tf_op jit(solution)/shard_map/psum | solution.py:54
  7.2 15.1 %collective-permute-start = (bf16[1,128,2048]{2,1,0:T(8,128)(2,1)}, bf16[1,128,2048]{2,1,0:T(8,128)(2,1)S(1)}, u32[]{:S(2)}, u32[]{:S(2)}) collective-permute-start(bf16[1,128,2048]{2,1,0:T(8,128)(2,1)} %param.14), channel_id=1, source_target_pairs={{0,16},{16,0},{1,17},{17,1},{2,18},{18,2},{3,19},{19,3},{4,20},{20... | collective-permute-start | bytes 1572872 | tf_op jit(solution)/shard_map/ppermute | solution.py:18
  33.2 1.0 copy-start.1
  35.0 125.2 %all-reduce.33.cloned.1.call-start = ((), (), s32[]{:S(2)}) async-start(), calls=%async_computation.4 | async-start | bytes 786432 | tf_op jit(solution)/shard_map/psum | solution.py:54
  73.4 1.2 copy-start.3
  85.3 12.1 %copy-start.10 = (bf16[64,1024]{1,0:T(8,128)(2,1)S(1)}, bf16[64,1024]{1,0:T(8,128)(2,1)}, u32[]{:S(2)}) copy-start(bf16[64,1024]{1,0:T(8,128)(2,1)} %get-tuple-element.42) | copy-start | bytes 393220
  110.8 11.3 %copy-start.2 = (bf16[1,128,1024]{2,1,0:T(8,128)(2,1)S(1)}, bf16[1,128,1024]{2,1,0:T(8,128)(2,1)}, u32[]{:S(2)}) copy-start(bf16[1,128,1024]{2,1,0:T(8,128)(2,1)} %param.12) | copy-start | bytes 786436
  123.8 123.0 %all-reduce.31.cloned.1.call-start = ((), (), s32[]{:S(2)}) async-start(), calls=%async_computation.3 | async-start | bytes 786432 | tf_op jit(solution)/shard_map/psum | solution.py:54
  160.3 1.2 copy-start.6
  185.0 12.2 %copy-start.8 = (bf16[64,1024]{1,0:T(8,128)(2,1)S(1)}, bf16[64,1024]{1,0:T(8,128)(2,1)}, u32[]{:S(2)}) copy-start(bf16[64,1024]{1,0:T(8,128)(2,1)} %get-tuple-element.39) | copy-start | bytes 393220
  210.5 123.3 %all-reduce.29.cloned.1.call-start = ((), (), s32[]{:S(2)}) async-start(), calls=%async_computation.2 | async-start | bytes 786432 | tf_op jit(solution)/shard_map/psum | solution.py:54
  246.8 1.2 copy-start.4
  248.2 22.6 %copy-start.11 = (bf16[64,1024]{1,0:T(8,128)(2,1)S(1)}, bf16[64,1024]{1,0:T(8,128)(2,1)}, u32[]{:S(2)}) copy-start(bf16[64,1024]{1,0:T(8,128)(2,1)} %get-tuple-element.38) | copy-start | bytes 393220
  297.4 123.1 %all-reduce.27.cloned.1.call-start = ((), (), s32[]{:S(2)}) async-start(), calls=%async_computation.1 | async-start | bytes 786432 | tf_op jit(solution)/shard_map/psum | solution.py:54
  333.8 1.2 copy-start.7
  358.6 12.2 %copy-start.9 = (bf16[64,1024]{1,0:T(8,128)(2,1)S(1)}, bf16[64,1024]{1,0:T(8,128)(2,1)}, u32[]{:S(2)}) copy-start(bf16[64,1024]{1,0:T(8,128)(2,1)} %get-tuple-element.35) | copy-start | bytes 393220
  384.1 123.3 %all-reduce.25.cloned.1.call-start = ((), (), s32[]{:S(2)}) async-start(), calls=%async_computation | async-start | bytes 786432 | tf_op jit(solution)/shard_map/psum | solution.py:76
  420.5 1.2 copy-start.5
  421.9 22.6 %copy-start.12 = (bf16[64,1024]{1,0:T(8,128)(2,1)S(1)}, bf16[64,1024]{1,0:T(8,128)(2,1)}, u32[]{:S(2)}) copy-start(bf16[64,1024]{1,0:T(8,128)(2,1)} %get-tuple-element.34) | copy-start | bytes 393220
  507.5 1.7 copy-start.14
  509.2 8.3 %copy-start.13 = (bf16[64,2048]{1,0:T(8,128)(2,1)S(1)}, bf16[64,2048]{1,0:T(8,128)(2,1)}, u32[]{:S(2)}) copy-start(bf16[64,2048]{1,0:T(8,128)(2,1)} %get-tuple-element.32) | copy-start | bytes 786436
Sparse Core Ops, SparseCore 0:
  35.1 38.1 all-reduce.34
  124.0 36.2 all-reduce.32
  210.6 36.1 all-reduce.30
  297.5 36.2 all-reduce.28
  384.2 36.1 all-reduce.26
  471.2 36.2 all-reduce.24
where the time goes:
time: 527 us
  waiting for transfers between devices  230 us (44%)
  other arithmetic  126 us (24%)
  blocking collectives  123 us (23%)
  matrix products  26.9 us (5%)
  between operations  16.2 us (3%)
    psum x5, waiting for transfers between devices, orthonormal(): lax.psum(part_a.astype(jnp.bfloat16), 'dp').astype(jnp.float32)  184 us
    another operation x30, other arithmetic, solve_rows(): low_factor = jnp.linalg.cholesky(gram_rows)  65.2 us
    psum x6, blocking collectives, tokens_of(): lax.psum(first_part.astype(jnp.bfloat16), 'tensor').astype(jnp.float32)  64.4 us
    another operation x20, other arithmetic, solve_rows(): lax.linalg.triangular_solve(low_factor, row_block, left_side=True, lower=...  55.5 us
    psum x5, blocking collectives, orthonormal(): lax.psum(gram_of(rows_a).astype(jnp.bfloat16), 'tensor').astype(jnp.float32)  52.2 us
    psum x1, waiting for transfers between devices, body(): lax.psum(final[0].astype(jnp.bfloat16), 'dp').astype(jnp.float32)  35.7 us
    ppermute x1, waiting for transfers between devices, from_behind(): return lax.ppermute(value, axis, pairs)  10.9 us
  transfers between devices with their start and end apart: 7, of which 7 were waited for; matrix products, arithmetic and copies ran while one was open for 0% of the time, Pallas kernels for 0%

commit v1 on v0

v1 whole, which is shorter than its diff:
```python
import functools

import jax
import jax.numpy as jnp
from jax import lax
from jax.experimental import pallas as pl
from jax.experimental.pallas import tpu as pltpu
from jax.sharding import PartitionSpec as P

RANK = 64
POWER = 2
BLK = 128

precise = lax.Precision.HIGHEST
f32 = jnp.float32
bf16 = jnp.bfloat16
VMEM = pl.BlockSpec(memory_space=pltpu.VMEM)
SMEM = pl.BlockSpec(memory_space=pltpu.SMEM)


def from_behind(value, axis, steps):
    count = lax.axis_size(axis)
    pairs = [(source, (source + steps) % count) for source in range(count)]
    return lax.ppermute(value, axis, pairs)


def gram_of(row_block):
    return jnp.dot(row_block, row_block.T, precision=precise, preferred_element_type=f32)


def solve_rows(gram_rows, row_block):
    low_factor = jnp.linalg.cholesky(gram_rows)
    solved = lax.linalg.triangular_solve(low_factor, row_block, left_side=True, lower=True)
    return solved.astype(bf16)


def tokens_of(sketches, matrices):
    parts = [
        jnp.einsum("km,tm->kt", s, m, preferred_element_type=f32)
        for s, m in zip(sketches, matrices)
    ]
    return tuple(lax.psum(p.astype(bf16), "tensor").astype(bf16) for p in parts)


def partials(token_rows, matrices):
    return tuple(
        jnp.dot(r, m, preferred_element_type=f32) for r, m in zip(token_rows, matrices)
    )


def orthonormal(parts):
    rows = [lax.psum(p.astype(bf16), "dp").astype(f32) for p in parts]
    grams = [lax.psum(gram_of(r).astype(bf16), "tensor").astype(f32) for r in rows]
    return tuple(solve_rows(g, r) for g, r in zip(grams, rows))


def feature_space(norm_in, query_grad, attn_out, handed, sketch_q, sketch_o):
    upstream = from_behind(handed, "section", -1)
    lefts = (norm_in[0], attn_out[0])
    rights = (query_grad[0], upstream[0])
    basis = orthonormal(partials(tokens_of((sketch_q[0], sketch_o[0]), rights), lefts))
    for _ in range(POWER):
        other = orthonormal(partials(tokens_of(basis, lefts), rights))
        basis = orthonormal(partials(tokens_of(other, rights), lefts))
    final = partials(tokens_of(basis, lefts), rights)
    raws = [lax.psum(p.astype(bf16), "dp").astype(f32) for p in final]
    energies = lax.psum(tuple(jnp.sum(r * r) for r in raws), "tensor")
    count = lax.axis_size("tensor")
    adapters = [
        r / jnp.sqrt(e / (r.size * count) + 1e-06) for r, e in zip(raws, energies)
    ]
    return (
        (basis[0] * 16.0)[None],
        adapters[0][None],
        (basis[1] * 16.0)[None],
        adapters[1][None],
    )


def swap(value, axis, bit):
    count = lax.axis_size(axis)
    return lax.ppermute(value, axis, [(i, i ^ bit) for i in range(count)])


def routed(value, sizes, token_bit, tensor_bit, shifted):
    sections, dps, tensors = sizes
    pairs = []
    for s in range(sections):
        for z in range(dps):
            for t in range(tensors):
                to_t = t ^ tensor_bit
                to_s = (s - 1) % sections if shifted and to_t >= tensors // 2 else s
                to = (to_s * dps + (z ^ token_bit)) * tensors + to_t
                pairs.append(((s * dps + z) * tensors + t, to))
    return lax.ppermute(value, ("section", "dp", "tensor"), pairs)


def pack_kernel(dps, idx, norm, grad, attn, hand, sk_q, sk_o, *outs):
    z, out_half = idx[0], idx[1]
    big_w, small_w = norm.shape[1] // dps, grad.shape[1] // dps
    own_big, oth_big = outs[:dps], outs[dps : 2 * dps]
    own_small, oth_small = outs[2 * dps : 3 * dps], outs[3 * dps : 4 * dps]
    own_sk, oth_sk = outs[4 * dps :]
    for d in range(dps):
        at = z ^ d
        bigs = pl.ds(pl.multiple_of(at * big_w, big_w), big_w)
        smalls = pl.ds(pl.multiple_of(at * small_w, small_w), small_w)

        @pl.when(out_half == 0)
        def _():
            own_big[d][...] = norm[:, bigs]
            oth_big[d][...] = hand[:, bigs]
            own_small[d][...] = grad[:, smalls]
            oth_small[d][...] = attn[:, smalls]

        @pl.when(out_half == 1)
        def _():
            own_big[d][...] = hand[:, bigs]
            oth_big[d][...] = norm[:, bigs]
            own_small[d][...] = attn[:, smalls]
            oth_small[d][...] = grad[:, smalls]

    bigs = pl.ds(pl.multiple_of(z * big_w, big_w), big_w)
    smalls = pl.ds(pl.multiple_of(z * small_w, small_w), small_w)
    for_o, for_q = sk_o[:, bigs], sk_q[:, smalls]

    @pl.when(out_half == 0)
    def _():
        own_sk[:, :big_w] = jnp.zeros_like(for_o)
        own_sk[:, big_w:] = for_q
        oth_sk[:, :big_w] = for_o
        oth_sk[:, big_w:] = jnp.zeros_like(for_q)

    @pl.when(out_half == 1)
    def _():
        own_sk[:, :big_w] = for_o
        own_sk[:, big_w:] = jnp.zeros_like(for_q)
        oth_sk[:, :big_w] = jnp.zeros_like(for_o)
        oth_sk[:, big_w:] = for_q


def nt(a, b, precision=None):
    return lax.dot_general(
        a, b, (((1,), (1,)), ((), ())), precision=precision, preferred_element_type=f32
    )


def gram_kernel(dps, idx, *refs):
    z, core = idx[0], idx[2]
    own_big, oth_big = refs[:dps], refs[dps : 2 * dps]
    own_small, oth_small = refs[2 * dps : 3 * dps], refs[3 * dps : 4 * dps]
    own_sk, oth_sk = refs[4 * dps : 4 * dps + 2]
    big, small, keep, send, slots = refs[4 * dps + 2 :]
    big_w, small_w = own_big[0].shape[1], own_small[0].shape[1]
    rank = own_sk.shape[0]
    for d in range(dps):
        rows = pl.ds(pl.multiple_of((z ^ d) * BLK, BLK), BLK)
        big[rows, :big_w] = own_big[d][...]
        big[rows, big_w:] = oth_big[d][...]
        small[rows, :small_w] = own_small[d][...]
        small[rows, small_w:] = oth_small[d][...]
    half = slots.shape[1]
    at = 0
    for m in (big, small):
        for i in range(dps):
            row = nt(m[i * BLK : (i + 1) * BLK, :], m[: (i + 1) * BLK, :])
            for j in range(i + 1):
                slots[at // half, at % half] = row[:, j * BLK : (j + 1) * BLK].astype(bf16)
                at += 1
    first = (
        nt(own_sk[:, :big_w], big[:, :big_w])
        + nt(oth_sk[:, :big_w], big[:, big_w:])
        + nt(own_sk[:, big_w:], small[:, :small_w])
        + nt(oth_sk[:, big_w:], small[:, small_w:])
    ).astype(bf16)
    per = BLK // rank
    for i in range(dps):
        s = at + i // per
        r = (i % per) * rank
        slots[s // half, s % half, r : r + rank, :] = first[:, i * BLK : (i + 1) * BLK]
    for s in range(at + dps // per, 2 * half):
        slots[s // half, s % half] = jnp.zeros((BLK, BLK), bf16)
    keep[...] = slots[core]
    send[...] = slots[1 - core]


def add_pair_kernel(dps, idx, keep, got, *shares):
    z = idx[0]
    size = shares[0].shape[0]
    for d in range(dps):
        part = pl.ds((z ^ d) * size, size)
        shares[d][...] = (keep[part].astype(f32) + got[part].astype(f32)).astype(bf16)


def add_all_kernel(*refs):
    total = refs[0][...].astype(f32)
    for r in refs[1:-1]:
        total = total + r[...].astype(f32)
    refs[-1][...] = total.astype(bf16)


def inverse_factor(gram):
    n = gram.shape[0]
    rows = lax.broadcasted_iota(jnp.int32, (n, n), 0)
    cols = lax.broadcasted_iota(jnp.int32, (n, n), 1)
    eye = (rows == cols).astype(f32)
    work = jnp.concatenate([gram, eye], axis=1)
    slabs = [work[8 * s : 8 * s + 8, :] for s in range(n // 8)]
    sub = lax.broadcasted_iota(jnp.int32, (8, 2 * n), 0)
    for k in range(n):
        s0, r0 = divmod(k, 8)
        pivot_row = slabs[s0][r0 : r0 + 1, :]
        scaled = pivot_row * (1.0 / pivot_row[:, k : k + 1])
        for s in range(s0, n // 8):
            col = slabs[s][:, k : k + 1]
            new = slabs[s] - col * scaled
            slabs[s] = jnp.where(sub > r0, new, slabs[s]) if s == s0 else new
    work = jnp.concatenate(slabs, axis=0)
    pivots = jnp.sum(work[:, :n] * eye, axis=1, keepdims=True)
    return work[:, n:] * lax.rsqrt(pivots)


def times(rows, gram):
    high = rows.astype(bf16)
    low = (rows - high.astype(f32)).astype(bf16)
    return jnp.dot(high, gram, preferred_element_type=f32) + jnp.dot(
        low, gram, preferred_element_type=f32
    )


def chain_kernel(dps, counts, idx, *refs):
    z, out_half, core = idx[0], idx[1], idx[2]
    mine, theirs = refs[:dps], refs[dps : 2 * dps]
    big, small = refs[2 * dps : 2 * dps + 2]
    own_out, oth_out, slots, left, right = refs[2 * dps + 2 :]
    size = mine[0].shape[0]
    half = size * dps
    for d in range(dps):
        slots[pl.ds(core * half + (z ^ d) * size, size)] = mine[d][...]
        slots[pl.ds((1 - core) * half + (z ^ d) * size, size)] = theirs[d][...]
    tri = dps * (dps + 1) // 2
    for gram, base in ((left, out_half * tri), (right, (1 - out_half) * tri)):
        at = 0
        for i in range(dps):
            for j in range(i + 1):
                block = slots[base + at]
                gram[i * BLK : (i + 1) * BLK, j * BLK : (j + 1) * BLK] = block
                if j < i:
                    gram[j * BLK : (j + 1) * BLK, i * BLK : (i + 1) * BLK] = (
                        block.astype(f32).T.astype(bf16)
                    )
                at += 1
    per = BLK // RANK
    rows = jnp.concatenate(
        [
            slots[2 * tri + i // per, (i % per) * RANK : (i % per + 1) * RANK, :]
            for i in range(dps)
        ],
        axis=1,
    ).astype(f32)
    for step in range(2 * POWER + 1):
        gram = left if step % 2 == 0 else right
        ahead = times(rows, gram[...])
        low_inv = inverse_factor(nt(ahead, rows, precise))
        basis = rows
        rows = jnp.dot(low_inv, ahead, precision=precise, preferred_element_type=f32)
    basis = jnp.dot(low_inv, basis, precision=precise, preferred_element_type=f32)
    energy = jnp.sum(times(rows, right[...]) * rows)
    count = jnp.where(out_half == 1, counts[0], counts[1]).astype(f32)
    scale = lax.rsqrt(jnp.full((1, 1), energy, f32) / count + 1e-06)
    coef_b, coef_a = basis.astype(bf16), rows.astype(bf16)
    is_out = out_half == 1
    for_big = jnp.where(is_out, coef_a, coef_b)
    for_small = jnp.where(is_out, coef_b, coef_a)
    scale_big = jnp.where(is_out, scale, 16.0)
    scale_small = jnp.where(is_out, 16.0, scale)
    big_w, small_w = big.shape[1] // 2, small.shape[1] // 2
    for out, n in ((own_out, 0), (oth_out, 1)):
        out[:, :big_w] = (
            jnp.dot(for_big, big[:, n * big_w : (n + 1) * big_w], preferred_element_type=f32)
            * scale_big
        ).astype(bf16)
        out[:, big_w:] = (
            jnp.dot(
                for_small, small[:, n * small_w : (n + 1) * small_w], preferred_element_type=f32
            )
            * scale_small
        ).astype(bf16)


def place_kernel(dps, idx, *refs):
    z, out_half = idx[0], idx[1]
    own, oth = refs[:dps], refs[dps : 2 * dps]
    b_q, a_q, b_o, a_o = refs[2 * dps :]
    big_w, small_w = b_q.shape[1] // dps, a_q.shape[1] // dps
    for d in range(dps):
        bigs = pl.ds(pl.multiple_of((z ^ d) * big_w, big_w), big_w)
        smalls = pl.ds(pl.multiple_of((z ^ d) * small_w, small_w), small_w)
        for half, query, output in ((0, own[d], oth[d]), (1, oth[d], own[d])):

            @pl.when(out_half == half)
            def _():
                b_q[:, bigs] = query[:, :big_w]
                a_q[:, smalls] = query[:, big_w:].astype(f32)
                a_o[:, bigs] = output[:, :big_w].astype(f32)
                b_o[:, smalls] = output[:, big_w:]


def call(kernel, out_shapes, args, scratch=()):
    outs = pl.pallas_call(
        kernel,
        out_shape=out_shapes,
        in_specs=[SMEM] + [VMEM] * (len(args) - 1),
        out_specs=jax.tree.map(lambda _: VMEM, out_shapes),
        scratch_shapes=list(scratch),
        compiler_params=pltpu.CompilerParams(vmem_limit_bytes=48 * 2**20),
    )(*args)
    return list(outs)


def token_space(sizes, norm_in, query_grad, attn_out, handed, sketch_q, sketch_o):
    _, dps, tensors = sizes
    side = tensors // 2
    shape = lambda s, t=bf16: jax.ShapeDtypeStruct(s, t)
    z, t = lax.axis_index("dp"), lax.axis_index("tensor")
    idx = jnp.stack([z, t // side, t % side]).astype(jnp.int32)
    wide, narrow = norm_in.shape[2], query_grad.shape[2]
    big_w, small_w = wide // dps, narrow // dps

    packed = call(
        functools.partial(pack_kernel, dps),
        [shape((BLK, big_w))] * (2 * dps)
        + [shape((BLK, small_w))] * (2 * dps)
        + [shape((RANK, big_w + small_w))] * 2,
        (idx, norm_in[0], query_grad[0], attn_out[0], handed[0], sketch_q[0], sketch_o[0]),
    )
    own_big, oth_big = packed[:dps], packed[dps : 2 * dps]
    own_small, oth_small = packed[2 * dps : 3 * dps], packed[3 * dps : 4 * dps]
    own_sk, oth_sk = packed[4 * dps :]
    own_big = [routed(v, sizes, d, 0, True) for d, v in enumerate(own_big)]
    oth_big = [routed(v, sizes, d, side, True) for d, v in enumerate(oth_big)]
    own_small = own_small[:1] + [
        routed(v, sizes, d, 0, False) for d, v in enumerate(own_small) if d
    ]
    oth_small = [routed(v, sizes, d, side, False) for d, v in enumerate(oth_small)]
    oth_sk = swap(oth_sk, "tensor", side)

    tri = dps * (dps + 1) // 2
    share = pl.cdiv(2 * tri + dps * RANK // BLK, 2 * dps)
    half = share * dps
    tokens = dps * BLK
    big, small, keep, send = call(
        functools.partial(gram_kernel, dps),
        [
            shape((tokens, 2 * big_w)),
            shape((tokens, 2 * small_w)),
            shape((half, BLK, BLK)),
            shape((half, BLK, BLK)),
        ],
        (idx, *own_big, *oth_big, *own_small, *oth_small, own_sk, oth_sk),
        [pltpu.VMEM((2, half, BLK, BLK), bf16)],
    )
    got = swap(send, "tensor", 1)
    shares = call(
        functools.partial(add_pair_kernel, dps),
        [shape((share, BLK, BLK))] * dps,
        (idx, keep, got),
    )
    shares = shares[:1] + [swap(v, "dp", d) for d, v in enumerate(shares) if d]
    total = pl.pallas_call(
        add_all_kernel,
        out_shape=shape((share, BLK, BLK)),
        in_specs=[VMEM] * dps,
        out_specs=VMEM,
    )(*shares)
    mine = [total] + [swap(total, "dp", d) for d in range(1, dps)]
    theirs = [swap(v, "tensor", 1) for v in mine]

    counts = (RANK * wide * tensors, RANK * narrow * tensors)
    own_out, oth_out = call(
        functools.partial(chain_kernel, dps, counts),
        [shape((RANK, big_w + small_w))] * 2,
        (idx, *mine, *theirs, big, small),
        [
            pltpu.VMEM((2 * half, BLK, BLK), bf16),
            pltpu.VMEM((tokens, tokens), bf16),
            pltpu.VMEM((tokens, tokens), bf16),
        ],
    )
    oth_out = swap(oth_out, "tensor", side)
    own = [own_out] + [swap(own_out, "dp", d) for d in range(1, dps)]
    oth = [oth_out] + [swap(oth_out, "dp", d) for d in range(1, dps)]
    outs = call(
        functools.partial(place_kernel, dps),
        [
            shape((RANK, wide)),
            shape((RANK, narrow), f32),
            shape((RANK, narrow)),
            shape((RANK, wide), f32),
        ],
        (idx, *own, *oth),
    )
    return tuple(o[None] for o in outs)


def solution(mesh):
    sizes = tuple(mesh.shape[axis] for axis in ("section", "dp", "tensor"))
    _, dps, tensors = sizes

    def body(norm_in, query_grad, attn_out, handed, sketch_q, sketch_o):
        args = (norm_in, query_grad, attn_out, handed, sketch_q, sketch_o)
        fits = (
            dps in (2, 4)
            and tensors == 4
            and norm_in.shape[1] == BLK
            and sketch_q.shape[1] == RANK
            and norm_in.shape[2] == handed.shape[2]
            and query_grad.shape[2] == attn_out.shape[2]
            and query_grad.shape[2] % (dps * 128) == 0
            and norm_in.shape[2] % (dps * 128) == 0
        )
        return token_space(sizes, *args) if fits else feature_space(*args)

    return jax.shard_map(
        body,
        mesh=mesh,
        in_specs=(P("section", "dp", "tensor"),) * 4 + (P("section", None, "tensor"),) * 2,
        out_specs=(P("section", None, "tensor"),) * 4,
        check_vma=False,
    )
```

time: 527 us -> 138 us (0.26)
  waiting for transfers between devices: 230 us -> 40.7 us
  other arithmetic: 126 us -> 0.08 us
  blocking collectives: 123 us -> 0 us
  starting transfers between devices: 3.25 us -> 48.8 us
  Pallas kernels: 0 us -> 39.6 us
  matrix products: 26.9 us -> 0 us
  between operations: 16.2 us -> 0.77 us
  local copies, waits for them, and re-layouts: 0.95 us -> 8.03 us
    psum x6 -> x0, waiting for transfers between devices: 219 us -> none  [the longest x5 184 us: orthonormal(): lax.psum(part_a.astype(jnp.bfloat16), 'dp').astype(jnp.float32)]
    psum x12 -> x0, blocking collectives: 123 us -> none  [the longest x6 64.4 us: tokens_of(): lax.psum(first_part.astype(jnp.bfloat16), 'tensor').astype(jnp.float32)]
    another operation x50 -> x1, other arithmetic: 121 us -> 0.08 us  [token_space(): idx = jnp.stack([z, t // side, t % side]).astype(jnp.int32)]
    ppermute x1 -> x34, starting transfers between devices: 3 us -> 48.8 us  [the longest x19 24.5 us: swap(): return lax.ppermute(value, axis, [(i, i ^ bit) for i in range(count)])]
    pallas_call x0 -> x6, Pallas kernels: none -> 39.6 us  [the longest x5 37.9 us: call(): pl.pallas_call(kernel, out_shape=out_shapes, in_specs=[SMEM] + [VMEM] * (...]
    ppermute x1 -> x34, waiting for transfers between devices: 10.9 us -> 40.7 us  [the longest x19 28.9 us: swap(): return lax.ppermute(value, axis, [(i, i ^ bit) for i in range(count)])]
    dot_general x34 -> x0, matrix products: 21.6 us -> none  [the longest x10 6.97 us: gram_of(): jnp.dot(row_block, row_block.T, precision=precise, preferred_element_type...]
    unnamed x32 -> x22, local copies, waits for them, and re-layouts: 0.14 us -> 8.03 us
  transfers between devices with their start and end apart: 7 -> 34, of which waited for: 7 -> 14; matrix products, arithmetic and copies ran while one was open for 0% -> 0% of each run, Pallas kernels for 0% -> 0%
where the time goes in v1:
time: 138 us
  starting transfers between devices  48.8 us (35%)
  waiting for transfers between devices  40.7 us (29%)
  Pallas kernels  39.6 us (29%)
  local copies, waits for them, and re-layouts  8.03 us (6%)
    pallas_call x5, Pallas kernels, call(): pl.pallas_call(kernel, out_shape=out_shapes, in_specs=[SMEM] + [VMEM] * (...  37.9 us
    ppermute x19, waiting for transfers between devices, swap(): return lax.ppermute(value, axis, [(i, i ^ bit) for i in range(count)])  28.9 us
    ppermute x19, starting transfers between devices, swap(): return lax.ppermute(value, axis, [(i, i ^ bit) for i in range(count)])  24.5 us
    ppermute x15, starting transfers between devices, routed(): return lax.ppermute(value, ('section', 'dp', 'tensor'), pairs)  24.2 us
    ppermute x15, waiting for transfers between devices, routed(): return lax.ppermute(value, ('section', 'dp', 'tensor'), pairs)  11.8 us
    unnamed x22, local copies, waits for them, and re-layouts  8.03 us
  transfers between devices with their start and end apart: 34, of which 14 were waited for; matrix products, arithmetic and copies ran while one was open for 0% of the time, Pallas kernels for 0%

profile of v1, /device:TPU:0, one launch (start us, length us, event | category | flops | bytes accessed | tf_op | source)
XLA Modules:
  0.0 138.0 jit_solution(16751852726017830493)
XLA Ops:
  0.7 1.0 copy-done
  1.8 1.0 copy-done.1
  2.8 0.9 copy-done.3
  3.8 0.9 copy-done.4
  4.7 0.9 copy-done.5
  5.7 0.9 copy-done.6
  6.6 0.7 shard_map.93
  7.3 3.1 %collective-permute-start.8 = (bf16[128,256]{1,0:T(8,128)(2,1)S(1)}, bf16[128,256]{1,0:T(8,128)(2,1)S(1)}, u32[]{:S(2)}, u32[]{:S(2)}) collective-permute-start(bf16[128,256]{1,0:T(8,128)(2,1)S(1)} %get-tuple-element.45), channel_id=1, source_target_pairs={{0,4},{1,5},{2,6},{3,7},{4,0},{5,1},{6,2},{7,3},{8,12},{9,13},{10,... | collective-permute-start | bytes 196616 | tf_op jit(solution)/shard_map/ppermute | solution.py:95
  10.4 2.6 %collective-permute-start.9 = (bf16[128,256]{1,0:T(8,128)(2,1)S(1)}, bf16[128,256]{1,0:T(8,128)(2,1)S(1)}, u32[]{:S(2)}, u32[]{:S(2)}) collective-permute-start(bf16[128,256]{1,0:T(8,128)(2,1)S(1)} %get-tuple-element.46), channel_id=1, source_target_pairs={{0,8},{1,9},{2,10},{3,11},{4,12},{5,13},{6,14},{7,15},{8,0},{9,1},... | collective-permute-start | bytes 196616 | tf_op jit(solution)/shard_map/ppermute | solution.py:95
  13.0 1.7 %collective-permute-start.11 = (bf16[128,256]{1,0:T(8,128)(2,1)S(1)}, bf16[128,256]{1,0:T(8,128)(2,1)S(1)}, u32[]{:S(2)}, u32[]{:S(2)}) collective-permute-start(bf16[128,256]{1,0:T(8,128)(2,1)S(1)} %get-tuple-element.48), channel_id=1, source_target_pairs={{0,2},{1,3},{2,0},{3,1},{4,6},{5,7},{6,4},{7,5},{8,10},{9,11},{10,... | collective-permute-start | bytes 196616 | tf_op jit(solution)/shard_map/ppermute | solution.py:95
  15.4 4.5 %collective-permute-start.13 = (bf16[128,256]{1,0:T(8,128)(2,1)S(1)}, bf16[128,256]{1,0:T(8,128)(2,1)S(1)}, u32[]{:S(2)}, u32[]{:S(2)}) collective-permute-start(bf16[128,256]{1,0:T(8,128)(2,1)S(1)} %get-tuple-element.50), channel_id=1, source_target_pairs={{0,10},{1,11},{2,8},{3,9},{4,14},{5,15},{6,12},{7,13},{8,2},{9,3},... | collective-permute-start | bytes 196616 | tf_op jit(solution)/shard_map/ppermute | solution.py:95
  19.8 0.7 collective-permute-start
  20.6 1.8 %collective-permute-start.2 = (bf16[128,512]{1,0:T(8,128)(2,1)S(1)}, bf16[128,512]{1,0:T(8,128)(2,1)S(1)}, u32[]{:S(2)}, u32[]{:S(2)}) collective-permute-start(bf16[128,512]{1,0:T(8,128)(2,1)S(1)} %get-tuple-element.38), channel_id=1, source_target_pairs={{0,8},{1,9},{2,26},{3,27},{4,12},{5,13},{6,30},{7,31},{8,0},{9,1},... | collective-permute-start | bytes 393224 | tf_op jit(solution)/shard_map/ppermute | solution.py:95
  22.3 5.3 %collective-permute-start.15 = (bf16[64,768]{1,0:T(8,128)(2,1)S(1)}, bf16[64,768]{1,0:T(8,128)(2,1)S(1)}, u32[]{:S(2)}, u32[]{:S(2)}) collective-permute-start(bf16[64,768]{1,0:T(8,128)(2,1)S(1)} %get-tuple-element.53), channel_id=1, source_target_pairs={{0,2},{1,3},{2,0},{3,1},{4,6},{5,7},{6,4},{7,5},{8,10},{9,11},{10,... | collective-permute-start | bytes 294920 | tf_op jit(solution)/shard_map/ppermute | solution.py:82
  27.7 0.9 collective-permute-start.14
  28.6 6.8 %collective-permute-done.14.refs_15_ = bf16[128,256]{1,0:T(8,128)(2,1)S(1)} collective-permute-done((bf16[128,256]{1,0:T(8,128)(2,1)S(1)}, bf16[128,256]{1,0:T(8,128)(2,1)S(1)}, u32[]{:S(2)}, u32[]{:S(2)}) %collective-permute-start.14) | collective-permute-done | bytes 65568 | tf_op jit(solution)/shard_map/ppermute | solution.py:95
  35.4 0.7 collective-permute-start.3
  36.1 1.0 collective-permute-start.4
  37.1 3.9 %collective-permute-start.6 = (bf16[128,512]{1,0:T(8,128)(2,1)S(1)}, bf16[128,512]{1,0:T(8,128)(2,1)S(1)}, u32[]{:S(2)}, u32[]{:S(2)}) collective-permute-start(bf16[128,512]{1,0:T(8,128)(2,1)S(1)} %get-tuple-element.42), channel_id=1, source_target_pairs={{0,26},{1,27},{2,8},{3,9},{4,30},{5,31},{6,12},{7,13},{8,18},{9,19... | collective-permute-start | bytes 393224 | tf_op jit(solution)/shard_map/ppermute | solution.py:95
  41.0 2.8 %collective-permute-start.7 = (bf16[128,512]{1,0:T(8,128)(2,1)S(1)}, bf16[128,512]{1,0:T(8,128)(2,1)S(1)}, u32[]{:S(2)}, u32[]{:S(2)}) collective-permute-start(bf16[128,512]{1,0:T(8,128)(2,1)S(1)} %get-tuple-element.43), channel_id=1, source_target_pairs={{0,30},{1,31},{2,12},{3,13},{4,26},{5,27},{6,8},{7,9},{8,22},{9,23... | collective-permute-start | bytes 393224 | tf_op jit(solution)/shard_map/ppermute | solution.py:95
  43.8 2.1 %collective-permute-done.5.refs_5_ = bf16[128,512]{1,0:T(8,128)(2,1)S(1)} collective-permute-done((bf16[128,512]{1,0:T(8,128)(2,1)S(1)}, bf16[128,512]{1,0:T(8,128)(2,1)S(1)}, u32[]{:S(2)}, u32[]{:S(2)}) %collective-permute-start.5) | collective-permute-done | bytes 131104 | tf_op jit(solution)/shard_map/ppermute | solution.py:95
  45.8 1.5 %collective-permute-done.6.refs_6_ = bf16[128,512]{1,0:T(8,128)(2,1)S(1)} collective-permute-done((bf16[128,512]{1,0:T(8,128)(2,1)S(1)}, bf16[128,512]{1,0:T(8,128)(2,1)S(1)}, u32[]{:S(2)}, u32[]{:S(2)}) %collective-permute-start.6) | collective-permute-done | bytes 131104 | tf_op jit(solution)/shard_map/ppermute | solution.py:95
  47.3 1.5 %collective-permute-done.7.refs_7_ = bf16[128,512]{1,0:T(8,128)(2,1)S(1)} collective-permute-done((bf16[128,512]{1,0:T(8,128)(2,1)S(1)}, bf16[128,512]{1,0:T(8,128)(2,1)S(1)}, u32[]{:S(2)}, u32[]{:S(2)}) %collective-permute-start.7) | collective-permute-done | bytes 131104 | tf_op jit(solution)/shard_map/ppermute | solution.py:95
  48.8 2.4 %shard_map.94 = (bf16[512,1024]{1,0:T(8,128)(2,1)S(1)}, bf16[512,512]{1,0:T(8,128)(2,1)S(1)}, bf16[12,128,128]{2,1,0:T(8,128)(2,1)S(1)}, bf16[12,128,128]{2,1,0:T(8,128)(2,1)S(1)}) custom-call(s32[3]{0:T(128)S(1)} %pad_add_fusion.idx, bf16[128,512]{1,0:T(8,128)(2,1)S(1)} %collective-permute-done.refs_0_, ...), custom_call_target="tpu_custom_call" | custom-call | tf_op jit(solution)/shard_map/pallas_call | solution.py:310
  51.3 1.7 %collective-permute-done.16.got = bf16[12,128,128]{2,1,0:T(8,128)(2,1)S(1)} collective-permute-done((bf16[12,128,128]{2,1,0:T(8,128)(2,1)S(1)}, bf16[12,128,128]{2,1,0:T(8,128)(2,1)S(1)}, u32[]{:S(2)}, u32[]{:S(2)}) %collective-permute-start.16) | collective-permute-done | bytes 393248 | tf_op jit(solution)/shard_map/ppermute | solution.py:82
  53.0 0.6 shard_map.95
  54.3 2.7 %collective-permute-start.17 = (bf16[3,128,128]{2,1,0:T(8,128)(2,1)S(1)}, bf16[3,128,128]{2,1,0:T(8,128)(2,1)S(1)}, u32[]{:S(2)}, u32[]{:S(2)}) collective-permute-start(bf16[3,128,128]{2,1,0:T(8,128)(2,1)S(1)} %get-tuple-element.57), channel_id=1, source_target_pairs={{0,4},{4,0},{8,12},{12,8},{1,5},{5,1},{9,13},{13,9},{2,6},{6,2},{1... | collective-permute-start | bytes 294920 | tf_op jit(solution)/shard_map/ppermute | solution.py:82
  57.5 1.9 %collective-permute-start.19 = (bf16[3,128,128]{2,1,0:T(8,128)(2,1)S(1)}, bf16[3,128,128]{2,1,0:T(8,128)(2,1)S(1)}, u32[]{:S(2)}, u32[]{:S(2)}) collective-permute-start(bf16[3,128,128]{2,1,0:T(8,128)(2,1)S(1)} %get-tuple-element.59), channel_id=1, source_target_pairs={{0,12},{4,8},{8,4},{12,0},{1,13},{5,9},{9,5},{13,1},{2,14},{6,10},... | collective-permute-start | bytes 294920 | tf_op jit(solution)/shard_map/ppermute | solution.py:82
  59.4 0.8 collective-permute-done.17.refs_1_
  60.2 7.4 %collective-permute-done.18.refs_2_ = bf16[3,128,128]{2,1,0:T(8,128)(2,1)S(1)} collective-permute-done((bf16[3,128,128]{2,1,0:T(8,128)(2,1)S(1)}, bf16[3,128,128]{2,1,0:T(8,128)(2,1)S(1)}, u32[]{:S(2)}, u32[]{:S(2)}) %collective-permute-start.18) | collective-permute-done | bytes 98336 | tf_op jit(solution)/shard_map/ppermute | solution.py:82
  68.2 1.7 %shard_map.96.refs_0_ = bf16[3,128,128]{2,1,0:T(8,128)(2,1)} custom-call(bf16[3,128,128]{2,1,0:T(8,128)(2,1)} %copy-done.7, bf16[3,128,128]{2,1,0:T(8,128)(2,1)} %copy-done.8, bf16[3,128,128]{2,1,0:T(8,128)(2,1)} %copy-done.9, bf16[3,128,128]{2,1,0:T(8,128)(2,1)} %copy-done.10), custom_call_target="tpu_custom_call" | custom-call | tf_op jit(solution)/shard_map/pallas_call | solution.py:370
  70.0 1.9 %collective-permute-start.22 = (bf16[3,128,128]{2,1,0:T(8,128)(2,1)}, bf16[3,128,128]{2,1,0:T(8,128)(2,1)S(1)}, u32[]{:S(2)}, u32[]{:S(2)}) collective-permute-start(bf16[3,128,128]{2,1,0:T(8,128)(2,1)} %shard_map.96.refs_0_), channel_id=1, source_target_pairs={{0,12},{4,8},{8,4},{12,0},{1,13},{5,9},{9,5},{13,1},{2,14},{6,10},... | collective-permute-start | bytes 294920 | tf_op jit(solution)/shard_map/ppermute | solution.py:82
  71.9 1.3 collective-permute-start.21
  73.2 1.2 collective-permute-start.20
  74.4 3.3 %collective-permute-done.22.refs_3_ = bf16[3,128,128]{2,1,0:T(8,128)(2,1)S(1)} collective-permute-done((bf16[3,128,128]{2,1,0:T(8,128)(2,1)}, bf16[3,128,128]{2,1,0:T(8,128)(2,1)S(1)}, u32[]{:S(2)}, u32[]{:S(2)}) %collective-permute-start.22) | collective-permute-done | bytes 98336 | tf_op jit(solution)/shard_map/ppermute | solution.py:82
  77.6 3.1 %collective-permute-done.21.refs_2_ = bf16[3,128,128]{2,1,0:T(8,128)(2,1)S(1)} collective-permute-done((bf16[3,128,128]{2,1,0:T(8,128)(2,1)}, bf16[3,128,128]{2,1,0:T(8,128)(2,1)S(1)}, u32[]{:S(2)}, u32[]{:S(2)}) %collective-permute-start.21) | collective-permute-done | bytes 98336 | tf_op jit(solution)/shard_map/ppermute | solution.py:82
  81.3 0.8 collective-permute-done.25.refs_6_
  82.2 0.9 copy-done.2
  83.1 32.4 %shard_map.97 = (bf16[64,768]{1,0:T(8,128)(2,1)S(1)}, bf16[64,768]{1,0:T(8,128)(2,1)S(1)}) custom-call(s32[3]{0:T(128)S(1)} %pad_add_fusion.idx, bf16[3,128,128]{2,1,0:T(8,128)(2,1)S(1)} %copy-done.2, bf16[3,128,128]{2,1,0:T(8,128)(2,1)S(1)} %collective-permute-done.20.refs_1_, bf16[3,128,128]{2,1,0:T(8,128)(2,1)S(1)} %collective-permute-done.21.refs_2_, ...), custom_call_target="tpu_custom_call" | custom-call | tf_op jit(solution)/shard_map/pallas_call | solution.py:310
  115.6 1.6 %collective-permute-start.30 = (bf16[64,768]{1,0:T(8,128)(2,1)S(1)}, bf16[64,768]{1,0:T(8,128)(2,1)S(1)}, u32[]{:S(2)}, u32[]{:S(2)}) collective-permute-start(bf16[64,768]{1,0:T(8,128)(2,1)S(1)} %get-tuple-element.63), channel_id=1, source_target_pairs={{0,2},{1,3},{2,0},{3,1},{4,6},{5,7},{6,4},{7,5},{8,10},{9,11},{10,... | collective-permute-start | bytes 294920 | tf_op jit(solution)/shard_map/ppermute | solution.py:82
  117.2 1.9 %collective-permute-start.29 = (bf16[64,768]{1,0:T(8,128)(2,1)S(1)}, bf16[64,768]{1,0:T(8,128)(2,1)S(1)}, u32[]{:S(2)}, u32[]{:S(2)}) collective-permute-start(bf16[64,768]{1,0:T(8,128)(2,1)S(1)} %get-tuple-element.62.refs_0_), channel_id=1, source_target_pairs={{0,12},{4,8},{8,4},{12,0},{1,13},{5,9},{9,5},{13,1},{2,14},{6,10},... | collective-permute-start | bytes 294920 | tf_op jit(solution)/shard_map/ppermute | solution.py:82
  119.1 2.5 %collective-permute-start.27 = (bf16[64,768]{1,0:T(8,128)(2,1)S(1)}, bf16[64,768]{1,0:T(8,128)(2,1)S(1)}, u32[]{:S(2)}, u32[]{:S(2)}) collective-permute-start(bf16[64,768]{1,0:T(8,128)(2,1)S(1)} %get-tuple-element.62.refs_0_), channel_id=1, source_target_pairs={{0,4},{4,0},{8,12},{12,8},{1,5},{5,1},{9,13},{13,9},{2,6},{6,2},{1... | collective-permute-start | bytes 294920 | tf_op jit(solution)/shard_map/ppermute | solution.py:82
  121.6 1.9 %collective-permute-start.33 = (bf16[64,768]{1,0:T(8,128)(2,1)S(1)}, bf16[64,768]{1,0:T(8,128)(2,1)S(1)}, u32[]{:S(2)}, u32[]{:S(2)}) collective-permute-start(bf16[64,768]{1,0:T(8,128)(2,1)S(1)} %collective-permute-done.30.refs_4_), channel_id=1, source_target_pairs={{0,12},{4,8},{8,4},{12,0},{1,13},{5,9},{9,5},{13,1},{2,14},{6,10},... | collective-permute-start | bytes 294920 | tf_op jit(solution)/shard_map/ppermute | solution.py:82
  123.5 1.2 collective-permute-done.29.refs_3_
  124.7 1.2 collective-permute-start.31
  126.0 5.5 %collective-permute-done.28.refs_2_ = bf16[64,768]{1,0:T(8,128)(2,1)S(1)} collective-permute-done((bf16[64,768]{1,0:T(8,128)(2,1)S(1)}, bf16[64,768]{1,0:T(8,128)(2,1)S(1)}, u32[]{:S(2)}, u32[]{:S(2)}) %collective-permute-start.28) | collective-permute-done | bytes 98336 | tf_op jit(solution)/shard_map/ppermute | solution.py:82
  131.4 5.0 %collective-permute-done.32.refs_6_ = bf16[64,768]{1,0:T(8,128)(2,1)S(1)} collective-permute-done((bf16[64,768]{1,0:T(8,128)(2,1)S(1)}, bf16[64,768]{1,0:T(8,128)(2,1)S(1)}, u32[]{:S(2)}, u32[]{:S(2)}) %collective-permute-start.32) | collective-permute-done | bytes 98336 | tf_op jit(solution)/shard_map/ppermute | solution.py:82
  136.4 1.7 %shard_map.98 = (bf16[64,2048]{1,0:T(8,128)(2,1)}, f32[64,1024]{1,0:T(8,128)}, bf16[64,1024]{1,0:T(8,128)(2,1)}, f32[64,2048]{1,0:T(8,128)}) custom-call(s32[3]{0:T(128)S(1)} %pad_add_fusion.idx, bf16[64,768]{1,0:T(8,128)(2,1)S(1)} %get-tuple-element.62.refs_0_, bf16[64,768]{1,0:T(8,128)(2,1)S(1)} %collective-permute-done.27.refs_1_, ...), custom_call_target="tpu_custom_call" | custom-call | tf_op jit(solution)/shard_map/pallas_call | solution.py:310
  (49 shorter events, 3.4 us)
Async XLA Ops:
  0.7 1.0 copy-start
  1.8 1.0 copy-start.1
  2.8 0.9 copy-start.3
  3.8 0.9 copy-start.4
  4.7 0.9 copy-start.5
  5.7 0.9 copy-start.6
  7.3 8.0 %collective-permute-start.8 = (bf16[128,256]{1,0:T(8,128)(2,1)S(1)}, bf16[128,256]{1,0:T(8,128)(2,1)S(1)}, u32[]{:S(2)}, u32[]{:S(2)}) collective-permute-start(bf16[128,256]{1,0:T(8,128)(2,1)S(1)} %get-tuple-element.45), channel_id=1, source_target_pairs={{0,4},{1,5},{2,6},{3,7},{4,0},{5,1},{6,2},{7,3},{8,12},{9,13},{10,... | collective-permute-start | bytes 196616 | tf_op jit(solution)/shard_map/ppermute | solution.py:95
  10.4 9.4 %collective-permute-start.9 = (bf16[128,256]{1,0:T(8,128)(2,1)S(1)}, bf16[128,256]{1,0:T(8,128)(2,1)S(1)}, u32[]{:S(2)}, u32[]{:S(2)}) collective-permute-start(bf16[128,256]{1,0:T(8,128)(2,1)S(1)} %get-tuple-element.46), channel_id=1, source_target_pairs={{0,8},{1,9},{2,10},{3,11},{4,12},{5,13},{6,14},{7,15},{8,0},{9,1},... | collective-permute-start | bytes 196616 | tf_op jit(solution)/shard_map/ppermute | solution.py:95
  13.0 7.5 %collective-permute-start.10 = (bf16[128,256]{1,0:T(8,128)(2,1)S(1)}, bf16[128,256]{1,0:T(8,128)(2,1)S(1)}, u32[]{:S(2)}, u32[]{:S(2)}) collective-permute-start(bf16[128,256]{1,0:T(8,128)(2,1)S(1)} %get-tuple-element.47), channel_id=1, source_target_pairs={{0,12},{1,13},{2,14},{3,15},{4,8},{5,9},{6,10},{7,11},{8,4},{9,5},... | collective-permute-start | bytes 196616 | tf_op jit(solution)/shard_map/ppermute | solution.py:95
  13.0 7.6 %collective-permute-start.11 = (bf16[128,256]{1,0:T(8,128)(2,1)S(1)}, bf16[128,256]{1,0:T(8,128)(2,1)S(1)}, u32[]{:S(2)}, u32[]{:S(2)}) collective-permute-start(bf16[128,256]{1,0:T(8,128)(2,1)S(1)} %get-tuple-element.48), channel_id=1, source_target_pairs={{0,2},{1,3},{2,0},{3,1},{4,6},{5,7},{6,4},{7,5},{8,10},{9,11},{10,... | collective-permute-start | bytes 196616 | tf_op jit(solution)/shard_map/ppermute | solution.py:95
  14.7 7.6 %collective-permute-start.12 = (bf16[128,256]{1,0:T(8,128)(2,1)S(1)}, bf16[128,256]{1,0:T(8,128)(2,1)S(1)}, u32[]{:S(2)}, u32[]{:S(2)}) collective-permute-start(bf16[128,256]{1,0:T(8,128)(2,1)S(1)} %get-tuple-element.49), channel_id=1, source_target_pairs={{0,6},{1,7},{2,4},{3,5},{4,2},{5,3},{6,0},{7,1},{8,14},{9,15},{10,... | collective-permute-start | bytes 196616 | tf_op jit(solution)/shard_map/ppermute | solution.py:95
  15.4 12.3 %collective-permute-start.13 = (bf16[128,256]{1,0:T(8,128)(2,1)S(1)}, bf16[128,256]{1,0:T(8,128)(2,1)S(1)}, u32[]{:S(2)}, u32[]{:S(2)}) collective-permute-start(bf16[128,256]{1,0:T(8,128)(2,1)S(1)} %get-tuple-element.50), channel_id=1, source_target_pairs={{0,10},{1,11},{2,8},{3,9},{4,14},{5,15},{6,12},{7,13},{8,2},{9,3},... | collective-permute-start | bytes 196616 | tf_op jit(solution)/shard_map/ppermute | solution.py:95
  19.8 17.3 %collective-permute-start = (bf16[128,512]{1,0:T(8,128)(2,1)S(1)}, bf16[128,512]{1,0:T(8,128)(2,1)S(1)}, u32[]{:S(2)}, u32[]{:S(2)}) collective-permute-start(bf16[128,512]{1,0:T(8,128)(2,1)S(1)} %get-tuple-element.36), channel_id=1, source_target_pairs={{0,0},{1,1},{2,18},{3,19},{4,4},{5,5},{6,22},{7,23},{8,8},{9,9},{1... | collective-permute-start | bytes 393224 | tf_op jit(solution)/shard_map/ppermute | solution.py:95
  20.5 16.6 %collective-permute-start.1 = (bf16[128,512]{1,0:T(8,128)(2,1)S(1)}, bf16[128,512]{1,0:T(8,128)(2,1)S(1)}, u32[]{:S(2)}, u32[]{:S(2)}) collective-permute-start(bf16[128,512]{1,0:T(8,128)(2,1)S(1)} %get-tuple-element.37), channel_id=1, source_target_pairs={{0,4},{1,5},{2,22},{3,23},{4,0},{5,1},{6,18},{7,19},{8,12},{9,13},... | collective-permute-start | bytes 393224 | tf_op jit(solution)/shard_map/ppermute | solution.py:95
  20.6 20.4 %collective-permute-start.2 = (bf16[128,512]{1,0:T(8,128)(2,1)S(1)}, bf16[128,512]{1,0:T(8,128)(2,1)S(1)}, u32[]{:S(2)}, u32[]{:S(2)}) collective-permute-start(bf16[128,512]{1,0:T(8,128)(2,1)S(1)} %get-tuple-element.38), channel_id=1, source_target_pairs={{0,8},{1,9},{2,26},{3,27},{4,12},{5,13},{6,30},{7,31},{8,0},{9,1},... | collective-permute-start | bytes 393224 | tf_op jit(solution)/shard_map/ppermute | solution.py:95
  22.3 13.8 %collective-permute-start.15 = (bf16[64,768]{1,0:T(8,128)(2,1)S(1)}, bf16[64,768]{1,0:T(8,128)(2,1)S(1)}, u32[]{:S(2)}, u32[]{:S(2)}) collective-permute-start(bf16[64,768]{1,0:T(8,128)(2,1)S(1)} %get-tuple-element.53), channel_id=1, source_target_pairs={{0,2},{1,3},{2,0},{3,1},{4,6},{5,7},{6,4},{7,5},{8,10},{9,11},{10,... | collective-permute-start | bytes 294920 | tf_op jit(solution)/shard_map/ppermute | solution.py:82
  27.7 7.7 %collective-permute-start.14 = (bf16[128,256]{1,0:T(8,128)(2,1)S(1)}, bf16[128,256]{1,0:T(8,128)(2,1)S(1)}, u32[]{:S(2)}, u32[]{:S(2)}) collective-permute-start(bf16[128,256]{1,0:T(8,128)(2,1)S(1)} %get-tuple-element.51), channel_id=1, source_target_pairs={{0,14},{1,15},{2,12},{3,13},{4,10},{5,11},{6,8},{7,9},{8,6},{9,7},... | collective-permute-start | bytes 196616 | tf_op jit(solution)/shard_map/ppermute | solution.py:95
  35.4 8.4 %collective-permute-start.3 = (bf16[128,512]{1,0:T(8,128)(2,1)S(1)}, bf16[128,512]{1,0:T(8,128)(2,1)S(1)}, u32[]{:S(2)}, u32[]{:S(2)}) collective-permute-start(bf16[128,512]{1,0:T(8,128)(2,1)S(1)} %get-tuple-element.39), channel_id=1, source_target_pairs={{0,12},{1,13},{2,30},{3,31},{4,8},{5,9},{6,26},{7,27},{8,4},{9,5},... | collective-permute-start | bytes 393224 | tf_op jit(solution)/shard_map/ppermute | solution.py:95
  36.1 7.7 %collective-permute-start.4 = (bf16[128,512]{1,0:T(8,128)(2,1)S(1)}, bf16[128,512]{1,0:T(8,128)(2,1)S(1)}, u32[]{:S(2)}, u32[]{:S(2)}) collective-permute-start(bf16[128,512]{1,0:T(8,128)(2,1)S(1)} %get-tuple-element.40), channel_id=1, source_target_pairs={{0,18},{1,19},{2,0},{3,1},{4,22},{5,23},{6,4},{7,5},{8,26},{9,27},... | collective-permute-start | bytes 393224 | tf_op jit(solution)/shard_map/ppermute | solution.py:95
  37.1 8.7 %collective-permute-start.5 = (bf16[128,512]{1,0:T(8,128)(2,1)S(1)}, bf16[128,512]{1,0:T(8,128)(2,1)S(1)}, u32[]{:S(2)}, u32[]{:S(2)}) collective-permute-start(bf16[128,512]{1,0:T(8,128)(2,1)S(1)} %get-tuple-element.41), channel_id=1, source_target_pairs={{0,22},{1,23},{2,4},{3,5},{4,18},{5,19},{6,0},{7,1},{8,30},{9,31},... | collective-permute-start | bytes 393224 | tf_op jit(solution)/shard_map/ppermute | solution.py:95
  37.1 10.2 %collective-permute-start.6 = (bf16[128,512]{1,0:T(8,128)(2,1)S(1)}, bf16[128,512]{1,0:T(8,128)(2,1)S(1)}, u32[]{:S(2)}, u32[]{:S(2)}) collective-permute-start(bf16[128,512]{1,0:T(8,128)(2,1)S(1)} %get-tuple-element.42), channel_id=1, source_target_pairs={{0,26},{1,27},{2,8},{3,9},{4,30},{5,31},{6,12},{7,13},{8,18},{9,19... | collective-permute-start | bytes 393224 | tf_op jit(solution)/shard_map/ppermute | solution.py:95
  41.0 7.8 %collective-permute-start.7 = (bf16[128,512]{1,0:T(8,128)(2,1)S(1)}, bf16[128,512]{1,0:T(8,128)(2,1)S(1)}, u32[]{:S(2)}, u32[]{:S(2)}) collective-permute-start(bf16[128,512]{1,0:T(8,128)(2,1)S(1)} %get-tuple-element.43), channel_id=1, source_target_pairs={{0,30},{1,31},{2,12},{3,13},{4,26},{5,27},{6,8},{7,9},{8,22},{9,23... | collective-permute-start | bytes 393224 | tf_op jit(solution)/shard_map/ppermute | solution.py:95
  51.2 1.8 %collective-permute-start.16 = (bf16[12,128,128]{2,1,0:T(8,128)(2,1)S(1)}, bf16[12,128,128]{2,1,0:T(8,128)(2,1)S(1)}, u32[]{:S(2)}, u32[]{:S(2)}) collective-permute-start(bf16[12,128,128]{2,1,0:T(8,128)(2,1)S(1)} %get-tuple-element.55), channel_id=1, source_target_pairs={{0,1},{1,0},{2,3},{3,2},{4,5},{5,4},{6,7},{7,6},{8,9},{9,8},{10,11... | collective-permute-start | bytes 1179656 | tf_op jit(solution)/shard_map/ppermute | solution.py:82
  53.7 0.6 copy-start.7
  54.3 5.9 %collective-permute-start.17 = (bf16[3,128,128]{2,1,0:T(8,128)(2,1)S(1)}, bf16[3,128,128]{2,1,0:T(8,128)(2,1)S(1)}, u32[]{:S(2)}, u32[]{:S(2)}) collective-permute-start(bf16[3,128,128]{2,1,0:T(8,128)(2,1)S(1)} %get-tuple-element.57), channel_id=1, source_target_pairs={{0,4},{4,0},{8,12},{12,8},{1,5},{5,1},{9,13},{13,9},{2,6},{6,2},{1... | collective-permute-start | bytes 294920 | tf_op jit(solution)/shard_map/ppermute | solution.py:82
  57.0 10.6 %collective-permute-start.18 = (bf16[3,128,128]{2,1,0:T(8,128)(2,1)S(1)}, bf16[3,128,128]{2,1,0:T(8,128)(2,1)S(1)}, u32[]{:S(2)}, u32[]{:S(2)}) collective-permute-start(bf16[3,128,128]{2,1,0:T(8,128)(2,1)S(1)} %get-tuple-element.58), channel_id=1, source_target_pairs={{0,8},{4,12},{8,0},{12,4},{1,9},{5,13},{9,1},{13,5},{2,10},{6,14},... | collective-permute-start | bytes 294920 | tf_op jit(solution)/shard_map/ppermute | solution.py:82
  57.5 10.0 %collective-permute-start.19 = (bf16[3,128,128]{2,1,0:T(8,128)(2,1)S(1)}, bf16[3,128,128]{2,1,0:T(8,128)(2,1)S(1)}, u32[]{:S(2)}, u32[]{:S(2)}) collective-permute-start(bf16[3,128,128]{2,1,0:T(8,128)(2,1)S(1)} %get-tuple-element.59), channel_id=1, source_target_pairs={{0,12},{4,8},{8,4},{12,0},{1,13},{5,9},{9,5},{13,1},{2,14},{6,10},... | collective-permute-start | bytes 294920 | tf_op jit(solution)/shard_map/ppermute | solution.py:82
  60.2 7.4 %copy-start.8 = (bf16[3,128,128]{2,1,0:T(8,128)(2,1)}, bf16[3,128,128]{2,1,0:T(8,128)(2,1)S(1)}, u32[]{:S(2)}) copy-start(bf16[3,128,128]{2,1,0:T(8,128)(2,1)S(1)} %collective-permute-done.17.refs_1_) | copy-start | bytes 294916
  67.6 0.6 copy-start.9
  67.6 0.7 copy-start.10
  70.0 7.7 %collective-permute-start.22 = (bf16[3,128,128]{2,1,0:T(8,128)(2,1)}, bf16[3,128,128]{2,1,0:T(8,128)(2,1)S(1)}, u32[]{:S(2)}, u32[]{:S(2)}) collective-permute-start(bf16[3,128,128]{2,1,0:T(8,128)(2,1)} %shard_map.96.refs_0_), channel_id=1, source_target_pairs={{0,12},{4,8},{8,4},{12,0},{1,13},{5,9},{9,5},{13,1},{2,14},{6,10},... | collective-permute-start | bytes 294920 | tf_op jit(solution)/shard_map/ppermute | solution.py:82
  71.9 8.9 %collective-permute-start.21 = (bf16[3,128,128]{2,1,0:T(8,128)(2,1)}, bf16[3,128,128]{2,1,0:T(8,128)(2,1)S(1)}, u32[]{:S(2)}, u32[]{:S(2)}) collective-permute-start(bf16[3,128,128]{2,1,0:T(8,128)(2,1)} %shard_map.96.refs_0_), channel_id=1, source_target_pairs={{0,8},{4,12},{8,0},{12,4},{1,9},{5,13},{9,1},{13,5},{2,10},{6,14},... | collective-permute-start | bytes 294920 | tf_op jit(solution)/shard_map/ppermute | solution.py:82
  73.2 7.6 %collective-permute-start.20 = (bf16[3,128,128]{2,1,0:T(8,128)(2,1)}, bf16[3,128,128]{2,1,0:T(8,128)(2,1)S(1)}, u32[]{:S(2)}, u32[]{:S(2)}) collective-permute-start(bf16[3,128,128]{2,1,0:T(8,128)(2,1)} %shard_map.96.refs_0_), channel_id=1, source_target_pairs={{0,4},{4,0},{8,12},{12,8},{1,5},{5,1},{9,13},{13,9},{2,6},{6,2},{1... | collective-permute-start | bytes 294920 | tf_op jit(solution)/shard_map/ppermute | solution.py:82
  74.4 6.9 %collective-permute-start.23 = (bf16[3,128,128]{2,1,0:T(8,128)(2,1)}, bf16[3,128,128]{2,1,0:T(8,128)(2,1)S(1)}, u32[]{:S(2)}, u32[]{:S(2)}) collective-permute-start(bf16[3,128,128]{2,1,0:T(8,128)(2,1)} %shard_map.96.refs_0_), channel_id=1, source_target_pairs={{0,1},{1,0},{2,3},{3,2},{4,5},{5,4},{6,7},{7,6},{8,9},{9,8},{10,11... | collective-permute-start | bytes 294920 | tf_op jit(solution)/shard_map/ppermute | solution.py:82
  77.6 3.7 %collective-permute-start.26 = (bf16[3,128,128]{2,1,0:T(8,128)(2,1)S(1)}, bf16[3,128,128]{2,1,0:T(8,128)(2,1)S(1)}, u32[]{:S(2)}, u32[]{:S(2)}) collective-permute-start(bf16[3,128,128]{2,1,0:T(8,128)(2,1)S(1)} %collective-permute-done.22.refs_3_), channel_id=1, source_target_pairs={{0,1},{1,0},{2,3},{3,2},{4,5},{5,4},{6,7},{7,6},{8,9},{9,8},{10,11... | collective-permute-start | bytes 294920 | tf_op jit(solution)/shard_map/ppermute | solution.py:82
  80.8 1.3 collective-permute-start.25
  80.8 1.5 %collective-permute-start.24 = (bf16[3,128,128]{2,1,0:T(8,128)(2,1)S(1)}, bf16[3,128,128]{2,1,0:T(8,128)(2,1)S(1)}, u32[]{:S(2)}, u32[]{:S(2)}) collective-permute-start(bf16[3,128,128]{2,1,0:T(8,128)(2,1)S(1)} %collective-permute-done.20.refs_1_), channel_id=1, source_target_pairs={{0,1},{1,0},{2,3},{3,2},{4,5},{5,4},{6,7},{7,6},{8,9},{9,8},{10,11... | collective-permute-start | bytes 294920 | tf_op jit(solution)/shard_map/ppermute | solution.py:82
  82.2 0.9 copy-start.2
  115.6 6.0 %collective-permute-start.30 = (bf16[64,768]{1,0:T(8,128)(2,1)S(1)}, bf16[64,768]{1,0:T(8,128)(2,1)S(1)}, u32[]{:S(2)}, u32[]{:S(2)}) collective-permute-start(bf16[64,768]{1,0:T(8,128)(2,1)S(1)} %get-tuple-element.63), channel_id=1, source_target_pairs={{0,2},{1,3},{2,0},{3,1},{4,6},{5,7},{6,4},{7,5},{8,10},{9,11},{10,... | collective-permute-start | bytes 294920 | tf_op jit(solution)/shard_map/ppermute | solution.py:82
  117.2 7.5 %collective-permute-start.29 = (bf16[64,768]{1,0:T(8,128)(2,1)S(1)}, bf16[64,768]{1,0:T(8,128)(2,1)S(1)}, u32[]{:S(2)}, u32[]{:S(2)}) collective-permute-start(bf16[64,768]{1,0:T(8,128)(2,1)S(1)} %get-tuple-element.62.refs_0_), channel_id=1, source_target_pairs={{0,12},{4,8},{8,4},{12,0},{1,13},{5,9},{9,5},{13,1},{2,14},{6,10},... | collective-permute-start | bytes 294920 | tf_op jit(solution)/shard_map/ppermute | solution.py:82
  119.1 12.3 %collective-permute-start.28 = (bf16[64,768]{1,0:T(8,128)(2,1)S(1)}, bf16[64,768]{1,0:T(8,128)(2,1)S(1)}, u32[]{:S(2)}, u32[]{:S(2)}) collective-permute-start(bf16[64,768]{1,0:T(8,128)(2,1)S(1)} %get-tuple-element.62.refs_0_), channel_id=1, source_target_pairs={{0,8},{4,12},{8,0},{12,4},{1,9},{5,13},{9,1},{13,5},{2,10},{6,14},... | collective-permute-start | bytes 294920 | tf_op jit(solution)/shard_map/ppermute | solution.py:82
  119.1 12.3 %collective-permute-start.27 = (bf16[64,768]{1,0:T(8,128)(2,1)S(1)}, bf16[64,768]{1,0:T(8,128)(2,1)S(1)}, u32[]{:S(2)}, u32[]{:S(2)}) collective-permute-start(bf16[64,768]{1,0:T(8,128)(2,1)S(1)} %get-tuple-element.62.refs_0_), channel_id=1, source_target_pairs={{0,4},{4,0},{8,12},{12,8},{1,5},{5,1},{9,13},{13,9},{2,6},{6,2},{1... | collective-permute-start | bytes 294920 | tf_op jit(solution)/shard_map/ppermute | solution.py:82
  121.6 9.9 %collective-permute-start.33 = (bf16[64,768]{1,0:T(8,128)(2,1)S(1)}, bf16[64,768]{1,0:T(8,128)(2,1)S(1)}, u32[]{:S(2)}, u32[]{:S(2)}) collective-permute-start(bf16[64,768]{1,0:T(8,128)(2,1)S(1)} %collective-permute-done.30.refs_4_), channel_id=1, source_target_pairs={{0,12},{4,8},{8,4},{12,0},{1,13},{5,9},{9,5},{13,1},{2,14},{6,10},... | collective-permute-start | bytes 294920 | tf_op jit(solution)/shard_map/ppermute | solution.py:82
  123.5 12.9 %collective-permute-start.32 = (bf16[64,768]{1,0:T(8,128)(2,1)S(1)}, bf16[64,768]{1,0:T(8,128)(2,1)S(1)}, u32[]{:S(2)}, u32[]{:S(2)}) collective-permute-start(bf16[64,768]{1,0:T(8,128)(2,1)S(1)} %collective-permute-done.30.refs_4_), channel_id=1, source_target_pairs={{0,8},{4,12},{8,0},{12,4},{1,9},{5,13},{9,1},{13,5},{2,10},{6,14},... | collective-permute-start | bytes 294920 | tf_op jit(solution)/shard_map/ppermute | solution.py:82
  124.7 11.7 %collective-permute-start.31 = (bf16[64,768]{1,0:T(8,128)(2,1)S(1)}, bf16[64,768]{1,0:T(8,128)(2,1)S(1)}, u32[]{:S(2)}, u32[]{:S(2)}) collective-permute-start(bf16[64,768]{1,0:T(8,128)(2,1)S(1)} %collective-permute-done.30.refs_4_), channel_id=1, source_target_pairs={{0,4},{4,0},{8,12},{12,8},{1,5},{5,1},{9,13},{13,9},{2,6},{6,2},{1... | collective-permute-start | bytes 294920 | tf_op jit(solution)/shard_map/ppermute | solution.py:82

commit v2 on v1

--- a/solution.py
+++ b/solution.py
@@ -95,48 +95,40 @@
     return lax.ppermute(value, ("section", "dp", "tensor"), pairs)
 
 
-def pack_kernel(dps, idx, norm, grad, attn, hand, sk_q, sk_o, *outs):
+def pack_kernel(dps, idx, norm, grad, attn, hand, sk_q, sk_o, *refs):
     z, out_half = idx[0], idx[1]
-    big_w, small_w = norm.shape[1] // dps, grad.shape[1] // dps
-    own_big, oth_big = outs[:dps], outs[dps : 2 * dps]
-    own_small, oth_small = outs[2 * dps : 3 * dps], outs[3 * dps : 4 * dps]
+    outs, sems = refs[:-1], refs[-1]
+    big_w, small_w = outs[0].shape[1], outs[2 * dps].shape[1]
     own_sk, oth_sk = outs[4 * dps :]
-    for d in range(dps):
-        at = z ^ d
-        bigs = pl.ds(pl.multiple_of(at * big_w, big_w), big_w)
-        smalls = pl.ds(pl.multiple_of(at * small_w, small_w), small_w)
-
-        @pl.when(out_half == 0)
-        def _():
-            own_big[d][...] = norm[:, bigs]
-            oth_big[d][...] = hand[:, bigs]
-            own_small[d][...] = grad[:, smalls]
-            oth_small[d][...] = attn[:, smalls]
-
-        @pl.when(out_half == 1)
-        def _():
-            own_big[d][...] = hand[:, bigs]
-            oth_big[d][...] = norm[:, bigs]
-            own_small[d][...] = attn[:, smalls]
-            oth_small[d][...] = grad[:, smalls]
-
-    bigs = pl.ds(pl.multiple_of(z * big_w, big_w), big_w)
-    smalls = pl.ds(pl.multiple_of(z * small_w, small_w), small_w)
-    for_o, for_q = sk_o[:, bigs], sk_q[:, smalls]
+
+    def window(ref, width, at):
+        return ref.at[:, pl.ds(pl.multiple_of(at * width, width), width)]
+
+    def move(own_wide, oth_wide, own_thin, oth_thin, sk_wide, sk_thin):
+        pairs = []
+        for n, (ref, width) in enumerate(
+            ((own_wide, big_w), (oth_wide, big_w), (own_thin, small_w), (oth_thin, small_w))
+        ):
+            pairs += [(window(ref, width, z ^ d), outs[n * dps + d]) for d in range(dps)]
+        pairs.append((window(sk_o, big_w, z), sk_wide.at[:, :big_w]))
+        pairs.append((window(sk_q, small_w, z), sk_thin.at[:, big_w:]))
+        copies = [
+            pltpu.make_async_copy(src, dst, sems.at[n]) for n, (src, dst) in enumerate(pairs)
+        ]
+        for c in copies:
+            c.start()
+        sk_wide[:, big_w:] = jnp.zeros((sk_wide.shape[0], small_w), bf16)
+        sk_thin[:, :big_w] = jnp.zeros((sk_thin.shape[0], big_w), bf16)
+        for c in copies:
+            c.wait()
 
     @pl.when(out_half == 0)
     def _():
-        own_sk[:, :big_w] = jnp.zeros_like(for_o)
-        own_sk[:, big_w:] = for_q
-        oth_sk[:, :big_w] = for_o
-        oth_sk[:, big_w:] = jnp.zeros_like(for_q)
+        move(norm, hand, grad, attn, oth_sk, own_sk)
 
     @pl.when(out_half == 1)
     def _():
-        own_sk[:, :big_w] = for_o
-        own_sk[:, big_w:] = jnp.zeros_like(for_q)
-        oth_sk[:, :big_w] = jnp.zeros_like(for_o)
-        oth_sk[:, big_w:] = for_q
+        move(hand, norm, attn, grad, own_sk, oth_sk)
 
 
 def nt(a, b, precision=None):
@@ -200,32 +192,69 @@
 
 
 def inverse_factor(gram):
-    n = gram.shape[0]
+    n, nb = gram.shape[0], 8
     rows = lax.broadcasted_iota(jnp.int32, (n, n), 0)
     cols = lax.broadcasted_iota(jnp.int32, (n, n), 1)
-    eye = (rows == cols).astype(f32)
-    work = jnp.concatenate([gram, eye], axis=1)
-    slabs = [work[8 * s : 8 * s + 8, :] for s in range(n // 8)]
-    sub = lax.broadcasted_iota(jnp.int32, (8, 2 * n), 0)
-    for k in range(n):
-        s0, r0 = divmod(k, 8)
-        pivot_row = slabs[s0][r0 : r0 + 1, :]
-        scaled = pivot_row * (1.0 / pivot_row[:, k : k + 1])
-        for s in range(s0, n // 8):
-            col = slabs[s][:, k : k + 1]
-            new = slabs[s] - col * scaled
-            slabs[s] = jnp.where(sub > r0, new, slabs[s]) if s == s0 else new
-    work = jnp.concatenate(slabs, axis=0)
-    pivots = jnp.sum(work[:, :n] * eye, axis=1, keepdims=True)
-    return work[:, n:] * lax.rsqrt(pivots)
+    work = jnp.concatenate([(rows == cols).astype(f32), gram], axis=1)
+    count = n // nb
+    slabs = [work[nb * s : nb * s + nb, :] for s in range(count)]
+    sub = lax.broadcasted_iota(jnp.int32, (nb, 2 * n), 0)
+
+    def lane(x, k):
+        return jnp.broadcast_to(x[:, n + k : n + k + 1], (nb, 2 * n))
+
+    def row(x, i):
+        return jnp.broadcast_to(x[i : i + 1, :], (nb, 2 * n))
+
+    done = []
+    for b in range(count):
+        cols_of = [lane(slabs[b], nb * b + j) for j in range(nb)]
+        pivot_rows = [row(slabs[b], i) for i in range(nb)]
+        splat = [[row(cols_of[j], i) for j in range(i + 1)] for i in range(nb)]
+        below = {s: [lane(slabs[s], nb * b + j) for j in range(nb)] for s in range(b + 1, count)}
+        out = None
+        for k in range(nb):
+            inv = 1.0 / splat[k][k]
+            at = pivot_rows[k]
+            final = at * lax.rsqrt(splat[k][k])
+            out = final if out is None else jnp.where(sub == k, final, out)
+            for i in range(k + 1, nb):
+                mult = splat[i][k] * inv
+                for j in range(k + 1, i + 1):
+                    splat[i][j] = splat[i][j] - mult * splat[j][k]
+                pivot_rows[i] = pivot_rows[i] - mult * at
+            for s in range(b + 1, count):
+                mult = below[s][k] * inv
+                for j in range(k + 1, nb):
+                    below[s][j] = below[s][j] - mult * splat[j][k]
+                slabs[s] = slabs[s] - mult * at
+        done.append(out)
+    return jnp.concatenate(done, axis=0)[:, :n]
+
+
+def split(x):
+    high = x.astype(bf16)
+    return high, (x - high.astype(f32)).astype(bf16)
 
 
 def times(rows, gram):
-    high = rows.astype(bf16)
-    low = (rows - high.astype(f32)).astype(bf16)
-    return jnp.dot(high, gram, preferred_element_type=f32) + jnp.dot(
-        low, gram, preferred_element_type=f32
-    )
+    n = rows.shape[0]
+    both = jnp.dot(jnp.concatenate(split(rows), axis=0), gram, preferred_element_type=f32)
+    return both[:n] + both[n:]
+
+
+def product(a, b):
+    (ah, al), (bh, bl) = split(a), split(b)
+    return jnp.dot(
+        jnp.concatenate([ah, ah, al], axis=1),
+        jnp.concatenate([bh, bl, bh], axis=0),
+        preferred_element_type=f32,
+    )
+
+
+def product_nt(a, b):
+    (ah, al), (bh, bl) = split(a), split(b)
+    return nt(jnp.concatenate([ah, ah, al], axis=1), jnp.concatenate([bh, bl, bh], axis=1))
 
 
 def chain_kernel(dps, counts, idx, *refs):
@@ -258,13 +287,23 @@
         ],
         axis=1,
     ).astype(f32)
-    for step in range(2 * POWER + 1):
-        gram = left if step % 2 == 0 else right
-        ahead = times(rows, gram[...])
-        low_inv = inverse_factor(nt(ahead, rows, precise))
-        basis = rows
-        rows = jnp.dot(low_inv, ahead, precision=precise, preferred_element_type=f32)
-    basis = jnp.dot(low_inv, basis, precision=precise, preferred_element_type=f32)
+    ahead = times(rows, left[...])
+    gram = product_nt(ahead, rows)
+    for step in range(2 * POWER):
+        following = (right if step % 2 == 0 else left)[...]
+        beyond = times(ahead, following)
+        inner = product_nt(beyond, ahead)
+        low_inv = inverse_factor(gram)
+        rows = product(low_inv, ahead)
+        if step < 2 * POWER - 1:
+            gram = product_nt(product(low_inv, inner), low_inv)
+            ahead = product(low_inv, beyond)
+        else:
+            ahead = times(rows, following)
+            gram = product_nt(ahead, rows)
+    low_inv = inverse_factor(gram)
+    basis = product(low_inv, rows)
+    rows = product(low_inv, ahead)
     energy = jnp.sum(times(rows, right[...]) * rows)
     count = jnp.where(out_half == 1, counts[0], counts[1]).astype(f32)
     scale = lax.rsqrt(jnp.full((1, 1), energy, f32) / count + 1e-06)
@@ -306,11 +345,11 @@
                 b_o[:, smalls] = output[:, big_w:]
 
 
-def call(kernel, out_shapes, args, scratch=()):
+def call(kernel, out_shapes, args, scratch=(), space=VMEM):
     outs = pl.pallas_call(
         kernel,
         out_shape=out_shapes,
-        in_specs=[SMEM] + [VMEM] * (len(args) - 1),
+        in_specs=[SMEM] + [space] * (len(args) - 1),
         out_specs=jax.tree.map(lambda _: VMEM, out_shapes),
         scratch_shapes=list(scratch),
         compiler_params=pltpu.CompilerParams(vmem_limit_bytes=48 * 2**20),
@@ -333,6 +372,8 @@
         + [shape((BLK, small_w))] * (2 * dps)
         + [shape((RANK, big_w + small_w))] * 2,
         (idx, norm_in[0], query_grad[0], attn_out[0], handed[0], sketch_q[0], sketch_o[0]),
+        [pltpu.SemaphoreType.DMA((4 * dps + 2,))],
+        pl.BlockSpec(memory_space=pl.ANY),
     )
     own_big, oth_big = packed[:dps], packed[dps : 2 * dps]
     own_small, oth_small = packed[2 * dps : 3 * dps], packed[3 * dps : 4 * dps]

time: 138 us -> 119 us (0.86)
  Pallas kernels: 39.6 us -> 20.2 us
    pallas_call x5, Pallas kernels: 37.9 us -> 18.5 us  [call(): pl.pallas_call(kernel, out_shape=out_shapes, in_specs=[SMEM] + [space] *...]
where the time goes in v2:
time: 119 us
  starting transfers between devices  48.8 us (41%)
  waiting for transfers between devices  40.7 us (34%)
  Pallas kernels  20.2 us (17%)
  local copies, waits for them, and re-layouts  8.03 us (7%)
    ppermute x19, waiting for transfers between devices, swap(): return lax.ppermute(value, axis, [(i, i ^ bit) for i in range(count)])  28.9 us
    ppermute x19, starting transfers between devices, swap(): return lax.ppermute(value, axis, [(i, i ^ bit) for i in range(count)])  24.6 us
    ppermute x15, starting transfers between devices, routed(): return lax.ppermute(value, ('section', 'dp', 'tensor'), pairs)  24.2 us
    pallas_call x5, Pallas kernels, call(): pl.pallas_call(kernel, out_shape=out_shapes, in_specs=[SMEM] + [space] *...  18.5 us
    ppermute x15, waiting for transfers between devices, routed(): return lax.ppermute(value, ('section', 'dp', 'tensor'), pairs)  11.8 us
    unnamed x22, local copies, waits for them, and re-layouts  8.03 us
  transfers between devices with their start and end apart: 34, of which 14 were waited for; matrix products, arithmetic and copies ran while one was open for 0% of the time, Pallas kernels for 0%

profile of v2, /device:TPU:0, one launch (start us, length us, event | category | flops | bytes accessed | tf_op | source)
XLA Modules:
  0.0 118.7 jit_solution(6942928732727372279)
XLA Ops:
  0.7 1.0 copy-done
  1.8 1.0 copy-done.1
  2.8 0.9 copy-done.3
  3.8 0.9 copy-done.4
  4.7 0.9 copy-done.5
  5.7 0.9 copy-done.6
  6.6 1.1 shard_map.93
  7.6 3.1 %collective-permute-start.8 = (bf16[128,256]{1,0:T(8,128)(2,1)S(1)}, bf16[128,256]{1,0:T(8,128)(2,1)S(1)}, u32[]{:S(2)}, u32[]{:S(2)}) collective-permute-start(bf16[128,256]{1,0:T(8,128)(2,1)S(1)} %get-tuple-element.45), channel_id=1, source_target_pairs={{0,4},{1,5},{2,6},{3,7},{4,0},{5,1},{6,2},{7,3},{8,12},{9,13},{10,... | collective-permute-start | bytes 196616 | tf_op jit(solution)/shard_map/ppermute | solution.py:95
  10.7 2.6 %collective-permute-start.9 = (bf16[128,256]{1,0:T(8,128)(2,1)S(1)}, bf16[128,256]{1,0:T(8,128)(2,1)S(1)}, u32[]{:S(2)}, u32[]{:S(2)}) collective-permute-start(bf16[128,256]{1,0:T(8,128)(2,1)S(1)} %get-tuple-element.46), channel_id=1, source_target_pairs={{0,8},{1,9},{2,10},{3,11},{4,12},{5,13},{6,14},{7,15},{8,0},{9,1},... | collective-permute-start | bytes 196616 | tf_op jit(solution)/shard_map/ppermute | solution.py:95
  13.3 1.7 %collective-permute-start.11 = (bf16[128,256]{1,0:T(8,128)(2,1)S(1)}, bf16[128,256]{1,0:T(8,128)(2,1)S(1)}, u32[]{:S(2)}, u32[]{:S(2)}) collective-permute-start(bf16[128,256]{1,0:T(8,128)(2,1)S(1)} %get-tuple-element.48), channel_id=1, source_target_pairs={{0,2},{1,3},{2,0},{3,1},{4,6},{5,7},{6,4},{7,5},{8,10},{9,11},{10,... | collective-permute-start | bytes 196616 | tf_op jit(solution)/shard_map/ppermute | solution.py:95
  15.7 4.5 %collective-permute-start.13 = (bf16[128,256]{1,0:T(8,128)(2,1)S(1)}, bf16[128,256]{1,0:T(8,128)(2,1)S(1)}, u32[]{:S(2)}, u32[]{:S(2)}) collective-permute-start(bf16[128,256]{1,0:T(8,128)(2,1)S(1)} %get-tuple-element.50), channel_id=1, source_target_pairs={{0,10},{1,11},{2,8},{3,9},{4,14},{5,15},{6,12},{7,13},{8,2},{9,3},... | collective-permute-start | bytes 196616 | tf_op jit(solution)/shard_map/ppermute | solution.py:95
  20.1 0.7 collective-permute-start
  20.9 1.8 %collective-permute-start.2 = (bf16[128,512]{1,0:T(8,128)(2,1)S(1)}, bf16[128,512]{1,0:T(8,128)(2,1)S(1)}, u32[]{:S(2)}, u32[]{:S(2)}) collective-permute-start(bf16[128,512]{1,0:T(8,128)(2,1)S(1)} %get-tuple-element.38), channel_id=1, source_target_pairs={{0,8},{1,9},{2,26},{3,27},{4,12},{5,13},{6,30},{7,31},{8,0},{9,1},... | collective-permute-start | bytes 393224 | tf_op jit(solution)/shard_map/ppermute | solution.py:95
  22.7 5.3 %collective-permute-start.15 = (bf16[64,768]{1,0:T(8,128)(2,1)S(1)}, bf16[64,768]{1,0:T(8,128)(2,1)S(1)}, u32[]{:S(2)}, u32[]{:S(2)}) collective-permute-start(bf16[64,768]{1,0:T(8,128)(2,1)S(1)} %get-tuple-element.53), channel_id=1, source_target_pairs={{0,2},{1,3},{2,0},{3,1},{4,6},{5,7},{6,4},{7,5},{8,10},{9,11},{10,... | collective-permute-start | bytes 294920 | tf_op jit(solution)/shard_map/ppermute | solution.py:82
  28.0 0.9 collective-permute-start.14
  28.9 6.8 %collective-permute-done.14.refs_15_ = bf16[128,256]{1,0:T(8,128)(2,1)S(1)} collective-permute-done((bf16[128,256]{1,0:T(8,128)(2,1)S(1)}, bf16[128,256]{1,0:T(8,128)(2,1)S(1)}, u32[]{:S(2)}, u32[]{:S(2)}) %collective-permute-start.14) | collective-permute-done | bytes 65568 | tf_op jit(solution)/shard_map/ppermute | solution.py:95
  35.7 0.7 collective-permute-start.3
  36.4 1.0 collective-permute-start.4
  37.5 3.9 %collective-permute-start.6 = (bf16[128,512]{1,0:T(8,128)(2,1)S(1)}, bf16[128,512]{1,0:T(8,128)(2,1)S(1)}, u32[]{:S(2)}, u32[]{:S(2)}) collective-permute-start(bf16[128,512]{1,0:T(8,128)(2,1)S(1)} %get-tuple-element.42), channel_id=1, source_target_pairs={{0,26},{1,27},{2,8},{3,9},{4,30},{5,31},{6,12},{7,13},{8,18},{9,19... | collective-permute-start | bytes 393224 | tf_op jit(solution)/shard_map/ppermute | solution.py:95
  41.3 2.8 %collective-permute-start.7 = (bf16[128,512]{1,0:T(8,128)(2,1)S(1)}, bf16[128,512]{1,0:T(8,128)(2,1)S(1)}, u32[]{:S(2)}, u32[]{:S(2)}) collective-permute-start(bf16[128,512]{1,0:T(8,128)(2,1)S(1)} %get-tuple-element.43), channel_id=1, source_target_pairs={{0,30},{1,31},{2,12},{3,13},{4,26},{5,27},{6,8},{7,9},{8,22},{9,23... | collective-permute-start | bytes 393224 | tf_op jit(solution)/shard_map/ppermute | solution.py:95
  44.1 2.1 %collective-permute-done.5.refs_5_ = bf16[128,512]{1,0:T(8,128)(2,1)S(1)} collective-permute-done((bf16[128,512]{1,0:T(8,128)(2,1)S(1)}, bf16[128,512]{1,0:T(8,128)(2,1)S(1)}, u32[]{:S(2)}, u32[]{:S(2)}) %collective-permute-start.5) | collective-permute-done | bytes 131104 | tf_op jit(solution)/shard_map/ppermute | solution.py:95
  46.1 1.5 %collective-permute-done.6.refs_6_ = bf16[128,512]{1,0:T(8,128)(2,1)S(1)} collective-permute-done((bf16[128,512]{1,0:T(8,128)(2,1)S(1)}, bf16[128,512]{1,0:T(8,128)(2,1)S(1)}, u32[]{:S(2)}, u32[]{:S(2)}) %collective-permute-start.6) | collective-permute-done | bytes 131104 | tf_op jit(solution)/shard_map/ppermute | solution.py:95
  47.6 1.5 %collective-permute-done.7.refs_7_ = bf16[128,512]{1,0:T(8,128)(2,1)S(1)} collective-permute-done((bf16[128,512]{1,0:T(8,128)(2,1)S(1)}, bf16[128,512]{1,0:T(8,128)(2,1)S(1)}, u32[]{:S(2)}, u32[]{:S(2)}) %collective-permute-start.7) | collective-permute-done | bytes 131104 | tf_op jit(solution)/shard_map/ppermute | solution.py:95
  49.1 2.4 %shard_map.94 = (bf16[512,1024]{1,0:T(8,128)(2,1)S(1)}, bf16[512,512]{1,0:T(8,128)(2,1)S(1)}, bf16[12,128,128]{2,1,0:T(8,128)(2,1)S(1)}, bf16[12,128,128]{2,1,0:T(8,128)(2,1)S(1)}) custom-call(s32[3]{0:T(128)S(1)} %pad_add_fusion.idx, bf16[128,512]{1,0:T(8,128)(2,1)S(1)} %collective-permute-done.refs_0_, ...), custom_call_target="tpu_custom_call" | custom-call | tf_op jit(solution)/shard_map/pallas_call | solution.py:349
  51.6 1.7 %collective-permute-done.16.got = bf16[12,128,128]{2,1,0:T(8,128)(2,1)S(1)} collective-permute-done((bf16[12,128,128]{2,1,0:T(8,128)(2,1)S(1)}, bf16[12,128,128]{2,1,0:T(8,128)(2,1)S(1)}, u32[]{:S(2)}, u32[]{:S(2)}) %collective-permute-start.16) | collective-permute-done | bytes 393248 | tf_op jit(solution)/shard_map/ppermute | solution.py:82
  53.3 0.6 shard_map.95
  54.6 2.7 %collective-permute-start.17 = (bf16[3,128,128]{2,1,0:T(8,128)(2,1)S(1)}, bf16[3,128,128]{2,1,0:T(8,128)(2,1)S(1)}, u32[]{:S(2)}, u32[]{:S(2)}) collective-permute-start(bf16[3,128,128]{2,1,0:T(8,128)(2,1)S(1)} %get-tuple-element.57), channel_id=1, source_target_pairs={{0,4},{4,0},{8,12},{12,8},{1,5},{5,1},{9,13},{13,9},{2,6},{6,2},{1... | collective-permute-start | bytes 294920 | tf_op jit(solution)/shard_map/ppermute | solution.py:82
  57.8 1.9 %collective-permute-start.19 = (bf16[3,128,128]{2,1,0:T(8,128)(2,1)S(1)}, bf16[3,128,128]{2,1,0:T(8,128)(2,1)S(1)}, u32[]{:S(2)}, u32[]{:S(2)}) collective-permute-start(bf16[3,128,128]{2,1,0:T(8,128)(2,1)S(1)} %get-tuple-element.59), channel_id=1, source_target_pairs={{0,12},{4,8},{8,4},{12,0},{1,13},{5,9},{9,5},{13,1},{2,14},{6,10},... | collective-permute-start | bytes 294920 | tf_op jit(solution)/shard_map/ppermute | solution.py:82
  59.7 0.8 collective-permute-done.17.refs_1_
  60.5 7.4 %collective-permute-done.18.refs_2_ = bf16[3,128,128]{2,1,0:T(8,128)(2,1)S(1)} collective-permute-done((bf16[3,128,128]{2,1,0:T(8,128)(2,1)S(1)}, bf16[3,128,128]{2,1,0:T(8,128)(2,1)S(1)}, u32[]{:S(2)}, u32[]{:S(2)}) %collective-permute-start.18) | collective-permute-done | bytes 98336 | tf_op jit(solution)/shard_map/ppermute | solution.py:82
  68.6 1.7 %shard_map.96.refs_0_ = bf16[3,128,128]{2,1,0:T(8,128)(2,1)} custom-call(bf16[3,128,128]{2,1,0:T(8,128)(2,1)} %copy-done.7, bf16[3,128,128]{2,1,0:T(8,128)(2,1)} %copy-done.8, bf16[3,128,128]{2,1,0:T(8,128)(2,1)} %copy-done.9, bf16[3,128,128]{2,1,0:T(8,128)(2,1)} %copy-done.10), custom_call_target="tpu_custom_call" | custom-call | tf_op jit(solution)/shard_map/pallas_call | solution.py:411
  70.3 1.9 %collective-permute-start.22 = (bf16[3,128,128]{2,1,0:T(8,128)(2,1)}, bf16[3,128,128]{2,1,0:T(8,128)(2,1)S(1)}, u32[]{:S(2)}, u32[]{:S(2)}) collective-permute-start(bf16[3,128,128]{2,1,0:T(8,128)(2,1)} %shard_map.96.refs_0_), channel_id=1, source_target_pairs={{0,12},{4,8},{8,4},{12,0},{1,13},{5,9},{9,5},{13,1},{2,14},{6,10},... | collective-permute-start | bytes 294920 | tf_op jit(solution)/shard_map/ppermute | solution.py:82
  72.2 1.3 %collective-permute-start.21 = (bf16[3,128,128]{2,1,0:T(8,128)(2,1)}, bf16[3,128,128]{2,1,0:T(8,128)(2,1)S(1)}, u32[]{:S(2)}, u32[]{:S(2)}) collective-permute-start(bf16[3,128,128]{2,1,0:T(8,128)(2,1)} %shard_map.96.refs_0_), channel_id=1, source_target_pairs={{0,8},{4,12},{8,0},{12,4},{1,9},{5,13},{9,1},{13,5},{2,10},{6,14},... | collective-permute-start | bytes 294920 | tf_op jit(solution)/shard_map/ppermute | solution.py:82
  73.5 1.2 collective-permute-start.20
  74.7 3.3 %collective-permute-done.22.refs_3_ = bf16[3,128,128]{2,1,0:T(8,128)(2,1)S(1)} collective-permute-done((bf16[3,128,128]{2,1,0:T(8,128)(2,1)}, bf16[3,128,128]{2,1,0:T(8,128)(2,1)S(1)}, u32[]{:S(2)}, u32[]{:S(2)}) %collective-permute-start.22) | collective-permute-done | bytes 98336 | tf_op jit(solution)/shard_map/ppermute | solution.py:82
  78.0 3.1 %collective-permute-done.21.refs_2_ = bf16[3,128,128]{2,1,0:T(8,128)(2,1)S(1)} collective-permute-done((bf16[3,128,128]{2,1,0:T(8,128)(2,1)}, bf16[3,128,128]{2,1,0:T(8,128)(2,1)S(1)}, u32[]{:S(2)}, u32[]{:S(2)}) %collective-permute-start.21) | collective-permute-done | bytes 98336 | tf_op jit(solution)/shard_map/ppermute | solution.py:82
  81.6 0.8 collective-permute-done.25.refs_6_
  82.5 0.9 copy-done.2
  83.4 12.7 %shard_map.97 = (bf16[64,768]{1,0:T(8,128)(2,1)S(1)}, bf16[64,768]{1,0:T(8,128)(2,1)S(1)}) custom-call(s32[3]{0:T(128)S(1)} %pad_add_fusion.idx, bf16[3,128,128]{2,1,0:T(8,128)(2,1)S(1)} %copy-done.2, bf16[3,128,128]{2,1,0:T(8,128)(2,1)S(1)} %collective-permute-done.20.refs_1_, bf16[3,128,128]{2,1,0:T(8,128)(2,1)S(1)} %collective-permute-done.21.refs_2_, ...), custom_call_target="tpu_custom_call" | custom-call | tf_op jit(solution)/shard_map/pallas_call | solution.py:349
  96.2 1.6 %collective-permute-start.30 = (bf16[64,768]{1,0:T(8,128)(2,1)S(1)}, bf16[64,768]{1,0:T(8,128)(2,1)S(1)}, u32[]{:S(2)}, u32[]{:S(2)}) collective-permute-start(bf16[64,768]{1,0:T(8,128)(2,1)S(1)} %get-tuple-element.63), channel_id=1, source_target_pairs={{0,2},{1,3},{2,0},{3,1},{4,6},{5,7},{6,4},{7,5},{8,10},{9,11},{10,... | collective-permute-start | bytes 294920 | tf_op jit(solution)/shard_map/ppermute | solution.py:82
  97.8 1.9 %collective-permute-start.29 = (bf16[64,768]{1,0:T(8,128)(2,1)S(1)}, bf16[64,768]{1,0:T(8,128)(2,1)S(1)}, u32[]{:S(2)}, u32[]{:S(2)}) collective-permute-start(bf16[64,768]{1,0:T(8,128)(2,1)S(1)} %get-tuple-element.62.refs_0_), channel_id=1, source_target_pairs={{0,12},{4,8},{8,4},{12,0},{1,13},{5,9},{9,5},{13,1},{2,14},{6,10},... | collective-permute-start | bytes 294920 | tf_op jit(solution)/shard_map/ppermute | solution.py:82
  99.7 2.5 %collective-permute-start.27 = (bf16[64,768]{1,0:T(8,128)(2,1)S(1)}, bf16[64,768]{1,0:T(8,128)(2,1)S(1)}, u32[]{:S(2)}, u32[]{:S(2)}) collective-permute-start(bf16[64,768]{1,0:T(8,128)(2,1)S(1)} %get-tuple-element.62.refs_0_), channel_id=1, source_target_pairs={{0,4},{4,0},{8,12},{12,8},{1,5},{5,1},{9,13},{13,9},{2,6},{6,2},{1... | collective-permute-start | bytes 294920 | tf_op jit(solution)/shard_map/ppermute | solution.py:82
  102.2 1.9 %collective-permute-start.33 = (bf16[64,768]{1,0:T(8,128)(2,1)S(1)}, bf16[64,768]{1,0:T(8,128)(2,1)S(1)}, u32[]{:S(2)}, u32[]{:S(2)}) collective-permute-start(bf16[64,768]{1,0:T(8,128)(2,1)S(1)} %collective-permute-done.30.refs_4_), channel_id=1, source_target_pairs={{0,12},{4,8},{8,4},{12,0},{1,13},{5,9},{9,5},{13,1},{2,14},{6,10},... | collective-permute-start | bytes 294920 | tf_op jit(solution)/shard_map/ppermute | solution.py:82
  104.1 1.2 %collective-permute-done.29.refs_3_ = bf16[64,768]{1,0:T(8,128)(2,1)S(1)} collective-permute-done((bf16[64,768]{1,0:T(8,128)(2,1)S(1)}, bf16[64,768]{1,0:T(8,128)(2,1)S(1)}, u32[]{:S(2)}, u32[]{:S(2)}) %collective-permute-start.29) | collective-permute-done | bytes 98336 | tf_op jit(solution)/shard_map/ppermute | solution.py:82
  105.3 1.2 %collective-permute-start.31 = (bf16[64,768]{1,0:T(8,128)(2,1)S(1)}, bf16[64,768]{1,0:T(8,128)(2,1)S(1)}, u32[]{:S(2)}, u32[]{:S(2)}) collective-permute-start(bf16[64,768]{1,0:T(8,128)(2,1)S(1)} %collective-permute-done.30.refs_4_), channel_id=1, source_target_pairs={{0,4},{4,0},{8,12},{12,8},{1,5},{5,1},{9,13},{13,9},{2,6},{6,2},{1... | collective-permute-start | bytes 294920 | tf_op jit(solution)/shard_map/ppermute | solution.py:82
  106.6 5.5 %collective-permute-done.28.refs_2_ = bf16[64,768]{1,0:T(8,128)(2,1)S(1)} collective-permute-done((bf16[64,768]{1,0:T(8,128)(2,1)S(1)}, bf16[64,768]{1,0:T(8,128)(2,1)S(1)}, u32[]{:S(2)}, u32[]{:S(2)}) %collective-permute-start.28) | collective-permute-done | bytes 98336 | tf_op jit(solution)/shard_map/ppermute | solution.py:82
  112.0 5.0 %collective-permute-done.32.refs_6_ = bf16[64,768]{1,0:T(8,128)(2,1)S(1)} collective-permute-done((bf16[64,768]{1,0:T(8,128)(2,1)S(1)}, bf16[64,768]{1,0:T(8,128)(2,1)S(1)}, u32[]{:S(2)}, u32[]{:S(2)}) %collective-permute-start.32) | collective-permute-done | bytes 98336 | tf_op jit(solution)/shard_map/ppermute | solution.py:82
  117.0 1.7 %shard_map.98 = (bf16[64,2048]{1,0:T(8,128)(2,1)}, f32[64,1024]{1,0:T(8,128)}, bf16[64,1024]{1,0:T(8,128)(2,1)}, f32[64,2048]{1,0:T(8,128)}) custom-call(s32[3]{0:T(128)S(1)} %pad_add_fusion.idx, bf16[64,768]{1,0:T(8,128)(2,1)S(1)} %get-tuple-element.62.refs_0_, bf16[64,768]{1,0:T(8,128)(2,1)S(1)} %collective-permute-done.27.refs_1_, ...), custom_call_target="tpu_custom_call" | custom-call | tf_op jit(solution)/shard_map/pallas_call | solution.py:349
  (49 shorter events, 3.4 us)
Async XLA Ops:
  0.7 1.0 copy-start
  1.8 1.0 copy-start.1
  2.8 0.9 copy-start.3
  3.8 0.9 copy-start.4
  4.7 0.9 copy-start.5
  5.7 0.9 copy-start.6
  7.6 8.0 %collective-permute-start.8 = (bf16[128,256]{1,0:T(8,128)(2,1)S(1)}, bf16[128,256]{1,0:T(8,128)(2,1)S(1)}, u32[]{:S(2)}, u32[]{:S(2)}) collective-permute-start(bf16[128,256]{1,0:T(8,128)(2,1)S(1)} %get-tuple-element.45), channel_id=1, source_target_pairs={{0,4},{1,5},{2,6},{3,7},{4,0},{5,1},{6,2},{7,3},{8,12},{9,13},{10,... | collective-permute-start | bytes 196616 | tf_op jit(solution)/shard_map/ppermute | solution.py:95
  10.7 9.4 %collective-permute-start.9 = (bf16[128,256]{1,0:T(8,128)(2,1)S(1)}, bf16[128,256]{1,0:T(8,128)(2,1)S(1)}, u32[]{:S(2)}, u32[]{:S(2)}) collective-permute-start(bf16[128,256]{1,0:T(8,128)(2,1)S(1)} %get-tuple-element.46), channel_id=1, source_target_pairs={{0,8},{1,9},{2,10},{3,11},{4,12},{5,13},{6,14},{7,15},{8,0},{9,1},... | collective-permute-start | bytes 196616 | tf_op jit(solution)/shard_map/ppermute | solution.py:95
  13.3 7.5 %collective-permute-start.10 = (bf16[128,256]{1,0:T(8,128)(2,1)S(1)}, bf16[128,256]{1,0:T(8,128)(2,1)S(1)}, u32[]{:S(2)}, u32[]{:S(2)}) collective-permute-start(bf16[128,256]{1,0:T(8,128)(2,1)S(1)} %get-tuple-element.47), channel_id=1, source_target_pairs={{0,12},{1,13},{2,14},{3,15},{4,8},{5,9},{6,10},{7,11},{8,4},{9,5},... | collective-permute-start | bytes 196616 | tf_op jit(solution)/shard_map/ppermute | solution.py:95
  13.3 7.6 %collective-permute-start.11 = (bf16[128,256]{1,0:T(8,128)(2,1)S(1)}, bf16[128,256]{1,0:T(8,128)(2,1)S(1)}, u32[]{:S(2)}, u32[]{:S(2)}) collective-permute-start(bf16[128,256]{1,0:T(8,128)(2,1)S(1)} %get-tuple-element.48), channel_id=1, source_target_pairs={{0,2},{1,3},{2,0},{3,1},{4,6},{5,7},{6,4},{7,5},{8,10},{9,11},{10,... | collective-permute-start | bytes 196616 | tf_op jit(solution)/shard_map/ppermute | solution.py:95
  15.1 7.6 %collective-permute-start.12 = (bf16[128,256]{1,0:T(8,128)(2,1)S(1)}, bf16[128,256]{1,0:T(8,128)(2,1)S(1)}, u32[]{:S(2)}, u32[]{:S(2)}) collective-permute-start(bf16[128,256]{1,0:T(8,128)(2,1)S(1)} %get-tuple-element.49), channel_id=1, source_target_pairs={{0,6},{1,7},{2,4},{3,5},{4,2},{5,3},{6,0},{7,1},{8,14},{9,15},{10,... | collective-permute-start | bytes 196616 | tf_op jit(solution)/shard_map/ppermute | solution.py:95
  15.7 12.3 %collective-permute-start.13 = (bf16[128,256]{1,0:T(8,128)(2,1)S(1)}, bf16[128,256]{1,0:T(8,128)(2,1)S(1)}, u32[]{:S(2)}, u32[]{:S(2)}) collective-permute-start(bf16[128,256]{1,0:T(8,128)(2,1)S(1)} %get-tuple-element.50), channel_id=1, source_target_pairs={{0,10},{1,11},{2,8},{3,9},{4,14},{5,15},{6,12},{7,13},{8,2},{9,3},... | collective-permute-start | bytes 196616 | tf_op jit(solution)/shard_map/ppermute | solution.py:95
  20.1 17.3 %collective-permute-start = (bf16[128,512]{1,0:T(8,128)(2,1)S(1)}, bf16[128,512]{1,0:T(8,128)(2,1)S(1)}, u32[]{:S(2)}, u32[]{:S(2)}) collective-permute-start(bf16[128,512]{1,0:T(8,128)(2,1)S(1)} %get-tuple-element.36), channel_id=1, source_target_pairs={{0,0},{1,1},{2,18},{3,19},{4,4},{5,5},{6,22},{7,23},{8,8},{9,9},{1... | collective-permute-start | bytes 393224 | tf_op jit(solution)/shard_map/ppermute | solution.py:95
  20.8 16.6 %collective-permute-start.1 = (bf16[128,512]{1,0:T(8,128)(2,1)S(1)}, bf16[128,512]{1,0:T(8,128)(2,1)S(1)}, u32[]{:S(2)}, u32[]{:S(2)}) collective-permute-start(bf16[128,512]{1,0:T(8,128)(2,1)S(1)} %get-tuple-element.37), channel_id=1, source_target_pairs={{0,4},{1,5},{2,22},{3,23},{4,0},{5,1},{6,18},{7,19},{8,12},{9,13},... | collective-permute-start | bytes 393224 | tf_op jit(solution)/shard_map/ppermute | solution.py:95
  20.9 20.4 %collective-permute-start.2 = (bf16[128,512]{1,0:T(8,128)(2,1)S(1)}, bf16[128,512]{1,0:T(8,128)(2,1)S(1)}, u32[]{:S(2)}, u32[]{:S(2)}) collective-permute-start(bf16[128,512]{1,0:T(8,128)(2,1)S(1)} %get-tuple-element.38), channel_id=1, source_target_pairs={{0,8},{1,9},{2,26},{3,27},{4,12},{5,13},{6,30},{7,31},{8,0},{9,1},... | collective-permute-start | bytes 393224 | tf_op jit(solution)/shard_map/ppermute | solution.py:95
  22.7 13.8 %collective-permute-start.15 = (bf16[64,768]{1,0:T(8,128)(2,1)S(1)}, bf16[64,768]{1,0:T(8,128)(2,1)S(1)}, u32[]{:S(2)}, u32[]{:S(2)}) collective-permute-start(bf16[64,768]{1,0:T(8,128)(2,1)S(1)} %get-tuple-element.53), channel_id=1, source_target_pairs={{0,2},{1,3},{2,0},{3,1},{4,6},{5,7},{6,4},{7,5},{8,10},{9,11},{10,... | collective-permute-start | bytes 294920 | tf_op jit(solution)/shard_map/ppermute | solution.py:82
  28.0 7.7 %collective-permute-start.14 = (bf16[128,256]{1,0:T(8,128)(2,1)S(1)}, bf16[128,256]{1,0:T(8,128)(2,1)S(1)}, u32[]{:S(2)}, u32[]{:S(2)}) collective-permute-start(bf16[128,256]{1,0:T(8,128)(2,1)S(1)} %get-tuple-element.51), channel_id=1, source_target_pairs={{0,14},{1,15},{2,12},{3,13},{4,10},{5,11},{6,8},{7,9},{8,6},{9,7},... | collective-permute-start | bytes 196616 | tf_op jit(solution)/shard_map/ppermute | solution.py:95
  35.7 8.4 %collective-permute-start.3 = (bf16[128,512]{1,0:T(8,128)(2,1)S(1)}, bf16[128,512]{1,0:T(8,128)(2,1)S(1)}, u32[]{:S(2)}, u32[]{:S(2)}) collective-permute-start(bf16[128,512]{1,0:T(8,128)(2,1)S(1)} %get-tuple-element.39), channel_id=1, source_target_pairs={{0,12},{1,13},{2,30},{3,31},{4,8},{5,9},{6,26},{7,27},{8,4},{9,5},... | collective-permute-start | bytes 393224 | tf_op jit(solution)/shard_map/ppermute | solution.py:95
  36.4 7.7 %collective-permute-start.4 = (bf16[128,512]{1,0:T(8,128)(2,1)S(1)}, bf16[128,512]{1,0:T(8,128)(2,1)S(1)}, u32[]{:S(2)}, u32[]{:S(2)}) collective-permute-start(bf16[128,512]{1,0:T(8,128)(2,1)S(1)} %get-tuple-element.40), channel_id=1, source_target_pairs={{0,18},{1,19},{2,0},{3,1},{4,22},{5,23},{6,4},{7,5},{8,26},{9,27},... | collective-permute-start | bytes 393224 | tf_op jit(solution)/shard_map/ppermute | solution.py:95
  37.4 8.7 %collective-permute-start.5 = (bf16[128,512]{1,0:T(8,128)(2,1)S(1)}, bf16[128,512]{1,0:T(8,128)(2,1)S(1)}, u32[]{:S(2)}, u32[]{:S(2)}) collective-permute-start(bf16[128,512]{1,0:T(8,128)(2,1)S(1)} %get-tuple-element.41), channel_id=1, source_target_pairs={{0,22},{1,23},{2,4},{3,5},{4,18},{5,19},{6,0},{7,1},{8,30},{9,31},... | collective-permute-start | bytes 393224 | tf_op jit(solution)/shard_map/ppermute | solution.py:95
  37.5 10.2 %collective-permute-start.6 = (bf16[128,512]{1,0:T(8,128)(2,1)S(1)}, bf16[128,512]{1,0:T(8,128)(2,1)S(1)}, u32[]{:S(2)}, u32[]{:S(2)}) collective-permute-start(bf16[128,512]{1,0:T(8,128)(2,1)S(1)} %get-tuple-element.42), channel_id=1, source_target_pairs={{0,26},{1,27},{2,8},{3,9},{4,30},{5,31},{6,12},{7,13},{8,18},{9,19... | collective-permute-start | bytes 393224 | tf_op jit(solution)/shard_map/ppermute | solution.py:95
  41.3 7.8 %collective-permute-start.7 = (bf16[128,512]{1,0:T(8,128)(2,1)S(1)}, bf16[128,512]{1,0:T(8,128)(2,1)S(1)}, u32[]{:S(2)}, u32[]{:S(2)}) collective-permute-start(bf16[128,512]{1,0:T(8,128)(2,1)S(1)} %get-tuple-element.43), channel_id=1, source_target_pairs={{0,30},{1,31},{2,12},{3,13},{4,26},{5,27},{6,8},{7,9},{8,22},{9,23... | collective-permute-start | bytes 393224 | tf_op jit(solution)/shard_map/ppermute | solution.py:95
  51.5 1.8 %collective-permute-start.16 = (bf16[12,128,128]{2,1,0:T(8,128)(2,1)S(1)}, bf16[12,128,128]{2,1,0:T(8,128)(2,1)S(1)}, u32[]{:S(2)}, u32[]{:S(2)}) collective-permute-start(bf16[12,128,128]{2,1,0:T(8,128)(2,1)S(1)} %get-tuple-element.55), channel_id=1, source_target_pairs={{0,1},{1,0},{2,3},{3,2},{4,5},{5,4},{6,7},{7,6},{8,9},{9,8},{10,11... | collective-permute-start | bytes 1179656 | tf_op jit(solution)/shard_map/ppermute | solution.py:82
  54.0 0.6 copy-start.7
  54.6 5.9 %collective-permute-start.17 = (bf16[3,128,128]{2,1,0:T(8,128)(2,1)S(1)}, bf16[3,128,128]{2,1,0:T(8,128)(2,1)S(1)}, u32[]{:S(2)}, u32[]{:S(2)}) collective-permute-start(bf16[3,128,128]{2,1,0:T(8,128)(2,1)S(1)} %get-tuple-element.57), channel_id=1, source_target_pairs={{0,4},{4,0},{8,12},{12,8},{1,5},{5,1},{9,13},{13,9},{2,6},{6,2},{1... | collective-permute-start | bytes 294920 | tf_op jit(solution)/shard_map/ppermute | solution.py:82
  57.3 10.5 %collective-permute-start.18 = (bf16[3,128,128]{2,1,0:T(8,128)(2,1)S(1)}, bf16[3,128,128]{2,1,0:T(8,128)(2,1)S(1)}, u32[]{:S(2)}, u32[]{:S(2)}) collective-permute-start(bf16[3,128,128]{2,1,0:T(8,128)(2,1)S(1)} %get-tuple-element.58), channel_id=1, source_target_pairs={{0,8},{4,12},{8,0},{12,4},{1,9},{5,13},{9,1},{13,5},{2,10},{6,14},... | collective-permute-start | bytes 294920 | tf_op jit(solution)/shard_map/ppermute | solution.py:82
  57.8 10.0 %collective-permute-start.19 = (bf16[3,128,128]{2,1,0:T(8,128)(2,1)S(1)}, bf16[3,128,128]{2,1,0:T(8,128)(2,1)S(1)}, u32[]{:S(2)}, u32[]{:S(2)}) collective-permute-start(bf16[3,128,128]{2,1,0:T(8,128)(2,1)S(1)} %get-tuple-element.59), channel_id=1, source_target_pairs={{0,12},{4,8},{8,4},{12,0},{1,13},{5,9},{9,5},{13,1},{2,14},{6,10},... | collective-permute-start | bytes 294920 | tf_op jit(solution)/shard_map/ppermute | solution.py:82
  60.5 7.4 %copy-start.8 = (bf16[3,128,128]{2,1,0:T(8,128)(2,1)}, bf16[3,128,128]{2,1,0:T(8,128)(2,1)S(1)}, u32[]{:S(2)}) copy-start(bf16[3,128,128]{2,1,0:T(8,128)(2,1)S(1)} %collective-permute-done.17.refs_1_) | copy-start | bytes 294916
  67.9 0.6 copy-start.9
  67.9 0.7 copy-start.10
  70.3 7.7 %collective-permute-start.22 = (bf16[3,128,128]{2,1,0:T(8,128)(2,1)}, bf16[3,128,128]{2,1,0:T(8,128)(2,1)S(1)}, u32[]{:S(2)}, u32[]{:S(2)}) collective-permute-start(bf16[3,128,128]{2,1,0:T(8,128)(2,1)} %shard_map.96.refs_0_), channel_id=1, source_target_pairs={{0,12},{4,8},{8,4},{12,0},{1,13},{5,9},{9,5},{13,1},{2,14},{6,10},... | collective-permute-start | bytes 294920 | tf_op jit(solution)/shard_map/ppermute | solution.py:82
  72.2 8.9 %collective-permute-start.21 = (bf16[3,128,128]{2,1,0:T(8,128)(2,1)}, bf16[3,128,128]{2,1,0:T(8,128)(2,1)S(1)}, u32[]{:S(2)}, u32[]{:S(2)}) collective-permute-start(bf16[3,128,128]{2,1,0:T(8,128)(2,1)} %shard_map.96.refs_0_), channel_id=1, source_target_pairs={{0,8},{4,12},{8,0},{12,4},{1,9},{5,13},{9,1},{13,5},{2,10},{6,14},... | collective-permute-start | bytes 294920 | tf_op jit(solution)/shard_map/ppermute | solution.py:82
  73.5 7.6 %collective-permute-start.20 = (bf16[3,128,128]{2,1,0:T(8,128)(2,1)}, bf16[3,128,128]{2,1,0:T(8,128)(2,1)S(1)}, u32[]{:S(2)}, u32[]{:S(2)}) collective-permute-start(bf16[3,128,128]{2,1,0:T(8,128)(2,1)} %shard_map.96.refs_0_), channel_id=1, source_target_pairs={{0,4},{4,0},{8,12},{12,8},{1,5},{5,1},{9,13},{13,9},{2,6},{6,2},{1... | collective-permute-start | bytes 294920 | tf_op jit(solution)/shard_map/ppermute | solution.py:82
  74.7 6.9 %collective-permute-start.23 = (bf16[3,128,128]{2,1,0:T(8,128)(2,1)}, bf16[3,128,128]{2,1,0:T(8,128)(2,1)S(1)}, u32[]{:S(2)}, u32[]{:S(2)}) collective-permute-start(bf16[3,128,128]{2,1,0:T(8,128)(2,1)} %shard_map.96.refs_0_), channel_id=1, source_target_pairs={{0,1},{1,0},{2,3},{3,2},{4,5},{5,4},{6,7},{7,6},{8,9},{9,8},{10,11... | collective-permute-start | bytes 294920 | tf_op jit(solution)/shard_map/ppermute | solution.py:82
  77.9 3.6 %collective-permute-start.26 = (bf16[3,128,128]{2,1,0:T(8,128)(2,1)S(1)}, bf16[3,128,128]{2,1,0:T(8,128)(2,1)S(1)}, u32[]{:S(2)}, u32[]{:S(2)}) collective-permute-start(bf16[3,128,128]{2,1,0:T(8,128)(2,1)S(1)} %collective-permute-done.22.refs_3_), channel_id=1, source_target_pairs={{0,1},{1,0},{2,3},{3,2},{4,5},{5,4},{6,7},{7,6},{8,9},{9,8},{10,11... | collective-permute-start | bytes 294920 | tf_op jit(solution)/shard_map/ppermute | solution.py:82
  81.1 1.3 %collective-permute-start.25 = (bf16[3,128,128]{2,1,0:T(8,128)(2,1)S(1)}, bf16[3,128,128]{2,1,0:T(8,128)(2,1)S(1)}, u32[]{:S(2)}, u32[]{:S(2)}) collective-permute-start(bf16[3,128,128]{2,1,0:T(8,128)(2,1)S(1)} %collective-permute-done.21.refs_2_), channel_id=1, source_target_pairs={{0,1},{1,0},{2,3},{3,2},{4,5},{5,4},{6,7},{7,6},{8,9},{9,8},{10,11... | collective-permute-start | bytes 294920 | tf_op jit(solution)/shard_map/ppermute | solution.py:82
  81.1 1.5 %collective-permute-start.24 = (bf16[3,128,128]{2,1,0:T(8,128)(2,1)S(1)}, bf16[3,128,128]{2,1,0:T(8,128)(2,1)S(1)}, u32[]{:S(2)}, u32[]{:S(2)}) collective-permute-start(bf16[3,128,128]{2,1,0:T(8,128)(2,1)S(1)} %collective-permute-done.20.refs_1_), channel_id=1, source_target_pairs={{0,1},{1,0},{2,3},{3,2},{4,5},{5,4},{6,7},{7,6},{8,9},{9,8},{10,11... | collective-permute-start | bytes 294920 | tf_op jit(solution)/shard_map/ppermute | solution.py:82
  82.5 0.9 copy-start.2
  96.2 6.0 %collective-permute-start.30 = (bf16[64,768]{1,0:T(8,128)(2,1)S(1)}, bf16[64,768]{1,0:T(8,128)(2,1)S(1)}, u32[]{:S(2)}, u32[]{:S(2)}) collective-permute-start(bf16[64,768]{1,0:T(8,128)(2,1)S(1)} %get-tuple-element.63), channel_id=1, source_target_pairs={{0,2},{1,3},{2,0},{3,1},{4,6},{5,7},{6,4},{7,5},{8,10},{9,11},{10,... | collective-permute-start | bytes 294920 | tf_op jit(solution)/shard_map/ppermute | solution.py:82
  97.8 7.5 %collective-permute-start.29 = (bf16[64,768]{1,0:T(8,128)(2,1)S(1)}, bf16[64,768]{1,0:T(8,128)(2,1)S(1)}, u32[]{:S(2)}, u32[]{:S(2)}) collective-permute-start(bf16[64,768]{1,0:T(8,128)(2,1)S(1)} %get-tuple-element.62.refs_0_), channel_id=1, source_target_pairs={{0,12},{4,8},{8,4},{12,0},{1,13},{5,9},{9,5},{13,1},{2,14},{6,10},... | collective-permute-start | bytes 294920 | tf_op jit(solution)/shard_map/ppermute | solution.py:82
  99.7 12.3 %collective-permute-start.28 = (bf16[64,768]{1,0:T(8,128)(2,1)S(1)}, bf16[64,768]{1,0:T(8,128)(2,1)S(1)}, u32[]{:S(2)}, u32[]{:S(2)}) collective-permute-start(bf16[64,768]{1,0:T(8,128)(2,1)S(1)} %get-tuple-element.62.refs_0_), channel_id=1, source_target_pairs={{0,8},{4,12},{8,0},{12,4},{1,9},{5,13},{9,1},{13,5},{2,10},{6,14},... | collective-permute-start | bytes 294920 | tf_op jit(solution)/shard_map/ppermute | solution.py:82
  99.7 12.3 %collective-permute-start.27 = (bf16[64,768]{1,0:T(8,128)(2,1)S(1)}, bf16[64,768]{1,0:T(8,128)(2,1)S(1)}, u32[]{:S(2)}, u32[]{:S(2)}) collective-permute-start(bf16[64,768]{1,0:T(8,128)(2,1)S(1)} %get-tuple-element.62.refs_0_), channel_id=1, source_target_pairs={{0,4},{4,0},{8,12},{12,8},{1,5},{5,1},{9,13},{13,9},{2,6},{6,2},{1... | collective-permute-start | bytes 294920 | tf_op jit(solution)/shard_map/ppermute | solution.py:82
  102.2 9.9 %collective-permute-start.33 = (bf16[64,768]{1,0:T(8,128)(2,1)S(1)}, bf16[64,768]{1,0:T(8,128)(2,1)S(1)}, u32[]{:S(2)}, u32[]{:S(2)}) collective-permute-start(bf16[64,768]{1,0:T(8,128)(2,1)S(1)} %collective-permute-done.30.refs_4_), channel_id=1, source_target_pairs={{0,12},{4,8},{8,4},{12,0},{1,13},{5,9},{9,5},{13,1},{2,14},{6,10},... | collective-permute-start | bytes 294920 | tf_op jit(solution)/shard_map/ppermute | solution.py:82
  104.1 12.9 %collective-permute-start.32 = (bf16[64,768]{1,0:T(8,128)(2,1)S(1)}, bf16[64,768]{1,0:T(8,128)(2,1)S(1)}, u32[]{:S(2)}, u32[]{:S(2)}) collective-permute-start(bf16[64,768]{1,0:T(8,128)(2,1)S(1)} %collective-permute-done.30.refs_4_), channel_id=1, source_target_pairs={{0,8},{4,12},{8,0},{12,4},{1,9},{5,13},{9,1},{13,5},{2,10},{6,14},... | collective-permute-start | bytes 294920 | tf_op jit(solution)/shard_map/ppermute | solution.py:82
  105.3 11.7 %collective-permute-start.31 = (bf16[64,768]{1,0:T(8,128)(2,1)S(1)}, bf16[64,768]{1,0:T(8,128)(2,1)S(1)}, u32[]{:S(2)}, u32[]{:S(2)}) collective-permute-start(bf16[64,768]{1,0:T(8,128)(2,1)S(1)} %collective-permute-done.30.refs_4_), channel_id=1, source_target_pairs={{0,4},{4,0},{8,12},{12,8},{1,5},{5,1},{9,13},{13,9},{2,6},{6,2},{1... | collective-permute-start | bytes 294920 | tf_op jit(solution)/shard_map/ppermute | solution.py:82

commit v3 on v2

v3 whole, which is shorter than its diff:
```python
import functools

import jax
import jax.numpy as jnp
from jax import lax
from jax.experimental import pallas as pl
from jax.experimental.pallas import tpu as pltpu
from jax.sharding import PartitionSpec as P

RANK = 64
POWER = 2
BLK = 128

precise = lax.Precision.HIGHEST
f32 = jnp.float32
bf16 = jnp.bfloat16
VMEM = pl.BlockSpec(memory_space=pltpu.VMEM)
SMEM = pl.BlockSpec(memory_space=pltpu.SMEM)


def from_behind(value, axis, steps):
    count = lax.axis_size(axis)
    pairs = [(source, (source + steps) % count) for source in range(count)]
    return lax.ppermute(value, axis, pairs)


def gram_of(row_block):
    return jnp.dot(row_block, row_block.T, precision=precise, preferred_element_type=f32)


def solve_rows(gram_rows, row_block):
    low_factor = jnp.linalg.cholesky(gram_rows)
    solved = lax.linalg.triangular_solve(low_factor, row_block, left_side=True, lower=True)
    return solved.astype(bf16)


def tokens_of(sketches, matrices):
    parts = [
        jnp.einsum("km,tm->kt", s, m, preferred_element_type=f32)
        for s, m in zip(sketches, matrices)
    ]
    return tuple(lax.psum(p.astype(bf16), "tensor").astype(bf16) for p in parts)


def partials(token_rows, matrices):
    return tuple(
        jnp.dot(r, m, preferred_element_type=f32) for r, m in zip(token_rows, matrices)
    )


def orthonormal(parts):
    rows = [lax.psum(p.astype(bf16), "dp").astype(f32) for p in parts]
    grams = [lax.psum(gram_of(r).astype(bf16), "tensor").astype(f32) for r in rows]
    return tuple(solve_rows(g, r) for g, r in zip(grams, rows))


def feature_space(norm_in, query_grad, attn_out, handed, sketch_q, sketch_o):
    upstream = from_behind(handed, "section", -1)
    lefts = (norm_in[0], attn_out[0])
    rights = (query_grad[0], upstream[0])
    basis = orthonormal(partials(tokens_of((sketch_q[0], sketch_o[0]), rights), lefts))
    for _ in range(POWER):
        other = orthonormal(partials(tokens_of(basis, lefts), rights))
        basis = orthonormal(partials(tokens_of(other, rights), lefts))
    final = partials(tokens_of(basis, lefts), rights)
    raws = [lax.psum(p.astype(bf16), "dp").astype(f32) for p in final]
    energies = lax.psum(tuple(jnp.sum(r * r) for r in raws), "tensor")
    count = lax.axis_size("tensor")
    adapters = [
        r / jnp.sqrt(e / (r.size * count) + 1e-06) for r, e in zip(raws, energies)
    ]
    return (
        (basis[0] * 16.0)[None],
        adapters[0][None],
        (basis[1] * 16.0)[None],
        adapters[1][None],
    )


def swap(value, axis, bit):
    count = lax.axis_size(axis)
    return lax.ppermute(value, axis, [(i, i ^ bit) for i in range(count)])


def routed(value, sizes, token_bit, shifted):
    sections, dps, tensors = sizes
    side = tensors // 2
    pairs = []
    for s in range(sections):
        for z in range(dps):
            for t in range(tensors):
                to_t = t ^ side if t % side else t
                to_s = (s - 1) % sections if shifted and to_t >= side else s
                to = (to_s * dps + (z ^ token_bit)) * tensors + to_t
                pairs.append(((s * dps + z) * tensors + t, to))
    return lax.ppermute(value, ("section", "dp", "tensor"), pairs)


def window(ref, width, at):
    return ref.at[:, pl.ds(pl.multiple_of(at * width, width), width)]


def move(pairs, sems):
    copies = [pltpu.make_async_copy(src, dst, sems.at[n]) for n, (src, dst) in enumerate(pairs)]
    for c in copies:
        c.start()
    for c in copies:
        c.wait()


def give_kernel(dps, idx, norm, grad, attn, hand, sk_q, sk_o, give, sems):
    z, kind = idx[0], idx[3]
    wide, narrow = norm.shape[1], grad.shape[1]
    big_w, small_w = wide // dps, narrow // dps
    rows = RANK // dps

    def sketch(ref, width, start):
        part = ref.at[:, pl.ds(pl.multiple_of(z * width, width), width)]
        return [
            (
                part.at[i * rows : (i + 1) * rows],
                give.at[BLK:, i * (big_w + small_w) + start : i * (big_w + small_w) + start + width],
            )
            for i in range(dps)
        ]

    give[BLK:, :] = jnp.zeros((rows, wide + narrow), bf16)

    @pl.when(kind == 0)
    def _():
        pairs = [(hand, give.at[:BLK, :wide]), (attn, give.at[:BLK, wide:])]
        move(pairs + sketch(sk_o, big_w, 0), sems)

    @pl.when(kind == 1)
    def _():
        pairs = [(norm, give.at[:BLK, :wide]), (grad, give.at[:BLK, wide:])]
        move(pairs + sketch(sk_q, small_w, big_w), sems)


def merge_kernel(dps, idx, norm, grad, attn, hand, sk_q, sk_o, got, *refs):
    z, kind = idx[0], idx[3]
    bigs, smalls, sems = refs[:dps], refs[dps : 2 * dps], refs[-1]
    big_w, small_w = bigs[0].shape[1] // 2, smalls[0].shape[1] // 2
    wide, rows = norm.shape[1], RANK // dps

    def keep(wide_ref, thin_ref, extra):
        pairs = [extra]
        for d in range(dps):
            pairs.append((window(wide_ref, big_w, z ^ d), bigs[d].at[:, :big_w]))
            pairs.append((window(thin_ref, small_w, z ^ d), smalls[d].at[:BLK, :small_w]))
        copies = [
            pltpu.make_async_copy(src, dst, sems.at[n]) for n, (src, dst) in enumerate(pairs)
        ]
        for c in copies:
            c.start()
        fill()
        for c in copies:
            c.wait()

    def fill():
        for d in range(dps):
            at = pl.multiple_of((z ^ d) * big_w, big_w)
            bigs[d][:, big_w:] = got[:BLK, pl.ds(at, big_w)]
            at = pl.multiple_of(wide + (z ^ d) * small_w, small_w)
            smalls[d][:BLK, small_w:] = got[:BLK, pl.ds(at, small_w)]
        for i in range(dps):
            at = i * (big_w + small_w)
            below = slice(BLK + RANK + i * rows, BLK + RANK + (i + 1) * rows)
            smalls[0][below, :] = got[BLK:, at : at + big_w]
            below = slice(BLK + 2 * RANK + i * rows, BLK + 2 * RANK + (i + 1) * rows)
            smalls[0][below, small_w:] = got[BLK:, at + big_w : at + big_w + small_w]

    @pl.when(kind == 0)
    def _():
        smalls[0][BLK : BLK + RANK, :] = jnp.zeros((RANK, big_w), bf16)
        dst = smalls[0].at[BLK + 2 * RANK :, :small_w]
        keep(norm, grad, (window(sk_q, small_w, z), dst))

    @pl.when(kind == 1)
    def _():
        smalls[0][BLK + 2 * RANK :, :small_w] = jnp.zeros((RANK, small_w), bf16)
        dst = smalls[0].at[BLK : BLK + RANK, :]
        keep(hand, attn, (window(sk_o, big_w, z), dst))


def nt(a, b, precision=None):
    return lax.dot_general(
        a, b, (((1,), (1,)), ((), ())), precision=precision, preferred_element_type=f32
    )


def packed_rows(dps):
    per_gram = (dps * (dps - 1) // 2 + dps // 2) * BLK
    used = 2 * per_gram + dps * RANK + 16
    return per_gram, pl.cdiv(used, 4 * 16) * 4 * 16


def gram_kernel(dps, idx, *refs):
    z, core = idx[0], idx[2]
    bigs, smalls = refs[:dps], refs[dps : 2 * dps]
    big, small, keep, send, flat = refs[2 * dps :]
    half_w = big.shape[1] // 2
    for d in range(dps):
        rows = pl.ds(pl.multiple_of((z ^ d) * BLK, BLK), BLK)
        big[rows, :] = bigs[d][...]
        small[rows, :] = smalls[d][:BLK, :]
    per_gram, total = packed_rows(dps)
    r = lax.broadcasted_iota(jnp.int32, (BLK, BLK), 0)
    c = lax.broadcasted_iota(jnp.int32, (BLK, BLK), 1)
    at, diagonals = 0, []

    def put(value):
        nonlocal at
        flat[at : at + value.shape[0], :] = value.astype(bf16)
        at += value.shape[0]

    for m in (big, small):
        on = []
        for i in range(dps):
            row = nt(m[i * BLK : (i + 1) * BLK, :], m[: (i + 1) * BLK, :])
            for j in range(i):
                put(row[:, j * BLK : (j + 1) * BLK])
            on.append(row[:, i * BLK :])
        for i in range(0, dps, 2):
            put(jnp.where(r > c, on[i], on[i + 1]))
        diagonals += [jnp.sum(jnp.where(r == c, v, 0.0), axis=0, keepdims=True) for v in on]
        diagonals.append(jnp.zeros((8 - dps, BLK), f32))
    sk = smalls[0]
    first = (
        nt(sk[BLK : BLK + RANK, :], big[:, :half_w])
        + nt(sk[BLK + RANK : BLK + 2 * RANK, :], big[:, half_w:])
        + nt(sk[BLK + 2 * RANK :, :], small[...])
    )
    for i in range(dps):
        put(first[:, i * BLK : (i + 1) * BLK])
    put(jnp.concatenate(diagonals, axis=0))
    put(jnp.zeros((total - at, BLK), f32))
    half = total // 2
    keep[...] = flat[pl.ds(pl.multiple_of(core * half, 16), half), :]
    send[...] = flat[pl.ds(pl.multiple_of((1 - core) * half, 16), half), :]


def add_halves_kernel(idx, mine, got, keep, send):
    size, bit = keep.shape[0], idx[0] % 2
    for out, which in ((keep, bit), (send, 1 - bit)):
        part = pl.ds(pl.multiple_of(which * size, 16), size)
        out[...] = (mine[part, :].astype(f32) + got[part, :].astype(f32)).astype(bf16)


def add_kernel(mine, got, out):
    out[...] = (mine[...].astype(f32) + got[...].astype(f32)).astype(bf16)


def inverse_factor(gram):
    n, nb = gram.shape[0], 8
    rows = lax.broadcasted_iota(jnp.int32, (n, n), 0)
    cols = lax.broadcasted_iota(jnp.int32, (n, n), 1)
    work = jnp.concatenate([(rows == cols).astype(f32), gram], axis=1)
    count = n // nb
    slabs = [work[nb * s : nb * s + nb, :] for s in range(count)]
    sub = lax.broadcasted_iota(jnp.int32, (nb, 2 * n), 0)

    def lane(x, k):
        return jnp.broadcast_to(x[:, n + k : n + k + 1], (nb, 2 * n))

    def row(x, i):
        return jnp.broadcast_to(x[i : i + 1, :], (nb, 2 * n))

    done = []
    for b in range(count):
        cols_of = [lane(slabs[b], nb * b + j) for j in range(nb)]
        pivot_rows = [row(slabs[b], i) for i in range(nb)]
        splat = [[row(cols_of[j], i) for j in range(i + 1)] for i in range(nb)]
        below = {s: [lane(slabs[s], nb * b + j) for j in range(nb)] for s in range(b + 1, count)}
        out = None
        for k in range(nb):
            inv = 1.0 / splat[k][k]
            at = pivot_rows[k]
            final = at * lax.rsqrt(splat[k][k])
            out = final if out is None else jnp.where(sub == k, final, out)
            for i in range(k + 1, nb):
                mult = splat[i][k] * inv
                for j in range(k + 1, i + 1):
                    splat[i][j] = splat[i][j] - mult * splat[j][k]
                pivot_rows[i] = pivot_rows[i] - mult * at
            for s in range(b + 1, count):
                mult = below[s][k] * inv
                for j in range(k + 1, nb):
                    below[s][j] = below[s][j] - mult * splat[j][k]
                slabs[s] = slabs[s] - mult * at
        done.append(out)
    return jnp.concatenate(done, axis=0)[:, :n]


def split(x):
    high = x.astype(bf16)
    return high, (x - high.astype(f32)).astype(bf16)


def times(rows, gram):
    n = rows.shape[0]
    both = jnp.dot(jnp.concatenate(split(rows), axis=0), gram, preferred_element_type=f32)
    return both[:n] + both[n:]


def product(a, b):
    (ah, al), (bh, bl) = split(a), split(b)
    return jnp.dot(
        jnp.concatenate([ah, ah, al], axis=1),
        jnp.concatenate([bh, bl, bh], axis=0),
        preferred_element_type=f32,
    )


def product_nt(a, b):
    (ah, al), (bh, bl) = split(a), split(b)
    return nt(jnp.concatenate([ah, ah, al], axis=1), jnp.concatenate([bh, bl, bh], axis=1))


def chain_kernel(dps, counts, idx, *refs):
    z, out_half, core = idx[0], idx[1], idx[2]
    quarters, big, small, out, flat, left, right = refs[:4], *refs[4:]
    size, bit = quarters[0].shape[0], z % 2
    for n, ref in enumerate(quarters):
        which = 2 * (core ^ (n // 2)) + (bit ^ (n % 2))
        flat[pl.ds(pl.multiple_of(which * size, 16), size), :] = ref[...]
    per_gram, _ = packed_rows(dps)
    r = lax.broadcasted_iota(jnp.int32, (BLK, BLK), 0)
    c = lax.broadcasted_iota(jnp.int32, (BLK, BLK), 1)
    start = 2 * per_gram
    rows = jnp.concatenate(
        [flat[start + i * RANK : start + (i + 1) * RANK, :] for i in range(dps)], axis=1
    ).astype(f32)
    start += dps * RANK
    diagonals = flat[start : start + 16, :].astype(f32)
    is_out = out_half == 1
    for gram, which in ((left, out_half), (right, 1 - out_half)):
        base = which * per_gram

        def block(n):
            return flat[pl.ds(pl.multiple_of(base + n * BLK, BLK), BLK), :].astype(f32)

        def put(i, j, value):
            gram[i * BLK : (i + 1) * BLK, j * BLK : (j + 1) * BLK] = value.astype(bf16)

        n = 0
        for i in range(dps):
            for j in range(i):
                value = block(n)
                put(i, j, value)
                put(j, i, value.T)
                n += 1
        diag = jnp.where(which == 1, diagonals[8:, :], diagonals[:8, :])
        for i in range(0, dps, 2):
            value = block(n)
            turned = value.T
            put(i, i, jnp.where(r > c, value, jnp.where(r == c, diag[i : i + 1, :], turned)))
            put(
                i + 1,
                i + 1,
                jnp.where(r < c, value, jnp.where(r == c, diag[i + 1 : i + 2, :], turned)),
            )
            n += 1
    ahead = times(rows, left[...])
    gram = product_nt(ahead, rows)
    for step in range(2 * POWER):
        following = (right if step % 2 == 0 else left)[...]
        beyond = times(ahead, following)
        inner = product_nt(beyond, ahead)
        low_inv = inverse_factor(gram)
        rows = product(low_inv, ahead)
        if step < 2 * POWER - 1:
            gram = product_nt(product(low_inv, inner), low_inv)
            ahead = product(low_inv, beyond)
        else:
            ahead = times(rows, following)
            gram = product_nt(ahead, rows)
    low_inv = inverse_factor(gram)
    basis = product(low_inv, rows)
    rows = product(low_inv, ahead)
    energy = jnp.sum(times(rows, right[...]) * rows)
    count = jnp.where(out_half == 1, counts[0], counts[1]).astype(f32)
    scale = lax.rsqrt(jnp.full((1, 1), energy, f32) / count + 1e-06)
    coef_b, coef_a = basis.astype(bf16), rows.astype(bf16)
    for_big = jnp.where(is_out, coef_a, coef_b)
    for_small = jnp.where(is_out, coef_b, coef_a)
    scale_big = jnp.where(is_out, scale, 16.0)
    scale_small = jnp.where(is_out, 16.0, scale)
    big_w, small_w = big.shape[1] // 2, small.shape[1] // 2
    made_big = (jnp.dot(for_big, big[...], preferred_element_type=f32) * scale_big).astype(bf16)
    made_small = (jnp.dot(for_small, small[...], preferred_element_type=f32) * scale_small).astype(
        bf16
    )
    for n in range(2):
        part = slice(n * RANK, (n + 1) * RANK)
        out[part, :big_w] = made_big[:, n * big_w : (n + 1) * big_w]
        out[part, big_w:] = made_small[:, n * small_w : (n + 1) * small_w]


def place_kernel(dps, idx, *refs):
    z, kind = idx[0], idx[3]
    mine, theirs = refs[:dps], refs[dps : 2 * dps]
    b_q, a_q, b_o, a_o = refs[2 * dps :]
    big_w, small_w = b_q.shape[1] // dps, a_q.shape[1] // dps
    for d in range(dps):
        bigs = pl.ds(pl.multiple_of((z ^ d) * big_w, big_w), big_w)
        smalls = pl.ds(pl.multiple_of((z ^ d) * small_w, small_w), small_w)
        here, there = mine[d].at[:RANK], theirs[d].at[RANK:]
        for which, query, output in ((0, here, there), (1, there, here)):

            @pl.when(kind == which)
            def _():
                b_q[:, bigs] = query[:, :big_w]
                a_q[:, smalls] = query[:, big_w:].astype(f32)
                a_o[:, bigs] = output[:, :big_w].astype(f32)
                b_o[:, smalls] = output[:, big_w:]


def call(kernel, out_shapes, args, scratch=(), spaces=()):
    spaces = [SMEM] + [VMEM] * (len(args) - 1) if not spaces else spaces
    return pl.pallas_call(
        kernel,
        out_shape=out_shapes,
        in_specs=spaces,
        out_specs=jax.tree.map(lambda _: VMEM, out_shapes),
        scratch_shapes=list(scratch),
        compiler_params=pltpu.CompilerParams(vmem_limit_bytes=48 * 2**20),
    )(*args)


def token_space(sizes, norm_in, query_grad, attn_out, handed, sketch_q, sketch_o):
    _, dps, tensors = sizes
    side = tensors // 2

    def shape(*dims, dtype=bf16):
        return jax.ShapeDtypeStruct(dims, dtype)

    z, t = lax.axis_index("dp"), lax.axis_index("tensor")
    half, core = t // side, t % side
    idx = jnp.stack([z, half, core, half ^ core]).astype(jnp.int32)
    wide, narrow = norm_in.shape[2], query_grad.shape[2]
    big_w, small_w = wide // dps, narrow // dps
    tokens = dps * BLK
    args = (norm_in[0], query_grad[0], attn_out[0], handed[0], sketch_q[0], sketch_o[0])
    in_hbm = [SMEM] + [pl.BlockSpec(memory_space=pltpu.HBM)] * len(args)

    give = call(
        functools.partial(give_kernel, dps),
        shape(BLK + RANK // dps, wide + narrow),
        (idx, *args),
        [pltpu.SemaphoreType.DMA((2 + dps,))],
        in_hbm,
    )
    got = swap(give, "tensor", 1)
    packed = call(
        functools.partial(merge_kernel, dps),
        [shape(BLK, 2 * big_w)] * dps
        + [shape(BLK + 3 * RANK, 2 * small_w)]
        + [shape(BLK, 2 * small_w)] * (dps - 1),
        (idx, *args, got),
        [pltpu.SemaphoreType.DMA((2 * dps + 1,))],
        in_hbm + [VMEM],
    )
    bigs = [routed(v, sizes, d, True) for d, v in enumerate(packed[:dps])]
    smalls = [routed(v, sizes, d, False) for d, v in enumerate(packed[dps:])]

    _, total = packed_rows(dps)
    big, small, keep, send = call(
        functools.partial(gram_kernel, dps),
        [
            shape(tokens, 2 * big_w),
            shape(tokens, 2 * small_w),
            shape(total // 2, BLK),
            shape(total // 2, BLK),
        ],
        (idx, *bigs, *smalls),
        [pltpu.VMEM((total, BLK), bf16)],
    )
    quarter = shape(total // 4, BLK)
    keep, send = call(add_halves_kernel, [quarter] * 2, (idx, keep, swap(send, "tensor", 1)))
    for bit, value in ((1, send), (2, None)):
        value = swap(keep if value is None else value, "dp", bit)
        keep = call(add_kernel, quarter, (keep, value), (), [VMEM] * 2)
    beside = swap(keep, "dp", 1)
    quarters = (keep, beside, swap(keep, "tensor", 1), swap(beside, "tensor", 1))

    counts = (RANK * wide * tensors, RANK * narrow * tensors)
    out = call(
        functools.partial(chain_kernel, dps, counts),
        shape(2 * RANK, big_w + small_w),
        (idx, *quarters, big, small),
        [
            pltpu.VMEM((total, BLK), bf16),
            pltpu.VMEM((tokens, tokens), bf16),
            pltpu.VMEM((tokens, tokens), bf16),
        ],
    )
    mine = [routed(out, sizes, d, False) for d in range(3)]
    mine.append(swap(mine[2], "dp", 1))
    theirs = [swap(v, "tensor", 1) for v in mine]
    outs = call(
        functools.partial(place_kernel, dps),
        [
            shape(RANK, wide),
            shape(RANK, narrow, dtype=f32),
            shape(RANK, narrow),
            shape(RANK, wide, dtype=f32),
        ],
        (idx, *mine, *theirs),
    )
    return tuple(o[None] for o in outs)


def solution(mesh):
    sizes = tuple(mesh.shape[axis] for axis in ("section", "dp", "tensor"))
    _, dps, tensors = sizes

    def body(norm_in, query_grad, attn_out, handed, sketch_q, sketch_o):
        args = (norm_in, query_grad, attn_out, handed, sketch_q, sketch_o)
        fits = (
            dps == 4
            and tensors == 4
            and norm_in.shape[1] == BLK
            and sketch_q.shape[1] == RANK
            and norm_in.shape[2] == handed.shape[2]
            and query_grad.shape[2] == attn_out.shape[2]
            and norm_in.shape[2] == 2 * query_grad.shape[2]
            and query_grad.shape[2] % (dps * 128) == 0
        )
        return token_space(sizes, *args) if fits else feature_space(*args)

    return jax.shard_map(
        body,
        mesh=mesh,
        in_specs=(P("section", "dp", "tensor"),) * 4 + (P("section", None, "tensor"),) * 2,
        out_specs=(P("section", None, "tensor"),) * 4,
        check_vma=False,
    )
```

time: 119 us -> 115 us (0.966)
  starting transfers between devices: 48.8 us -> 26.1 us
  waiting for transfers between devices: 40.7 us -> 62.2 us
  local copies, waits for them, and re-layouts: 8.03 us -> 5.84 us
    ppermute x15 -> x11, waiting for transfers between devices: 11.8 us -> 33.8 us  [routed(): return lax.ppermute(value, ('section', 'dp', 'tensor'), pairs)]
    ppermute x19 -> x12, starting transfers between devices: 24.6 us -> 10.4 us  [swap(): return lax.ppermute(value, axis, [(i, i ^ bit) for i in range(count)])]
    ppermute x15 -> x11, starting transfers between devices: 24.2 us -> 15.7 us  [routed(): return lax.ppermute(value, ('section', 'dp', 'tensor'), pairs)]
    unnamed x22 -> x12, local copies, waits for them, and re-layouts: 8.03 us -> 5.84 us
    pallas_call x6 -> x8, Pallas kernels: 20.2 us -> 19.1 us  [call(): pl.pallas_call(kernel, out_shape=out_shapes, in_specs=spaces, out_specs=j...]
    ppermute x19 -> x12, waiting for transfers between devices: 28.9 us -> 28.4 us  [swap(): return lax.ppermute(value, axis, [(i, i ^ bit) for i in range(count)])]
  transfers between devices with their start and end apart: 34 -> 23, of which waited for: 14 -> 12; matrix products, arithmetic and copies ran while one was open for 0% -> 0% of each run, Pallas kernels for 0% -> 0%
where the time goes in v3:
time: 115 us; the launch traced here: 114 us
  waiting for transfers between devices  62.2 us (54%)
  starting transfers between devices  26.1 us (23%)
  Pallas kernels  19.1 us (17%)
  local copies, waits for them, and re-layouts  5.84 us (5%)
    ppermute x11, waiting for transfers between devices, routed(): return lax.ppermute(value, ('section', 'dp', 'tensor'), pairs)  33.8 us
    ppermute x12, waiting for transfers between devices, swap(): return lax.ppermute(value, axis, [(i, i ^ bit) for i in range(count)])  28.4 us
    pallas_call x8, Pallas kernels, call(): pl.pallas_call(kernel, out_shape=out_shapes, in_specs=spaces, out_specs=j...  19.1 us
    ppermute x11, starting transfers between devices, routed(): return lax.ppermute(value, ('section', 'dp', 'tensor'), pairs)  15.7 us
    ppermute x12, starting transfers between devices, swap(): return lax.ppermute(value, axis, [(i, i ^ bit) for i in range(count)])  10.4 us
    unnamed x12, local copies, waits for them, and re-layouts  5.84 us
  transfers between devices with their start and end apart: 23, of which 12 were waited for; matrix products, arithmetic and copies ran while one was open for 0% of the time, Pallas kernels for 0%

profile of v3, /device:TPU:0, one launch (start us, length us, event | category | flops | bytes accessed | tf_op | source)
XLA Modules:
  0.0 114.2 jit_solution(16413987766181731925)
XLA Ops:
  0.6 0.1 pad_add_fusion.idx
  0.7 1.0 copy-done
  1.8 1.0 copy-done.1
  2.8 0.9 copy-done.2
  3.8 0.9 copy-done.3
  4.7 0.9 copy-done.4
  5.7 0.9 copy-done.5
  6.6 0.7 shard_map.93
  7.3 0.5 collective-permute-start
  7.8 2.1 %collective-permute-done.got = bf16[144,3072]{1,0:T(8,128)(2,1)S(1)} collective-permute-done((bf16[144,3072]{1,0:T(8,128)(2,1)S(1)}, bf16[144,3072]{1,0:T(8,128)(2,1)S(1)}, u32[]{:S(2)}, u32[]{:S(2)}) %collective-permute-start) | collective-permute-done | bytes 884768 | tf_op jit(solution)/shard_map/ppermute | solution.py:82
  9.8 0.9 shard_map.94
  10.7 3.0 %collective-permute-start.6 = (bf16[128,512]{1,0:T(8,128)(2,1)S(1)}, bf16[128,512]{1,0:T(8,128)(2,1)S(1)}, u32[]{:S(2)}, u32[]{:S(2)}) collective-permute-start(bf16[128,512]{1,0:T(8,128)(2,1)S(1)} %get-tuple-element.27), channel_id=1, source_target_pairs={{0,4},{1,7},{2,6},{3,5},{4,0},{5,3},{6,2},{7,1},{8,12},{9,15},{10,... | collective-permute-start | bytes 393224 | tf_op jit(solution)/shard_map/ppermute | solution.py:96
  13.7 2.6 %collective-permute-start.7 = (bf16[128,512]{1,0:T(8,128)(2,1)S(1)}, bf16[128,512]{1,0:T(8,128)(2,1)S(1)}, u32[]{:S(2)}, u32[]{:S(2)}) collective-permute-start(bf16[128,512]{1,0:T(8,128)(2,1)S(1)} %get-tuple-element.28), channel_id=1, source_target_pairs={{0,8},{1,11},{2,10},{3,9},{4,12},{5,15},{6,14},{7,13},{8,0},{9,3},... | collective-permute-start | bytes 393224 | tf_op jit(solution)/shard_map/ppermute | solution.py:96
  16.3 0.0 collective-permute-start.8
  16.3 0.7 collective-permute-start.5
  17.0 0.7 collective-permute-start.1
  17.7 0.0 collective-permute-done.6.refs_5_
  17.7 2.3 %collective-permute-start.2 = (bf16[128,1024]{1,0:T(8,128)(2,1)S(1)}, bf16[128,1024]{1,0:T(8,128)(2,1)S(1)}, u32[]{:S(2)}, u32[]{:S(2)}) collective-permute-start(bf16[128,1024]{1,0:T(8,128)(2,1)S(1)} %get-tuple-element.23), channel_id=1, source_target_pairs={{0,4},{1,23},{2,22},{3,5},{4,0},{5,19},{6,18},{7,1},{8,12},{9,31},... | collective-permute-start | bytes 786440 | tf_op jit(solution)/shard_map/ppermute | solution.py:96
  20.0 6.7 %collective-permute-done.7.refs_6_ = bf16[128,512]{1,0:T(8,128)(2,1)S(1)} collective-permute-done((bf16[128,512]{1,0:T(8,128)(2,1)S(1)}, bf16[128,512]{1,0:T(8,128)(2,1)S(1)}, u32[]{:S(2)}, u32[]{:S(2)}) %collective-permute-start.7) | collective-permute-done | bytes 131104 | tf_op jit(solution)/shard_map/ppermute | solution.py:96
  26.7 0.0 collective-permute-start.3
  26.7 0.0 collective-permute-done.8.refs_7_
  26.7 2.5 %collective-permute-start.4 = (bf16[128,1024]{1,0:T(8,128)(2,1)S(1)}, bf16[128,1024]{1,0:T(8,128)(2,1)S(1)}, u32[]{:S(2)}, u32[]{:S(2)}) collective-permute-start(bf16[128,1024]{1,0:T(8,128)(2,1)S(1)} %get-tuple-element.25), channel_id=1, source_target_pairs={{0,12},{1,31},{2,30},{3,13},{4,8},{5,27},{6,26},{7,9},{8,4},{9,23}... | collective-permute-start | bytes 786440 | tf_op jit(solution)/shard_map/ppermute | solution.py:96
  29.2 0.0 collective-permute-done.2.refs_1_
  29.2 18.2 %collective-permute-done.3.refs_2_ = bf16[128,1024]{1,0:T(8,128)(2,1)S(1)} collective-permute-done((bf16[128,1024]{1,0:T(8,128)(2,1)S(1)}, bf16[128,1024]{1,0:T(8,128)(2,1)S(1)}, u32[]{:S(2)}, u32[]{:S(2)}) %collective-permute-start.3) | collective-permute-done | bytes 262176 | tf_op jit(solution)/shard_map/ppermute | solution.py:96
  47.4 0.0 collective-permute-done.4.refs_3_
  47.4 2.4 %shard_map.95 = (bf16[512,1024]{1,0:T(8,128)(2,1)S(1)}, bf16[512,512]{1,0:T(8,128)(2,1)S(1)}, bf16[1184,128]{1,0:T(8,128)(2,1)S(1)}, bf16[1184,128]{1,0:T(8,128)(2,1)S(1)}) custom-call(s32[4]{0:T(128)S(1)} %pad_add_fusion.idx, bf16[128,1024]{1,0:T(8,128)(2,1)S(1)} %collective-permute-done.1.refs_0_, bf16[128,1024]{1,0:T(8,128)(2,1)S(1)} %collective-permute-done.2.refs_1_, ...), custom_call_target="tpu_custom_call" | custom-call | tf_op jit(solution)/shard_map/pallas_call | solution.py:421
  49.8 0.1 collective-permute-start.9
  49.9 1.6 %collective-permute-done.9.got = bf16[1184,128]{1,0:T(8,128)(2,1)S(1)} collective-permute-done((bf16[1184,128]{1,0:T(8,128)(2,1)S(1)}, bf16[1184,128]{1,0:T(8,128)(2,1)S(1)}, u32[]{:S(2)}, u32[]{:S(2)}) %collective-permute-start.9) | collective-permute-done | bytes 303136 | tf_op jit(solution)/shard_map/ppermute | solution.py:82
  51.5 0.6 shard_map.96
  52.1 6.3 %collective-permute-start.10 = (bf16[592,128]{1,0:T(8,128)(2,1)S(1)}, bf16[592,128]{1,0:T(8,128)(2,1)S(1)}, u32[]{:S(2)}, u32[]{:S(2)}) collective-permute-start(bf16[592,128]{1,0:T(8,128)(2,1)S(1)} %get-tuple-element.33), channel_id=1, source_target_pairs={{0,4},{4,0},{8,12},{12,8},{1,5},{5,1},{9,13},{13,9},{2,6},{6,2},{1... | collective-permute-start | bytes 454664 | tf_op jit(solution)/shard_map/ppermute | solution.py:82
  58.3 4.2 %collective-permute-done.10.got = bf16[592,128]{1,0:T(8,128)(2,1)S(1)} collective-permute-done((bf16[592,128]{1,0:T(8,128)(2,1)S(1)}, bf16[592,128]{1,0:T(8,128)(2,1)S(1)}, u32[]{:S(2)}, u32[]{:S(2)}) %collective-permute-start.10) | collective-permute-done | bytes 151584 | tf_op jit(solution)/shard_map/ppermute | solution.py:82
  62.6 2.8 %collective-permute-start.11 = (bf16[592,128]{1,0:T(8,128)(2,1)S(1)}, bf16[592,128]{1,0:T(8,128)(2,1)S(1)}, u32[]{:S(2)}, u32[]{:S(2)}) collective-permute-start(bf16[592,128]{1,0:T(8,128)(2,1)S(1)} %shard_map.97.mine), channel_id=1, source_target_pairs={{0,8},{4,12},{8,0},{12,4},{1,9},{5,13},{9,1},{13,5},{2,10},{6,14},... | collective-permute-start | bytes 454664 | tf_op jit(solution)/shard_map/ppermute | solution.py:82
  65.5 6.9 %collective-permute-done.11.got = bf16[592,128]{1,0:T(8,128)(2,1)S(1)} collective-permute-done((bf16[592,128]{1,0:T(8,128)(2,1)S(1)}, bf16[592,128]{1,0:T(8,128)(2,1)S(1)}, u32[]{:S(2)}, u32[]{:S(2)}) %collective-permute-start.11) | collective-permute-done | bytes 151584 | tf_op jit(solution)/shard_map/ppermute | solution.py:82
  72.4 0.1 collective-permute-start.12
  72.5 0.1 collective-permute-start.13
  72.6 5.1 %collective-permute-done.12.refs_1_ = bf16[592,128]{1,0:T(8,128)(2,1)S(1)} collective-permute-done((bf16[592,128]{1,0:T(8,128)(2,1)S(1)}, bf16[592,128]{1,0:T(8,128)(2,1)S(1)}, u32[]{:S(2)}, u32[]{:S(2)}) %collective-permute-start.12) | collective-permute-done | bytes 151584 | tf_op jit(solution)/shard_map/ppermute | solution.py:82
  77.7 1.4 %collective-permute-done.14.refs_3_ = bf16[592,128]{1,0:T(8,128)(2,1)S(1)} collective-permute-done((bf16[592,128]{1,0:T(8,128)(2,1)S(1)}, bf16[592,128]{1,0:T(8,128)(2,1)S(1)}, u32[]{:S(2)}, u32[]{:S(2)}) %collective-permute-start.14) | collective-permute-done | bytes 151584 | tf_op jit(solution)/shard_map/ppermute | solution.py:82
  79.0 12.8 %shard_map.99 = bf16[128,768]{1,0:T(8,128)(2,1)S(1)} custom-call(s32[4]{0:T(128)S(1)} %pad_add_fusion.idx, bf16[592,128]{1,0:T(8,128)(2,1)S(1)} %shard_map.98.refs_0_, bf16[592,128]{1,0:T(8,128)(2,1)S(1)} %collective-permute-done.12.refs_1_, bf16[592,128]{1,0:T(8,128)(2,1)S(1)} %collective-permute-done.13.refs_2_, ...), custom_call_target="tpu_custom_call" | custom-call | tf_op jit(solution)/shard_map/pallas_call | solution.py:421
  91.8 1.2 %collective-permute-start.17 = (bf16[128,768]{1,0:T(8,128)(2,1)S(1)}, bf16[128,768]{1,0:T(8,128)(2,1)S(1)}, u32[]{:S(2)}, u32[]{:S(2)}) collective-permute-start(bf16[128,768]{1,0:T(8,128)(2,1)S(1)} %shard_map.99), channel_id=1, source_target_pairs={{0,8},{1,11},{2,10},{3,9},{4,12},{5,15},{6,14},{7,13},{8,0},{9,3},... | collective-permute-start | bytes 589832 | tf_op jit(solution)/shard_map/ppermute | solution.py:96
  93.0 2.0 %collective-permute-start.16 = (bf16[128,768]{1,0:T(8,128)(2,1)S(1)}, bf16[128,768]{1,0:T(8,128)(2,1)S(1)}, u32[]{:S(2)}, u32[]{:S(2)}) collective-permute-start(bf16[128,768]{1,0:T(8,128)(2,1)S(1)} %shard_map.99), channel_id=1, source_target_pairs={{0,4},{1,7},{2,6},{3,5},{4,0},{5,3},{6,2},{7,1},{8,12},{9,15},{10,... | collective-permute-start | bytes 589832 | tf_op jit(solution)/shard_map/ppermute | solution.py:96
  95.0 0.7 collective-permute-start.15
  95.7 8.7 %collective-permute-done.17.refs_2_ = bf16[128,768]{1,0:T(8,128)(2,1)S(1)} collective-permute-done((bf16[128,768]{1,0:T(8,128)(2,1)S(1)}, bf16[128,768]{1,0:T(8,128)(2,1)S(1)}, u32[]{:S(2)}, u32[]{:S(2)}) %collective-permute-start.17) | collective-permute-done | bytes 196640 | tf_op jit(solution)/shard_map/ppermute | solution.py:96
  104.4 0.2 collective-permute-done.16.refs_1_
  104.7 0.6 collective-permute-start.20
  105.3 0.0 collective-permute-start.19
  105.3 5.8 %collective-permute-done.18.refs_3_ = bf16[128,768]{1,0:T(8,128)(2,1)S(1)} collective-permute-done((bf16[128,768]{1,0:T(8,128)(2,1)S(1)}, bf16[128,768]{1,0:T(8,128)(2,1)S(1)}, u32[]{:S(2)}, u32[]{:S(2)}) %collective-permute-start.18) | collective-permute-done | bytes 196640 | tf_op jit(solution)/shard_map/ppermute | solution.py:82
  111.1 1.4 %collective-permute-done.22.refs_7_ = bf16[128,768]{1,0:T(8,128)(2,1)S(1)} collective-permute-done((bf16[128,768]{1,0:T(8,128)(2,1)S(1)}, bf16[128,768]{1,0:T(8,128)(2,1)S(1)}, u32[]{:S(2)}, u32[]{:S(2)}) %collective-permute-start.22) | collective-permute-done | bytes 196640 | tf_op jit(solution)/shard_map/ppermute | solution.py:82
  112.5 1.7 %shard_map.100 = (bf16[64,2048]{1,0:T(8,128)(2,1)}, f32[64,1024]{1,0:T(8,128)}, bf16[64,1024]{1,0:T(8,128)(2,1)}, f32[64,2048]{1,0:T(8,128)}) custom-call(s32[4]{0:T(128)S(1)} %pad_add_fusion.idx, bf16[128,768]{1,0:T(8,128)(2,1)S(1)} %collective-permute-done.15.refs_0_, bf16[128,768]{1,0:T(8,128)(2,1)S(1)} %collective-permute-done.16.refs_1_, ...), custom_call_target="tpu_custom_call" | custom-call | tf_op jit(solution)/shard_map/pallas_call | solution.py:421
  (19 shorter events, 0.1 us)
Async XLA Ops:
  0.7 1.0 copy-start
  1.8 1.0 copy-start.1
  2.8 0.9 copy-start.2
  3.8 0.9 copy-start.3
  4.7 0.9 copy-start.4
  5.7 0.9 copy-start.5
  7.3 2.6 %collective-permute-start = (bf16[144,3072]{1,0:T(8,128)(2,1)S(1)}, bf16[144,3072]{1,0:T(8,128)(2,1)S(1)}, u32[]{:S(2)}, u32[]{:S(2)}) collective-permute-start(bf16[144,3072]{1,0:T(8,128)(2,1)S(1)} %shard_map.93), channel_id=1, source_target_pairs={{0,1},{1,0},{2,3},{3,2},{4,5},{5,4},{6,7},{7,6},{8,9},{9,8},{10,11... | collective-permute-start | bytes 2654216 | tf_op jit(solution)/shard_map/ppermute | solution.py:82
  10.7 7.0 %collective-permute-start.6 = (bf16[128,512]{1,0:T(8,128)(2,1)S(1)}, bf16[128,512]{1,0:T(8,128)(2,1)S(1)}, u32[]{:S(2)}, u32[]{:S(2)}) collective-permute-start(bf16[128,512]{1,0:T(8,128)(2,1)S(1)} %get-tuple-element.27), channel_id=1, source_target_pairs={{0,4},{1,7},{2,6},{3,5},{4,0},{5,3},{6,2},{7,1},{8,12},{9,15},{10,... | collective-permute-start | bytes 393224 | tf_op jit(solution)/shard_map/ppermute | solution.py:96
  13.7 12.9 %collective-permute-start.7 = (bf16[128,512]{1,0:T(8,128)(2,1)S(1)}, bf16[128,512]{1,0:T(8,128)(2,1)S(1)}, u32[]{:S(2)}, u32[]{:S(2)}) collective-permute-start(bf16[128,512]{1,0:T(8,128)(2,1)S(1)} %get-tuple-element.28), channel_id=1, source_target_pairs={{0,8},{1,11},{2,10},{3,9},{4,12},{5,15},{6,14},{7,13},{8,0},{9,3},... | collective-permute-start | bytes 393224 | tf_op jit(solution)/shard_map/ppermute | solution.py:96
  16.3 10.4 %collective-permute-start.8 = (bf16[128,512]{1,0:T(8,128)(2,1)S(1)}, bf16[128,512]{1,0:T(8,128)(2,1)S(1)}, u32[]{:S(2)}, u32[]{:S(2)}) collective-permute-start(bf16[128,512]{1,0:T(8,128)(2,1)S(1)} %get-tuple-element.29), channel_id=1, source_target_pairs={{0,12},{1,15},{2,14},{3,13},{4,8},{5,11},{6,10},{7,9},{8,4},{9,7},... | collective-permute-start | bytes 393224 | tf_op jit(solution)/shard_map/ppermute | solution.py:96
  16.3 31.0 %collective-permute-start.5 = (bf16[320,512]{1,0:T(8,128)(2,1)S(1)}, bf16[320,512]{1,0:T(8,128)(2,1)S(1)}, u32[]{:S(2)}, u32[]{:S(2)}) collective-permute-start(bf16[320,512]{1,0:T(8,128)(2,1)S(1)} %get-tuple-element.26), channel_id=1, source_target_pairs={{0,0},{1,3},{2,2},{3,1},{4,4},{5,7},{6,6},{7,5},{8,8},{9,11},{10,1... | collective-permute-start | bytes 983048 | tf_op jit(solution)/shard_map/ppermute | solution.py:96
  17.0 12.2 %collective-permute-start.1 = (bf16[128,1024]{1,0:T(8,128)(2,1)S(1)}, bf16[128,1024]{1,0:T(8,128)(2,1)S(1)}, u32[]{:S(2)}, u32[]{:S(2)}) collective-permute-start(bf16[128,1024]{1,0:T(8,128)(2,1)S(1)} %get-tuple-element.22), channel_id=1, source_target_pairs={{0,0},{1,19},{2,18},{3,1},{4,4},{5,23},{6,22},{7,5},{8,8},{9,27},{... | collective-permute-start | bytes 786440 | tf_op jit(solution)/shard_map/ppermute | solution.py:96
  17.7 11.5 %collective-permute-start.2 = (bf16[128,1024]{1,0:T(8,128)(2,1)S(1)}, bf16[128,1024]{1,0:T(8,128)(2,1)S(1)}, u32[]{:S(2)}, u32[]{:S(2)}) collective-permute-start(bf16[128,1024]{1,0:T(8,128)(2,1)S(1)} %get-tuple-element.23), channel_id=1, source_target_pairs={{0,4},{1,23},{2,22},{3,5},{4,0},{5,19},{6,18},{7,1},{8,12},{9,31},... | collective-permute-start | bytes 786440 | tf_op jit(solution)/shard_map/ppermute | solution.py:96
  26.7 20.7 %collective-permute-start.3 = (bf16[128,1024]{1,0:T(8,128)(2,1)S(1)}, bf16[128,1024]{1,0:T(8,128)(2,1)S(1)}, u32[]{:S(2)}, u32[]{:S(2)}) collective-permute-start(bf16[128,1024]{1,0:T(8,128)(2,1)S(1)} %get-tuple-element.24), channel_id=1, source_target_pairs={{0,8},{1,27},{2,26},{3,9},{4,12},{5,31},{6,30},{7,13},{8,0},{9,19}... | collective-permute-start | bytes 786440 | tf_op jit(solution)/shard_map/ppermute | solution.py:96
  26.7 20.7 %collective-permute-start.4 = (bf16[128,1024]{1,0:T(8,128)(2,1)S(1)}, bf16[128,1024]{1,0:T(8,128)(2,1)S(1)}, u32[]{:S(2)}, u32[]{:S(2)}) collective-permute-start(bf16[128,1024]{1,0:T(8,128)(2,1)S(1)} %get-tuple-element.25), channel_id=1, source_target_pairs={{0,12},{1,31},{2,30},{3,13},{4,8},{5,27},{6,26},{7,9},{8,4},{9,23}... | collective-permute-start | bytes 786440 | tf_op jit(solution)/shard_map/ppermute | solution.py:96
  49.8 1.7 %collective-permute-start.9 = (bf16[1184,128]{1,0:T(8,128)(2,1)S(1)}, bf16[1184,128]{1,0:T(8,128)(2,1)S(1)}, u32[]{:S(2)}, u32[]{:S(2)}) collective-permute-start(bf16[1184,128]{1,0:T(8,128)(2,1)S(1)} %get-tuple-element.31), channel_id=1, source_target_pairs={{0,1},{1,0},{2,3},{3,2},{4,5},{5,4},{6,7},{7,6},{8,9},{9,8},{10,11... | collective-permute-start | bytes 909320 | tf_op jit(solution)/shard_map/ppermute | solution.py:82
  52.1 10.5 %collective-permute-start.10 = (bf16[592,128]{1,0:T(8,128)(2,1)S(1)}, bf16[592,128]{1,0:T(8,128)(2,1)S(1)}, u32[]{:S(2)}, u32[]{:S(2)}) collective-permute-start(bf16[592,128]{1,0:T(8,128)(2,1)S(1)} %get-tuple-element.33), channel_id=1, source_target_pairs={{0,4},{4,0},{8,12},{12,8},{1,5},{5,1},{9,13},{13,9},{2,6},{6,2},{1... | collective-permute-start | bytes 454664 | tf_op jit(solution)/shard_map/ppermute | solution.py:82
  62.6 9.7 %collective-permute-start.11 = (bf16[592,128]{1,0:T(8,128)(2,1)S(1)}, bf16[592,128]{1,0:T(8,128)(2,1)S(1)}, u32[]{:S(2)}, u32[]{:S(2)}) collective-permute-start(bf16[592,128]{1,0:T(8,128)(2,1)S(1)} %shard_map.97.mine), channel_id=1, source_target_pairs={{0,8},{4,12},{8,0},{12,4},{1,9},{5,13},{9,1},{13,5},{2,10},{6,14},... | collective-permute-start | bytes 454664 | tf_op jit(solution)/shard_map/ppermute | solution.py:82
  72.4 5.3 %collective-permute-start.12 = (bf16[592,128]{1,0:T(8,128)(2,1)S(1)}, bf16[592,128]{1,0:T(8,128)(2,1)S(1)}, u32[]{:S(2)}, u32[]{:S(2)}) collective-permute-start(bf16[592,128]{1,0:T(8,128)(2,1)S(1)} %shard_map.98.refs_0_), channel_id=1, source_target_pairs={{0,4},{4,0},{8,12},{12,8},{1,5},{5,1},{9,13},{13,9},{2,6},{6,2},{1... | collective-permute-start | bytes 454664 | tf_op jit(solution)/shard_map/ppermute | solution.py:82
  72.5 5.2 %collective-permute-start.13 = (bf16[592,128]{1,0:T(8,128)(2,1)S(1)}, bf16[592,128]{1,0:T(8,128)(2,1)S(1)}, u32[]{:S(2)}, u32[]{:S(2)}) collective-permute-start(bf16[592,128]{1,0:T(8,128)(2,1)S(1)} %shard_map.98.refs_0_), channel_id=1, source_target_pairs={{0,1},{1,0},{2,3},{3,2},{4,5},{5,4},{6,7},{7,6},{8,9},{9,8},{10,11... | collective-permute-start | bytes 454664 | tf_op jit(solution)/shard_map/ppermute | solution.py:82
  77.7 1.4 %collective-permute-start.14 = (bf16[592,128]{1,0:T(8,128)(2,1)S(1)}, bf16[592,128]{1,0:T(8,128)(2,1)S(1)}, u32[]{:S(2)}, u32[]{:S(2)}) collective-permute-start(bf16[592,128]{1,0:T(8,128)(2,1)S(1)} %collective-permute-done.12.refs_1_), channel_id=1, source_target_pairs={{0,1},{1,0},{2,3},{3,2},{4,5},{5,4},{6,7},{7,6},{8,9},{9,8},{10,11... | collective-permute-start | bytes 454664 | tf_op jit(solution)/shard_map/ppermute | solution.py:82
  91.8 12.6 %collective-permute-start.17 = (bf16[128,768]{1,0:T(8,128)(2,1)S(1)}, bf16[128,768]{1,0:T(8,128)(2,1)S(1)}, u32[]{:S(2)}, u32[]{:S(2)}) collective-permute-start(bf16[128,768]{1,0:T(8,128)(2,1)S(1)} %shard_map.99), channel_id=1, source_target_pairs={{0,8},{1,11},{2,10},{3,9},{4,12},{5,15},{6,14},{7,13},{8,0},{9,3},... | collective-permute-start | bytes 589832 | tf_op jit(solution)/shard_map/ppermute | solution.py:96
  93.0 11.7 %collective-permute-start.16 = (bf16[128,768]{1,0:T(8,128)(2,1)S(1)}, bf16[128,768]{1,0:T(8,128)(2,1)S(1)}, u32[]{:S(2)}, u32[]{:S(2)}) collective-permute-start(bf16[128,768]{1,0:T(8,128)(2,1)S(1)} %shard_map.99), channel_id=1, source_target_pairs={{0,4},{1,7},{2,6},{3,5},{4,0},{5,3},{6,2},{7,1},{8,12},{9,15},{10,... | collective-permute-start | bytes 589832 | tf_op jit(solution)/shard_map/ppermute | solution.py:96
  95.0 10.3 %collective-permute-start.15 = (bf16[128,768]{1,0:T(8,128)(2,1)S(1)}, bf16[128,768]{1,0:T(8,128)(2,1)S(1)}, u32[]{:S(2)}, u32[]{:S(2)}) collective-permute-start(bf16[128,768]{1,0:T(8,128)(2,1)S(1)} %shard_map.99), channel_id=1, source_target_pairs={{0,0},{1,3},{2,2},{3,1},{4,4},{5,7},{6,6},{7,5},{8,8},{9,11},{10,1... | collective-permute-start | bytes 589832 | tf_op jit(solution)/shard_map/ppermute | solution.py:96
  104.4 6.6 %collective-permute-start.18 = (bf16[128,768]{1,0:T(8,128)(2,1)S(1)}, bf16[128,768]{1,0:T(8,128)(2,1)S(1)}, u32[]{:S(2)}, u32[]{:S(2)}) collective-permute-start(bf16[128,768]{1,0:T(8,128)(2,1)S(1)} %collective-permute-done.17.refs_2_), channel_id=1, source_target_pairs={{0,4},{4,0},{8,12},{12,8},{1,5},{5,1},{9,13},{13,9},{2,6},{6,2},{1... | collective-permute-start | bytes 589832 | tf_op jit(solution)/shard_map/ppermute | solution.py:82
  104.4 6.6 %collective-permute-start.21 = (bf16[128,768]{1,0:T(8,128)(2,1)S(1)}, bf16[128,768]{1,0:T(8,128)(2,1)S(1)}, u32[]{:S(2)}, u32[]{:S(2)}) collective-permute-start(bf16[128,768]{1,0:T(8,128)(2,1)S(1)} %collective-permute-done.17.refs_2_), channel_id=1, source_target_pairs={{0,1},{1,0},{2,3},{3,2},{4,5},{5,4},{6,7},{7,6},{8,9},{9,8},{10,11... | collective-permute-start | bytes 589832 | tf_op jit(solution)/shard_map/ppermute | solution.py:82
  104.7 6.4 %collective-permute-start.20 = (bf16[128,768]{1,0:T(8,128)(2,1)S(1)}, bf16[128,768]{1,0:T(8,128)(2,1)S(1)}, u32[]{:S(2)}, u32[]{:S(2)}) collective-permute-start(bf16[128,768]{1,0:T(8,128)(2,1)S(1)} %collective-permute-done.16.refs_1_), channel_id=1, source_target_pairs={{0,1},{1,0},{2,3},{3,2},{4,5},{5,4},{6,7},{7,6},{8,9},{9,8},{10,11... | collective-permute-start | bytes 589832 | tf_op jit(solution)/shard_map/ppermute | solution.py:82
  105.3 5.8 %collective-permute-start.19 = (bf16[128,768]{1,0:T(8,128)(2,1)S(1)}, bf16[128,768]{1,0:T(8,128)(2,1)S(1)}, u32[]{:S(2)}, u32[]{:S(2)}) collective-permute-start(bf16[128,768]{1,0:T(8,128)(2,1)S(1)} %collective-permute-done.15.refs_0_), channel_id=1, source_target_pairs={{0,1},{1,0},{2,3},{3,2},{4,5},{5,4},{6,7},{7,6},{8,9},{9,8},{10,11... | collective-permute-start | bytes 589832 | tf_op jit(solution)/shard_map/ppermute | solution.py:82
  111.1 1.4 %collective-permute-start.22 = (bf16[128,768]{1,0:T(8,128)(2,1)S(1)}, bf16[128,768]{1,0:T(8,128)(2,1)S(1)}, u32[]{:S(2)}, u32[]{:S(2)}) collective-permute-start(bf16[128,768]{1,0:T(8,128)(2,1)S(1)} %collective-permute-done.18.refs_3_), channel_id=1, source_target_pairs={{0,1},{1,0},{2,3},{3,2},{4,5},{5,4},{6,7},{7,6},{8,9},{9,8},{10,11... | collective-permute-start | bytes 589832 | tf_op jit(solution)/shard_map/ppermute | solution.py:82

commit v4 on v3

--- a/solution.py
+++ b/solution.py
@@ -10,6 +10,7 @@
 RANK = 64
 POWER = 2
 BLK = 128
+FAR_FIRST = (2, 3, 1, 0)
 
 precise = lax.Precision.HIGHEST
 f32 = jnp.float32
@@ -191,60 +192,73 @@
 
 def packed_rows(dps):
     per_gram = (dps * (dps - 1) // 2 + dps // 2) * BLK
-    used = 2 * per_gram + dps * RANK + 16
-    return per_gram, pl.cdiv(used, 4 * 16) * 4 * 16
-
-
-def gram_kernel(dps, idx, *refs):
-    z, core = idx[0], idx[2]
-    bigs, smalls = refs[:dps], refs[dps : 2 * dps]
-    big, small, keep, send, flat = refs[2 * dps :]
-    half_w = big.shape[1] // 2
-    for d in range(dps):
-        rows = pl.ds(pl.multiple_of((z ^ d) * BLK, BLK), BLK)
-        big[rows, :] = bigs[d][...]
-        small[rows, :] = smalls[d][:BLK, :]
-    per_gram, total = packed_rows(dps)
+    thin = pl.cdiv(per_gram + 16, 32) * 32
+    rest = per_gram + dps * RANK + 16
+    wide = pl.cdiv(thin + rest, 64) * 64 - thin
+    return per_gram, thin, wide
+
+
+def pack_gram(m, flat, dps):
     r = lax.broadcasted_iota(jnp.int32, (BLK, BLK), 0)
     c = lax.broadcasted_iota(jnp.int32, (BLK, BLK), 1)
-    at, diagonals = 0, []
-
-    def put(value):
-        nonlocal at
-        flat[at : at + value.shape[0], :] = value.astype(bf16)
-        at += value.shape[0]
-
-    for m in (big, small):
-        on = []
-        for i in range(dps):
-            row = nt(m[i * BLK : (i + 1) * BLK, :], m[: (i + 1) * BLK, :])
-            for j in range(i):
-                put(row[:, j * BLK : (j + 1) * BLK])
-            on.append(row[:, i * BLK :])
-        for i in range(0, dps, 2):
-            put(jnp.where(r > c, on[i], on[i + 1]))
-        diagonals += [jnp.sum(jnp.where(r == c, v, 0.0), axis=0, keepdims=True) for v in on]
-        diagonals.append(jnp.zeros((8 - dps, BLK), f32))
-    sk = smalls[0]
+    at, on = 0, []
+    for i in range(dps):
+        row = nt(m[i * BLK : (i + 1) * BLK, :], m[: (i + 1) * BLK, :])
+        for j in range(i):
+            flat[at : at + BLK, :] = row[:, j * BLK : (j + 1) * BLK].astype(bf16)
+            at += BLK
+        on.append(row[:, i * BLK :])
+    for i in range(0, dps, 2):
+        flat[at : at + BLK, :] = jnp.where(r > c, on[i], on[i + 1]).astype(bf16)
+        at += BLK
+    diagonals = [jnp.sum(jnp.where(r == c, v, 0.0), axis=0, keepdims=True) for v in on]
+    diagonals.append(jnp.zeros((16 - dps, BLK), f32))
+    return at, jnp.concatenate(diagonals, axis=0).astype(bf16)
+
+
+def hand_out(core, flat, keep, send):
+    half = flat.shape[0] // 2
+    keep[...] = flat[pl.ds(pl.multiple_of(core * half, 16), half), :]
+    send[...] = flat[pl.ds(pl.multiple_of((1 - core) * half, 16), half), :]
+
+
+def thin_gram_kernel(dps, idx, *refs):
+    z, core = idx[0], idx[2]
+    smalls, small, keep, send, flat = refs[:dps], *refs[dps:]
+    for d, ref in zip(FAR_FIRST, smalls):
+        small[pl.ds(pl.multiple_of((z ^ d) * BLK, BLK), BLK), :] = ref[:BLK, :]
+    at, diagonals = pack_gram(small, flat, dps)
+    flat[at:, :] = jnp.zeros((flat.shape[0] - at, BLK), bf16)
+    flat[at : at + 16, :] = diagonals
+    hand_out(core, flat, keep, send)
+
+
+def wide_gram_kernel(dps, idx, *refs):
+    z, core = idx[0], idx[2]
+    bigs, small, sk, big, keep, send, flat = refs[:dps], *refs[dps:]
+    half_w = big.shape[1] // 2
+    for d, ref in zip(FAR_FIRST, bigs):
+        big[pl.ds(pl.multiple_of((z ^ d) * BLK, BLK), BLK), :] = ref[...]
+    at, diagonals = pack_gram(big, flat, dps)
     first = (
         nt(sk[BLK : BLK + RANK, :], big[:, :half_w])
         + nt(sk[BLK + RANK : BLK + 2 * RANK, :], big[:, half_w:])
         + nt(sk[BLK + 2 * RANK :, :], small[...])
-    )
+    ).astype(bf16)
     for i in range(dps):
-        put(first[:, i * BLK : (i + 1) * BLK])
-    put(jnp.concatenate(diagonals, axis=0))
-    put(jnp.zeros((total - at, BLK), f32))
-    half = total // 2
-    keep[...] = flat[pl.ds(pl.multiple_of(core * half, 16), half), :]
-    send[...] = flat[pl.ds(pl.multiple_of((1 - core) * half, 16), half), :]
-
-
-def add_halves_kernel(idx, mine, got, keep, send):
-    size, bit = keep.shape[0], idx[0] % 2
+        flat[at : at + RANK, :] = first[:, i * BLK : (i + 1) * BLK]
+        at += RANK
+    flat[at:, :] = jnp.zeros((flat.shape[0] - at, BLK), bf16)
+    flat[at : at + 16, :] = diagonals
+    hand_out(core, flat, keep, send)
+
+
+def add_halves_kernel(idx, thin_mine, thin_got, wide_mine, wide_got, keep, send, both):
+    size, bit, split_at = keep.shape[0], idx[0] % 2, thin_mine.shape[0]
+    both[:split_at, :] = (thin_mine[...].astype(f32) + thin_got[...].astype(f32)).astype(bf16)
+    both[split_at:, :] = (wide_mine[...].astype(f32) + wide_got[...].astype(f32)).astype(bf16)
     for out, which in ((keep, bit), (send, 1 - bit)):
-        part = pl.ds(pl.multiple_of(which * size, 16), size)
-        out[...] = (mine[part, :].astype(f32) + got[part, :].astype(f32)).astype(bf16)
+        out[...] = both[pl.ds(pl.multiple_of(which * size, 16), size), :]
 
 
 def add_kernel(mine, got, out):
@@ -319,26 +333,29 @@
 
 def chain_kernel(dps, counts, idx, *refs):
     z, out_half, core = idx[0], idx[1], idx[2]
-    quarters, big, small, out, flat, left, right = refs[:4], *refs[4:]
+    quarters, big, small, out, flat, thin, wide, left, right = refs[:4], *refs[4:]
     size, bit = quarters[0].shape[0], z % 2
     for n, ref in enumerate(quarters):
         which = 2 * (core ^ (n // 2)) + (bit ^ (n % 2))
         flat[pl.ds(pl.multiple_of(which * size, 16), size), :] = ref[...]
-    per_gram, _ = packed_rows(dps)
+    per_gram, thin_rows, wide_rows = packed_rows(dps)
+    for n in range(2):
+        at, split_at = n * 2 * size, n * 2 * size + thin_rows // 2
+        thin[n * (thin_rows // 2) : (n + 1) * (thin_rows // 2), :] = flat[at:split_at, :]
+        wide[n * (wide_rows // 2) : (n + 1) * (wide_rows // 2), :] = flat[split_at : at + 2 * size, :]
     r = lax.broadcasted_iota(jnp.int32, (BLK, BLK), 0)
     c = lax.broadcasted_iota(jnp.int32, (BLK, BLK), 1)
-    start = 2 * per_gram
     rows = jnp.concatenate(
-        [flat[start + i * RANK : start + (i + 1) * RANK, :] for i in range(dps)], axis=1
+        [wide[per_gram + i * RANK : per_gram + (i + 1) * RANK, :] for i in range(dps)], axis=1
     ).astype(f32)
-    start += dps * RANK
-    diagonals = flat[start : start + 16, :].astype(f32)
+    wide_diag = wide[per_gram + dps * RANK : per_gram + dps * RANK + 16, :].astype(f32)
+    thin_diag = thin[per_gram : per_gram + 16, :].astype(f32)
     is_out = out_half == 1
-    for gram, which in ((left, out_half), (right, 1 - out_half)):
-        base = which * per_gram
+    for gram, is_wide in ((left, out_half == 0), (right, is_out)):
 
         def block(n):
-            return flat[pl.ds(pl.multiple_of(base + n * BLK, BLK), BLK), :].astype(f32)
+            part = slice(n * BLK, (n + 1) * BLK)
+            return jnp.where(is_wide, wide[part, :].astype(f32), thin[part, :].astype(f32))
 
         def put(i, j, value):
             gram[i * BLK : (i + 1) * BLK, j * BLK : (j + 1) * BLK] = value.astype(bf16)
@@ -350,7 +367,7 @@
                 put(i, j, value)
                 put(j, i, value.T)
                 n += 1
-        diag = jnp.where(which == 1, diagonals[8:, :], diagonals[:8, :])
+        diag = jnp.where(is_wide, wide_diag, thin_diag)
         for i in range(0, dps, 2):
             value = block(n)
             turned = value.T
@@ -441,7 +458,10 @@
     wide, narrow = norm_in.shape[2], query_grad.shape[2]
     big_w, small_w = wide // dps, narrow // dps
     tokens = dps * BLK
-    args = (norm_in[0], query_grad[0], attn_out[0], handed[0], sketch_q[0], sketch_o[0])
+    args = tuple(
+        pltpu.with_memory_space_constraint(v[0], pltpu.HBM)
+        for v in (norm_in, query_grad, attn_out, handed, sketch_q, sketch_o)
+    )
     in_hbm = [SMEM] + [pl.BlockSpec(memory_space=pltpu.HBM)] * len(args)
 
     give = call(
@@ -461,23 +481,36 @@
         [pltpu.SemaphoreType.DMA((2 * dps + 1,))],
         in_hbm + [VMEM],
     )
-    bigs = [routed(v, sizes, d, True) for d, v in enumerate(packed[:dps])]
-    smalls = [routed(v, sizes, d, False) for d, v in enumerate(packed[dps:])]
-
-    _, total = packed_rows(dps)
-    big, small, keep, send = call(
-        functools.partial(gram_kernel, dps),
-        [
-            shape(tokens, 2 * big_w),
-            shape(tokens, 2 * small_w),
-            shape(total // 2, BLK),
-            shape(total // 2, BLK),
-        ],
-        (idx, *bigs, *smalls),
-        [pltpu.VMEM((total, BLK), bf16)],
-    )
+    smalls = [routed(packed[dps + d], sizes, d, False) for d in FAR_FIRST]
+    bigs = [routed(packed[d], sizes, d, True) for d in FAR_FIRST[:2]]
+
+    _, thin_rows, wide_rows = packed_rows(dps)
+
+    def gram(kernel, m, rows, operands):
+        m, keep, send = call(
+            functools.partial(kernel, dps),
+            [m, shape(rows // 2, BLK), shape(rows // 2, BLK)],
+            (idx, *operands),
+            [pltpu.VMEM((rows, BLK), bf16)],
+        )
+        return m, keep, swap(send, "tensor", 1)
+
+    small, *thin = gram(thin_gram_kernel, shape(tokens, 2 * small_w), thin_rows, smalls)
+    near = lax.optimization_barrier((packed[1], packed[0], thin[0]))
+    thin[0] = near[2]
+    bigs += [routed(v, sizes, d, True) for v, d in zip(near, FAR_FIRST[2:])]
+    bigs[0], thin[1] = lax.optimization_barrier((bigs[0], thin[1]))
+    big, *rest = gram(
+        wide_gram_kernel, shape(tokens, 2 * big_w), wide_rows, (*bigs, small, smalls[-1])
+    )
+    total = thin_rows + wide_rows
     quarter = shape(total // 4, BLK)
-    keep, send = call(add_halves_kernel, [quarter] * 2, (idx, keep, swap(send, "tensor", 1)))
+    keep, send = call(
+        add_halves_kernel,
+        [quarter] * 2,
+        (idx, *thin, *rest),
+        [pltpu.VMEM((total // 2, BLK), bf16)],
+    )
     for bit, value in ((1, send), (2, None)):
         value = swap(keep if value is None else value, "dp", bit)
         keep = call(add_kernel, quarter, (keep, value), (), [VMEM] * 2)
@@ -491,6 +524,8 @@
         (idx, *quarters, big, small),
         [
             pltpu.VMEM((total, BLK), bf16),
+            pltpu.VMEM((thin_rows, BLK), bf16),
+            pltpu.VMEM((wide_rows, BLK), bf16),
             pltpu.VMEM((tokens, tokens), bf16),
             pltpu.VMEM((tokens, tokens), bf16),
         ],

time: 115 us -> 113 us (0.983)
  starting transfers between devices: 26.1 us -> 48.6 us
  waiting for transfers between devices: 62.2 us -> 41 us
  local copies, waits for them, and re-layouts: 5.84 us -> 0 us
  Pallas kernels: 19.1 us -> 22 us
    ppermute x11, waiting for transfers between devices: 33.8 us -> 10.8 us  [routed(): return lax.ppermute(value, ('section', 'dp', 'tensor'), pairs)]
    ppermute x11, starting transfers between devices: 15.7 us -> 30.7 us  [routed(): return lax.ppermute(value, ('section', 'dp', 'tensor'), pairs)]
    ppermute x12 -> x13, starting transfers between devices: 10.4 us -> 17.9 us  [swap(): return lax.ppermute(value, axis, [(i, i ^ bit) for i in range(count)])]
    unnamed x12 -> x0, local copies, waits for them, and re-layouts: 5.84 us -> none
    pallas_call x8 -> x9, Pallas kernels: 19.1 us -> 22 us  [call(): pl.pallas_call(kernel, out_shape=out_shapes, in_specs=spaces, out_specs=j...]
    ppermute x12 -> x13, waiting for transfers between devices: 28.4 us -> 30.1 us  [swap(): return lax.ppermute(value, axis, [(i, i ^ bit) for i in range(count)])]
  transfers between devices with their start and end apart: 23 -> 24, of which waited for: 12 -> 11; matrix products, arithmetic and copies ran while one was open for 0% -> 0% of each run, Pallas kernels for 0% -> 1%
where the time goes in v4:
time: 113 us; the launch traced here: 112 us
  starting transfers between devices  48.6 us (43%)
  waiting for transfers between devices  41 us (36%)
  Pallas kernels  22 us (19%)
    ppermute x11, starting transfers between devices, routed(): return lax.ppermute(value, ('section', 'dp', 'tensor'), pairs)  30.7 us
    ppermute x13, waiting for transfers between devices, swap(): return lax.ppermute(value, axis, [(i, i ^ bit) for i in range(count)])  30.1 us
    pallas_call x9, Pallas kernels, call(): pl.pallas_call(kernel, out_shape=out_shapes, in_specs=spaces, out_specs=j...  22 us
    ppermute x13, starting transfers between devices, swap(): return lax.ppermute(value, axis, [(i, i ^ bit) for i in range(count)])  17.9 us
    ppermute x11, waiting for transfers between devices, routed(): return lax.ppermute(value, ('section', 'dp', 'tensor'), pairs)  10.8 us
  transfers between devices with their start and end apart: 24, of which 11 were waited for; matrix products, arithmetic and copies ran while one was open for 0% of the time, Pallas kernels for 1%

profile of v4, /device:TPU:0, one launch (start us, length us, event | category | flops | bytes accessed | tf_op | source)
XLA Modules:
  0.0 112.4 jit_solution(1126902970384161384)
XLA Ops:
  0.6 0.1 pad_add_fusion.idx
  0.7 1.7 %shard_map.93 = bf16[144,3072]{1,0:T(8,128)(2,1)S(1)} custom-call(s32[4]{0:T(128)S(1)} %pad_add_fusion.idx, bf16[128,2048]{1,0:T(8,128)(2,1)} %bitcast.14, bf16[128,1024]{1,0:T(8,128)(2,1)} %bitcast.18, bf16[128,1024]{1,0:T(8,128)(2,1)} %bitcast.20, bf16[128,2048]{1,0:T(8,128)(2,1)} %bitcast.16, bf16[64,1024]{1,0:T(8,128)(2,1)} %bitcast.24, ...), custom_call_target="tpu_custom_call" | custom-call | tf_op jit(solution)/shard_map/pallas_call | solution.py:438
  2.4 0.5 collective-permute-start
  3.0 2.1 %collective-permute-done.got = bf16[144,3072]{1,0:T(8,128)(2,1)S(1)} collective-permute-done((bf16[144,3072]{1,0:T(8,128)(2,1)S(1)}, bf16[144,3072]{1,0:T(8,128)(2,1)S(1)}, u32[]{:S(2)}, u32[]{:S(2)}) %collective-permute-start) | collective-permute-done | bytes 884768 | tf_op jit(solution)/shard_map/ppermute | solution.py:83
  5.0 1.8 %shard_map.94 = (bf16[128,1024]{1,0:T(8,128)(2,1)S(1)}, bf16[128,1024]{1,0:T(8,128)(2,1)S(1)}, bf16[128,1024]{1,0:T(8,128)(2,1)S(1)}, bf16[128,1024]{1,0:T(8,128...) custom-call(s32[4]{0:T(128)S(1)} %pad_add_fusion.idx, ...), custom_call_target="tpu_custom_call" | custom-call | tf_op jit(solution)/shard_map/pallas_call | solution.py:438
  6.9 0.7 collective-permute-start.4
  7.6 4.0 %collective-permute-start.1 = (bf16[128,512]{1,0:T(8,128)(2,1)S(1)}, bf16[128,512]{1,0:T(8,128)(2,1)S(1)}, u32[]{:S(2)}, u32[]{:S(2)}) collective-permute-start(bf16[128,512]{1,0:T(8,128)(2,1)S(1)} %get-tuple-element.31), channel_id=1, source_target_pairs={{0,8},{1,11},{2,10},{3,9},{4,12},{5,15},{6,14},{7,13},{8,0},{9,3},... | collective-permute-start | bytes 393224 | tf_op jit(solution)/shard_map/ppermute | solution.py:97
  11.6 1.3 %collective-permute-start.2 = (bf16[128,512]{1,0:T(8,128)(2,1)S(1)}, bf16[128,512]{1,0:T(8,128)(2,1)S(1)}, u32[]{:S(2)}, u32[]{:S(2)}) collective-permute-start(bf16[128,512]{1,0:T(8,128)(2,1)S(1)} %get-tuple-element.32), channel_id=1, source_target_pairs={{0,12},{1,15},{2,14},{3,13},{4,8},{5,11},{6,10},{7,9},{8,4},{9,7},... | collective-permute-start | bytes 393224 | tf_op jit(solution)/shard_map/ppermute | solution.py:97
  12.9 0.2 collective-permute-start.3
  13.2 2.8 %collective-permute-start.5 = (bf16[128,1024]{1,0:T(8,128)(2,1)S(1)}, bf16[128,1024]{1,0:T(8,128)(2,1)S(1)}, u32[]{:S(2)}, u32[]{:S(2)}) collective-permute-start(bf16[128,1024]{1,0:T(8,128)(2,1)S(1)} %get-tuple-element.37), channel_id=1, source_target_pairs={{0,8},{1,27},{2,26},{3,9},{4,12},{5,31},{6,30},{7,13},{8,0},{9,19}... | collective-permute-start | bytes 786440 | tf_op jit(solution)/shard_map/ppermute | solution.py:97
  16.0 0.0 collective-permute-done.1.refs_0_
  16.0 10.9 %collective-permute-start.7 = (bf16[128,1024]{1,0:T(8,128)(2,1)S(1)}, bf16[128,1024]{1,0:T(8,128)(2,1)S(1)}, u32[]{:S(2)}, u32[]{:S(2)}) collective-permute-start(bf16[128,1024]{1,0:T(8,128)(2,1)S(1)} %get-tuple-element.41), channel_id=1, source_target_pairs={{0,12},{1,31},{2,30},{3,13},{4,8},{5,27},{6,26},{7,9},{8,4},{9,23}... | collective-permute-start | bytes 786440 | tf_op jit(solution)/shard_map/ppermute | solution.py:97
  26.9 0.0 collective-permute-done.2.refs_1_
  26.9 0.0 collective-permute-done.3.refs_2_
  26.9 0.0 collective-permute-done.4.refs_3_.refs_5_
  26.9 1.1 %shard_map.95 = (bf16[512,512]{1,0:T(8,128)(2,1)S(1)}, bf16[528,128]{1,0:T(8,128)(2,1)S(1)}, bf16[528,128]{1,0:T(8,128)(2,1)S(1)}) custom-call(s32[4]{0:T(128)S(1)} %pad_add_fusion.idx, bf16[128,512]{1,0:T(8,128)(2,1)S(1)} %collective-permute-done.1.refs_0_, bf16[128,512]{1,0:T(8,128)(2,1)S(1)} %collective-permute-done.2.refs_1_, ...), custom_call_target="tpu_custom_call" | custom-call | tf_op jit(solution)/shard_map/pallas_call | solution.py:438
  28.0 6.9 %collective-permute-start.8 = (bf16[128,1024]{1,0:T(8,128)(2,1)S(1)}, bf16[128,1024]{1,0:T(8,128)(2,1)S(1)}, u32[]{:S(2)}, u32[]{:S(2)}) collective-permute-start(bf16[128,1024]{1,0:T(8,128)(2,1)S(1)} %get-tuple-element.42), channel_id=1, source_target_pairs={{0,4},{1,23},{2,22},{3,5},{4,0},{5,19},{6,18},{7,1},{8,12},{9,31},... | collective-permute-start | bytes 786440 | tf_op jit(solution)/shard_map/ppermute | solution.py:97
  34.9 0.7 collective-permute-start.9
  35.6 7.9 %collective-permute-start.6 = (bf16[528,128]{1,0:T(8,128)(2,1)S(1)}, bf16[528,128]{1,0:T(8,128)(2,1)S(1)}, u32[]{:S(2)}, u32[]{:S(2)}) collective-permute-start(bf16[528,128]{1,0:T(8,128)(2,1)S(1)} %get-tuple-element.38), channel_id=1, source_target_pairs={{0,1},{1,0},{2,3},{3,2},{4,5},{5,4},{6,7},{7,6},{8,9},{9,8},{10,11... | collective-permute-start | bytes 405512 | tf_op jit(solution)/shard_map/ppermute | solution.py:83
  43.5 1.0 collective-permute-done.6.thin_got
  44.5 0.0 collective-permute-done.7.refs_1_
  44.5 1.6 %collective-permute-done.8.refs_2_ = bf16[128,1024]{1,0:T(8,128)(2,1)S(1)} collective-permute-done((bf16[128,1024]{1,0:T(8,128)(2,1)S(1)}, bf16[128,1024]{1,0:T(8,128)(2,1)S(1)}, u32[]{:S(2)}, u32[]{:S(2)}) %collective-permute-start.8) | collective-permute-done | bytes 262176 | tf_op jit(solution)/shard_map/ppermute | solution.py:97
  46.1 2.0 %shard_map.96 = (bf16[512,1024]{1,0:T(8,128)(2,1)S(1)}, bf16[656,128]{1,0:T(8,128)(2,1)S(1)}, bf16[656,128]{1,0:T(8,128)(2,1)S(1)}) custom-call(s32[4]{0:T(128)S(1)} %pad_add_fusion.idx, bf16[128,1024]{1,0:T(8,128)(2,1)S(1)} %collective-permute-done.5.refs_0_, bf16[128,1024]{1,0:T(8,128)(2,1)S(1)} %collective-permute-done.7.refs_1_, ...), custom_call_target="tpu_custom_call" | custom-call | tf_op jit(solution)/shard_map/pallas_call | solution.py:438
  48.1 3.1 %collective-permute-start.10 = (bf16[656,128]{1,0:T(8,128)(2,1)S(1)}, bf16[656,128]{1,0:T(8,128)(2,1)S(1)}, u32[]{:S(2)}, u32[]{:S(2)}) collective-permute-start(bf16[656,128]{1,0:T(8,128)(2,1)S(1)} %get-tuple-element.46), channel_id=1, source_target_pairs={{0,1},{1,0},{2,3},{3,2},{4,5},{5,4},{6,7},{7,6},{8,9},{9,8},{10,11... | collective-permute-start | bytes 503816 | tf_op jit(solution)/shard_map/ppermute | solution.py:83
  51.2 1.0 collective-permute-done.10.wide_got
  52.2 0.7 shard_map.97
  52.9 2.9 %collective-permute-start.11 = (bf16[592,128]{1,0:T(8,128)(2,1)S(1)}, bf16[592,128]{1,0:T(8,128)(2,1)S(1)}, u32[]{:S(2)}, u32[]{:S(2)}) collective-permute-start(bf16[592,128]{1,0:T(8,128)(2,1)S(1)} %get-tuple-element.48), channel_id=1, source_target_pairs={{0,4},{4,0},{8,12},{12,8},{1,5},{5,1},{9,13},{13,9},{2,6},{6,2},{1... | collective-permute-start | bytes 454664 | tf_op jit(solution)/shard_map/ppermute | solution.py:83
  55.8 4.5 %collective-permute-done.11.got = bf16[592,128]{1,0:T(8,128)(2,1)S(1)} collective-permute-done((bf16[592,128]{1,0:T(8,128)(2,1)S(1)}, bf16[592,128]{1,0:T(8,128)(2,1)S(1)}, u32[]{:S(2)}, u32[]{:S(2)}) %collective-permute-start.11) | collective-permute-done | bytes 151584 | tf_op jit(solution)/shard_map/ppermute | solution.py:83
  60.3 2.3 %collective-permute-start.12 = (bf16[592,128]{1,0:T(8,128)(2,1)S(1)}, bf16[592,128]{1,0:T(8,128)(2,1)S(1)}, u32[]{:S(2)}, u32[]{:S(2)}) collective-permute-start(bf16[592,128]{1,0:T(8,128)(2,1)S(1)} %shard_map.98.mine), channel_id=1, source_target_pairs={{0,8},{4,12},{8,0},{12,4},{1,9},{5,13},{9,1},{13,5},{2,10},{6,14},... | collective-permute-start | bytes 454664 | tf_op jit(solution)/shard_map/ppermute | solution.py:83
  62.6 7.6 %collective-permute-done.12.got = bf16[592,128]{1,0:T(8,128)(2,1)S(1)} collective-permute-done((bf16[592,128]{1,0:T(8,128)(2,1)S(1)}, bf16[592,128]{1,0:T(8,128)(2,1)S(1)}, u32[]{:S(2)}, u32[]{:S(2)}) %collective-permute-start.12) | collective-permute-done | bytes 151584 | tf_op jit(solution)/shard_map/ppermute | solution.py:83
  70.2 0.1 collective-permute-start.13
  70.3 0.1 collective-permute-start.14
  70.4 5.1 %collective-permute-done.13.refs_1_ = bf16[592,128]{1,0:T(8,128)(2,1)S(1)} collective-permute-done((bf16[592,128]{1,0:T(8,128)(2,1)S(1)}, bf16[592,128]{1,0:T(8,128)(2,1)S(1)}, u32[]{:S(2)}, u32[]{:S(2)}) %collective-permute-start.13) | collective-permute-done | bytes 151584 | tf_op jit(solution)/shard_map/ppermute | solution.py:83
  75.5 0.0 collective-permute-start.15
  75.5 0.0 collective-permute-done.14.refs_2_
  75.5 1.4 %collective-permute-done.15.refs_3_ = bf16[592,128]{1,0:T(8,128)(2,1)S(1)} collective-permute-done((bf16[592,128]{1,0:T(8,128)(2,1)S(1)}, bf16[592,128]{1,0:T(8,128)(2,1)S(1)}, u32[]{:S(2)}, u32[]{:S(2)}) %collective-permute-start.15) | collective-permute-done | bytes 151584 | tf_op jit(solution)/shard_map/ppermute | solution.py:83
  76.8 12.8 %shard_map.100 = bf16[128,768]{1,0:T(8,128)(2,1)S(1)} custom-call(s32[4]{0:T(128)S(1)} %pad_add_fusion.idx, bf16[592,128]{1,0:T(8,128)(2,1)S(1)} %shard_map.99.refs_0_, bf16[592,128]{1,0:T(8,128)(2,1)S(1)} %collective-permute-done.13.refs_1_, bf16[592,128]{1,0:T(8,128)(2,1)S(1)} %collective-permute-done.14.refs_2_, ...), custom_call_target="tpu_custom_call" | custom-call | tf_op jit(solution)/shard_map/pallas_call | solution.py:438
  89.7 0.5 collective-permute-start.18
  90.1 2.0 %collective-permute-start.17 = (bf16[128,768]{1,0:T(8,128)(2,1)S(1)}, bf16[128,768]{1,0:T(8,128)(2,1)S(1)}, u32[]{:S(2)}, u32[]{:S(2)}) collective-permute-start(bf16[128,768]{1,0:T(8,128)(2,1)S(1)} %shard_map.100), channel_id=1, source_target_pairs={{0,4},{1,7},{2,6},{3,5},{4,0},{5,3},{6,2},{7,1},{8,12},{9,15},{10,... | collective-permute-start | bytes 589832 | tf_op jit(solution)/shard_map/ppermute | solution.py:97
  92.2 0.7 collective-permute-start.16
  92.8 9.2 %collective-permute-done.18.refs_2_ = bf16[128,768]{1,0:T(8,128)(2,1)S(1)} collective-permute-done((bf16[128,768]{1,0:T(8,128)(2,1)S(1)}, bf16[128,768]{1,0:T(8,128)(2,1)S(1)}, u32[]{:S(2)}, u32[]{:S(2)}) %collective-permute-start.18) | collective-permute-done | bytes 196640 | tf_op jit(solution)/shard_map/ppermute | solution.py:97
  102.1 0.0 collective-permute-start.19
  102.1 0.4 collective-permute-start.22
  102.5 0.6 collective-permute-start.21
  103.2 0.0 collective-permute-start.20
  103.2 6.2 %collective-permute-done.19.refs_3_ = bf16[128,768]{1,0:T(8,128)(2,1)S(1)} collective-permute-done((bf16[128,768]{1,0:T(8,128)(2,1)S(1)}, bf16[128,768]{1,0:T(8,128)(2,1)S(1)}, u32[]{:S(2)}, u32[]{:S(2)}) %collective-permute-start.19) | collective-permute-done | bytes 196640 | tf_op jit(solution)/shard_map/ppermute | solution.py:83
  109.3 1.4 %collective-permute-done.23.refs_7_ = bf16[128,768]{1,0:T(8,128)(2,1)S(1)} collective-permute-done((bf16[128,768]{1,0:T(8,128)(2,1)S(1)}, bf16[128,768]{1,0:T(8,128)(2,1)S(1)}, u32[]{:S(2)}, u32[]{:S(2)}) %collective-permute-start.23) | collective-permute-done | bytes 196640 | tf_op jit(solution)/shard_map/ppermute | solution.py:83
  110.8 1.7 %shard_map.101 = (bf16[64,2048]{1,0:T(8,128)(2,1)}, f32[64,1024]{1,0:T(8,128)}, bf16[64,1024]{1,0:T(8,128)(2,1)}, f32[64,2048]{1,0:T(8,128)}) custom-call(s32[4]{0:T(128)S(1)} %pad_add_fusion.idx, bf16[128,768]{1,0:T(8,128)(2,1)S(1)} %collective-permute-done.16.refs_0_, bf16[128,768]{1,0:T(8,128)(2,1)S(1)} %collective-permute-done.17.refs_1_, ...), custom_call_target="tpu_custom_call" | custom-call | tf_op jit(solution)/shard_map/pallas_call | solution.py:438
  (10 shorter events, 0.1 us)
Async XLA Ops:
  2.4 2.6 %collective-permute-start = (bf16[144,3072]{1,0:T(8,128)(2,1)S(1)}, bf16[144,3072]{1,0:T(8,128)(2,1)S(1)}, u32[]{:S(2)}, u32[]{:S(2)}) collective-permute-start(bf16[144,3072]{1,0:T(8,128)(2,1)S(1)} %shard_map.93), channel_id=1, source_target_pairs={{0,1},{1,0},{2,3},{3,2},{4,5},{5,4},{6,7},{7,6},{8,9},{9,8},{10,11... | collective-permute-start | bytes 2654216 | tf_op jit(solution)/shard_map/ppermute | solution.py:83
  6.9 20.0 %collective-permute-start.4 = (bf16[320,512]{1,0:T(8,128)(2,1)S(1)}, bf16[320,512]{1,0:T(8,128)(2,1)S(1)}, u32[]{:S(2)}, u32[]{:S(2)}) collective-permute-start(bf16[320,512]{1,0:T(8,128)(2,1)S(1)} %get-tuple-element.34), channel_id=1, source_target_pairs={{0,0},{1,3},{2,2},{3,1},{4,4},{5,7},{6,6},{7,5},{8,8},{9,11},{10,1... | collective-permute-start | bytes 983048 | tf_op jit(solution)/shard_map/ppermute | solution.py:97
  7.6 8.4 %collective-permute-start.1 = (bf16[128,512]{1,0:T(8,128)(2,1)S(1)}, bf16[128,512]{1,0:T(8,128)(2,1)S(1)}, u32[]{:S(2)}, u32[]{:S(2)}) collective-permute-start(bf16[128,512]{1,0:T(8,128)(2,1)S(1)} %get-tuple-element.31), channel_id=1, source_target_pairs={{0,8},{1,11},{2,10},{3,9},{4,12},{5,15},{6,14},{7,13},{8,0},{9,3},... | collective-permute-start | bytes 393224 | tf_op jit(solution)/shard_map/ppermute | solution.py:97
  11.6 15.3 %collective-permute-start.2 = (bf16[128,512]{1,0:T(8,128)(2,1)S(1)}, bf16[128,512]{1,0:T(8,128)(2,1)S(1)}, u32[]{:S(2)}, u32[]{:S(2)}) collective-permute-start(bf16[128,512]{1,0:T(8,128)(2,1)S(1)} %get-tuple-element.32), channel_id=1, source_target_pairs={{0,12},{1,15},{2,14},{3,13},{4,8},{5,11},{6,10},{7,9},{8,4},{9,7},... | collective-permute-start | bytes 393224 | tf_op jit(solution)/shard_map/ppermute | solution.py:97
  12.9 14.0 %collective-permute-start.3 = (bf16[128,512]{1,0:T(8,128)(2,1)S(1)}, bf16[128,512]{1,0:T(8,128)(2,1)S(1)}, u32[]{:S(2)}, u32[]{:S(2)}) collective-permute-start(bf16[128,512]{1,0:T(8,128)(2,1)S(1)} %get-tuple-element.33), channel_id=1, source_target_pairs={{0,4},{1,7},{2,6},{3,5},{4,0},{5,3},{6,2},{7,1},{8,12},{9,15},{10,... | collective-permute-start | bytes 393224 | tf_op jit(solution)/shard_map/ppermute | solution.py:97
  13.2 30.3 %collective-permute-start.5 = (bf16[128,1024]{1,0:T(8,128)(2,1)S(1)}, bf16[128,1024]{1,0:T(8,128)(2,1)S(1)}, u32[]{:S(2)}, u32[]{:S(2)}) collective-permute-start(bf16[128,1024]{1,0:T(8,128)(2,1)S(1)} %get-tuple-element.37), channel_id=1, source_target_pairs={{0,8},{1,27},{2,26},{3,9},{4,12},{5,31},{6,30},{7,13},{8,0},{9,19}... | collective-permute-start | bytes 786440 | tf_op jit(solution)/shard_map/ppermute | solution.py:97
  16.0 28.5 %collective-permute-start.7 = (bf16[128,1024]{1,0:T(8,128)(2,1)S(1)}, bf16[128,1024]{1,0:T(8,128)(2,1)S(1)}, u32[]{:S(2)}, u32[]{:S(2)}) collective-permute-start(bf16[128,1024]{1,0:T(8,128)(2,1)S(1)} %get-tuple-element.41), channel_id=1, source_target_pairs={{0,12},{1,31},{2,30},{3,13},{4,8},{5,27},{6,26},{7,9},{8,4},{9,23}... | collective-permute-start | bytes 786440 | tf_op jit(solution)/shard_map/ppermute | solution.py:97
  28.0 18.0 %collective-permute-start.8 = (bf16[128,1024]{1,0:T(8,128)(2,1)S(1)}, bf16[128,1024]{1,0:T(8,128)(2,1)S(1)}, u32[]{:S(2)}, u32[]{:S(2)}) collective-permute-start(bf16[128,1024]{1,0:T(8,128)(2,1)S(1)} %get-tuple-element.42), channel_id=1, source_target_pairs={{0,4},{1,23},{2,22},{3,5},{4,0},{5,19},{6,18},{7,1},{8,12},{9,31},... | collective-permute-start | bytes 786440 | tf_op jit(solution)/shard_map/ppermute | solution.py:97
  34.9 11.1 %collective-permute-start.9 = (bf16[128,1024]{1,0:T(8,128)(2,1)S(1)}, bf16[128,1024]{1,0:T(8,128)(2,1)S(1)}, u32[]{:S(2)}, u32[]{:S(2)}) collective-permute-start(bf16[128,1024]{1,0:T(8,128)(2,1)S(1)} %get-tuple-element.43), channel_id=1, source_target_pairs={{0,0},{1,19},{2,18},{3,1},{4,4},{5,23},{6,22},{7,5},{8,8},{9,27},{... | collective-permute-start | bytes 786440 | tf_op jit(solution)/shard_map/ppermute | solution.py:97
  35.6 8.9 %collective-permute-start.6 = (bf16[528,128]{1,0:T(8,128)(2,1)S(1)}, bf16[528,128]{1,0:T(8,128)(2,1)S(1)}, u32[]{:S(2)}, u32[]{:S(2)}) collective-permute-start(bf16[528,128]{1,0:T(8,128)(2,1)S(1)} %get-tuple-element.38), channel_id=1, source_target_pairs={{0,1},{1,0},{2,3},{3,2},{4,5},{5,4},{6,7},{7,6},{8,9},{9,8},{10,11... | collective-permute-start | bytes 405512 | tf_op jit(solution)/shard_map/ppermute | solution.py:83
  48.1 4.2 %collective-permute-start.10 = (bf16[656,128]{1,0:T(8,128)(2,1)S(1)}, bf16[656,128]{1,0:T(8,128)(2,1)S(1)}, u32[]{:S(2)}, u32[]{:S(2)}) collective-permute-start(bf16[656,128]{1,0:T(8,128)(2,1)S(1)} %get-tuple-element.46), channel_id=1, source_target_pairs={{0,1},{1,0},{2,3},{3,2},{4,5},{5,4},{6,7},{7,6},{8,9},{9,8},{10,11... | collective-permute-start | bytes 503816 | tf_op jit(solution)/shard_map/ppermute | solution.py:83
  52.9 7.4 %collective-permute-start.11 = (bf16[592,128]{1,0:T(8,128)(2,1)S(1)}, bf16[592,128]{1,0:T(8,128)(2,1)S(1)}, u32[]{:S(2)}, u32[]{:S(2)}) collective-permute-start(bf16[592,128]{1,0:T(8,128)(2,1)S(1)} %get-tuple-element.48), channel_id=1, source_target_pairs={{0,4},{4,0},{8,12},{12,8},{1,5},{5,1},{9,13},{13,9},{2,6},{6,2},{1... | collective-permute-start | bytes 454664 | tf_op jit(solution)/shard_map/ppermute | solution.py:83
  60.3 9.8 %collective-permute-start.12 = (bf16[592,128]{1,0:T(8,128)(2,1)S(1)}, bf16[592,128]{1,0:T(8,128)(2,1)S(1)}, u32[]{:S(2)}, u32[]{:S(2)}) collective-permute-start(bf16[592,128]{1,0:T(8,128)(2,1)S(1)} %shard_map.98.mine), channel_id=1, source_target_pairs={{0,8},{4,12},{8,0},{12,4},{1,9},{5,13},{9,1},{13,5},{2,10},{6,14},... | collective-permute-start | bytes 454664 | tf_op jit(solution)/shard_map/ppermute | solution.py:83
  70.2 5.3 %collective-permute-start.13 = (bf16[592,128]{1,0:T(8,128)(2,1)S(1)}, bf16[592,128]{1,0:T(8,128)(2,1)S(1)}, u32[]{:S(2)}, u32[]{:S(2)}) collective-permute-start(bf16[592,128]{1,0:T(8,128)(2,1)S(1)} %shard_map.99.refs_0_), channel_id=1, source_target_pairs={{0,4},{4,0},{8,12},{12,8},{1,5},{5,1},{9,13},{13,9},{2,6},{6,2},{1... | collective-permute-start | bytes 454664 | tf_op jit(solution)/shard_map/ppermute | solution.py:83
  70.3 5.2 %collective-permute-start.14 = (bf16[592,128]{1,0:T(8,128)(2,1)S(1)}, bf16[592,128]{1,0:T(8,128)(2,1)S(1)}, u32[]{:S(2)}, u32[]{:S(2)}) collective-permute-start(bf16[592,128]{1,0:T(8,128)(2,1)S(1)} %shard_map.99.refs_0_), channel_id=1, source_target_pairs={{0,1},{1,0},{2,3},{3,2},{4,5},{5,4},{6,7},{7,6},{8,9},{9,8},{10,11... | collective-permute-start | bytes 454664 | tf_op jit(solution)/shard_map/ppermute | solution.py:83
  75.5 1.4 %collective-permute-start.15 = (bf16[592,128]{1,0:T(8,128)(2,1)S(1)}, bf16[592,128]{1,0:T(8,128)(2,1)S(1)}, u32[]{:S(2)}, u32[]{:S(2)}) collective-permute-start(bf16[592,128]{1,0:T(8,128)(2,1)S(1)} %collective-permute-done.13.refs_1_), channel_id=1, source_target_pairs={{0,1},{1,0},{2,3},{3,2},{4,5},{5,4},{6,7},{7,6},{8,9},{9,8},{10,11... | collective-permute-start | bytes 454664 | tf_op jit(solution)/shard_map/ppermute | solution.py:83
  89.7 12.4 %collective-permute-start.18 = (bf16[128,768]{1,0:T(8,128)(2,1)S(1)}, bf16[128,768]{1,0:T(8,128)(2,1)S(1)}, u32[]{:S(2)}, u32[]{:S(2)}) collective-permute-start(bf16[128,768]{1,0:T(8,128)(2,1)S(1)} %shard_map.100), channel_id=1, source_target_pairs={{0,8},{1,11},{2,10},{3,9},{4,12},{5,15},{6,14},{7,13},{8,0},{9,3},... | collective-permute-start | bytes 589832 | tf_op jit(solution)/shard_map/ppermute | solution.py:97
  90.1 12.4 %collective-permute-start.17 = (bf16[128,768]{1,0:T(8,128)(2,1)S(1)}, bf16[128,768]{1,0:T(8,128)(2,1)S(1)}, u32[]{:S(2)}, u32[]{:S(2)}) collective-permute-start(bf16[128,768]{1,0:T(8,128)(2,1)S(1)} %shard_map.100), channel_id=1, source_target_pairs={{0,4},{1,7},{2,6},{3,5},{4,0},{5,3},{6,2},{7,1},{8,12},{9,15},{10,... | collective-permute-start | bytes 589832 | tf_op jit(solution)/shard_map/ppermute | solution.py:97
  92.2 11.0 %collective-permute-start.16 = (bf16[128,768]{1,0:T(8,128)(2,1)S(1)}, bf16[128,768]{1,0:T(8,128)(2,1)S(1)}, u32[]{:S(2)}, u32[]{:S(2)}) collective-permute-start(bf16[128,768]{1,0:T(8,128)(2,1)S(1)} %shard_map.100), channel_id=1, source_target_pairs={{0,0},{1,3},{2,2},{3,1},{4,4},{5,7},{6,6},{7,5},{8,8},{9,11},{10,1... | collective-permute-start | bytes 589832 | tf_op jit(solution)/shard_map/ppermute | solution.py:97
  102.1 7.2 %collective-permute-start.19 = (bf16[128,768]{1,0:T(8,128)(2,1)S(1)}, bf16[128,768]{1,0:T(8,128)(2,1)S(1)}, u32[]{:S(2)}, u32[]{:S(2)}) collective-permute-start(bf16[128,768]{1,0:T(8,128)(2,1)S(1)} %collective-permute-done.18.refs_2_), channel_id=1, source_target_pairs={{0,4},{4,0},{8,12},{12,8},{1,5},{5,1},{9,13},{13,9},{2,6},{6,2},{1... | collective-permute-start | bytes 589832 | tf_op jit(solution)/shard_map/ppermute | solution.py:83
  102.1 7.2 %collective-permute-start.22 = (bf16[128,768]{1,0:T(8,128)(2,1)S(1)}, bf16[128,768]{1,0:T(8,128)(2,1)S(1)}, u32[]{:S(2)}, u32[]{:S(2)}) collective-permute-start(bf16[128,768]{1,0:T(8,128)(2,1)S(1)} %collective-permute-done.18.refs_2_), channel_id=1, source_target_pairs={{0,1},{1,0},{2,3},{3,2},{4,5},{5,4},{6,7},{7,6},{8,9},{9,8},{10,11... | collective-permute-start | bytes 589832 | tf_op jit(solution)/shard_map/ppermute | solution.py:83
  102.5 6.8 %collective-permute-start.21 = (bf16[128,768]{1,0:T(8,128)(2,1)S(1)}, bf16[128,768]{1,0:T(8,128)(2,1)S(1)}, u32[]{:S(2)}, u32[]{:S(2)}) collective-permute-start(bf16[128,768]{1,0:T(8,128)(2,1)S(1)} %collective-permute-done.17.refs_1_), channel_id=1, source_target_pairs={{0,1},{1,0},{2,3},{3,2},{4,5},{5,4},{6,7},{7,6},{8,9},{9,8},{10,11... | collective-permute-start | bytes 589832 | tf_op jit(solution)/shard_map/ppermute | solution.py:83
  103.2 6.2 %collective-permute-start.20 = (bf16[128,768]{1,0:T(8,128)(2,1)S(1)}, bf16[128,768]{1,0:T(8,128)(2,1)S(1)}, u32[]{:S(2)}, u32[]{:S(2)}) collective-permute-start(bf16[128,768]{1,0:T(8,128)(2,1)S(1)} %collective-permute-done.16.refs_0_), channel_id=1, source_target_pairs={{0,1},{1,0},{2,3},{3,2},{4,5},{5,4},{6,7},{7,6},{8,9},{9,8},{10,11... | collective-permute-start | bytes 589832 | tf_op jit(solution)/shard_map/ppermute | solution.py:83
  109.3 1.4 %collective-permute-start.23 = (bf16[128,768]{1,0:T(8,128)(2,1)S(1)}, bf16[128,768]{1,0:T(8,128)(2,1)S(1)}, u32[]{:S(2)}, u32[]{:S(2)}) collective-permute-start(bf16[128,768]{1,0:T(8,128)(2,1)S(1)} %collective-permute-done.19.refs_3_), channel_id=1, source_target_pairs={{0,1},{1,0},{2,3},{3,2},{4,5},{5,4},{6,7},{7,6},{8,9},{9,8},{10,11... | collective-permute-start | bytes 589832 | tf_op jit(solution)/shard_map/ppermute | solution.py:83

commit v5 on v4

--- a/solution.py
+++ b/solution.py
@@ -482,7 +482,7 @@
         in_hbm + [VMEM],
     )
     smalls = [routed(packed[dps + d], sizes, d, False) for d in FAR_FIRST]
-    bigs = [routed(packed[d], sizes, d, True) for d in FAR_FIRST[:2]]
+    bigs = [routed(packed[d], sizes, d, True) for d in FAR_FIRST[:-1]]
 
     _, thin_rows, wide_rows = packed_rows(dps)
 
@@ -496,9 +496,8 @@
         return m, keep, swap(send, "tensor", 1)
 
     small, *thin = gram(thin_gram_kernel, shape(tokens, 2 * small_w), thin_rows, smalls)
-    near = lax.optimization_barrier((packed[1], packed[0], thin[0]))
-    thin[0] = near[2]
-    bigs += [routed(v, sizes, d, True) for v, d in zip(near, FAR_FIRST[2:])]
+    last, thin[0] = lax.optimization_barrier((packed[0], thin[0]))
+    bigs.append(routed(last, sizes, 0, True))
     bigs[0], thin[1] = lax.optimization_barrier((bigs[0], thin[1]))
     big, *rest = gram(
         wide_gram_kernel, shape(tokens, 2 * big_w), wide_rows, (*bigs, small, smalls[-1])

time: 113 us -> 112 us (level)
  no operation moved by 1% of the time
where the time goes in v5:
time: 112 us
  starting transfers between devices  48.4 us (43%)
  waiting for transfers between devices  40.6 us (36%)
  Pallas kernels  22 us (20%)
    ppermute x11, starting transfers between devices, routed(): return lax.ppermute(value, ('section', 'dp', 'tensor'), pairs)  30.6 us
    ppermute x13, waiting for transfers between devices, swap(): return lax.ppermute(value, axis, [(i, i ^ bit) for i in range(count)])  30.2 us
    pallas_call x9, Pallas kernels, call(): pl.pallas_call(kernel, out_shape=out_shapes, in_specs=spaces, out_specs=j...  22 us
    ppermute x13, starting transfers between devices, swap(): return lax.ppermute(value, axis, [(i, i ^ bit) for i in range(count)])  17.8 us
    ppermute x11, waiting for transfers between devices, routed(): return lax.ppermute(value, ('section', 'dp', 'tensor'), pairs)  10.4 us
  transfers between devices with their start and end apart: 24, of which 11 were waited for; matrix products, arithmetic and copies ran while one was open for 0% of the time, Pallas kernels for 1%

profile of v5, /device:TPU:0, one launch (start us, length us, event | category | flops | bytes accessed | tf_op | source)
XLA Modules:
  0.0 111.7 jit_solution(16558560688227682299)
XLA Ops:
  0.6 0.1 pad_add_fusion.idx
  0.7 1.7 %shard_map.93 = bf16[144,3072]{1,0:T(8,128)(2,1)S(1)} custom-call(s32[4]{0:T(128)S(1)} %pad_add_fusion.idx, bf16[128,2048]{1,0:T(8,128)(2,1)} %bitcast.14, bf16[128,1024]{1,0:T(8,128)(2,1)} %bitcast.18, bf16[128,1024]{1,0:T(8,128)(2,1)} %bitcast.20, bf16[128,2048]{1,0:T(8,128)(2,1)} %bitcast.16, bf16[64,1024]{1,0:T(8,128)(2,1)} %bitcast.24, ...), custom_call_target="tpu_custom_call" | custom-call | tf_op jit(solution)/shard_map/pallas_call | solution.py:438
  2.4 0.5 collective-permute-start
  3.0 2.1 %collective-permute-done.got = bf16[144,3072]{1,0:T(8,128)(2,1)S(1)} collective-permute-done((bf16[144,3072]{1,0:T(8,128)(2,1)S(1)}, bf16[144,3072]{1,0:T(8,128)(2,1)S(1)}, u32[]{:S(2)}, u32[]{:S(2)}) %collective-permute-start) | collective-permute-done | bytes 884768 | tf_op jit(solution)/shard_map/ppermute | solution.py:83
  5.0 1.8 %shard_map.94 = (bf16[128,1024]{1,0:T(8,128)(2,1)S(1)}, bf16[128,1024]{1,0:T(8,128)(2,1)S(1)}, bf16[128,1024]{1,0:T(8,128)(2,1)S(1)}, bf16[128,1024]{1,0:T(8,128...) custom-call(s32[4]{0:T(128)S(1)} %pad_add_fusion.idx, ...), custom_call_target="tpu_custom_call" | custom-call | tf_op jit(solution)/shard_map/pallas_call | solution.py:438
  6.9 0.7 collective-permute-start.4
  7.6 4.0 %collective-permute-start.1 = (bf16[128,512]{1,0:T(8,128)(2,1)S(1)}, bf16[128,512]{1,0:T(8,128)(2,1)S(1)}, u32[]{:S(2)}, u32[]{:S(2)}) collective-permute-start(bf16[128,512]{1,0:T(8,128)(2,1)S(1)} %get-tuple-element.29), channel_id=1, source_target_pairs={{0,8},{1,11},{2,10},{3,9},{4,12},{5,15},{6,14},{7,13},{8,0},{9,3},... | collective-permute-start | bytes 393224 | tf_op jit(solution)/shard_map/ppermute | solution.py:97
  11.6 1.3 %collective-permute-start.2 = (bf16[128,512]{1,0:T(8,128)(2,1)S(1)}, bf16[128,512]{1,0:T(8,128)(2,1)S(1)}, u32[]{:S(2)}, u32[]{:S(2)}) collective-permute-start(bf16[128,512]{1,0:T(8,128)(2,1)S(1)} %get-tuple-element.30), channel_id=1, source_target_pairs={{0,12},{1,15},{2,14},{3,13},{4,8},{5,11},{6,10},{7,9},{8,4},{9,7},... | collective-permute-start | bytes 393224 | tf_op jit(solution)/shard_map/ppermute | solution.py:97
  12.9 0.2 collective-permute-start.3
  13.2 2.8 %collective-permute-start.5 = (bf16[128,1024]{1,0:T(8,128)(2,1)S(1)}, bf16[128,1024]{1,0:T(8,128)(2,1)S(1)}, u32[]{:S(2)}, u32[]{:S(2)}) collective-permute-start(bf16[128,1024]{1,0:T(8,128)(2,1)S(1)} %get-tuple-element.35), channel_id=1, source_target_pairs={{0,8},{1,27},{2,26},{3,9},{4,12},{5,31},{6,30},{7,13},{8,0},{9,19}... | collective-permute-start | bytes 786440 | tf_op jit(solution)/shard_map/ppermute | solution.py:97
  16.0 0.0 collective-permute-done.1.refs_0_
  16.0 10.9 %collective-permute-start.7 = (bf16[128,1024]{1,0:T(8,128)(2,1)S(1)}, bf16[128,1024]{1,0:T(8,128)(2,1)S(1)}, u32[]{:S(2)}, u32[]{:S(2)}) collective-permute-start(bf16[128,1024]{1,0:T(8,128)(2,1)S(1)} %get-tuple-element.39), channel_id=1, source_target_pairs={{0,12},{1,31},{2,30},{3,13},{4,8},{5,27},{6,26},{7,9},{8,4},{9,23}... | collective-permute-start | bytes 786440 | tf_op jit(solution)/shard_map/ppermute | solution.py:97
  26.9 0.0 collective-permute-done.2.refs_1_
  26.9 6.9 %collective-permute-start.8 = (bf16[128,1024]{1,0:T(8,128)(2,1)S(1)}, bf16[128,1024]{1,0:T(8,128)(2,1)S(1)}, u32[]{:S(2)}, u32[]{:S(2)}) collective-permute-start(bf16[128,1024]{1,0:T(8,128)(2,1)S(1)} %get-tuple-element.40), channel_id=1, source_target_pairs={{0,4},{1,23},{2,22},{3,5},{4,0},{5,19},{6,18},{7,1},{8,12},{9,31},... | collective-permute-start | bytes 786440 | tf_op jit(solution)/shard_map/ppermute | solution.py:97
  33.7 0.0 collective-permute-done.4.refs_3_.refs_5_
  33.7 1.1 %shard_map.95 = (bf16[512,512]{1,0:T(8,128)(2,1)S(1)}, bf16[528,128]{1,0:T(8,128)(2,1)S(1)}, bf16[528,128]{1,0:T(8,128)(2,1)S(1)}) custom-call(s32[4]{0:T(128)S(1)} %pad_add_fusion.idx, bf16[128,512]{1,0:T(8,128)(2,1)S(1)} %collective-permute-done.1.refs_0_, bf16[128,512]{1,0:T(8,128)(2,1)S(1)} %collective-permute-done.2.refs_1_, ...), custom_call_target="tpu_custom_call" | custom-call | tf_op jit(solution)/shard_map/pallas_call | solution.py:438
  34.9 0.7 collective-permute-start.9
  35.6 7.9 %collective-permute-start.6 = (bf16[528,128]{1,0:T(8,128)(2,1)S(1)}, bf16[528,128]{1,0:T(8,128)(2,1)S(1)}, u32[]{:S(2)}, u32[]{:S(2)}) collective-permute-start(bf16[528,128]{1,0:T(8,128)(2,1)S(1)} %get-tuple-element.36), channel_id=1, source_target_pairs={{0,1},{1,0},{2,3},{3,2},{4,5},{5,4},{6,7},{7,6},{8,9},{9,8},{10,11... | collective-permute-start | bytes 405512 | tf_op jit(solution)/shard_map/ppermute | solution.py:83
  43.4 0.0 collective-permute-done.5.refs_0_
  43.4 1.0 collective-permute-done.6.thin_got
  44.4 0.0 collective-permute-done.7.refs_1_
  44.4 1.1 collective-permute-done.8.refs_2_
  45.5 0.0 collective-permute-done.9.refs_3_
  45.5 2.0 %shard_map.96 = (bf16[512,1024]{1,0:T(8,128)(2,1)S(1)}, bf16[656,128]{1,0:T(8,128)(2,1)S(1)}, bf16[656,128]{1,0:T(8,128)(2,1)S(1)}) custom-call(s32[4]{0:T(128)S(1)} %pad_add_fusion.idx, bf16[128,1024]{1,0:T(8,128)(2,1)S(1)} %collective-permute-done.5.refs_0_, bf16[128,1024]{1,0:T(8,128)(2,1)S(1)} %collective-permute-done.7.refs_1_, ...), custom_call_target="tpu_custom_call" | custom-call | tf_op jit(solution)/shard_map/pallas_call | solution.py:438
  47.6 3.6 %collective-permute-start.10 = (bf16[656,128]{1,0:T(8,128)(2,1)S(1)}, bf16[656,128]{1,0:T(8,128)(2,1)S(1)}, u32[]{:S(2)}, u32[]{:S(2)}) collective-permute-start(bf16[656,128]{1,0:T(8,128)(2,1)S(1)} %get-tuple-element.44), channel_id=1, source_target_pairs={{0,1},{1,0},{2,3},{3,2},{4,5},{5,4},{6,7},{7,6},{8,9},{9,8},{10,11... | collective-permute-start | bytes 503816 | tf_op jit(solution)/shard_map/ppermute | solution.py:83
  51.2 1.0 collective-permute-done.10.wide_got
  52.2 0.7 shard_map.97
  52.9 2.3 %collective-permute-start.11 = (bf16[592,128]{1,0:T(8,128)(2,1)S(1)}, bf16[592,128]{1,0:T(8,128)(2,1)S(1)}, u32[]{:S(2)}, u32[]{:S(2)}) collective-permute-start(bf16[592,128]{1,0:T(8,128)(2,1)S(1)} %get-tuple-element.46), channel_id=1, source_target_pairs={{0,4},{4,0},{8,12},{12,8},{1,5},{5,1},{9,13},{13,9},{2,6},{6,2},{1... | collective-permute-start | bytes 454664 | tf_op jit(solution)/shard_map/ppermute | solution.py:83
  55.2 4.5 %collective-permute-done.11.got = bf16[592,128]{1,0:T(8,128)(2,1)S(1)} collective-permute-done((bf16[592,128]{1,0:T(8,128)(2,1)S(1)}, bf16[592,128]{1,0:T(8,128)(2,1)S(1)}, u32[]{:S(2)}, u32[]{:S(2)}) %collective-permute-start.11) | collective-permute-done | bytes 151584 | tf_op jit(solution)/shard_map/ppermute | solution.py:83
  59.7 2.3 %collective-permute-start.12 = (bf16[592,128]{1,0:T(8,128)(2,1)S(1)}, bf16[592,128]{1,0:T(8,128)(2,1)S(1)}, u32[]{:S(2)}, u32[]{:S(2)}) collective-permute-start(bf16[592,128]{1,0:T(8,128)(2,1)S(1)} %shard_map.98.mine), channel_id=1, source_target_pairs={{0,8},{4,12},{8,0},{12,4},{1,9},{5,13},{9,1},{13,5},{2,10},{6,14},... | collective-permute-start | bytes 454664 | tf_op jit(solution)/shard_map/ppermute | solution.py:83
  62.0 7.6 %collective-permute-done.12.got = bf16[592,128]{1,0:T(8,128)(2,1)S(1)} collective-permute-done((bf16[592,128]{1,0:T(8,128)(2,1)S(1)}, bf16[592,128]{1,0:T(8,128)(2,1)S(1)}, u32[]{:S(2)}, u32[]{:S(2)}) %collective-permute-start.12) | collective-permute-done | bytes 151584 | tf_op jit(solution)/shard_map/ppermute | solution.py:83
  69.6 0.1 collective-permute-start.13
  69.7 0.1 collective-permute-start.14
  69.7 5.1 %collective-permute-done.13.refs_1_ = bf16[592,128]{1,0:T(8,128)(2,1)S(1)} collective-permute-done((bf16[592,128]{1,0:T(8,128)(2,1)S(1)}, bf16[592,128]{1,0:T(8,128)(2,1)S(1)}, u32[]{:S(2)}, u32[]{:S(2)}) %collective-permute-start.13) | collective-permute-done | bytes 151584 | tf_op jit(solution)/shard_map/ppermute | solution.py:83
  74.8 0.0 collective-permute-start.15
  74.8 0.0 collective-permute-done.14.refs_2_
  74.8 1.4 %collective-permute-done.15.refs_3_ = bf16[592,128]{1,0:T(8,128)(2,1)S(1)} collective-permute-done((bf16[592,128]{1,0:T(8,128)(2,1)S(1)}, bf16[592,128]{1,0:T(8,128)(2,1)S(1)}, u32[]{:S(2)}, u32[]{:S(2)}) %collective-permute-start.15) | collective-permute-done | bytes 151584 | tf_op jit(solution)/shard_map/ppermute | solution.py:83
  76.2 12.8 %shard_map.100 = bf16[128,768]{1,0:T(8,128)(2,1)S(1)} custom-call(s32[4]{0:T(128)S(1)} %pad_add_fusion.idx, bf16[592,128]{1,0:T(8,128)(2,1)S(1)} %shard_map.99.refs_0_, bf16[592,128]{1,0:T(8,128)(2,1)S(1)} %collective-permute-done.13.refs_1_, bf16[592,128]{1,0:T(8,128)(2,1)S(1)} %collective-permute-done.14.refs_2_, ...), custom_call_target="tpu_custom_call" | custom-call | tf_op jit(solution)/shard_map/pallas_call | solution.py:438
  89.0 0.4 collective-permute-start.18
  89.4 2.0 %collective-permute-start.17 = (bf16[128,768]{1,0:T(8,128)(2,1)S(1)}, bf16[128,768]{1,0:T(8,128)(2,1)S(1)}, u32[]{:S(2)}, u32[]{:S(2)}) collective-permute-start(bf16[128,768]{1,0:T(8,128)(2,1)S(1)} %shard_map.100), channel_id=1, source_target_pairs={{0,4},{1,7},{2,6},{3,5},{4,0},{5,3},{6,2},{7,1},{8,12},{9,15},{10,... | collective-permute-start | bytes 589832 | tf_op jit(solution)/shard_map/ppermute | solution.py:97
  91.4 0.7 collective-permute-start.16
  92.1 9.3 %collective-permute-done.18.refs_2_ = bf16[128,768]{1,0:T(8,128)(2,1)S(1)} collective-permute-done((bf16[128,768]{1,0:T(8,128)(2,1)S(1)}, bf16[128,768]{1,0:T(8,128)(2,1)S(1)}, u32[]{:S(2)}, u32[]{:S(2)}) %collective-permute-start.18) | collective-permute-done | bytes 196640 | tf_op jit(solution)/shard_map/ppermute | solution.py:97
  101.4 0.5 collective-permute-start.22
  101.8 0.6 collective-permute-start.21
  102.5 0.0 collective-permute-start.20
  102.5 6.2 %collective-permute-done.19.refs_3_ = bf16[128,768]{1,0:T(8,128)(2,1)S(1)} collective-permute-done((bf16[128,768]{1,0:T(8,128)(2,1)S(1)}, bf16[128,768]{1,0:T(8,128)(2,1)S(1)}, u32[]{:S(2)}, u32[]{:S(2)}) %collective-permute-start.19) | collective-permute-done | bytes 196640 | tf_op jit(solution)/shard_map/ppermute | solution.py:83
  108.7 1.4 %collective-permute-done.23.refs_7_ = bf16[128,768]{1,0:T(8,128)(2,1)S(1)} collective-permute-done((bf16[128,768]{1,0:T(8,128)(2,1)S(1)}, bf16[128,768]{1,0:T(8,128)(2,1)S(1)}, u32[]{:S(2)}, u32[]{:S(2)}) %collective-permute-start.23) | collective-permute-done | bytes 196640 | tf_op jit(solution)/shard_map/ppermute | solution.py:83
  110.1 1.7 %shard_map.101 = (bf16[64,2048]{1,0:T(8,128)(2,1)}, f32[64,1024]{1,0:T(8,128)}, bf16[64,1024]{1,0:T(8,128)(2,1)}, f32[64,2048]{1,0:T(8,128)}) custom-call(s32[4]{0:T(128)S(1)} %pad_add_fusion.idx, bf16[128,768]{1,0:T(8,128)(2,1)S(1)} %collective-permute-done.16.refs_0_, bf16[128,768]{1,0:T(8,128)(2,1)S(1)} %collective-permute-done.17.refs_1_, ...), custom_call_target="tpu_custom_call" | custom-call | tf_op jit(solution)/shard_map/pallas_call | solution.py:438
  (10 shorter events, 0.1 us)
Async XLA Ops:
  2.4 2.6 %collective-permute-start = (bf16[144,3072]{1,0:T(8,128)(2,1)S(1)}, bf16[144,3072]{1,0:T(8,128)(2,1)S(1)}, u32[]{:S(2)}, u32[]{:S(2)}) collective-permute-start(bf16[144,3072]{1,0:T(8,128)(2,1)S(1)} %shard_map.93), channel_id=1, source_target_pairs={{0,1},{1,0},{2,3},{3,2},{4,5},{5,4},{6,7},{7,6},{8,9},{9,8},{10,11... | collective-permute-start | bytes 2654216 | tf_op jit(solution)/shard_map/ppermute | solution.py:83
  6.9 26.9 %collective-permute-start.4 = (bf16[320,512]{1,0:T(8,128)(2,1)S(1)}, bf16[320,512]{1,0:T(8,128)(2,1)S(1)}, u32[]{:S(2)}, u32[]{:S(2)}) collective-permute-start(bf16[320,512]{1,0:T(8,128)(2,1)S(1)} %get-tuple-element.32), channel_id=1, source_target_pairs={{0,0},{1,3},{2,2},{3,1},{4,4},{5,7},{6,6},{7,5},{8,8},{9,11},{10,1... | collective-permute-start | bytes 983048 | tf_op jit(solution)/shard_map/ppermute | solution.py:97
  7.6 8.4 %collective-permute-start.1 = (bf16[128,512]{1,0:T(8,128)(2,1)S(1)}, bf16[128,512]{1,0:T(8,128)(2,1)S(1)}, u32[]{:S(2)}, u32[]{:S(2)}) collective-permute-start(bf16[128,512]{1,0:T(8,128)(2,1)S(1)} %get-tuple-element.29), channel_id=1, source_target_pairs={{0,8},{1,11},{2,10},{3,9},{4,12},{5,15},{6,14},{7,13},{8,0},{9,3},... | collective-permute-start | bytes 393224 | tf_op jit(solution)/shard_map/ppermute | solution.py:97
  11.6 15.3 %collective-permute-start.2 = (bf16[128,512]{1,0:T(8,128)(2,1)S(1)}, bf16[128,512]{1,0:T(8,128)(2,1)S(1)}, u32[]{:S(2)}, u32[]{:S(2)}) collective-permute-start(bf16[128,512]{1,0:T(8,128)(2,1)S(1)} %get-tuple-element.30), channel_id=1, source_target_pairs={{0,12},{1,15},{2,14},{3,13},{4,8},{5,11},{6,10},{7,9},{8,4},{9,7},... | collective-permute-start | bytes 393224 | tf_op jit(solution)/shard_map/ppermute | solution.py:97
  12.9 20.8 %collective-permute-start.3 = (bf16[128,512]{1,0:T(8,128)(2,1)S(1)}, bf16[128,512]{1,0:T(8,128)(2,1)S(1)}, u32[]{:S(2)}, u32[]{:S(2)}) collective-permute-start(bf16[128,512]{1,0:T(8,128)(2,1)S(1)} %get-tuple-element.31), channel_id=1, source_target_pairs={{0,4},{1,7},{2,6},{3,5},{4,0},{5,3},{6,2},{7,1},{8,12},{9,15},{10,... | collective-permute-start | bytes 393224 | tf_op jit(solution)/shard_map/ppermute | solution.py:97
  13.2 30.3 %collective-permute-start.5 = (bf16[128,1024]{1,0:T(8,128)(2,1)S(1)}, bf16[128,1024]{1,0:T(8,128)(2,1)S(1)}, u32[]{:S(2)}, u32[]{:S(2)}) collective-permute-start(bf16[128,1024]{1,0:T(8,128)(2,1)S(1)} %get-tuple-element.35), channel_id=1, source_target_pairs={{0,8},{1,27},{2,26},{3,9},{4,12},{5,31},{6,30},{7,13},{8,0},{9,19}... | collective-permute-start | bytes 786440 | tf_op jit(solution)/shard_map/ppermute | solution.py:97
  16.0 28.5 %collective-permute-start.7 = (bf16[128,1024]{1,0:T(8,128)(2,1)S(1)}, bf16[128,1024]{1,0:T(8,128)(2,1)S(1)}, u32[]{:S(2)}, u32[]{:S(2)}) collective-permute-start(bf16[128,1024]{1,0:T(8,128)(2,1)S(1)} %get-tuple-element.39), channel_id=1, source_target_pairs={{0,12},{1,31},{2,30},{3,13},{4,8},{5,27},{6,26},{7,9},{8,4},{9,23}... | collective-permute-start | bytes 786440 | tf_op jit(solution)/shard_map/ppermute | solution.py:97
  26.9 18.7 %collective-permute-start.8 = (bf16[128,1024]{1,0:T(8,128)(2,1)S(1)}, bf16[128,1024]{1,0:T(8,128)(2,1)S(1)}, u32[]{:S(2)}, u32[]{:S(2)}) collective-permute-start(bf16[128,1024]{1,0:T(8,128)(2,1)S(1)} %get-tuple-element.40), channel_id=1, source_target_pairs={{0,4},{1,23},{2,22},{3,5},{4,0},{5,19},{6,18},{7,1},{8,12},{9,31},... | collective-permute-start | bytes 786440 | tf_op jit(solution)/shard_map/ppermute | solution.py:97
  34.9 10.7 %collective-permute-start.9 = (bf16[128,1024]{1,0:T(8,128)(2,1)S(1)}, bf16[128,1024]{1,0:T(8,128)(2,1)S(1)}, u32[]{:S(2)}, u32[]{:S(2)}) collective-permute-start(bf16[128,1024]{1,0:T(8,128)(2,1)S(1)} %get-tuple-element.41), channel_id=1, source_target_pairs={{0,0},{1,19},{2,18},{3,1},{4,4},{5,23},{6,22},{7,5},{8,8},{9,27},{... | collective-permute-start | bytes 786440 | tf_op jit(solution)/shard_map/ppermute | solution.py:97
  35.6 8.9 %collective-permute-start.6 = (bf16[528,128]{1,0:T(8,128)(2,1)S(1)}, bf16[528,128]{1,0:T(8,128)(2,1)S(1)}, u32[]{:S(2)}, u32[]{:S(2)}) collective-permute-start(bf16[528,128]{1,0:T(8,128)(2,1)S(1)} %get-tuple-element.36), channel_id=1, source_target_pairs={{0,1},{1,0},{2,3},{3,2},{4,5},{5,4},{6,7},{7,6},{8,9},{9,8},{10,11... | collective-permute-start | bytes 405512 | tf_op jit(solution)/shard_map/ppermute | solution.py:83
  47.6 4.6 %collective-permute-start.10 = (bf16[656,128]{1,0:T(8,128)(2,1)S(1)}, bf16[656,128]{1,0:T(8,128)(2,1)S(1)}, u32[]{:S(2)}, u32[]{:S(2)}) collective-permute-start(bf16[656,128]{1,0:T(8,128)(2,1)S(1)} %get-tuple-element.44), channel_id=1, source_target_pairs={{0,1},{1,0},{2,3},{3,2},{4,5},{5,4},{6,7},{7,6},{8,9},{9,8},{10,11... | collective-permute-start | bytes 503816 | tf_op jit(solution)/shard_map/ppermute | solution.py:83
  52.9 6.8 %collective-permute-start.11 = (bf16[592,128]{1,0:T(8,128)(2,1)S(1)}, bf16[592,128]{1,0:T(8,128)(2,1)S(1)}, u32[]{:S(2)}, u32[]{:S(2)}) collective-permute-start(bf16[592,128]{1,0:T(8,128)(2,1)S(1)} %get-tuple-element.46), channel_id=1, source_target_pairs={{0,4},{4,0},{8,12},{12,8},{1,5},{5,1},{9,13},{13,9},{2,6},{6,2},{1... | collective-permute-start | bytes 454664 | tf_op jit(solution)/shard_map/ppermute | solution.py:83
  59.7 9.8 %collective-permute-start.12 = (bf16[592,128]{1,0:T(8,128)(2,1)S(1)}, bf16[592,128]{1,0:T(8,128)(2,1)S(1)}, u32[]{:S(2)}, u32[]{:S(2)}) collective-permute-start(bf16[592,128]{1,0:T(8,128)(2,1)S(1)} %shard_map.98.mine), channel_id=1, source_target_pairs={{0,8},{4,12},{8,0},{12,4},{1,9},{5,13},{9,1},{13,5},{2,10},{6,14},... | collective-permute-start | bytes 454664 | tf_op jit(solution)/shard_map/ppermute | solution.py:83
  69.6 5.3 %collective-permute-start.13 = (bf16[592,128]{1,0:T(8,128)(2,1)S(1)}, bf16[592,128]{1,0:T(8,128)(2,1)S(1)}, u32[]{:S(2)}, u32[]{:S(2)}) collective-permute-start(bf16[592,128]{1,0:T(8,128)(2,1)S(1)} %shard_map.99.refs_0_), channel_id=1, source_target_pairs={{0,4},{4,0},{8,12},{12,8},{1,5},{5,1},{9,13},{13,9},{2,6},{6,2},{1... | collective-permute-start | bytes 454664 | tf_op jit(solution)/shard_map/ppermute | solution.py:83
  69.7 5.2 %collective-permute-start.14 = (bf16[592,128]{1,0:T(8,128)(2,1)S(1)}, bf16[592,128]{1,0:T(8,128)(2,1)S(1)}, u32[]{:S(2)}, u32[]{:S(2)}) collective-permute-start(bf16[592,128]{1,0:T(8,128)(2,1)S(1)} %shard_map.99.refs_0_), channel_id=1, source_target_pairs={{0,1},{1,0},{2,3},{3,2},{4,5},{5,4},{6,7},{7,6},{8,9},{9,8},{10,11... | collective-permute-start | bytes 454664 | tf_op jit(solution)/shard_map/ppermute | solution.py:83
  74.8 1.4 %collective-permute-start.15 = (bf16[592,128]{1,0:T(8,128)(2,1)S(1)}, bf16[592,128]{1,0:T(8,128)(2,1)S(1)}, u32[]{:S(2)}, u32[]{:S(2)}) collective-permute-start(bf16[592,128]{1,0:T(8,128)(2,1)S(1)} %collective-permute-done.13.refs_1_), channel_id=1, source_target_pairs={{0,1},{1,0},{2,3},{3,2},{4,5},{5,4},{6,7},{7,6},{8,9},{9,8},{10,11... | collective-permute-start | bytes 454664 | tf_op jit(solution)/shard_map/ppermute | solution.py:83
  89.0 12.3 %collective-permute-start.18 = (bf16[128,768]{1,0:T(8,128)(2,1)S(1)}, bf16[128,768]{1,0:T(8,128)(2,1)S(1)}, u32[]{:S(2)}, u32[]{:S(2)}) collective-permute-start(bf16[128,768]{1,0:T(8,128)(2,1)S(1)} %shard_map.100), channel_id=1, source_target_pairs={{0,8},{1,11},{2,10},{3,9},{4,12},{5,15},{6,14},{7,13},{8,0},{9,3},... | collective-permute-start | bytes 589832 | tf_op jit(solution)/shard_map/ppermute | solution.py:97
  89.4 12.4 %collective-permute-start.17 = (bf16[128,768]{1,0:T(8,128)(2,1)S(1)}, bf16[128,768]{1,0:T(8,128)(2,1)S(1)}, u32[]{:S(2)}, u32[]{:S(2)}) collective-permute-start(bf16[128,768]{1,0:T(8,128)(2,1)S(1)} %shard_map.100), channel_id=1, source_target_pairs={{0,4},{1,7},{2,6},{3,5},{4,0},{5,3},{6,2},{7,1},{8,12},{9,15},{10,... | collective-permute-start | bytes 589832 | tf_op jit(solution)/shard_map/ppermute | solution.py:97
  91.4 11.0 %collective-permute-start.16 = (bf16[128,768]{1,0:T(8,128)(2,1)S(1)}, bf16[128,768]{1,0:T(8,128)(2,1)S(1)}, u32[]{:S(2)}, u32[]{:S(2)}) collective-permute-start(bf16[128,768]{1,0:T(8,128)(2,1)S(1)} %shard_map.100), channel_id=1, source_target_pairs={{0,0},{1,3},{2,2},{3,1},{4,4},{5,7},{6,6},{7,5},{8,8},{9,11},{10,1... | collective-permute-start | bytes 589832 | tf_op jit(solution)/shard_map/ppermute | solution.py:97
  101.4 7.3 %collective-permute-start.19 = (bf16[128,768]{1,0:T(8,128)(2,1)S(1)}, bf16[128,768]{1,0:T(8,128)(2,1)S(1)}, u32[]{:S(2)}, u32[]{:S(2)}) collective-permute-start(bf16[128,768]{1,0:T(8,128)(2,1)S(1)} %collective-permute-done.18.refs_2_), channel_id=1, source_target_pairs={{0,4},{4,0},{8,12},{12,8},{1,5},{5,1},{9,13},{13,9},{2,6},{6,2},{1... | collective-permute-start | bytes 589832 | tf_op jit(solution)/shard_map/ppermute | solution.py:83
  101.4 7.3 %collective-permute-start.22 = (bf16[128,768]{1,0:T(8,128)(2,1)S(1)}, bf16[128,768]{1,0:T(8,128)(2,1)S(1)}, u32[]{:S(2)}, u32[]{:S(2)}) collective-permute-start(bf16[128,768]{1,0:T(8,128)(2,1)S(1)} %collective-permute-done.18.refs_2_), channel_id=1, source_target_pairs={{0,1},{1,0},{2,3},{3,2},{4,5},{5,4},{6,7},{7,6},{8,9},{9,8},{10,11... | collective-permute-start | bytes 589832 | tf_op jit(solution)/shard_map/ppermute | solution.py:83
  101.8 6.8 %collective-permute-start.21 = (bf16[128,768]{1,0:T(8,128)(2,1)S(1)}, bf16[128,768]{1,0:T(8,128)(2,1)S(1)}, u32[]{:S(2)}, u32[]{:S(2)}) collective-permute-start(bf16[128,768]{1,0:T(8,128)(2,1)S(1)} %collective-permute-done.17.refs_1_), channel_id=1, source_target_pairs={{0,1},{1,0},{2,3},{3,2},{4,5},{5,4},{6,7},{7,6},{8,9},{9,8},{10,11... | collective-permute-start | bytes 589832 | tf_op jit(solution)/shard_map/ppermute | solution.py:83
  102.5 6.2 %collective-permute-start.20 = (bf16[128,768]{1,0:T(8,128)(2,1)S(1)}, bf16[128,768]{1,0:T(8,128)(2,1)S(1)}, u32[]{:S(2)}, u32[]{:S(2)}) collective-permute-start(bf16[128,768]{1,0:T(8,128)(2,1)S(1)} %collective-permute-done.16.refs_0_), channel_id=1, source_target_pairs={{0,1},{1,0},{2,3},{3,2},{4,5},{5,4},{6,7},{7,6},{8,9},{9,8},{10,11... | collective-permute-start | bytes 589832 | tf_op jit(solution)/shard_map/ppermute | solution.py:83
  108.6 1.4 %collective-permute-start.23 = (bf16[128,768]{1,0:T(8,128)(2,1)S(1)}, bf16[128,768]{1,0:T(8,128)(2,1)S(1)}, u32[]{:S(2)}, u32[]{:S(2)}) collective-permute-start(bf16[128,768]{1,0:T(8,128)(2,1)S(1)} %collective-permute-done.19.refs_3_), channel_id=1, source_target_pairs={{0,1},{1,0},{2,3},{3,2},{4,5},{5,4},{6,7},{7,6},{8,9},{9,8},{10,11... | collective-permute-start | bytes 589832 | tf_op jit(solution)/shard_map/ppermute | solution.py:83

commit v6 on v5

--- a/solution.py
+++ b/solution.py
@@ -138,50 +138,69 @@
         move(pairs + sketch(sk_q, small_w, big_w), sems)
 
 
-def merge_kernel(dps, idx, norm, grad, attn, hand, sk_q, sk_o, got, *refs):
-    z, kind = idx[0], idx[3]
-    bigs, smalls, sems = refs[:dps], refs[dps : 2 * dps], refs[-1]
-    big_w, small_w = bigs[0].shape[1] // 2, smalls[0].shape[1] // 2
-    wide, rows = norm.shape[1], RANK // dps
-
-    def keep(wide_ref, thin_ref, extra):
-        pairs = [extra]
+def merge_kernel(dps, kind, fill, pairs, sems):
+    for which in (0, 1):
+
+        @pl.when(kind == which)
+        def _():
+            copies = [
+                pltpu.make_async_copy(src, dst, sems.at[n])
+                for n, (src, dst) in enumerate(pairs[which])
+            ]
+            for c in copies:
+                c.start()
+            fill(which)
+            for c in copies:
+                c.wait()
+
+
+def merge_thin_kernel(dps, idx, grad, attn, got, *refs):
+    z, kind, smalls, sems = idx[0], idx[3], refs[:dps], refs[-1]
+    small_w = smalls[0].shape[1] // 2
+    wide = got.shape[1] - grad.shape[1]
+
+    def fill(_):
         for d in range(dps):
-            pairs.append((window(wide_ref, big_w, z ^ d), bigs[d].at[:, :big_w]))
-            pairs.append((window(thin_ref, small_w, z ^ d), smalls[d].at[:BLK, :small_w]))
-        copies = [
-            pltpu.make_async_copy(src, dst, sems.at[n]) for n, (src, dst) in enumerate(pairs)
+            at = pl.multiple_of(wide + (z ^ d) * small_w, small_w)
+            smalls[d][:, small_w:] = got[:BLK, pl.ds(at, small_w)]
+
+    def keep(ref):
+        return [
+            (window(ref, small_w, z ^ d), smalls[d].at[:, :small_w]) for d in range(dps)
         ]
-        for c in copies:
-            c.start()
-        fill()
-        for c in copies:
-            c.wait()
-
-    def fill():
+
+    merge_kernel(dps, kind, fill, (keep(grad), keep(attn)), sems)
+
+
+def merge_wide_kernel(dps, idx, norm, hand, sk_q, sk_o, got, *refs):
+    z, kind, bigs, sk, sems = idx[0], idx[3], refs[:dps], refs[dps], refs[-1]
+    big_w, small_w = bigs[0].shape[1] // 2, sk.shape[1] // 2
+    rows = RANK // dps
+
+    def fill(which):
         for d in range(dps):
             at = pl.multiple_of((z ^ d) * big_w, big_w)
             bigs[d][:, big_w:] = got[:BLK, pl.ds(at, big_w)]
-            at = pl.multiple_of(wide + (z ^ d) * small_w, small_w)
-            smalls[d][:BLK, small_w:] = got[:BLK, pl.ds(at, small_w)]
         for i in range(dps):
             at = i * (big_w + small_w)
-            below = slice(BLK + RANK + i * rows, BLK + RANK + (i + 1) * rows)
-            smalls[0][below, :] = got[BLK:, at : at + big_w]
-            below = slice(BLK + 2 * RANK + i * rows, BLK + 2 * RANK + (i + 1) * rows)
-            smalls[0][below, small_w:] = got[BLK:, at + big_w : at + big_w + small_w]
-
-    @pl.when(kind == 0)
-    def _():
-        smalls[0][BLK : BLK + RANK, :] = jnp.zeros((RANK, big_w), bf16)
-        dst = smalls[0].at[BLK + 2 * RANK :, :small_w]
-        keep(norm, grad, (window(sk_q, small_w, z), dst))
-
-    @pl.when(kind == 1)
-    def _():
-        smalls[0][BLK + 2 * RANK :, :small_w] = jnp.zeros((RANK, small_w), bf16)
-        dst = smalls[0].at[BLK : BLK + RANK, :]
-        keep(hand, attn, (window(sk_o, big_w, z), dst))
+            sk[RANK + i * rows : RANK + (i + 1) * rows, :] = got[BLK:, at : at + big_w]
+            below = slice(2 * RANK + i * rows, 2 * RANK + (i + 1) * rows)
+            sk[below, small_w:] = got[BLK:, at + big_w : at + big_w + small_w]
+        if which == 0:
+            sk[:RANK, :] = jnp.zeros((RANK, big_w), bf16)
+        else:
+            sk[2 * RANK :, :small_w] = jnp.zeros((RANK, small_w), bf16)
+
+    def keep(ref, sketch):
+        return [sketch] + [
+            (window(ref, big_w, z ^ d), bigs[d].at[:, :big_w]) for d in range(dps)
+        ]
+
+    pairs = (
+        keep(norm, (window(sk_q, small_w, z), sk.at[2 * RANK :, :small_w])),
+        keep(hand, (window(sk_o, big_w, z), sk.at[:RANK, :])),
+    )
+    merge_kernel(dps, kind, fill, pairs, sems)
 
 
 def nt(a, b, precision=None):
@@ -226,7 +245,7 @@
     z, core = idx[0], idx[2]
     smalls, small, keep, send, flat = refs[:dps], *refs[dps:]
     for d, ref in zip(FAR_FIRST, smalls):
-        small[pl.ds(pl.multiple_of((z ^ d) * BLK, BLK), BLK), :] = ref[:BLK, :]
+        small[pl.ds(pl.multiple_of((z ^ d) * BLK, BLK), BLK), :] = ref[...]
     at, diagonals = pack_gram(small, flat, dps)
     flat[at:, :] = jnp.zeros((flat.shape[0] - at, BLK), bf16)
     flat[at : at + 16, :] = diagonals
@@ -241,9 +260,9 @@
         big[pl.ds(pl.multiple_of((z ^ d) * BLK, BLK), BLK), :] = ref[...]
     at, diagonals = pack_gram(big, flat, dps)
     first = (
-        nt(sk[BLK : BLK + RANK, :], big[:, :half_w])
-        + nt(sk[BLK + RANK : BLK + 2 * RANK, :], big[:, half_w:])
-        + nt(sk[BLK + 2 * RANK :, :], small[...])
+        nt(sk[:RANK, :], big[:, :half_w])
+        + nt(sk[RANK : 2 * RANK, :], big[:, half_w:])
+        + nt(sk[2 * RANK :, :], small[...])
     ).astype(bf16)
     for i in range(dps):
         flat[at : at + RANK, :] = first[:, i * BLK : (i + 1) * BLK]
@@ -265,7 +284,7 @@
     out[...] = (mine[...].astype(f32) + got[...].astype(f32)).astype(bf16)
 
 
-def inverse_factor(gram):
+def inverse_factor(gram, spread):
     n, nb = gram.shape[0], 8
     rows = lax.broadcasted_iota(jnp.int32, (n, n), 0)
     cols = lax.broadcasted_iota(jnp.int32, (n, n), 1)
@@ -277,14 +296,18 @@
     def lane(x, k):
         return jnp.broadcast_to(x[:, n + k : n + k + 1], (nb, 2 * n))
 
-    def row(x, i):
-        return jnp.broadcast_to(x[i : i + 1, :], (nb, 2 * n))
+    def row(at):
+        return jnp.broadcast_to(spread[at : at + 1, :], (nb, 2 * n))
 
     done = []
     for b in range(count):
-        cols_of = [lane(slabs[b], nb * b + j) for j in range(nb)]
-        pivot_rows = [row(slabs[b], i) for i in range(nb)]
-        splat = [[row(cols_of[j], i) for j in range(i + 1)] for i in range(nb)]
+        base = b * nb * (nb + 1)
+        spread[base : base + nb, :] = slabs[b]
+        for j in range(nb):
+            at = base + nb * (j + 1)
+            spread[at : at + nb, :] = lane(slabs[b], nb * b + j)
+        pivot_rows = [row(base + i) for i in range(nb)]
+        splat = [[row(base + nb * (j + 1) + i) for j in range(i + 1)] for i in range(nb)]
         below = {s: [lane(slabs[s], nb * b + j) for j in range(nb)] for s in range(b + 1, count)}
         out = None
         for k in range(nb):
@@ -333,7 +356,10 @@
 
 def chain_kernel(dps, counts, idx, *refs):
     z, out_half, core = idx[0], idx[1], idx[2]
-    quarters, big, small, out, flat, thin, wide, left, right = refs[:4], *refs[4:]
+    quarters, big, small, out, stays, leaves, flat, thin, wide, left, right, spread = (
+        refs[:4],
+        *refs[4:],
+    )
     size, bit = quarters[0].shape[0], z % 2
     for n, ref in enumerate(quarters):
         which = 2 * (core ^ (n // 2)) + (bit ^ (n % 2))
@@ -384,7 +410,7 @@
         following = (right if step % 2 == 0 else left)[...]
         beyond = times(ahead, following)
         inner = product_nt(beyond, ahead)
-        low_inv = inverse_factor(gram)
+        low_inv = inverse_factor(gram, spread)
         rows = product(low_inv, ahead)
         if step < 2 * POWER - 1:
             gram = product_nt(product(low_inv, inner), low_inv)
@@ -392,7 +418,7 @@
         else:
             ahead = times(rows, following)
             gram = product_nt(ahead, rows)
-    low_inv = inverse_factor(gram)
+    low_inv = inverse_factor(gram, spread)
     basis = product(low_inv, rows)
     rows = product(low_inv, ahead)
     energy = jnp.sum(times(rows, right[...]) * rows)
@@ -408,10 +434,10 @@
     made_small = (jnp.dot(for_small, small[...], preferred_element_type=f32) * scale_small).astype(
         bf16
     )
-    for n in range(2):
-        part = slice(n * RANK, (n + 1) * RANK)
-        out[part, :big_w] = made_big[:, n * big_w : (n + 1) * big_w]
-        out[part, big_w:] = made_small[:, n * small_w : (n + 1) * small_w]
+    for n, half in enumerate((stays, leaves)):
+        half[:, :big_w] = made_big[:, n * big_w : (n + 1) * big_w]
+        half[:, big_w:] = made_small[:, n * small_w : (n + 1) * small_w]
+        out[n * RANK : (n + 1) * RANK, :] = half[...]
 
 
 def place_kernel(dps, idx, *refs):
@@ -422,7 +448,7 @@
     for d in range(dps):
         bigs = pl.ds(pl.multiple_of((z ^ d) * big_w, big_w), big_w)
         smalls = pl.ds(pl.multiple_of((z ^ d) * small_w, small_w), small_w)
-        here, there = mine[d].at[:RANK], theirs[d].at[RANK:]
+        here, there = mine[d].at[:RANK], theirs[d].at[theirs[d].shape[0] - RANK :]
         for which, query, output in ((0, here, there), (1, there, here)):
 
             @pl.when(kind == which)
@@ -458,31 +484,37 @@
     wide, narrow = norm_in.shape[2], query_grad.shape[2]
     big_w, small_w = wide // dps, narrow // dps
     tokens = dps * BLK
-    args = tuple(
+    hbm = pl.BlockSpec(memory_space=pltpu.HBM)
+    norm, grad, attn, hand, sk_q, sk_o = (
         pltpu.with_memory_space_constraint(v[0], pltpu.HBM)
         for v in (norm_in, query_grad, attn_out, handed, sketch_q, sketch_o)
     )
-    in_hbm = [SMEM] + [pl.BlockSpec(memory_space=pltpu.HBM)] * len(args)
 
     give = call(
         functools.partial(give_kernel, dps),
         shape(BLK + RANK // dps, wide + narrow),
-        (idx, *args),
+        (idx, norm, grad, attn, hand, sk_q, sk_o),
         [pltpu.SemaphoreType.DMA((2 + dps,))],
-        in_hbm,
+        [SMEM] + [hbm] * 6,
     )
     got = swap(give, "tensor", 1)
+    smalls = call(
+        functools.partial(merge_thin_kernel, dps),
+        [shape(BLK, 2 * small_w)] * dps,
+        (idx, grad, attn, got),
+        [pltpu.SemaphoreType.DMA((dps,))],
+        [SMEM, hbm, hbm, VMEM],
+    )
     packed = call(
-        functools.partial(merge_kernel, dps),
-        [shape(BLK, 2 * big_w)] * dps
-        + [shape(BLK + 3 * RANK, 2 * small_w)]
-        + [shape(BLK, 2 * small_w)] * (dps - 1),
-        (idx, *args, got),
-        [pltpu.SemaphoreType.DMA((2 * dps + 1,))],
-        in_hbm + [VMEM],
-    )
-    smalls = [routed(packed[dps + d], sizes, d, False) for d in FAR_FIRST]
+        functools.partial(merge_wide_kernel, dps),
+        [shape(BLK, 2 * big_w)] * dps + [shape(3 * RANK, 2 * small_w)],
+        (idx, norm, hand, sk_q, sk_o, got),
+        [pltpu.SemaphoreType.DMA((dps + 1,))],
+        [SMEM, hbm, hbm, hbm, hbm, VMEM],
+    )
+    smalls = [routed(smalls[d], sizes, d, False) for d in FAR_FIRST]
     bigs = [routed(packed[d], sizes, d, True) for d in FAR_FIRST[:-1]]
+    sketch = routed(packed[dps], sizes, 0, False)
 
     _, thin_rows, wide_rows = packed_rows(dps)
 
@@ -500,7 +532,7 @@
     bigs.append(routed(last, sizes, 0, True))
     bigs[0], thin[1] = lax.optimization_barrier((bigs[0], thin[1]))
     big, *rest = gram(
-        wide_gram_kernel, shape(tokens, 2 * big_w), wide_rows, (*bigs, small, smalls[-1])
+        wide_gram_kernel, shape(tokens, 2 * big_w), wide_rows, (*bigs, small, sketch)
     )
     total = thin_rows + wide_rows
     quarter = shape(total // 4, BLK)
@@ -517,9 +549,9 @@
     quarters = (keep, beside, swap(keep, "tensor", 1), swap(beside, "tensor", 1))
 
     counts = (RANK * wide * tensors, RANK * narrow * tensors)
-    out = call(
+    whole, stays, leaves = call(
         functools.partial(chain_kernel, dps, counts),
-        shape(2 * RANK, big_w + small_w),
+        [shape(2 * RANK, big_w + small_w)] + [shape(RANK, big_w + small_w)] * 2,
         (idx, *quarters, big, small),
         [
             pltpu.VMEM((total, BLK), bf16),
@@ -527,11 +559,14 @@
             pltpu.VMEM((wide_rows, BLK), bf16),
             pltpu.VMEM((tokens, tokens), bf16),
             pltpu.VMEM((tokens, tokens), bf16),
+            pltpu.VMEM((9 * RANK, 2 * RANK), f32),
         ],
     )
-    mine = [routed(out, sizes, d, False) for d in range(3)]
-    mine.append(swap(mine[2], "dp", 1))
-    theirs = [swap(v, "tensor", 1) for v in mine]
+    leaves, stays = routed(leaves, sizes, 2, False), routed(stays, sizes, 2, False)
+    near, here = routed(whole, sizes, 1, False), routed(whole, sizes, 0, False)
+    leaves_on, stays_on = swap(leaves, "dp", 1), swap(stays, "dp", 1)
+    mine = (here, near, stays, stays_on)
+    theirs = [swap(v, "tensor", 1) for v in (here, near, leaves, leaves_on)]
     outs = call(
         functools.partial(place_kernel, dps),
         [

time: 112 us -> 111 us (level)
  starting transfers between devices: 48.4 us -> 42.9 us
  waiting for transfers between devices: 40.6 us -> 45.8 us
    ppermute x11 -> x13, starting transfers between devices: 30.6 us -> 19.4 us  [routed(): return lax.ppermute(value, ('section', 'dp', 'tensor'), pairs)]
    ppermute x11 -> x13, waiting for transfers between devices: 10.4 us -> 20.1 us  [routed(): return lax.ppermute(value, ('section', 'dp', 'tensor'), pairs)]
    ppermute x13 -> x14, starting transfers between devices: 17.8 us -> 23.6 us  [swap(): return lax.ppermute(value, axis, [(i, i ^ bit) for i in range(count)])]
    ppermute x13 -> x14, waiting for transfers between devices: 30.2 us -> 25.6 us  [swap(): return lax.ppermute(value, axis, [(i, i ^ bit) for i in range(count)])]
    pallas_call x9 -> x10, Pallas kernels: 22 us -> 21.6 us  [call(): pl.pallas_call(kernel, out_shape=out_shapes, in_specs=spaces, out_specs=j...]
  transfers between devices with their start and end apart: 24 -> 27, of which waited for: 11 -> 11; matrix products, arithmetic and copies ran while one was open for 0% -> 0% of each run, Pallas kernels for 1% -> 2%
where the time goes in v6:
time: 111 us
  waiting for transfers between devices  45.8 us (41%)
  starting transfers between devices  42.9 us (39%)
  Pallas kernels  21.6 us (19%)
    ppermute x14, waiting for transfers between devices, swap(): return lax.ppermute(value, axis, [(i, i ^ bit) for i in range(count)])  25.6 us
    ppermute x14, starting transfers between devices, swap(): return lax.ppermute(value, axis, [(i, i ^ bit) for i in range(count)])  23.6 us
    pallas_call x10, Pallas kernels, call(): pl.pallas_call(kernel, out_shape=out_shapes, in_specs=spaces, out_specs=j...  21.6 us
    ppermute x13, waiting for transfers between devices, routed(): return lax.ppermute(value, ('section', 'dp', 'tensor'), pairs)  20.1 us
    ppermute x13, starting transfers between devices, routed(): return lax.ppermute(value, ('section', 'dp', 'tensor'), pairs)  19.4 us
  transfers between devices with their start and end apart: 27, of which 11 were waited for; matrix products, arithmetic and copies ran while one was open for 0% of the time, Pallas kernels for 2%

profile of v6, /device:TPU:0, one launch (start us, length us, event | category | flops | bytes accessed | tf_op | source)
XLA Modules:
  0.0 111.2 jit_solution(17251501746400169071)
XLA Ops:
  0.6 0.1 pad_add_fusion.idx
  0.7 1.7 %shard_map.93 = bf16[144,3072]{1,0:T(8,128)(2,1)S(1)} custom-call(s32[4]{0:T(128)S(1)} %pad_add_fusion.idx, bf16[128,2048]{1,0:T(8,128)(2,1)} %bitcast.14, bf16[128,1024]{1,0:T(8,128)(2,1)} %bitcast.20, bf16[128,1024]{1,0:T(8,128)(2,1)} %bitcast.22, bf16[128,2048]{1,0:T(8,128)(2,1)} %bitcast.16, bf16[64,1024]{1,0:T(8,128)(2,1)} %bitcast.24, ...), custom_call_target="tpu_custom_call" | custom-call | tf_op jit(solution)/shard_map/pallas_call | solution.py:464
  2.4 0.5 collective-permute-start
  3.0 2.1 %collective-permute-done.got = bf16[144,3072]{1,0:T(8,128)(2,1)S(1)} collective-permute-done((bf16[144,3072]{1,0:T(8,128)(2,1)S(1)}, bf16[144,3072]{1,0:T(8,128)(2,1)S(1)}, u32[]{:S(2)}, u32[]{:S(2)}) %collective-permute-start) | collective-permute-done | bytes 884768 | tf_op jit(solution)/shard_map/ppermute | solution.py:83
  5.0 1.7 %shard_map.94 = (bf16[128,1024]{1,0:T(8,128)(2,1)S(1)}, bf16[128,1024]{1,0:T(8,128)(2,1)S(1)}, bf16[128,1024]{1,0:T(8,128)(2,1)S(1)}, bf16[128,1024]{1,0:T(8,128)(2,1)S(1)}, bf16[192,512]{1,0:T(8,128)(2,1)S(1)}) custom-call(s32[4]{0:T(128)S(1)} %pad_add_fusion.idx, bf16[128,2048]{1,0:T(8,128)(2,1)} %bitcast.15, bf16[128,2048]{1,0:T(8,128)(2,1)} %bitcast.17, ...), custom_call_target="tpu_custom_call" | custom-call | tf_op jit(solution)/shard_map/pallas_call | solution.py:464
  6.7 4.0 %collective-permute-start.5 = (bf16[128,1024]{1,0:T(8,128)(2,1)S(1)}, bf16[128,1024]{1,0:T(8,128)(2,1)S(1)}, u32[]{:S(2)}, u32[]{:S(2)}) collective-permute-start(bf16[128,1024]{1,0:T(8,128)(2,1)S(1)} %get-tuple-element.39), channel_id=1, source_target_pairs={{0,8},{1,27},{2,26},{3,9},{4,12},{5,31},{6,30},{7,13},{8,0},{9,19}... | collective-permute-start | bytes 786440 | tf_op jit(solution)/shard_map/ppermute | solution.py:97
  10.7 1.5 %shard_map.95 = (bf16[128,512]{1,0:T(8,128)(2,1)S(1)}, bf16[128,512]{1,0:T(8,128)(2,1)S(1)}, bf16[128,512]{1,0:T(8,128)(2,1)S(1)}, bf16[128,512]{1,0:T(8,128)(2,1)S(1)}) custom-call(s32[4]{0:T(128)S(1)} %pad_add_fusion.idx, bf16[128,1024]{1,0:T(8,128)(2,1)} %bitcast.21, bf16[128,1024]{1,0:T(8,128)(2,1)} %bitcast.23, ...), custom_call_target="tpu_custom_call" | custom-call | tf_op jit(solution)/shard_map/pallas_call | solution.py:464
  12.3 0.1 collective-permute-start.1
  12.4 3.9 %collective-permute-start.2 = (bf16[128,512]{1,0:T(8,128)(2,1)S(1)}, bf16[128,512]{1,0:T(8,128)(2,1)S(1)}, u32[]{:S(2)}, u32[]{:S(2)}) collective-permute-start(bf16[128,512]{1,0:T(8,128)(2,1)S(1)} %get-tuple-element.34), channel_id=1, source_target_pairs={{0,12},{1,15},{2,14},{3,13},{4,8},{5,11},{6,10},{7,9},{8,4},{9,7},... | collective-permute-start | bytes 393224 | tf_op jit(solution)/shard_map/ppermute | solution.py:97
  16.3 0.7 collective-permute-start.4
  16.9 13.7 %collective-permute-done.1.refs_0_ = bf16[128,512]{1,0:T(8,128)(2,1)S(1)} collective-permute-done((bf16[128,512]{1,0:T(8,128)(2,1)S(1)}, bf16[128,512]{1,0:T(8,128)(2,1)S(1)}, u32[]{:S(2)}, u32[]{:S(2)}) %collective-permute-start.1) | collective-permute-done | bytes 131104 | tf_op jit(solution)/shard_map/ppermute | solution.py:97
  30.6 5.1 %collective-permute-start.7 = (bf16[128,1024]{1,0:T(8,128)(2,1)S(1)}, bf16[128,1024]{1,0:T(8,128)(2,1)S(1)}, u32[]{:S(2)}, u32[]{:S(2)}) collective-permute-start(bf16[128,1024]{1,0:T(8,128)(2,1)S(1)} %get-tuple-element.43), channel_id=1, source_target_pairs={{0,12},{1,31},{2,30},{3,13},{4,8},{5,27},{6,26},{7,9},{8,4},{9,23}... | collective-permute-start | bytes 786440 | tf_op jit(solution)/shard_map/ppermute | solution.py:97
  35.7 0.0 collective-permute-done.4.refs_3_
  35.7 1.1 %shard_map.96 = (bf16[512,512]{1,0:T(8,128)(2,1)S(1)}, bf16[528,128]{1,0:T(8,128)(2,1)S(1)}, bf16[528,128]{1,0:T(8,128)(2,1)S(1)}) custom-call(s32[4]{0:T(128)S(1)} %pad_add_fusion.idx, bf16[128,512]{1,0:T(8,128)(2,1)S(1)} %collective-permute-done.1.refs_0_, bf16[128,512]{1,0:T(8,128)(2,1)S(1)} %collective-permute-done.2.refs_1_, ...), custom_call_target="tpu_custom_call" | custom-call | tf_op jit(solution)/shard_map/pallas_call | solution.py:464
  36.8 0.7 collective-permute-start.9
  37.5 0.7 collective-permute-start.10
  38.2 0.0 collective-permute-done.5.refs_0_
  38.2 5.5 %collective-permute-start.6 = (bf16[528,128]{1,0:T(8,128)(2,1)S(1)}, bf16[528,128]{1,0:T(8,128)(2,1)S(1)}, u32[]{:S(2)}, u32[]{:S(2)}) collective-permute-start(bf16[528,128]{1,0:T(8,128)(2,1)S(1)} %get-tuple-element.40), channel_id=1, source_target_pairs={{0,1},{1,0},{2,3},{3,2},{4,5},{5,4},{6,7},{7,6},{8,9},{9,8},{10,11... | collective-permute-start | bytes 405512 | tf_op jit(solution)/shard_map/ppermute | solution.py:83
  43.7 1.0 collective-permute-done.6.thin_got
  44.7 3.8 %collective-permute-done.8.refs_2_ = bf16[128,1024]{1,0:T(8,128)(2,1)S(1)} collective-permute-done((bf16[128,1024]{1,0:T(8,128)(2,1)S(1)}, bf16[128,1024]{1,0:T(8,128)(2,1)S(1)}, u32[]{:S(2)}, u32[]{:S(2)}) %collective-permute-start.8) | collective-permute-done | bytes 262176 | tf_op jit(solution)/shard_map/ppermute | solution.py:97
  48.5 0.0 collective-permute-done.9.refs_3_
  48.5 2.0 %shard_map.97 = (bf16[512,1024]{1,0:T(8,128)(2,1)S(1)}, bf16[656,128]{1,0:T(8,128)(2,1)S(1)}, bf16[656,128]{1,0:T(8,128)(2,1)S(1)}) custom-call(s32[4]{0:T(128)S(1)} %pad_add_fusion.idx, bf16[128,1024]{1,0:T(8,128)(2,1)S(1)} %collective-permute-done.5.refs_0_, bf16[128,1024]{1,0:T(8,128)(2,1)S(1)} %collective-permute-done.7.refs_1_, ...), custom_call_target="tpu_custom_call" | custom-call | tf_op jit(solution)/shard_map/pallas_call | solution.py:464
  50.5 2.0 %collective-permute-start.11 = (bf16[656,128]{1,0:T(8,128)(2,1)S(1)}, bf16[656,128]{1,0:T(8,128)(2,1)S(1)}, u32[]{:S(2)}, u32[]{:S(2)}) collective-permute-start(bf16[656,128]{1,0:T(8,128)(2,1)S(1)} %get-tuple-element.49), channel_id=1, source_target_pairs={{0,1},{1,0},{2,3},{3,2},{4,5},{5,4},{6,7},{7,6},{8,9},{9,8},{10,11... | collective-permute-start | bytes 503816 | tf_op jit(solution)/shard_map/ppermute | solution.py:83
  52.6 1.0 collective-permute-done.11.wide_got
  53.6 0.7 shard_map.98
  54.3 2.6 %collective-permute-start.12 = (bf16[592,128]{1,0:T(8,128)(2,1)S(1)}, bf16[592,128]{1,0:T(8,128)(2,1)S(1)}, u32[]{:S(2)}, u32[]{:S(2)}) collective-permute-start(bf16[592,128]{1,0:T(8,128)(2,1)S(1)} %get-tuple-element.51), channel_id=1, source_target_pairs={{0,4},{4,0},{8,12},{12,8},{1,5},{5,1},{9,13},{13,9},{2,6},{6,2},{1... | collective-permute-start | bytes 454664 | tf_op jit(solution)/shard_map/ppermute | solution.py:83
  56.9 4.5 %collective-permute-done.12.got = bf16[592,128]{1,0:T(8,128)(2,1)S(1)} collective-permute-done((bf16[592,128]{1,0:T(8,128)(2,1)S(1)}, bf16[592,128]{1,0:T(8,128)(2,1)S(1)}, u32[]{:S(2)}, u32[]{:S(2)}) %collective-permute-start.12) | collective-permute-done | bytes 151584 | tf_op jit(solution)/shard_map/ppermute | solution.py:83
  61.4 1.7 %collective-permute-start.13 = (bf16[592,128]{1,0:T(8,128)(2,1)S(1)}, bf16[592,128]{1,0:T(8,128)(2,1)S(1)}, u32[]{:S(2)}, u32[]{:S(2)}) collective-permute-start(bf16[592,128]{1,0:T(8,128)(2,1)S(1)} %shard_map.99.mine), channel_id=1, source_target_pairs={{0,8},{4,12},{8,0},{12,4},{1,9},{5,13},{9,1},{13,5},{2,10},{6,14},... | collective-permute-start | bytes 454664 | tf_op jit(solution)/shard_map/ppermute | solution.py:83
  63.0 8.2 %collective-permute-done.13.got = bf16[592,128]{1,0:T(8,128)(2,1)S(1)} collective-permute-done((bf16[592,128]{1,0:T(8,128)(2,1)S(1)}, bf16[592,128]{1,0:T(8,128)(2,1)S(1)}, u32[]{:S(2)}, u32[]{:S(2)}) %collective-permute-start.13) | collective-permute-done | bytes 151584 | tf_op jit(solution)/shard_map/ppermute | solution.py:83
  71.2 0.1 collective-permute-start.14
  71.3 0.1 collective-permute-start.15
  71.4 5.1 %collective-permute-done.14.refs_1_ = bf16[592,128]{1,0:T(8,128)(2,1)S(1)} collective-permute-done((bf16[592,128]{1,0:T(8,128)(2,1)S(1)}, bf16[592,128]{1,0:T(8,128)(2,1)S(1)}, u32[]{:S(2)}, u32[]{:S(2)}) %collective-permute-start.14) | collective-permute-done | bytes 151584 | tf_op jit(solution)/shard_map/ppermute | solution.py:83
  76.5 0.0 collective-permute-start.16
  76.5 1.4 %collective-permute-done.16.refs_3_ = bf16[592,128]{1,0:T(8,128)(2,1)S(1)} collective-permute-done((bf16[592,128]{1,0:T(8,128)(2,1)S(1)}, bf16[592,128]{1,0:T(8,128)(2,1)S(1)}, u32[]{:S(2)}, u32[]{:S(2)}) %collective-permute-start.16) | collective-permute-done | bytes 151584 | tf_op jit(solution)/shard_map/ppermute | solution.py:83
  77.9 11.1 %shard_map.101 = (bf16[128,768]{1,0:T(8,128)(2,1)S(1)}, bf16[64,768]{1,0:T(8,128)(2,1)S(1)}, bf16[64,768]{1,0:T(8,128)(2,1)S(1)}) custom-call(s32[4]{0:T(128)S(1)} %pad_add_fusion.idx, bf16[592,128]{1,0:T(8,128)(2,1)S(1)} %shard_map.100.refs_0_, bf16[592,128]{1,0:T(8,128)(2,1)S(1)} %collective-permute-done.14.refs_1_, ...), custom_call_target="tpu_custom_call" | custom-call | tf_op jit(solution)/shard_map/pallas_call | solution.py:464
  89.0 0.1 collective-permute-start.18
  89.1 0.7 collective-permute-start.17
  89.7 3.4 %collective-permute-start.23 = (bf16[64,768]{1,0:T(8,128)(2,1)S(1)}, bf16[64,768]{1,0:T(8,128)(2,1)S(1)}, u32[]{:S(2)}, u32[]{:S(2)}) collective-permute-start(bf16[64,768]{1,0:T(8,128)(2,1)S(1)} %get-tuple-element.55), channel_id=1, source_target_pairs={{0,8},{1,11},{2,10},{3,9},{4,12},{5,15},{6,14},{7,13},{8,0},{9,3},... | collective-permute-start | bytes 294920 | tf_op jit(solution)/shard_map/ppermute | solution.py:97
  93.2 0.1 collective-permute-start.19
  93.3 2.6 %collective-permute-done.23 = bf16[64,768]{1,0:T(8,128)(2,1)S(1)} collective-permute-done((bf16[64,768]{1,0:T(8,128)(2,1)S(1)}, bf16[64,768]{1,0:T(8,128)(2,1)S(1)}, u32[]{:S(2)}, u32[]{:S(2)}) %collective-permute-start.23) | collective-permute-done | bytes 98336 | tf_op jit(solution)/shard_map/ppermute | solution.py:97
  95.9 2.9 %collective-permute-start.25 = (bf16[64,768]{1,0:T(8,128)(2,1)S(1)}, bf16[64,768]{1,0:T(8,128)(2,1)S(1)}, u32[]{:S(2)}, u32[]{:S(2)}) collective-permute-start(bf16[64,768]{1,0:T(8,128)(2,1)S(1)} %collective-permute-done.23), channel_id=1, source_target_pairs={{0,4},{4,0},{8,12},{12,8},{1,5},{5,1},{9,13},{13,9},{2,6},{6,2},{1... | collective-permute-start | bytes 294920 | tf_op jit(solution)/shard_map/ppermute | solution.py:83
  98.8 4.7 %collective-permute-start.22 = (bf16[128,768]{1,0:T(8,128)(2,1)S(1)}, bf16[128,768]{1,0:T(8,128)(2,1)S(1)}, u32[]{:S(2)}, u32[]{:S(2)}) collective-permute-start(bf16[128,768]{1,0:T(8,128)(2,1)S(1)} %collective-permute-done.18.refs_1_), channel_id=1, source_target_pairs={{0,1},{1,0},{2,3},{3,2},{4,5},{5,4},{6,7},{7,6},{8,9},{9,8},{10,11... | collective-permute-start | bytes 589832 | tf_op jit(solution)/shard_map/ppermute | solution.py:83
  103.6 0.1 collective-permute-start.21
  103.6 0.4 collective-permute-start.24
  104.1 1.7 %collective-permute-start.20 = (bf16[64,768]{1,0:T(8,128)(2,1)S(1)}, bf16[64,768]{1,0:T(8,128)(2,1)S(1)}, u32[]{:S(2)}, u32[]{:S(2)}) collective-permute-start(bf16[64,768]{1,0:T(8,128)(2,1)S(1)} %collective-permute-done.19.refs_2_), channel_id=1, source_target_pairs={{0,4},{4,0},{8,12},{12,8},{1,5},{5,1},{9,13},{13,9},{2,6},{6,2},{1... | collective-permute-start | bytes 294920 | tf_op jit(solution)/shard_map/ppermute | solution.py:83
  105.8 1.2 %collective-permute-start.26 = (bf16[64,768]{1,0:T(8,128)(2,1)S(1)}, bf16[64,768]{1,0:T(8,128)(2,1)S(1)}, u32[]{:S(2)}, u32[]{:S(2)}) collective-permute-start(bf16[64,768]{1,0:T(8,128)(2,1)S(1)} %collective-permute-done.25), channel_id=1, source_target_pairs={{0,1},{1,0},{2,3},{3,2},{4,5},{5,4},{6,7},{7,6},{8,9},{9,8},{10,11... | collective-permute-start | bytes 294920 | tf_op jit(solution)/shard_map/ppermute | solution.py:83
  107.0 2.5 %collective-permute-done.20.refs_3_ = bf16[64,768]{1,0:T(8,128)(2,1)S(1)} collective-permute-done((bf16[64,768]{1,0:T(8,128)(2,1)S(1)}, bf16[64,768]{1,0:T(8,128)(2,1)S(1)}, u32[]{:S(2)}, u32[]{:S(2)}) %collective-permute-start.20) | collective-permute-done | bytes 98336 | tf_op jit(solution)/shard_map/ppermute | solution.py:83
  109.5 1.7 %shard_map.102 = (bf16[64,2048]{1,0:T(8,128)(2,1)}, f32[64,1024]{1,0:T(8,128)}, bf16[64,1024]{1,0:T(8,128)(2,1)}, f32[64,2048]{1,0:T(8,128)}) custom-call(s32[4]{0:T(128)S(1)} %pad_add_fusion.idx, bf16[128,768]{1,0:T(8,128)(2,1)S(1)} %collective-permute-done.17.refs_0_, bf16[128,768]{1,0:T(8,128)(2,1)S(1)} %collective-permute-done.18.refs_1_, ...), custom_call_target="tpu_custom_call" | custom-call | tf_op jit(solution)/shard_map/pallas_call | solution.py:464
  (17 shorter events, 0.1 us)
Async XLA Ops:
  2.4 2.6 %collective-permute-start = (bf16[144,3072]{1,0:T(8,128)(2,1)S(1)}, bf16[144,3072]{1,0:T(8,128)(2,1)S(1)}, u32[]{:S(2)}, u32[]{:S(2)}) collective-permute-start(bf16[144,3072]{1,0:T(8,128)(2,1)S(1)} %shard_map.93), channel_id=1, source_target_pairs={{0,1},{1,0},{2,3},{3,2},{4,5},{5,4},{6,7},{7,6},{8,9},{9,8},{10,11... | collective-permute-start | bytes 2654216 | tf_op jit(solution)/shard_map/ppermute | solution.py:83
  6.7 31.5 %collective-permute-start.5 = (bf16[128,1024]{1,0:T(8,128)(2,1)S(1)}, bf16[128,1024]{1,0:T(8,128)(2,1)S(1)}, u32[]{:S(2)}, u32[]{:S(2)}) collective-permute-start(bf16[128,1024]{1,0:T(8,128)(2,1)S(1)} %get-tuple-element.39), channel_id=1, source_target_pairs={{0,8},{1,27},{2,26},{3,9},{4,12},{5,31},{6,30},{7,13},{8,0},{9,19}... | collective-permute-start | bytes 786440 | tf_op jit(solution)/shard_map/ppermute | solution.py:97
  12.3 18.3 %collective-permute-start.1 = (bf16[128,512]{1,0:T(8,128)(2,1)S(1)}, bf16[128,512]{1,0:T(8,128)(2,1)S(1)}, u32[]{:S(2)}, u32[]{:S(2)}) collective-permute-start(bf16[128,512]{1,0:T(8,128)(2,1)S(1)} %get-tuple-element.33), channel_id=1, source_target_pairs={{0,8},{1,11},{2,10},{3,9},{4,12},{5,15},{6,14},{7,13},{8,0},{9,3},... | collective-permute-start | bytes 393224 | tf_op jit(solution)/shard_map/ppermute | solution.py:97
  12.4 23.3 %collective-permute-start.2 = (bf16[128,512]{1,0:T(8,128)(2,1)S(1)}, bf16[128,512]{1,0:T(8,128)(2,1)S(1)}, u32[]{:S(2)}, u32[]{:S(2)}) collective-permute-start(bf16[128,512]{1,0:T(8,128)(2,1)S(1)} %get-tuple-element.34), channel_id=1, source_target_pairs={{0,12},{1,15},{2,14},{3,13},{4,8},{5,11},{6,10},{7,9},{8,4},{9,7},... | collective-permute-start | bytes 393224 | tf_op jit(solution)/shard_map/ppermute | solution.py:97
  16.3 19.4 %collective-permute-start.3 = (bf16[128,512]{1,0:T(8,128)(2,1)S(1)}, bf16[128,512]{1,0:T(8,128)(2,1)S(1)}, u32[]{:S(2)}, u32[]{:S(2)}) collective-permute-start(bf16[128,512]{1,0:T(8,128)(2,1)S(1)} %get-tuple-element.35), channel_id=1, source_target_pairs={{0,4},{1,7},{2,6},{3,5},{4,0},{5,3},{6,2},{7,1},{8,12},{9,15},{10,... | collective-permute-start | bytes 393224 | tf_op jit(solution)/shard_map/ppermute | solution.py:97
  16.3 19.4 %collective-permute-start.4 = (bf16[128,512]{1,0:T(8,128)(2,1)S(1)}, bf16[128,512]{1,0:T(8,128)(2,1)S(1)}, u32[]{:S(2)}, u32[]{:S(2)}) collective-permute-start(bf16[128,512]{1,0:T(8,128)(2,1)S(1)} %get-tuple-element.36), channel_id=1, source_target_pairs={{0,0},{1,3},{2,2},{3,1},{4,4},{5,7},{6,6},{7,5},{8,8},{9,11},{10,1... | collective-permute-start | bytes 393224 | tf_op jit(solution)/shard_map/ppermute | solution.py:97
  30.6 14.1 %collective-permute-start.7 = (bf16[128,1024]{1,0:T(8,128)(2,1)S(1)}, bf16[128,1024]{1,0:T(8,128)(2,1)S(1)}, u32[]{:S(2)}, u32[]{:S(2)}) collective-permute-start(bf16[128,1024]{1,0:T(8,128)(2,1)S(1)} %get-tuple-element.43), channel_id=1, source_target_pairs={{0,12},{1,31},{2,30},{3,13},{4,8},{5,27},{6,26},{7,9},{8,4},{9,23}... | collective-permute-start | bytes 786440 | tf_op jit(solution)/shard_map/ppermute | solution.py:97
  35.7 12.8 %collective-permute-start.8 = (bf16[128,1024]{1,0:T(8,128)(2,1)S(1)}, bf16[128,1024]{1,0:T(8,128)(2,1)S(1)}, u32[]{:S(2)}, u32[]{:S(2)}) collective-permute-start(bf16[128,1024]{1,0:T(8,128)(2,1)S(1)} %get-tuple-element.44), channel_id=1, source_target_pairs={{0,4},{1,23},{2,22},{3,5},{4,0},{5,19},{6,18},{7,1},{8,12},{9,31},... | collective-permute-start | bytes 786440 | tf_op jit(solution)/shard_map/ppermute | solution.py:97
  36.8 11.7 %collective-permute-start.9 = (bf16[128,1024]{1,0:T(8,128)(2,1)S(1)}, bf16[128,1024]{1,0:T(8,128)(2,1)S(1)}, u32[]{:S(2)}, u32[]{:S(2)}) collective-permute-start(bf16[128,1024]{1,0:T(8,128)(2,1)S(1)} %get-tuple-element.45), channel_id=1, source_target_pairs={{0,0},{1,19},{2,18},{3,1},{4,4},{5,23},{6,22},{7,5},{8,8},{9,27},{... | collective-permute-start | bytes 786440 | tf_op jit(solution)/shard_map/ppermute | solution.py:97
  37.5 7.2 %collective-permute-start.10 = (bf16[192,512]{1,0:T(8,128)(2,1)S(1)}, bf16[192,512]{1,0:T(8,128)(2,1)S(1)}, u32[]{:S(2)}, u32[]{:S(2)}) collective-permute-start(bf16[192,512]{1,0:T(8,128)(2,1)S(1)} %get-tuple-element.47), channel_id=1, source_target_pairs={{0,0},{1,3},{2,2},{3,1},{4,4},{5,7},{6,6},{7,5},{8,8},{9,11},{10,1... | collective-permute-start | bytes 589832 | tf_op jit(solution)/shard_map/ppermute | solution.py:97
  38.2 6.5 %collective-permute-start.6 = (bf16[528,128]{1,0:T(8,128)(2,1)S(1)}, bf16[528,128]{1,0:T(8,128)(2,1)S(1)}, u32[]{:S(2)}, u32[]{:S(2)}) collective-permute-start(bf16[528,128]{1,0:T(8,128)(2,1)S(1)} %get-tuple-element.40), channel_id=1, source_target_pairs={{0,1},{1,0},{2,3},{3,2},{4,5},{5,4},{6,7},{7,6},{8,9},{9,8},{10,11... | collective-permute-start | bytes 405512 | tf_op jit(solution)/shard_map/ppermute | solution.py:83
  50.5 3.1 %collective-permute-start.11 = (bf16[656,128]{1,0:T(8,128)(2,1)S(1)}, bf16[656,128]{1,0:T(8,128)(2,1)S(1)}, u32[]{:S(2)}, u32[]{:S(2)}) collective-permute-start(bf16[656,128]{1,0:T(8,128)(2,1)S(1)} %get-tuple-element.49), channel_id=1, source_target_pairs={{0,1},{1,0},{2,3},{3,2},{4,5},{5,4},{6,7},{7,6},{8,9},{9,8},{10,11... | collective-permute-start | bytes 503816 | tf_op jit(solution)/shard_map/ppermute | solution.py:83
  54.3 7.0 %collective-permute-start.12 = (bf16[592,128]{1,0:T(8,128)(2,1)S(1)}, bf16[592,128]{1,0:T(8,128)(2,1)S(1)}, u32[]{:S(2)}, u32[]{:S(2)}) collective-permute-start(bf16[592,128]{1,0:T(8,128)(2,1)S(1)} %get-tuple-element.51), channel_id=1, source_target_pairs={{0,4},{4,0},{8,12},{12,8},{1,5},{5,1},{9,13},{13,9},{2,6},{6,2},{1... | collective-permute-start | bytes 454664 | tf_op jit(solution)/shard_map/ppermute | solution.py:83
  61.4 9.8 %collective-permute-start.13 = (bf16[592,128]{1,0:T(8,128)(2,1)S(1)}, bf16[592,128]{1,0:T(8,128)(2,1)S(1)}, u32[]{:S(2)}, u32[]{:S(2)}) collective-permute-start(bf16[592,128]{1,0:T(8,128)(2,1)S(1)} %shard_map.99.mine), channel_id=1, source_target_pairs={{0,8},{4,12},{8,0},{12,4},{1,9},{5,13},{9,1},{13,5},{2,10},{6,14},... | collective-permute-start | bytes 454664 | tf_op jit(solution)/shard_map/ppermute | solution.py:83
  71.2 5.3 %collective-permute-start.14 = (bf16[592,128]{1,0:T(8,128)(2,1)S(1)}, bf16[592,128]{1,0:T(8,128)(2,1)S(1)}, u32[]{:S(2)}, u32[]{:S(2)}) collective-permute-start(bf16[592,128]{1,0:T(8,128)(2,1)S(1)} %shard_map.100.refs_0_), channel_id=1, source_target_pairs={{0,4},{4,0},{8,12},{12,8},{1,5},{5,1},{9,13},{13,9},{2,6},{6,2},{1... | collective-permute-start | bytes 454664 | tf_op jit(solution)/shard_map/ppermute | solution.py:83
  71.3 5.2 %collective-permute-start.15 = (bf16[592,128]{1,0:T(8,128)(2,1)S(1)}, bf16[592,128]{1,0:T(8,128)(2,1)S(1)}, u32[]{:S(2)}, u32[]{:S(2)}) collective-permute-start(bf16[592,128]{1,0:T(8,128)(2,1)S(1)} %shard_map.100.refs_0_), channel_id=1, source_target_pairs={{0,1},{1,0},{2,3},{3,2},{4,5},{5,4},{6,7},{7,6},{8,9},{9,8},{10,11... | collective-permute-start | bytes 454664 | tf_op jit(solution)/shard_map/ppermute | solution.py:83
  76.5 1.4 %collective-permute-start.16 = (bf16[592,128]{1,0:T(8,128)(2,1)S(1)}, bf16[592,128]{1,0:T(8,128)(2,1)S(1)}, u32[]{:S(2)}, u32[]{:S(2)}) collective-permute-start(bf16[592,128]{1,0:T(8,128)(2,1)S(1)} %collective-permute-done.14.refs_1_), channel_id=1, source_target_pairs={{0,1},{1,0},{2,3},{3,2},{4,5},{5,4},{6,7},{7,6},{8,9},{9,8},{10,11... | collective-permute-start | bytes 454664 | tf_op jit(solution)/shard_map/ppermute | solution.py:83
  89.0 9.8 %collective-permute-start.18 = (bf16[128,768]{1,0:T(8,128)(2,1)S(1)}, bf16[128,768]{1,0:T(8,128)(2,1)S(1)}, u32[]{:S(2)}, u32[]{:S(2)}) collective-permute-start(bf16[128,768]{1,0:T(8,128)(2,1)S(1)} %get-tuple-element.53), channel_id=1, source_target_pairs={{0,4},{1,7},{2,6},{3,5},{4,0},{5,3},{6,2},{7,1},{8,12},{9,15},{10,... | collective-permute-start | bytes 589832 | tf_op jit(solution)/shard_map/ppermute | solution.py:97
  89.1 14.5 %collective-permute-start.17 = (bf16[128,768]{1,0:T(8,128)(2,1)S(1)}, bf16[128,768]{1,0:T(8,128)(2,1)S(1)}, u32[]{:S(2)}, u32[]{:S(2)}) collective-permute-start(bf16[128,768]{1,0:T(8,128)(2,1)S(1)} %get-tuple-element.53), channel_id=1, source_target_pairs={{0,0},{1,3},{2,2},{3,1},{4,4},{5,7},{6,6},{7,5},{8,8},{9,11},{10,1... | collective-permute-start | bytes 589832 | tf_op jit(solution)/shard_map/ppermute | solution.py:97
  89.7 6.1 %collective-permute-start.23 = (bf16[64,768]{1,0:T(8,128)(2,1)S(1)}, bf16[64,768]{1,0:T(8,128)(2,1)S(1)}, u32[]{:S(2)}, u32[]{:S(2)}) collective-permute-start(bf16[64,768]{1,0:T(8,128)(2,1)S(1)} %get-tuple-element.55), channel_id=1, source_target_pairs={{0,8},{1,11},{2,10},{3,9},{4,12},{5,15},{6,14},{7,13},{8,0},{9,3},... | collective-permute-start | bytes 294920 | tf_op jit(solution)/shard_map/ppermute | solution.py:97
  93.2 10.9 %collective-permute-start.19 = (bf16[64,768]{1,0:T(8,128)(2,1)S(1)}, bf16[64,768]{1,0:T(8,128)(2,1)S(1)}, u32[]{:S(2)}, u32[]{:S(2)}) collective-permute-start(bf16[64,768]{1,0:T(8,128)(2,1)S(1)} %get-tuple-element.54), channel_id=1, source_target_pairs={{0,8},{1,11},{2,10},{3,9},{4,12},{5,15},{6,14},{7,13},{8,0},{9,3},... | collective-permute-start | bytes 294920 | tf_op jit(solution)/shard_map/ppermute | solution.py:97
  95.9 9.9 %collective-permute-start.25 = (bf16[64,768]{1,0:T(8,128)(2,1)S(1)}, bf16[64,768]{1,0:T(8,128)(2,1)S(1)}, u32[]{:S(2)}, u32[]{:S(2)}) collective-permute-start(bf16[64,768]{1,0:T(8,128)(2,1)S(1)} %collective-permute-done.23), channel_id=1, source_target_pairs={{0,4},{4,0},{8,12},{12,8},{1,5},{5,1},{9,13},{13,9},{2,6},{6,2},{1... | collective-permute-start | bytes 294920 | tf_op jit(solution)/shard_map/ppermute | solution.py:83
  98.8 10.7 %collective-permute-start.22 = (bf16[128,768]{1,0:T(8,128)(2,1)S(1)}, bf16[128,768]{1,0:T(8,128)(2,1)S(1)}, u32[]{:S(2)}, u32[]{:S(2)}) collective-permute-start(bf16[128,768]{1,0:T(8,128)(2,1)S(1)} %collective-permute-done.18.refs_1_), channel_id=1, source_target_pairs={{0,1},{1,0},{2,3},{3,2},{4,5},{5,4},{6,7},{7,6},{8,9},{9,8},{10,11... | collective-permute-start | bytes 589832 | tf_op jit(solution)/shard_map/ppermute | solution.py:83
  103.6 5.9 %collective-permute-start.21 = (bf16[128,768]{1,0:T(8,128)(2,1)S(1)}, bf16[128,768]{1,0:T(8,128)(2,1)S(1)}, u32[]{:S(2)}, u32[]{:S(2)}) collective-permute-start(bf16[128,768]{1,0:T(8,128)(2,1)S(1)} %collective-permute-done.17.refs_0_), channel_id=1, source_target_pairs={{0,1},{1,0},{2,3},{3,2},{4,5},{5,4},{6,7},{7,6},{8,9},{9,8},{10,11... | collective-permute-start | bytes 589832 | tf_op jit(solution)/shard_map/ppermute | solution.py:83
  103.6 5.8 %collective-permute-start.24 = (bf16[64,768]{1,0:T(8,128)(2,1)S(1)}, bf16[64,768]{1,0:T(8,128)(2,1)S(1)}, u32[]{:S(2)}, u32[]{:S(2)}) collective-permute-start(bf16[64,768]{1,0:T(8,128)(2,1)S(1)} %collective-permute-done.23), channel_id=1, source_target_pairs={{0,1},{1,0},{2,3},{3,2},{4,5},{5,4},{6,7},{7,6},{8,9},{9,8},{10,11... | collective-permute-start | bytes 294920 | tf_op jit(solution)/shard_map/ppermute | solution.py:83
  104.1 5.4 %collective-permute-start.20 = (bf16[64,768]{1,0:T(8,128)(2,1)S(1)}, bf16[64,768]{1,0:T(8,128)(2,1)S(1)}, u32[]{:S(2)}, u32[]{:S(2)}) collective-permute-start(bf16[64,768]{1,0:T(8,128)(2,1)S(1)} %collective-permute-done.19.refs_2_), channel_id=1, source_target_pairs={{0,4},{4,0},{8,12},{12,8},{1,5},{5,1},{9,13},{13,9},{2,6},{6,2},{1... | collective-permute-start | bytes 294920 | tf_op jit(solution)/shard_map/ppermute | solution.py:83
  105.8 3.7 %collective-permute-start.26 = (bf16[64,768]{1,0:T(8,128)(2,1)S(1)}, bf16[64,768]{1,0:T(8,128)(2,1)S(1)}, u32[]{:S(2)}, u32[]{:S(2)}) collective-permute-start(bf16[64,768]{1,0:T(8,128)(2,1)S(1)} %collective-permute-done.25), channel_id=1, source_target_pairs={{0,1},{1,0},{2,3},{3,2},{4,5},{5,4},{6,7},{7,6},{8,9},{9,8},{10,11... | collective-permute-start | bytes 294920 | tf_op jit(solution)/shard_map/ppermute | solution.py:83

commit v7 on v6

--- a/solution.py
+++ b/solution.py
@@ -10,7 +10,8 @@
 RANK = 64
 POWER = 2
 BLK = 128
-FAR_FIRST = (2, 3, 1, 0)
+THIN_ORDER = (2, 3, 1, 0)
+WIDE_ORDER = (2, 1, 0, 3)
 
 precise = lax.Precision.HIGHEST
 f32 = jnp.float32
@@ -244,7 +245,7 @@
 def thin_gram_kernel(dps, idx, *refs):
     z, core = idx[0], idx[2]
     smalls, small, keep, send, flat = refs[:dps], *refs[dps:]
-    for d, ref in zip(FAR_FIRST, smalls):
+    for d, ref in zip(THIN_ORDER, smalls):
         small[pl.ds(pl.multiple_of((z ^ d) * BLK, BLK), BLK), :] = ref[...]
     at, diagonals = pack_gram(small, flat, dps)
     flat[at:, :] = jnp.zeros((flat.shape[0] - at, BLK), bf16)
@@ -254,9 +255,9 @@
 
 def wide_gram_kernel(dps, idx, *refs):
     z, core = idx[0], idx[2]
-    bigs, small, sk, big, keep, send, flat = refs[:dps], *refs[dps:]
+    sk, bigs, small, big, keep, send, flat = refs[0], refs[1 : dps + 1], *refs[dps + 1 :]
     half_w = big.shape[1] // 2
-    for d, ref in zip(FAR_FIRST, bigs):
+    for d, ref in zip(WIDE_ORDER, bigs):
         big[pl.ds(pl.multiple_of((z ^ d) * BLK, BLK), BLK), :] = ref[...]
     at, diagonals = pack_gram(big, flat, dps)
     first = (
@@ -512,9 +513,9 @@
         [pltpu.SemaphoreType.DMA((dps + 1,))],
         [SMEM, hbm, hbm, hbm, hbm, VMEM],
     )
-    smalls = [routed(smalls[d], sizes, d, False) for d in FAR_FIRST]
-    bigs = [routed(packed[d], sizes, d, True) for d in FAR_FIRST[:-1]]
+    smalls = [routed(smalls[d], sizes, d, False) for d in THIN_ORDER]
     sketch = routed(packed[dps], sizes, 0, False)
+    bigs = [routed(packed[d], sizes, d, True) for d in WIDE_ORDER]
 
     _, thin_rows, wide_rows = packed_rows(dps)
 
@@ -528,11 +529,8 @@
         return m, keep, swap(send, "tensor", 1)
 
     small, *thin = gram(thin_gram_kernel, shape(tokens, 2 * small_w), thin_rows, smalls)
-    last, thin[0] = lax.optimization_barrier((packed[0], thin[0]))
-    bigs.append(routed(last, sizes, 0, True))
-    bigs[0], thin[1] = lax.optimization_barrier((bigs[0], thin[1]))
     big, *rest = gram(
-        wide_gram_kernel, shape(tokens, 2 * big_w), wide_rows, (*bigs, small, sketch)
+        wide_gram_kernel, shape(tokens, 2 * big_w), wide_rows, (sketch, *bigs, small)
     )
     total = thin_rows + wide_rows
     quarter = shape(total // 4, BLK)

time: 111 us -> 107 us (0.964)
  waiting for transfers between devices: 45.8 us -> 41.7 us
    ppermute x13, waiting for transfers between devices: 20.1 us -> 17.8 us  [routed(): return lax.ppermute(value, ('section', 'dp', 'tensor'), pairs)]
    ppermute x14, waiting for transfers between devices: 25.6 us -> 23.9 us  [swap(): return lax.ppermute(value, axis, [(i, i ^ bit) for i in range(count)])]
  transfers between devices with their start and end apart: 27 -> 27, of which waited for: 11 -> 10; matrix products, arithmetic and copies ran while one was open for 0% -> 0% of each run, Pallas kernels for 2% -> 3%
where the time goes in v7:
time: 107 us; the launch traced here: 106 us
  starting transfers between devices  42.1 us (39%)
  waiting for transfers between devices  41.7 us (39%)
  Pallas kernels  21.6 us (20%)
    ppermute x14, waiting for transfers between devices, swap(): return lax.ppermute(value, axis, [(i, i ^ bit) for i in range(count)])  23.9 us
    ppermute x14, starting transfers between devices, swap(): return lax.ppermute(value, axis, [(i, i ^ bit) for i in range(count)])  22.7 us
    pallas_call x10, Pallas kernels, call(): pl.pallas_call(kernel, out_shape=out_shapes, in_specs=spaces, out_specs=j...  21.6 us
    ppermute x13, starting transfers between devices, routed(): return lax.ppermute(value, ('section', 'dp', 'tensor'), pairs)  19.4 us
    ppermute x13, waiting for transfers between devices, routed(): return lax.ppermute(value, ('section', 'dp', 'tensor'), pairs)  17.8 us
  transfers between devices with their start and end apart: 27, of which 10 were waited for; matrix products, arithmetic and copies ran while one was open for 0% of the time, Pallas kernels for 3%

profile of v7, /device:TPU:0, one launch (start us, length us, event | category | flops | bytes accessed | tf_op | source)
XLA Modules:
  0.0 106.4 jit_solution(74352129175695364)
XLA Ops:
  0.6 0.1 pad_add_fusion.idx
  0.7 1.7 %shard_map.93 = bf16[144,3072]{1,0:T(8,128)(2,1)S(1)} custom-call(s32[4]{0:T(128)S(1)} %pad_add_fusion.idx, bf16[128,2048]{1,0:T(8,128)(2,1)} %bitcast.14, bf16[128,1024]{1,0:T(8,128)(2,1)} %bitcast.18, bf16[128,1024]{1,0:T(8,128)(2,1)} %bitcast.20, bf16[128,2048]{1,0:T(8,128)(2,1)} %bitcast.16, bf16[64,1024]{1,0:T(8,128)(2,1)} %bitcast.24, ...), custom_call_target="tpu_custom_call" | custom-call | tf_op jit(solution)/shard_map/pallas_call | solution.py:465
  2.4 0.5 collective-permute-start
  3.0 2.1 %collective-permute-done.got = bf16[144,3072]{1,0:T(8,128)(2,1)S(1)} collective-permute-done((bf16[144,3072]{1,0:T(8,128)(2,1)S(1)}, bf16[144,3072]{1,0:T(8,128)(2,1)S(1)}, u32[]{:S(2)}, u32[]{:S(2)}) %collective-permute-start) | collective-permute-done | bytes 884768 | tf_op jit(solution)/shard_map/ppermute | solution.py:84
  5.0 1.5 %shard_map.94 = (bf16[128,512]{1,0:T(8,128)(2,1)S(1)}, bf16[128,512]{1,0:T(8,128)(2,1)S(1)}, bf16[128,512]{1,0:T(8,128)(2,1)S(1)}, bf16[128,512]{1,0:T(8,128)(2,1)S(1)}) custom-call(s32[4]{0:T(128)S(1)} %pad_add_fusion.idx, bf16[128,1024]{1,0:T(8,128)(2,1)} %bitcast.19, bf16[128,1024]{1,0:T(8,128)(2,1)} %bitcast.21, ...), custom_call_target="tpu_custom_call" | custom-call | tf_op jit(solution)/shard_map/pallas_call | solution.py:465
  6.6 4.0 %collective-permute-start.1 = (bf16[128,512]{1,0:T(8,128)(2,1)S(1)}, bf16[128,512]{1,0:T(8,128)(2,1)S(1)}, u32[]{:S(2)}, u32[]{:S(2)}) collective-permute-start(bf16[128,512]{1,0:T(8,128)(2,1)S(1)} %get-tuple-element.28), channel_id=1, source_target_pairs={{0,8},{1,11},{2,10},{3,9},{4,12},{5,15},{6,14},{7,13},{8,0},{9,3},... | collective-permute-start | bytes 393224 | tf_op jit(solution)/shard_map/ppermute | solution.py:98
  10.6 1.3 %collective-permute-start.2 = (bf16[128,512]{1,0:T(8,128)(2,1)S(1)}, bf16[128,512]{1,0:T(8,128)(2,1)S(1)}, u32[]{:S(2)}, u32[]{:S(2)}) collective-permute-start(bf16[128,512]{1,0:T(8,128)(2,1)S(1)} %get-tuple-element.29), channel_id=1, source_target_pairs={{0,12},{1,15},{2,14},{3,13},{4,8},{5,11},{6,10},{7,9},{8,4},{9,7},... | collective-permute-start | bytes 393224 | tf_op jit(solution)/shard_map/ppermute | solution.py:98
  11.9 0.2 collective-permute-start.3
  12.2 0.7 collective-permute-start.4
  12.8 1.7 %shard_map.96 = (bf16[128,1024]{1,0:T(8,128)(2,1)S(1)}, bf16[128,1024]{1,0:T(8,128)(2,1)S(1)}, bf16[128,1024]{1,0:T(8,128)(2,1)S(1)}, bf16[128,1024]{1,0:T(8,128)(2,1)S(1)}, bf16[192,512]{1,0:T(8,128)(2,1)S(1)}) custom-call(s32[4]{0:T(128)S(1)} %pad_add_fusion.idx, bf16[128,2048]{1,0:T(8,128)(2,1)} %bitcast.15, bf16[128,2048]{1,0:T(8,128)(2,1)} %bitcast.17, ...), custom_call_target="tpu_custom_call" | custom-call | tf_op jit(solution)/shard_map/pallas_call | solution.py:465
  14.5 2.9 %collective-permute-start.7 = (bf16[128,1024]{1,0:T(8,128)(2,1)S(1)}, bf16[128,1024]{1,0:T(8,128)(2,1)S(1)}, u32[]{:S(2)}, u32[]{:S(2)}) collective-permute-start(bf16[128,1024]{1,0:T(8,128)(2,1)S(1)} %get-tuple-element.35), channel_id=1, source_target_pairs={{0,8},{1,27},{2,26},{3,9},{4,12},{5,31},{6,30},{7,13},{8,0},{9,19}... | collective-permute-start | bytes 786440 | tf_op jit(solution)/shard_map/ppermute | solution.py:98
  17.4 2.9 %collective-permute-done.1.refs_0_ = bf16[128,512]{1,0:T(8,128)(2,1)S(1)} collective-permute-done((bf16[128,512]{1,0:T(8,128)(2,1)S(1)}, bf16[128,512]{1,0:T(8,128)(2,1)S(1)}, u32[]{:S(2)}, u32[]{:S(2)}) %collective-permute-start.1) | collective-permute-done | bytes 131104 | tf_op jit(solution)/shard_map/ppermute | solution.py:98
  20.2 1.5 %collective-permute-start.8 = (bf16[128,1024]{1,0:T(8,128)(2,1)S(1)}, bf16[128,1024]{1,0:T(8,128)(2,1)S(1)}, u32[]{:S(2)}, u32[]{:S(2)}) collective-permute-start(bf16[128,1024]{1,0:T(8,128)(2,1)S(1)} %get-tuple-element.36), channel_id=1, source_target_pairs={{0,4},{1,23},{2,22},{3,5},{4,0},{5,19},{6,18},{7,1},{8,12},{9,31},... | collective-permute-start | bytes 786440 | tf_op jit(solution)/shard_map/ppermute | solution.py:98
  21.7 0.0 collective-permute-done.2.refs_1_
  21.7 0.7 collective-permute-start.9
  22.4 3.5 %collective-permute-start.10 = (bf16[128,1024]{1,0:T(8,128)(2,1)S(1)}, bf16[128,1024]{1,0:T(8,128)(2,1)S(1)}, u32[]{:S(2)}, u32[]{:S(2)}) collective-permute-start(bf16[128,1024]{1,0:T(8,128)(2,1)S(1)} %get-tuple-element.38), channel_id=1, source_target_pairs={{0,12},{1,31},{2,30},{3,13},{4,8},{5,27},{6,26},{7,9},{8,4},{9,23}... | collective-permute-start | bytes 786440 | tf_op jit(solution)/shard_map/ppermute | solution.py:98
  25.9 0.7 collective-permute-start.6
  26.6 1.1 %shard_map.95 = (bf16[512,512]{1,0:T(8,128)(2,1)S(1)}, bf16[528,128]{1,0:T(8,128)(2,1)S(1)}, bf16[528,128]{1,0:T(8,128)(2,1)S(1)}) custom-call(s32[4]{0:T(128)S(1)} %pad_add_fusion.idx, bf16[128,512]{1,0:T(8,128)(2,1)S(1)} %collective-permute-done.1.refs_0_, bf16[128,512]{1,0:T(8,128)(2,1)S(1)} %collective-permute-done.2.refs_1_, ...), custom_call_target="tpu_custom_call" | custom-call | tf_op jit(solution)/shard_map/pallas_call | solution.py:465
  27.7 12.2 %collective-permute-done.7.refs_1_ = bf16[128,1024]{1,0:T(8,128)(2,1)S(1)} collective-permute-done((bf16[128,1024]{1,0:T(8,128)(2,1)S(1)}, bf16[128,1024]{1,0:T(8,128)(2,1)S(1)}, u32[]{:S(2)}, u32[]{:S(2)}) %collective-permute-start.7) | collective-permute-done | bytes 262176 | tf_op jit(solution)/shard_map/ppermute | solution.py:98
  40.0 2.0 %shard_map.97 = (bf16[512,1024]{1,0:T(8,128)(2,1)S(1)}, bf16[656,128]{1,0:T(8,128)(2,1)S(1)}, bf16[656,128]{1,0:T(8,128)(2,1)S(1)}) custom-call(s32[4]{0:T(128)S(1)} %pad_add_fusion.idx, bf16[192,512]{1,0:T(8,128)(2,1)S(1)} %collective-permute-done.6.refs_0_, bf16[128,1024]{1,0:T(8,128)(2,1)S(1)} %collective-permute-done.7.refs_1_, ...), custom_call_target="tpu_custom_call" | custom-call | tf_op jit(solution)/shard_map/pallas_call | solution.py:465
  42.0 0.1 collective-permute-start.11
  42.1 0.5 collective-permute-start.5
  42.6 1.1 %collective-permute-done.5.thin_got = bf16[528,128]{1,0:T(8,128)(2,1)S(1)} collective-permute-done((bf16[528,128]{1,0:T(8,128)(2,1)S(1)}, bf16[528,128]{1,0:T(8,128)(2,1)S(1)}, u32[]{:S(2)}, u32[]{:S(2)}) %collective-permute-start.5) | collective-permute-done | bytes 135200 | tf_op jit(solution)/shard_map/ppermute | solution.py:84
  43.7 0.7 shard_map.98
  44.3 7.0 %collective-permute-start.12 = (bf16[592,128]{1,0:T(8,128)(2,1)S(1)}, bf16[592,128]{1,0:T(8,128)(2,1)S(1)}, u32[]{:S(2)}, u32[]{:S(2)}) collective-permute-start(bf16[592,128]{1,0:T(8,128)(2,1)S(1)} %get-tuple-element.43), channel_id=1, source_target_pairs={{0,4},{4,0},{8,12},{12,8},{1,5},{5,1},{9,13},{13,9},{2,6},{6,2},{1... | collective-permute-start | bytes 454664 | tf_op jit(solution)/shard_map/ppermute | solution.py:84
  51.3 4.4 %collective-permute-done.12.got = bf16[592,128]{1,0:T(8,128)(2,1)S(1)} collective-permute-done((bf16[592,128]{1,0:T(8,128)(2,1)S(1)}, bf16[592,128]{1,0:T(8,128)(2,1)S(1)}, u32[]{:S(2)}, u32[]{:S(2)}) %collective-permute-start.12) | collective-permute-done | bytes 151584 | tf_op jit(solution)/shard_map/ppermute | solution.py:84
  55.7 3.7 %collective-permute-start.13 = (bf16[592,128]{1,0:T(8,128)(2,1)S(1)}, bf16[592,128]{1,0:T(8,128)(2,1)S(1)}, u32[]{:S(2)}, u32[]{:S(2)}) collective-permute-start(bf16[592,128]{1,0:T(8,128)(2,1)S(1)} %shard_map.99.mine), channel_id=1, source_target_pairs={{0,8},{4,12},{8,0},{12,4},{1,9},{5,13},{9,1},{13,5},{2,10},{6,14},... | collective-permute-start | bytes 454664 | tf_op jit(solution)/shard_map/ppermute | solution.py:84
  59.5 6.8 %collective-permute-done.13.got = bf16[592,128]{1,0:T(8,128)(2,1)S(1)} collective-permute-done((bf16[592,128]{1,0:T(8,128)(2,1)S(1)}, bf16[592,128]{1,0:T(8,128)(2,1)S(1)}, u32[]{:S(2)}, u32[]{:S(2)}) %collective-permute-start.13) | collective-permute-done | bytes 151584 | tf_op jit(solution)/shard_map/ppermute | solution.py:84
  66.3 0.1 collective-permute-start.14
  66.4 0.1 collective-permute-start.15
  66.5 5.6 %collective-permute-done.14.refs_1_ = bf16[592,128]{1,0:T(8,128)(2,1)S(1)} collective-permute-done((bf16[592,128]{1,0:T(8,128)(2,1)S(1)}, bf16[592,128]{1,0:T(8,128)(2,1)S(1)}, u32[]{:S(2)}, u32[]{:S(2)}) %collective-permute-start.14) | collective-permute-done | bytes 151584 | tf_op jit(solution)/shard_map/ppermute | solution.py:84
  72.1 0.0 collective-permute-start.16
  72.1 0.0 collective-permute-done.15.refs_2_
  72.1 1.4 %collective-permute-done.16.refs_3_ = bf16[592,128]{1,0:T(8,128)(2,1)S(1)} collective-permute-done((bf16[592,128]{1,0:T(8,128)(2,1)S(1)}, bf16[592,128]{1,0:T(8,128)(2,1)S(1)}, u32[]{:S(2)}, u32[]{:S(2)}) %collective-permute-start.16) | collective-permute-done | bytes 151584 | tf_op jit(solution)/shard_map/ppermute | solution.py:84
  73.5 11.1 %shard_map.101 = (bf16[128,768]{1,0:T(8,128)(2,1)S(1)}, bf16[64,768]{1,0:T(8,128)(2,1)S(1)}, bf16[64,768]{1,0:T(8,128)(2,1)S(1)}) custom-call(s32[4]{0:T(128)S(1)} %pad_add_fusion.idx, bf16[592,128]{1,0:T(8,128)(2,1)S(1)} %shard_map.100.refs_0_, bf16[592,128]{1,0:T(8,128)(2,1)S(1)} %collective-permute-done.14.refs_1_, ...), custom_call_target="tpu_custom_call" | custom-call | tf_op jit(solution)/shard_map/pallas_call | solution.py:465
  84.6 0.4 collective-permute-start.18
  84.9 0.7 collective-permute-start.17
  85.6 2.5 %collective-permute-start.23 = (bf16[64,768]{1,0:T(8,128)(2,1)S(1)}, bf16[64,768]{1,0:T(8,128)(2,1)S(1)}, u32[]{:S(2)}, u32[]{:S(2)}) collective-permute-start(bf16[64,768]{1,0:T(8,128)(2,1)S(1)} %get-tuple-element.47), channel_id=1, source_target_pairs={{0,8},{1,11},{2,10},{3,9},{4,12},{5,15},{6,14},{7,13},{8,0},{9,3},... | collective-permute-start | bytes 294920 | tf_op jit(solution)/shard_map/ppermute | solution.py:98
  88.1 0.5 collective-permute-start.19
  88.6 2.7 %collective-permute-done.23 = bf16[64,768]{1,0:T(8,128)(2,1)S(1)} collective-permute-done((bf16[64,768]{1,0:T(8,128)(2,1)S(1)}, bf16[64,768]{1,0:T(8,128)(2,1)S(1)}, u32[]{:S(2)}, u32[]{:S(2)}) %collective-permute-start.23) | collective-permute-done | bytes 98336 | tf_op jit(solution)/shard_map/ppermute | solution.py:98
  91.3 3.1 %collective-permute-start.25 = (bf16[64,768]{1,0:T(8,128)(2,1)S(1)}, bf16[64,768]{1,0:T(8,128)(2,1)S(1)}, u32[]{:S(2)}, u32[]{:S(2)}) collective-permute-start(bf16[64,768]{1,0:T(8,128)(2,1)S(1)} %collective-permute-done.23), channel_id=1, source_target_pairs={{0,4},{4,0},{8,12},{12,8},{1,5},{5,1},{9,13},{13,9},{2,6},{6,2},{1... | collective-permute-start | bytes 294920 | tf_op jit(solution)/shard_map/ppermute | solution.py:84
  94.3 4.3 %collective-permute-start.22 = (bf16[128,768]{1,0:T(8,128)(2,1)S(1)}, bf16[128,768]{1,0:T(8,128)(2,1)S(1)}, u32[]{:S(2)}, u32[]{:S(2)}) collective-permute-start(bf16[128,768]{1,0:T(8,128)(2,1)S(1)} %collective-permute-done.18.refs_1_), channel_id=1, source_target_pairs={{0,1},{1,0},{2,3},{3,2},{4,5},{5,4},{6,7},{7,6},{8,9},{9,8},{10,11... | collective-permute-start | bytes 589832 | tf_op jit(solution)/shard_map/ppermute | solution.py:84
  98.6 0.1 collective-permute-start.21
  98.7 0.4 collective-permute-start.24
  99.1 1.7 %collective-permute-start.20 = (bf16[64,768]{1,0:T(8,128)(2,1)S(1)}, bf16[64,768]{1,0:T(8,128)(2,1)S(1)}, u32[]{:S(2)}, u32[]{:S(2)}) collective-permute-start(bf16[64,768]{1,0:T(8,128)(2,1)S(1)} %collective-permute-done.19.refs_2_), channel_id=1, source_target_pairs={{0,4},{4,0},{8,12},{12,8},{1,5},{5,1},{9,13},{13,9},{2,6},{6,2},{1... | collective-permute-start | bytes 294920 | tf_op jit(solution)/shard_map/ppermute | solution.py:84
  100.9 1.2 %collective-permute-start.26 = (bf16[64,768]{1,0:T(8,128)(2,1)S(1)}, bf16[64,768]{1,0:T(8,128)(2,1)S(1)}, u32[]{:S(2)}, u32[]{:S(2)}) collective-permute-start(bf16[64,768]{1,0:T(8,128)(2,1)S(1)} %collective-permute-done.25), channel_id=1, source_target_pairs={{0,1},{1,0},{2,3},{3,2},{4,5},{5,4},{6,7},{7,6},{8,9},{9,8},{10,11... | collective-permute-start | bytes 294920 | tf_op jit(solution)/shard_map/ppermute | solution.py:84
  102.1 2.6 %collective-permute-done.20.refs_3_ = bf16[64,768]{1,0:T(8,128)(2,1)S(1)} collective-permute-done((bf16[64,768]{1,0:T(8,128)(2,1)S(1)}, bf16[64,768]{1,0:T(8,128)(2,1)S(1)}, u32[]{:S(2)}, u32[]{:S(2)}) %collective-permute-start.20) | collective-permute-done | bytes 98336 | tf_op jit(solution)/shard_map/ppermute | solution.py:84
  104.7 1.7 %shard_map.102 = (bf16[64,2048]{1,0:T(8,128)(2,1)}, f32[64,1024]{1,0:T(8,128)}, bf16[64,1024]{1,0:T(8,128)(2,1)}, f32[64,2048]{1,0:T(8,128)}) custom-call(s32[4]{0:T(128)S(1)} %pad_add_fusion.idx, bf16[128,768]{1,0:T(8,128)(2,1)S(1)} %collective-permute-done.17.refs_0_, bf16[128,768]{1,0:T(8,128)(2,1)S(1)} %collective-permute-done.18.refs_1_, ...), custom_call_target="tpu_custom_call" | custom-call | tf_op jit(solution)/shard_map/pallas_call | solution.py:465
  (17 shorter events, 0.1 us)
Async XLA Ops:
  2.4 2.6 %collective-permute-start = (bf16[144,3072]{1,0:T(8,128)(2,1)S(1)}, bf16[144,3072]{1,0:T(8,128)(2,1)S(1)}, u32[]{:S(2)}, u32[]{:S(2)}) collective-permute-start(bf16[144,3072]{1,0:T(8,128)(2,1)S(1)} %shard_map.93), channel_id=1, source_target_pairs={{0,1},{1,0},{2,3},{3,2},{4,5},{5,4},{6,7},{7,6},{8,9},{9,8},{10,11... | collective-permute-start | bytes 2654216 | tf_op jit(solution)/shard_map/ppermute | solution.py:84
  6.6 13.7 %collective-permute-start.1 = (bf16[128,512]{1,0:T(8,128)(2,1)S(1)}, bf16[128,512]{1,0:T(8,128)(2,1)S(1)}, u32[]{:S(2)}, u32[]{:S(2)}) collective-permute-start(bf16[128,512]{1,0:T(8,128)(2,1)S(1)} %get-tuple-element.28), channel_id=1, source_target_pairs={{0,8},{1,11},{2,10},{3,9},{4,12},{5,15},{6,14},{7,13},{8,0},{9,3},... | collective-permute-start | bytes 393224 | tf_op jit(solution)/shard_map/ppermute | solution.py:98
  10.6 11.1 %collective-permute-start.2 = (bf16[128,512]{1,0:T(8,128)(2,1)S(1)}, bf16[128,512]{1,0:T(8,128)(2,1)S(1)}, u32[]{:S(2)}, u32[]{:S(2)}) collective-permute-start(bf16[128,512]{1,0:T(8,128)(2,1)S(1)} %get-tuple-element.29), channel_id=1, source_target_pairs={{0,12},{1,15},{2,14},{3,13},{4,8},{5,11},{6,10},{7,9},{8,4},{9,7},... | collective-permute-start | bytes 393224 | tf_op jit(solution)/shard_map/ppermute | solution.py:98
  11.9 10.5 %collective-permute-start.3 = (bf16[128,512]{1,0:T(8,128)(2,1)S(1)}, bf16[128,512]{1,0:T(8,128)(2,1)S(1)}, u32[]{:S(2)}, u32[]{:S(2)}) collective-permute-start(bf16[128,512]{1,0:T(8,128)(2,1)S(1)} %get-tuple-element.30), channel_id=1, source_target_pairs={{0,4},{1,7},{2,6},{3,5},{4,0},{5,3},{6,2},{7,1},{8,12},{9,15},{10,... | collective-permute-start | bytes 393224 | tf_op jit(solution)/shard_map/ppermute | solution.py:98
  12.2 13.7 %collective-permute-start.4 = (bf16[128,512]{1,0:T(8,128)(2,1)S(1)}, bf16[128,512]{1,0:T(8,128)(2,1)S(1)}, u32[]{:S(2)}, u32[]{:S(2)}) collective-permute-start(bf16[128,512]{1,0:T(8,128)(2,1)S(1)} %get-tuple-element.31), channel_id=1, source_target_pairs={{0,0},{1,3},{2,2},{3,1},{4,4},{5,7},{6,6},{7,5},{8,8},{9,11},{10,1... | collective-permute-start | bytes 393224 | tf_op jit(solution)/shard_map/ppermute | solution.py:98
  14.5 25.4 %collective-permute-start.7 = (bf16[128,1024]{1,0:T(8,128)(2,1)S(1)}, bf16[128,1024]{1,0:T(8,128)(2,1)S(1)}, u32[]{:S(2)}, u32[]{:S(2)}) collective-permute-start(bf16[128,1024]{1,0:T(8,128)(2,1)S(1)} %get-tuple-element.35), channel_id=1, source_target_pairs={{0,8},{1,27},{2,26},{3,9},{4,12},{5,31},{6,30},{7,13},{8,0},{9,19}... | collective-permute-start | bytes 786440 | tf_op jit(solution)/shard_map/ppermute | solution.py:98
  20.2 19.7 %collective-permute-start.8 = (bf16[128,1024]{1,0:T(8,128)(2,1)S(1)}, bf16[128,1024]{1,0:T(8,128)(2,1)S(1)}, u32[]{:S(2)}, u32[]{:S(2)}) collective-permute-start(bf16[128,1024]{1,0:T(8,128)(2,1)S(1)} %get-tuple-element.36), channel_id=1, source_target_pairs={{0,4},{1,23},{2,22},{3,5},{4,0},{5,19},{6,18},{7,1},{8,12},{9,31},... | collective-permute-start | bytes 786440 | tf_op jit(solution)/shard_map/ppermute | solution.py:98
  21.7 18.3 %collective-permute-start.9 = (bf16[128,1024]{1,0:T(8,128)(2,1)S(1)}, bf16[128,1024]{1,0:T(8,128)(2,1)S(1)}, u32[]{:S(2)}, u32[]{:S(2)}) collective-permute-start(bf16[128,1024]{1,0:T(8,128)(2,1)S(1)} %get-tuple-element.37), channel_id=1, source_target_pairs={{0,0},{1,19},{2,18},{3,1},{4,4},{5,23},{6,22},{7,5},{8,8},{9,27},{... | collective-permute-start | bytes 786440 | tf_op jit(solution)/shard_map/ppermute | solution.py:98
  22.4 17.6 %collective-permute-start.10 = (bf16[128,1024]{1,0:T(8,128)(2,1)S(1)}, bf16[128,1024]{1,0:T(8,128)(2,1)S(1)}, u32[]{:S(2)}, u32[]{:S(2)}) collective-permute-start(bf16[128,1024]{1,0:T(8,128)(2,1)S(1)} %get-tuple-element.38), channel_id=1, source_target_pairs={{0,12},{1,31},{2,30},{3,13},{4,8},{5,27},{6,26},{7,9},{8,4},{9,23}... | collective-permute-start | bytes 786440 | tf_op jit(solution)/shard_map/ppermute | solution.py:98
  25.9 1.8 %collective-permute-start.6 = (bf16[192,512]{1,0:T(8,128)(2,1)S(1)}, bf16[192,512]{1,0:T(8,128)(2,1)S(1)}, u32[]{:S(2)}, u32[]{:S(2)}) collective-permute-start(bf16[192,512]{1,0:T(8,128)(2,1)S(1)} %get-tuple-element.34), channel_id=1, source_target_pairs={{0,0},{1,3},{2,2},{3,1},{4,4},{5,7},{6,6},{7,5},{8,8},{9,11},{10,1... | collective-permute-start | bytes 589832 | tf_op jit(solution)/shard_map/ppermute | solution.py:98
  42.0 1.7 %collective-permute-start.11 = (bf16[656,128]{1,0:T(8,128)(2,1)S(1)}, bf16[656,128]{1,0:T(8,128)(2,1)S(1)}, u32[]{:S(2)}, u32[]{:S(2)}) collective-permute-start(bf16[656,128]{1,0:T(8,128)(2,1)S(1)} %get-tuple-element.41), channel_id=1, source_target_pairs={{0,1},{1,0},{2,3},{3,2},{4,5},{5,4},{6,7},{7,6},{8,9},{9,8},{10,11... | collective-permute-start | bytes 503816 | tf_op jit(solution)/shard_map/ppermute | solution.py:84
  42.1 1.6 %collective-permute-start.5 = (bf16[528,128]{1,0:T(8,128)(2,1)S(1)}, bf16[528,128]{1,0:T(8,128)(2,1)S(1)}, u32[]{:S(2)}, u32[]{:S(2)}) collective-permute-start(bf16[528,128]{1,0:T(8,128)(2,1)S(1)} %get-tuple-element.33), channel_id=1, source_target_pairs={{0,1},{1,0},{2,3},{3,2},{4,5},{5,4},{6,7},{7,6},{8,9},{9,8},{10,11... | collective-permute-start | bytes 405512 | tf_op jit(solution)/shard_map/ppermute | solution.py:84
  44.3 11.4 %collective-permute-start.12 = (bf16[592,128]{1,0:T(8,128)(2,1)S(1)}, bf16[592,128]{1,0:T(8,128)(2,1)S(1)}, u32[]{:S(2)}, u32[]{:S(2)}) collective-permute-start(bf16[592,128]{1,0:T(8,128)(2,1)S(1)} %get-tuple-element.43), channel_id=1, source_target_pairs={{0,4},{4,0},{8,12},{12,8},{1,5},{5,1},{9,13},{13,9},{2,6},{6,2},{1... | collective-permute-start | bytes 454664 | tf_op jit(solution)/shard_map/ppermute | solution.py:84
  55.7 10.5 %collective-permute-start.13 = (bf16[592,128]{1,0:T(8,128)(2,1)S(1)}, bf16[592,128]{1,0:T(8,128)(2,1)S(1)}, u32[]{:S(2)}, u32[]{:S(2)}) collective-permute-start(bf16[592,128]{1,0:T(8,128)(2,1)S(1)} %shard_map.99.mine), channel_id=1, source_target_pairs={{0,8},{4,12},{8,0},{12,4},{1,9},{5,13},{9,1},{13,5},{2,10},{6,14},... | collective-permute-start | bytes 454664 | tf_op jit(solution)/shard_map/ppermute | solution.py:84
  66.3 5.8 %collective-permute-start.14 = (bf16[592,128]{1,0:T(8,128)(2,1)S(1)}, bf16[592,128]{1,0:T(8,128)(2,1)S(1)}, u32[]{:S(2)}, u32[]{:S(2)}) collective-permute-start(bf16[592,128]{1,0:T(8,128)(2,1)S(1)} %shard_map.100.refs_0_), channel_id=1, source_target_pairs={{0,4},{4,0},{8,12},{12,8},{1,5},{5,1},{9,13},{13,9},{2,6},{6,2},{1... | collective-permute-start | bytes 454664 | tf_op jit(solution)/shard_map/ppermute | solution.py:84
  66.4 5.7 %collective-permute-start.15 = (bf16[592,128]{1,0:T(8,128)(2,1)S(1)}, bf16[592,128]{1,0:T(8,128)(2,1)S(1)}, u32[]{:S(2)}, u32[]{:S(2)}) collective-permute-start(bf16[592,128]{1,0:T(8,128)(2,1)S(1)} %shard_map.100.refs_0_), channel_id=1, source_target_pairs={{0,1},{1,0},{2,3},{3,2},{4,5},{5,4},{6,7},{7,6},{8,9},{9,8},{10,11... | collective-permute-start | bytes 454664 | tf_op jit(solution)/shard_map/ppermute | solution.py:84
  72.1 1.4 %collective-permute-start.16 = (bf16[592,128]{1,0:T(8,128)(2,1)S(1)}, bf16[592,128]{1,0:T(8,128)(2,1)S(1)}, u32[]{:S(2)}, u32[]{:S(2)}) collective-permute-start(bf16[592,128]{1,0:T(8,128)(2,1)S(1)} %collective-permute-done.14.refs_1_), channel_id=1, source_target_pairs={{0,1},{1,0},{2,3},{3,2},{4,5},{5,4},{6,7},{7,6},{8,9},{9,8},{10,11... | collective-permute-start | bytes 454664 | tf_op jit(solution)/shard_map/ppermute | solution.py:84
  84.6 9.8 %collective-permute-start.18 = (bf16[128,768]{1,0:T(8,128)(2,1)S(1)}, bf16[128,768]{1,0:T(8,128)(2,1)S(1)}, u32[]{:S(2)}, u32[]{:S(2)}) collective-permute-start(bf16[128,768]{1,0:T(8,128)(2,1)S(1)} %get-tuple-element.45), channel_id=1, source_target_pairs={{0,4},{1,7},{2,6},{3,5},{4,0},{5,3},{6,2},{7,1},{8,12},{9,15},{10,... | collective-permute-start | bytes 589832 | tf_op jit(solution)/shard_map/ppermute | solution.py:98
  84.9 13.7 %collective-permute-start.17 = (bf16[128,768]{1,0:T(8,128)(2,1)S(1)}, bf16[128,768]{1,0:T(8,128)(2,1)S(1)}, u32[]{:S(2)}, u32[]{:S(2)}) collective-permute-start(bf16[128,768]{1,0:T(8,128)(2,1)S(1)} %get-tuple-element.45), channel_id=1, source_target_pairs={{0,0},{1,3},{2,2},{3,1},{4,4},{5,7},{6,6},{7,5},{8,8},{9,11},{10,1... | collective-permute-start | bytes 589832 | tf_op jit(solution)/shard_map/ppermute | solution.py:98
  85.6 5.7 %collective-permute-start.23 = (bf16[64,768]{1,0:T(8,128)(2,1)S(1)}, bf16[64,768]{1,0:T(8,128)(2,1)S(1)}, u32[]{:S(2)}, u32[]{:S(2)}) collective-permute-start(bf16[64,768]{1,0:T(8,128)(2,1)S(1)} %get-tuple-element.47), channel_id=1, source_target_pairs={{0,8},{1,11},{2,10},{3,9},{4,12},{5,15},{6,14},{7,13},{8,0},{9,3},... | collective-permute-start | bytes 294920 | tf_op jit(solution)/shard_map/ppermute | solution.py:98
  88.1 11.0 %collective-permute-start.19 = (bf16[64,768]{1,0:T(8,128)(2,1)S(1)}, bf16[64,768]{1,0:T(8,128)(2,1)S(1)}, u32[]{:S(2)}, u32[]{:S(2)}) collective-permute-start(bf16[64,768]{1,0:T(8,128)(2,1)S(1)} %get-tuple-element.46), channel_id=1, source_target_pairs={{0,8},{1,11},{2,10},{3,9},{4,12},{5,15},{6,14},{7,13},{8,0},{9,3},... | collective-permute-start | bytes 294920 | tf_op jit(solution)/shard_map/ppermute | solution.py:98
  91.3 9.6 %collective-permute-start.25 = (bf16[64,768]{1,0:T(8,128)(2,1)S(1)}, bf16[64,768]{1,0:T(8,128)(2,1)S(1)}, u32[]{:S(2)}, u32[]{:S(2)}) collective-permute-start(bf16[64,768]{1,0:T(8,128)(2,1)S(1)} %collective-permute-done.23), channel_id=1, source_target_pairs={{0,4},{4,0},{8,12},{12,8},{1,5},{5,1},{9,13},{13,9},{2,6},{6,2},{1... | collective-permute-start | bytes 294920 | tf_op jit(solution)/shard_map/ppermute | solution.py:84
  94.3 10.3 %collective-permute-start.22 = (bf16[128,768]{1,0:T(8,128)(2,1)S(1)}, bf16[128,768]{1,0:T(8,128)(2,1)S(1)}, u32[]{:S(2)}, u32[]{:S(2)}) collective-permute-start(bf16[128,768]{1,0:T(8,128)(2,1)S(1)} %collective-permute-done.18.refs_1_), channel_id=1, source_target_pairs={{0,1},{1,0},{2,3},{3,2},{4,5},{5,4},{6,7},{7,6},{8,9},{9,8},{10,11... | collective-permute-start | bytes 589832 | tf_op jit(solution)/shard_map/ppermute | solution.py:84
  98.6 6.1 %collective-permute-start.21 = (bf16[128,768]{1,0:T(8,128)(2,1)S(1)}, bf16[128,768]{1,0:T(8,128)(2,1)S(1)}, u32[]{:S(2)}, u32[]{:S(2)}) collective-permute-start(bf16[128,768]{1,0:T(8,128)(2,1)S(1)} %collective-permute-done.17.refs_0_), channel_id=1, source_target_pairs={{0,1},{1,0},{2,3},{3,2},{4,5},{5,4},{6,7},{7,6},{8,9},{9,8},{10,11... | collective-permute-start | bytes 589832 | tf_op jit(solution)/shard_map/ppermute | solution.py:84
  98.7 6.0 %collective-permute-start.24 = (bf16[64,768]{1,0:T(8,128)(2,1)S(1)}, bf16[64,768]{1,0:T(8,128)(2,1)S(1)}, u32[]{:S(2)}, u32[]{:S(2)}) collective-permute-start(bf16[64,768]{1,0:T(8,128)(2,1)S(1)} %collective-permute-done.23), channel_id=1, source_target_pairs={{0,1},{1,0},{2,3},{3,2},{4,5},{5,4},{6,7},{7,6},{8,9},{9,8},{10,11... | collective-permute-start | bytes 294920 | tf_op jit(solution)/shard_map/ppermute | solution.py:84
  99.1 5.5 %collective-permute-start.20 = (bf16[64,768]{1,0:T(8,128)(2,1)S(1)}, bf16[64,768]{1,0:T(8,128)(2,1)S(1)}, u32[]{:S(2)}, u32[]{:S(2)}) collective-permute-start(bf16[64,768]{1,0:T(8,128)(2,1)S(1)} %collective-permute-done.19.refs_2_), channel_id=1, source_target_pairs={{0,4},{4,0},{8,12},{12,8},{1,5},{5,1},{9,13},{13,9},{2,6},{6,2},{1... | collective-permute-start | bytes 294920 | tf_op jit(solution)/shard_map/ppermute | solution.py:84
  100.9 3.8 %collective-permute-start.26 = (bf16[64,768]{1,0:T(8,128)(2,1)S(1)}, bf16[64,768]{1,0:T(8,128)(2,1)S(1)}, u32[]{:S(2)}, u32[]{:S(2)}) collective-permute-start(bf16[64,768]{1,0:T(8,128)(2,1)S(1)} %collective-permute-done.25), channel_id=1, source_target_pairs={{0,1},{1,0},{2,3},{3,2},{4,5},{5,4},{6,7},{7,6},{8,9},{9,8},{10,11... | collective-permute-start | bytes 294920 | tf_op jit(solution)/shard_map/ppermute | solution.py:84

commit v8 on v7

--- a/solution.py
+++ b/solution.py
@@ -10,8 +10,8 @@
 RANK = 64
 POWER = 2
 BLK = 128
-THIN_ORDER = (2, 3, 1, 0)
-WIDE_ORDER = (2, 1, 0, 3)
+THIN_ORDER = (2, 1, 0, 3)
+WIDE_ORDER = (2, 3, 1, 0)
 
 precise = lax.Precision.HIGHEST
 f32 = jnp.float32

time: 107 us -> 106 us (level)
  starting transfers between devices: 42.1 us -> 38.9 us
  waiting for transfers between devices: 41.7 us -> 44.7 us
    ppermute x13, waiting for transfers between devices: 17.8 us -> 20.7 us  [routed(): return lax.ppermute(value, ('section', 'dp', 'tensor'), pairs)]
    ppermute x14, starting transfers between devices: 22.7 us -> 21.1 us  [swap(): return lax.ppermute(value, axis, [(i, i ^ bit) for i in range(count)])]
    ppermute x13, starting transfers between devices: 19.4 us -> 17.8 us  [routed(): return lax.ppermute(value, ('section', 'dp', 'tensor'), pairs)]
  transfers between devices with their start and end apart: 27 -> 27, of which waited for: 10 -> 11; matrix products, arithmetic and copies ran while one was open for 0% -> 0% of each run, Pallas kernels for 3% -> 3%
where the time goes in v8:
time: 106 us
  waiting for transfers between devices  44.7 us (42%)
  starting transfers between devices  38.9 us (37%)
  Pallas kernels  21.6 us (20%)
    ppermute x14, waiting for transfers between devices, swap(): return lax.ppermute(value, axis, [(i, i ^ bit) for i in range(count)])  24.1 us
    pallas_call x10, Pallas kernels, call(): pl.pallas_call(kernel, out_shape=out_shapes, in_specs=spaces, out_specs=j...  21.6 us
    ppermute x14, starting transfers between devices, swap(): return lax.ppermute(value, axis, [(i, i ^ bit) for i in range(count)])  21.1 us
    ppermute x13, waiting for transfers between devices, routed(): return lax.ppermute(value, ('section', 'dp', 'tensor'), pairs)  20.7 us
    ppermute x13, starting transfers between devices, routed(): return lax.ppermute(value, ('section', 'dp', 'tensor'), pairs)  17.8 us
  transfers between devices with their start and end apart: 27, of which 11 were waited for; matrix products, arithmetic and copies ran while one was open for 0% of the time, Pallas kernels for 3%

profile of v8, /device:TPU:0, one launch (start us, length us, event | category | flops | bytes accessed | tf_op | source)
XLA Modules:
  0.0 106.1 jit_solution(7305463276105690095)
XLA Ops:
  0.6 0.1 pad_add_fusion.idx
  0.7 1.7 %shard_map.93 = bf16[144,3072]{1,0:T(8,128)(2,1)S(1)} custom-call(s32[4]{0:T(128)S(1)} %pad_add_fusion.idx, bf16[128,2048]{1,0:T(8,128)(2,1)} %bitcast.14, bf16[128,1024]{1,0:T(8,128)(2,1)} %bitcast.18, bf16[128,1024]{1,0:T(8,128)(2,1)} %bitcast.20, bf16[128,2048]{1,0:T(8,128)(2,1)} %bitcast.16, bf16[64,1024]{1,0:T(8,128)(2,1)} %bitcast.24, ...), custom_call_target="tpu_custom_call" | custom-call | tf_op jit(solution)/shard_map/pallas_call | solution.py:465
  2.4 0.5 collective-permute-start
  3.0 2.1 %collective-permute-done.got = bf16[144,3072]{1,0:T(8,128)(2,1)S(1)} collective-permute-done((bf16[144,3072]{1,0:T(8,128)(2,1)S(1)}, bf16[144,3072]{1,0:T(8,128)(2,1)S(1)}, u32[]{:S(2)}, u32[]{:S(2)}) %collective-permute-start) | collective-permute-done | bytes 884768 | tf_op jit(solution)/shard_map/ppermute | solution.py:84
  5.0 1.5 %shard_map.94 = (bf16[128,512]{1,0:T(8,128)(2,1)S(1)}, bf16[128,512]{1,0:T(8,128)(2,1)S(1)}, bf16[128,512]{1,0:T(8,128)(2,1)S(1)}, bf16[128,512]{1,0:T(8,128)(2,1)S(1)}) custom-call(s32[4]{0:T(128)S(1)} %pad_add_fusion.idx, bf16[128,1024]{1,0:T(8,128)(2,1)} %bitcast.19, bf16[128,1024]{1,0:T(8,128)(2,1)} %bitcast.21, ...), custom_call_target="tpu_custom_call" | custom-call | tf_op jit(solution)/shard_map/pallas_call | solution.py:465
  6.6 4.0 %collective-permute-start.1 = (bf16[128,512]{1,0:T(8,128)(2,1)S(1)}, bf16[128,512]{1,0:T(8,128)(2,1)S(1)}, u32[]{:S(2)}, u32[]{:S(2)}) collective-permute-start(bf16[128,512]{1,0:T(8,128)(2,1)S(1)} %get-tuple-element.28), channel_id=1, source_target_pairs={{0,8},{1,11},{2,10},{3,9},{4,12},{5,15},{6,14},{7,13},{8,0},{9,3},... | collective-permute-start | bytes 393224 | tf_op jit(solution)/shard_map/ppermute | solution.py:98
  10.6 1.6 %collective-permute-start.2 = (bf16[128,512]{1,0:T(8,128)(2,1)S(1)}, bf16[128,512]{1,0:T(8,128)(2,1)S(1)}, u32[]{:S(2)}, u32[]{:S(2)}) collective-permute-start(bf16[128,512]{1,0:T(8,128)(2,1)S(1)} %get-tuple-element.29), channel_id=1, source_target_pairs={{0,4},{1,7},{2,6},{3,5},{4,0},{5,3},{6,2},{7,1},{8,12},{9,15},{10,... | collective-permute-start | bytes 393224 | tf_op jit(solution)/shard_map/ppermute | solution.py:98
  12.1 0.7 collective-permute-start.3
  12.8 0.1 collective-permute-start.4
  12.9 1.7 %shard_map.96 = (bf16[128,1024]{1,0:T(8,128)(2,1)S(1)}, bf16[128,1024]{1,0:T(8,128)(2,1)S(1)}, bf16[128,1024]{1,0:T(8,128)(2,1)S(1)}, bf16[128,1024]{1,0:T(8,128)(2,1)S(1)}, bf16[192,512]{1,0:T(8,128)(2,1)S(1)}) custom-call(s32[4]{0:T(128)S(1)} %pad_add_fusion.idx, bf16[128,2048]{1,0:T(8,128)(2,1)} %bitcast.15, bf16[128,2048]{1,0:T(8,128)(2,1)} %bitcast.17, ...), custom_call_target="tpu_custom_call" | custom-call | tf_op jit(solution)/shard_map/pallas_call | solution.py:465
  14.6 1.9 %collective-permute-start.7 = (bf16[128,1024]{1,0:T(8,128)(2,1)S(1)}, bf16[128,1024]{1,0:T(8,128)(2,1)S(1)}, u32[]{:S(2)}, u32[]{:S(2)}) collective-permute-start(bf16[128,1024]{1,0:T(8,128)(2,1)S(1)} %get-tuple-element.35), channel_id=1, source_target_pairs={{0,8},{1,27},{2,26},{3,9},{4,12},{5,31},{6,30},{7,13},{8,0},{9,19}... | collective-permute-start | bytes 786440 | tf_op jit(solution)/shard_map/ppermute | solution.py:98
  16.6 0.9 collective-permute-done.1.refs_0_
  17.4 4.2 %collective-permute-start.8 = (bf16[128,1024]{1,0:T(8,128)(2,1)S(1)}, bf16[128,1024]{1,0:T(8,128)(2,1)S(1)}, u32[]{:S(2)}, u32[]{:S(2)}) collective-permute-start(bf16[128,1024]{1,0:T(8,128)(2,1)S(1)} %get-tuple-element.36), channel_id=1, source_target_pairs={{0,12},{1,31},{2,30},{3,13},{4,8},{5,27},{6,26},{7,9},{8,4},{9,23}... | collective-permute-start | bytes 786440 | tf_op jit(solution)/shard_map/ppermute | solution.py:98
  21.6 0.0 collective-permute-done.2.refs_1_
  21.6 0.0 collective-permute-start.9
  21.6 0.0 collective-permute-done.3.refs_2_
  21.6 0.7 collective-permute-start.10
  22.3 0.7 collective-permute-start.6
  23.0 1.1 %shard_map.95 = (bf16[512,512]{1,0:T(8,128)(2,1)S(1)}, bf16[528,128]{1,0:T(8,128)(2,1)S(1)}, bf16[528,128]{1,0:T(8,128)(2,1)S(1)}) custom-call(s32[4]{0:T(128)S(1)} %pad_add_fusion.idx, bf16[128,512]{1,0:T(8,128)(2,1)S(1)} %collective-permute-done.1.refs_0_, bf16[128,512]{1,0:T(8,128)(2,1)S(1)} %collective-permute-done.2.refs_1_, ...), custom_call_target="tpu_custom_call" | custom-call | tf_op jit(solution)/shard_map/pallas_call | solution.py:465
  24.2 15.4 %collective-permute-done.7.refs_1_ = bf16[128,1024]{1,0:T(8,128)(2,1)S(1)} collective-permute-done((bf16[128,1024]{1,0:T(8,128)(2,1)S(1)}, bf16[128,1024]{1,0:T(8,128)(2,1)S(1)}, u32[]{:S(2)}, u32[]{:S(2)}) %collective-permute-start.7) | collective-permute-done | bytes 262176 | tf_op jit(solution)/shard_map/ppermute | solution.py:98
  39.6 1.6 %collective-permute-done.9.refs_3_ = bf16[128,1024]{1,0:T(8,128)(2,1)S(1)} collective-permute-done((bf16[128,1024]{1,0:T(8,128)(2,1)S(1)}, bf16[128,1024]{1,0:T(8,128)(2,1)S(1)}, u32[]{:S(2)}, u32[]{:S(2)}) %collective-permute-start.9) | collective-permute-done | bytes 262176 | tf_op jit(solution)/shard_map/ppermute | solution.py:98
  41.3 2.0 %shard_map.97 = (bf16[512,1024]{1,0:T(8,128)(2,1)S(1)}, bf16[656,128]{1,0:T(8,128)(2,1)S(1)}, bf16[656,128]{1,0:T(8,128)(2,1)S(1)}) custom-call(s32[4]{0:T(128)S(1)} %pad_add_fusion.idx, bf16[192,512]{1,0:T(8,128)(2,1)S(1)} %collective-permute-done.6.refs_0_, bf16[128,1024]{1,0:T(8,128)(2,1)S(1)} %collective-permute-done.7.refs_1_, ...), custom_call_target="tpu_custom_call" | custom-call | tf_op jit(solution)/shard_map/pallas_call | solution.py:465
  43.3 2.0 %collective-permute-start.11 = (bf16[656,128]{1,0:T(8,128)(2,1)S(1)}, bf16[656,128]{1,0:T(8,128)(2,1)S(1)}, u32[]{:S(2)}, u32[]{:S(2)}) collective-permute-start(bf16[656,128]{1,0:T(8,128)(2,1)S(1)} %get-tuple-element.41), channel_id=1, source_target_pairs={{0,1},{1,0},{2,3},{3,2},{4,5},{5,4},{6,7},{7,6},{8,9},{9,8},{10,11... | collective-permute-start | bytes 503816 | tf_op jit(solution)/shard_map/ppermute | solution.py:84
  45.2 0.1 collective-permute-start.5
  45.3 1.3 %collective-permute-done.5.thin_got = bf16[528,128]{1,0:T(8,128)(2,1)S(1)} collective-permute-done((bf16[528,128]{1,0:T(8,128)(2,1)S(1)}, bf16[528,128]{1,0:T(8,128)(2,1)S(1)}, u32[]{:S(2)}, u32[]{:S(2)}) %collective-permute-start.5) | collective-permute-done | bytes 135200 | tf_op jit(solution)/shard_map/ppermute | solution.py:84
  46.6 0.7 shard_map.98
  47.3 4.0 %collective-permute-start.12 = (bf16[592,128]{1,0:T(8,128)(2,1)S(1)}, bf16[592,128]{1,0:T(8,128)(2,1)S(1)}, u32[]{:S(2)}, u32[]{:S(2)}) collective-permute-start(bf16[592,128]{1,0:T(8,128)(2,1)S(1)} %get-tuple-element.43), channel_id=1, source_target_pairs={{0,4},{4,0},{8,12},{12,8},{1,5},{5,1},{9,13},{13,9},{2,6},{6,2},{1... | collective-permute-start | bytes 454664 | tf_op jit(solution)/shard_map/ppermute | solution.py:84
  51.2 4.4 %collective-permute-done.12.got = bf16[592,128]{1,0:T(8,128)(2,1)S(1)} collective-permute-done((bf16[592,128]{1,0:T(8,128)(2,1)S(1)}, bf16[592,128]{1,0:T(8,128)(2,1)S(1)}, u32[]{:S(2)}, u32[]{:S(2)}) %collective-permute-start.12) | collective-permute-done | bytes 151584 | tf_op jit(solution)/shard_map/ppermute | solution.py:84
  55.7 3.7 %collective-permute-start.13 = (bf16[592,128]{1,0:T(8,128)(2,1)S(1)}, bf16[592,128]{1,0:T(8,128)(2,1)S(1)}, u32[]{:S(2)}, u32[]{:S(2)}) collective-permute-start(bf16[592,128]{1,0:T(8,128)(2,1)S(1)} %shard_map.99.mine), channel_id=1, source_target_pairs={{0,8},{4,12},{8,0},{12,4},{1,9},{5,13},{9,1},{13,5},{2,10},{6,14},... | collective-permute-start | bytes 454664 | tf_op jit(solution)/shard_map/ppermute | solution.py:84
  59.4 6.8 %collective-permute-done.13.got = bf16[592,128]{1,0:T(8,128)(2,1)S(1)} collective-permute-done((bf16[592,128]{1,0:T(8,128)(2,1)S(1)}, bf16[592,128]{1,0:T(8,128)(2,1)S(1)}, u32[]{:S(2)}, u32[]{:S(2)}) %collective-permute-start.13) | collective-permute-done | bytes 151584 | tf_op jit(solution)/shard_map/ppermute | solution.py:84
  66.2 0.1 collective-permute-start.14
  66.3 0.1 collective-permute-start.15
  66.4 5.6 %collective-permute-done.14.refs_1_ = bf16[592,128]{1,0:T(8,128)(2,1)S(1)} collective-permute-done((bf16[592,128]{1,0:T(8,128)(2,1)S(1)}, bf16[592,128]{1,0:T(8,128)(2,1)S(1)}, u32[]{:S(2)}, u32[]{:S(2)}) %collective-permute-start.14) | collective-permute-done | bytes 151584 | tf_op jit(solution)/shard_map/ppermute | solution.py:84
  72.0 1.4 %collective-permute-done.16.refs_3_ = bf16[592,128]{1,0:T(8,128)(2,1)S(1)} collective-permute-done((bf16[592,128]{1,0:T(8,128)(2,1)S(1)}, bf16[592,128]{1,0:T(8,128)(2,1)S(1)}, u32[]{:S(2)}, u32[]{:S(2)}) %collective-permute-start.16) | collective-permute-done | bytes 151584 | tf_op jit(solution)/shard_map/ppermute | solution.py:84
  73.4 11.1 %shard_map.101 = (bf16[128,768]{1,0:T(8,128)(2,1)S(1)}, bf16[64,768]{1,0:T(8,128)(2,1)S(1)}, bf16[64,768]{1,0:T(8,128)(2,1)S(1)}) custom-call(s32[4]{0:T(128)S(1)} %pad_add_fusion.idx, bf16[592,128]{1,0:T(8,128)(2,1)S(1)} %shard_map.100.refs_0_, bf16[592,128]{1,0:T(8,128)(2,1)S(1)} %collective-permute-done.14.refs_1_, ...), custom_call_target="tpu_custom_call" | custom-call | tf_op jit(solution)/shard_map/pallas_call | solution.py:465
  84.5 0.4 collective-permute-start.18
  84.8 0.7 collective-permute-start.17
  85.5 2.5 %collective-permute-start.23 = (bf16[64,768]{1,0:T(8,128)(2,1)S(1)}, bf16[64,768]{1,0:T(8,128)(2,1)S(1)}, u32[]{:S(2)}, u32[]{:S(2)}) collective-permute-start(bf16[64,768]{1,0:T(8,128)(2,1)S(1)} %get-tuple-element.47), channel_id=1, source_target_pairs={{0,8},{1,11},{2,10},{3,9},{4,12},{5,15},{6,14},{7,13},{8,0},{9,3},... | collective-permute-start | bytes 294920 | tf_op jit(solution)/shard_map/ppermute | solution.py:98
  88.0 0.5 collective-permute-start.19
  88.5 2.7 %collective-permute-done.23 = bf16[64,768]{1,0:T(8,128)(2,1)S(1)} collective-permute-done((bf16[64,768]{1,0:T(8,128)(2,1)S(1)}, bf16[64,768]{1,0:T(8,128)(2,1)S(1)}, u32[]{:S(2)}, u32[]{:S(2)}) %collective-permute-start.23) | collective-permute-done | bytes 98336 | tf_op jit(solution)/shard_map/ppermute | solution.py:98
  91.2 3.1 %collective-permute-start.25 = (bf16[64,768]{1,0:T(8,128)(2,1)S(1)}, bf16[64,768]{1,0:T(8,128)(2,1)S(1)}, u32[]{:S(2)}, u32[]{:S(2)}) collective-permute-start(bf16[64,768]{1,0:T(8,128)(2,1)S(1)} %collective-permute-done.23), channel_id=1, source_target_pairs={{0,4},{4,0},{8,12},{12,8},{1,5},{5,1},{9,13},{13,9},{2,6},{6,2},{1... | collective-permute-start | bytes 294920 | tf_op jit(solution)/shard_map/ppermute | solution.py:84
  94.3 4.2 %collective-permute-start.22 = (bf16[128,768]{1,0:T(8,128)(2,1)S(1)}, bf16[128,768]{1,0:T(8,128)(2,1)S(1)}, u32[]{:S(2)}, u32[]{:S(2)}) collective-permute-start(bf16[128,768]{1,0:T(8,128)(2,1)S(1)} %collective-permute-done.18.refs_1_), channel_id=1, source_target_pairs={{0,1},{1,0},{2,3},{3,2},{4,5},{5,4},{6,7},{7,6},{8,9},{9,8},{10,11... | collective-permute-start | bytes 589832 | tf_op jit(solution)/shard_map/ppermute | solution.py:84
  98.4 0.1 collective-permute-start.21
  98.5 0.4 collective-permute-start.24
  98.9 1.7 %collective-permute-start.20 = (bf16[64,768]{1,0:T(8,128)(2,1)S(1)}, bf16[64,768]{1,0:T(8,128)(2,1)S(1)}, u32[]{:S(2)}, u32[]{:S(2)}) collective-permute-start(bf16[64,768]{1,0:T(8,128)(2,1)S(1)} %collective-permute-done.19.refs_2_), channel_id=1, source_target_pairs={{0,4},{4,0},{8,12},{12,8},{1,5},{5,1},{9,13},{13,9},{2,6},{6,2},{1... | collective-permute-start | bytes 294920 | tf_op jit(solution)/shard_map/ppermute | solution.py:84
  100.7 1.2 %collective-permute-start.26 = (bf16[64,768]{1,0:T(8,128)(2,1)S(1)}, bf16[64,768]{1,0:T(8,128)(2,1)S(1)}, u32[]{:S(2)}, u32[]{:S(2)}) collective-permute-start(bf16[64,768]{1,0:T(8,128)(2,1)S(1)} %collective-permute-done.25), channel_id=1, source_target_pairs={{0,1},{1,0},{2,3},{3,2},{4,5},{5,4},{6,7},{7,6},{8,9},{9,8},{10,11... | collective-permute-start | bytes 294920 | tf_op jit(solution)/shard_map/ppermute | solution.py:84
  101.9 2.5 %collective-permute-done.20.refs_3_ = bf16[64,768]{1,0:T(8,128)(2,1)S(1)} collective-permute-done((bf16[64,768]{1,0:T(8,128)(2,1)S(1)}, bf16[64,768]{1,0:T(8,128)(2,1)S(1)}, u32[]{:S(2)}, u32[]{:S(2)}) %collective-permute-start.20) | collective-permute-done | bytes 98336 | tf_op jit(solution)/shard_map/ppermute | solution.py:84
  104.4 1.7 %shard_map.102 = (bf16[64,2048]{1,0:T(8,128)(2,1)}, f32[64,1024]{1,0:T(8,128)}, bf16[64,1024]{1,0:T(8,128)(2,1)}, f32[64,2048]{1,0:T(8,128)}) custom-call(s32[4]{0:T(128)S(1)} %pad_add_fusion.idx, bf16[128,768]{1,0:T(8,128)(2,1)S(1)} %collective-permute-done.17.refs_0_, bf16[128,768]{1,0:T(8,128)(2,1)S(1)} %collective-permute-done.18.refs_1_, ...), custom_call_target="tpu_custom_call" | custom-call | tf_op jit(solution)/shard_map/pallas_call | solution.py:465
  (17 shorter events, 0.1 us)
Async XLA Ops:
  2.4 2.6 %collective-permute-start = (bf16[144,3072]{1,0:T(8,128)(2,1)S(1)}, bf16[144,3072]{1,0:T(8,128)(2,1)S(1)}, u32[]{:S(2)}, u32[]{:S(2)}) collective-permute-start(bf16[144,3072]{1,0:T(8,128)(2,1)S(1)} %shard_map.93), channel_id=1, source_target_pairs={{0,1},{1,0},{2,3},{3,2},{4,5},{5,4},{6,7},{7,6},{8,9},{9,8},{10,11... | collective-permute-start | bytes 2654216 | tf_op jit(solution)/shard_map/ppermute | solution.py:84
  6.6 10.9 %collective-permute-start.1 = (bf16[128,512]{1,0:T(8,128)(2,1)S(1)}, bf16[128,512]{1,0:T(8,128)(2,1)S(1)}, u32[]{:S(2)}, u32[]{:S(2)}) collective-permute-start(bf16[128,512]{1,0:T(8,128)(2,1)S(1)} %get-tuple-element.28), channel_id=1, source_target_pairs={{0,8},{1,11},{2,10},{3,9},{4,12},{5,15},{6,14},{7,13},{8,0},{9,3},... | collective-permute-start | bytes 393224 | tf_op jit(solution)/shard_map/ppermute | solution.py:98
  10.6 11.0 %collective-permute-start.2 = (bf16[128,512]{1,0:T(8,128)(2,1)S(1)}, bf16[128,512]{1,0:T(8,128)(2,1)S(1)}, u32[]{:S(2)}, u32[]{:S(2)}) collective-permute-start(bf16[128,512]{1,0:T(8,128)(2,1)S(1)} %get-tuple-element.29), channel_id=1, source_target_pairs={{0,4},{1,7},{2,6},{3,5},{4,0},{5,3},{6,2},{7,1},{8,12},{9,15},{10,... | collective-permute-start | bytes 393224 | tf_op jit(solution)/shard_map/ppermute | solution.py:98
  12.1 9.5 %collective-permute-start.3 = (bf16[128,512]{1,0:T(8,128)(2,1)S(1)}, bf16[128,512]{1,0:T(8,128)(2,1)S(1)}, u32[]{:S(2)}, u32[]{:S(2)}) collective-permute-start(bf16[128,512]{1,0:T(8,128)(2,1)S(1)} %get-tuple-element.30), channel_id=1, source_target_pairs={{0,0},{1,3},{2,2},{3,1},{4,4},{5,7},{6,6},{7,5},{8,8},{9,11},{10,1... | collective-permute-start | bytes 393224 | tf_op jit(solution)/shard_map/ppermute | solution.py:98
  12.8 9.5 %collective-permute-start.4 = (bf16[128,512]{1,0:T(8,128)(2,1)S(1)}, bf16[128,512]{1,0:T(8,128)(2,1)S(1)}, u32[]{:S(2)}, u32[]{:S(2)}) collective-permute-start(bf16[128,512]{1,0:T(8,128)(2,1)S(1)} %get-tuple-element.31), channel_id=1, source_target_pairs={{0,12},{1,15},{2,14},{3,13},{4,8},{5,11},{6,10},{7,9},{8,4},{9,7},... | collective-permute-start | bytes 393224 | tf_op jit(solution)/shard_map/ppermute | solution.py:98
  14.6 25.0 %collective-permute-start.7 = (bf16[128,1024]{1,0:T(8,128)(2,1)S(1)}, bf16[128,1024]{1,0:T(8,128)(2,1)S(1)}, u32[]{:S(2)}, u32[]{:S(2)}) collective-permute-start(bf16[128,1024]{1,0:T(8,128)(2,1)S(1)} %get-tuple-element.35), channel_id=1, source_target_pairs={{0,8},{1,27},{2,26},{3,9},{4,12},{5,31},{6,30},{7,13},{8,0},{9,19}... | collective-permute-start | bytes 786440 | tf_op jit(solution)/shard_map/ppermute | solution.py:98
  17.4 22.2 %collective-permute-start.8 = (bf16[128,1024]{1,0:T(8,128)(2,1)S(1)}, bf16[128,1024]{1,0:T(8,128)(2,1)S(1)}, u32[]{:S(2)}, u32[]{:S(2)}) collective-permute-start(bf16[128,1024]{1,0:T(8,128)(2,1)S(1)} %get-tuple-element.36), channel_id=1, source_target_pairs={{0,12},{1,31},{2,30},{3,13},{4,8},{5,27},{6,26},{7,9},{8,4},{9,23}... | collective-permute-start | bytes 786440 | tf_op jit(solution)/shard_map/ppermute | solution.py:98
  21.6 19.6 %collective-permute-start.9 = (bf16[128,1024]{1,0:T(8,128)(2,1)S(1)}, bf16[128,1024]{1,0:T(8,128)(2,1)S(1)}, u32[]{:S(2)}, u32[]{:S(2)}) collective-permute-start(bf16[128,1024]{1,0:T(8,128)(2,1)S(1)} %get-tuple-element.37), channel_id=1, source_target_pairs={{0,4},{1,23},{2,22},{3,5},{4,0},{5,19},{6,18},{7,1},{8,12},{9,31},... | collective-permute-start | bytes 786440 | tf_op jit(solution)/shard_map/ppermute | solution.py:98
  21.6 19.6 %collective-permute-start.10 = (bf16[128,1024]{1,0:T(8,128)(2,1)S(1)}, bf16[128,1024]{1,0:T(8,128)(2,1)S(1)}, u32[]{:S(2)}, u32[]{:S(2)}) collective-permute-start(bf16[128,1024]{1,0:T(8,128)(2,1)S(1)} %get-tuple-element.38), channel_id=1, source_target_pairs={{0,0},{1,19},{2,18},{3,1},{4,4},{5,23},{6,22},{7,5},{8,8},{9,27},{... | collective-permute-start | bytes 786440 | tf_op jit(solution)/shard_map/ppermute | solution.py:98
  22.3 1.8 %collective-permute-start.6 = (bf16[192,512]{1,0:T(8,128)(2,1)S(1)}, bf16[192,512]{1,0:T(8,128)(2,1)S(1)}, u32[]{:S(2)}, u32[]{:S(2)}) collective-permute-start(bf16[192,512]{1,0:T(8,128)(2,1)S(1)} %get-tuple-element.34), channel_id=1, source_target_pairs={{0,0},{1,3},{2,2},{3,1},{4,4},{5,7},{6,6},{7,5},{8,8},{9,11},{10,1... | collective-permute-start | bytes 589832 | tf_op jit(solution)/shard_map/ppermute | solution.py:98
  43.3 3.3 %collective-permute-start.11 = (bf16[656,128]{1,0:T(8,128)(2,1)S(1)}, bf16[656,128]{1,0:T(8,128)(2,1)S(1)}, u32[]{:S(2)}, u32[]{:S(2)}) collective-permute-start(bf16[656,128]{1,0:T(8,128)(2,1)S(1)} %get-tuple-element.41), channel_id=1, source_target_pairs={{0,1},{1,0},{2,3},{3,2},{4,5},{5,4},{6,7},{7,6},{8,9},{9,8},{10,11... | collective-permute-start | bytes 503816 | tf_op jit(solution)/shard_map/ppermute | solution.py:84
  45.2 1.4 %collective-permute-start.5 = (bf16[528,128]{1,0:T(8,128)(2,1)S(1)}, bf16[528,128]{1,0:T(8,128)(2,1)S(1)}, u32[]{:S(2)}, u32[]{:S(2)}) collective-permute-start(bf16[528,128]{1,0:T(8,128)(2,1)S(1)} %get-tuple-element.33), channel_id=1, source_target_pairs={{0,1},{1,0},{2,3},{3,2},{4,5},{5,4},{6,7},{7,6},{8,9},{9,8},{10,11... | collective-permute-start | bytes 405512 | tf_op jit(solution)/shard_map/ppermute | solution.py:84
  47.3 8.3 %collective-permute-start.12 = (bf16[592,128]{1,0:T(8,128)(2,1)S(1)}, bf16[592,128]{1,0:T(8,128)(2,1)S(1)}, u32[]{:S(2)}, u32[]{:S(2)}) collective-permute-start(bf16[592,128]{1,0:T(8,128)(2,1)S(1)} %get-tuple-element.43), channel_id=1, source_target_pairs={{0,4},{4,0},{8,12},{12,8},{1,5},{5,1},{9,13},{13,9},{2,6},{6,2},{1... | collective-permute-start | bytes 454664 | tf_op jit(solution)/shard_map/ppermute | solution.py:84
  55.7 10.5 %collective-permute-start.13 = (bf16[592,128]{1,0:T(8,128)(2,1)S(1)}, bf16[592,128]{1,0:T(8,128)(2,1)S(1)}, u32[]{:S(2)}, u32[]{:S(2)}) collective-permute-start(bf16[592,128]{1,0:T(8,128)(2,1)S(1)} %shard_map.99.mine), channel_id=1, source_target_pairs={{0,8},{4,12},{8,0},{12,4},{1,9},{5,13},{9,1},{13,5},{2,10},{6,14},... | collective-permute-start | bytes 454664 | tf_op jit(solution)/shard_map/ppermute | solution.py:84
  66.2 5.8 %collective-permute-start.14 = (bf16[592,128]{1,0:T(8,128)(2,1)S(1)}, bf16[592,128]{1,0:T(8,128)(2,1)S(1)}, u32[]{:S(2)}, u32[]{:S(2)}) collective-permute-start(bf16[592,128]{1,0:T(8,128)(2,1)S(1)} %shard_map.100.refs_0_), channel_id=1, source_target_pairs={{0,4},{4,0},{8,12},{12,8},{1,5},{5,1},{9,13},{13,9},{2,6},{6,2},{1... | collective-permute-start | bytes 454664 | tf_op jit(solution)/shard_map/ppermute | solution.py:84
  66.3 5.7 %collective-permute-start.15 = (bf16[592,128]{1,0:T(8,128)(2,1)S(1)}, bf16[592,128]{1,0:T(8,128)(2,1)S(1)}, u32[]{:S(2)}, u32[]{:S(2)}) collective-permute-start(bf16[592,128]{1,0:T(8,128)(2,1)S(1)} %shard_map.100.refs_0_), channel_id=1, source_target_pairs={{0,1},{1,0},{2,3},{3,2},{4,5},{5,4},{6,7},{7,6},{8,9},{9,8},{10,11... | collective-permute-start | bytes 454664 | tf_op jit(solution)/shard_map/ppermute | solution.py:84
  72.0 1.4 %collective-permute-start.16 = (bf16[592,128]{1,0:T(8,128)(2,1)S(1)}, bf16[592,128]{1,0:T(8,128)(2,1)S(1)}, u32[]{:S(2)}, u32[]{:S(2)}) collective-permute-start(bf16[592,128]{1,0:T(8,128)(2,1)S(1)} %collective-permute-done.14.refs_1_), channel_id=1, source_target_pairs={{0,1},{1,0},{2,3},{3,2},{4,5},{5,4},{6,7},{7,6},{8,9},{9,8},{10,11... | collective-permute-start | bytes 454664 | tf_op jit(solution)/shard_map/ppermute | solution.py:84
  84.5 9.8 %collective-permute-start.18 = (bf16[128,768]{1,0:T(8,128)(2,1)S(1)}, bf16[128,768]{1,0:T(8,128)(2,1)S(1)}, u32[]{:S(2)}, u32[]{:S(2)}) collective-permute-start(bf16[128,768]{1,0:T(8,128)(2,1)S(1)} %get-tuple-element.45), channel_id=1, source_target_pairs={{0,4},{1,7},{2,6},{3,5},{4,0},{5,3},{6,2},{7,1},{8,12},{9,15},{10,... | collective-permute-start | bytes 589832 | tf_op jit(solution)/shard_map/ppermute | solution.py:98
  84.8 13.6 %collective-permute-start.17 = (bf16[128,768]{1,0:T(8,128)(2,1)S(1)}, bf16[128,768]{1,0:T(8,128)(2,1)S(1)}, u32[]{:S(2)}, u32[]{:S(2)}) collective-permute-start(bf16[128,768]{1,0:T(8,128)(2,1)S(1)} %get-tuple-element.45), channel_id=1, source_target_pairs={{0,0},{1,3},{2,2},{3,1},{4,4},{5,7},{6,6},{7,5},{8,8},{9,11},{10,1... | collective-permute-start | bytes 589832 | tf_op jit(solution)/shard_map/ppermute | solution.py:98
  85.5 5.7 %collective-permute-start.23 = (bf16[64,768]{1,0:T(8,128)(2,1)S(1)}, bf16[64,768]{1,0:T(8,128)(2,1)S(1)}, u32[]{:S(2)}, u32[]{:S(2)}) collective-permute-start(bf16[64,768]{1,0:T(8,128)(2,1)S(1)} %get-tuple-element.47), channel_id=1, source_target_pairs={{0,8},{1,11},{2,10},{3,9},{4,12},{5,15},{6,14},{7,13},{8,0},{9,3},... | collective-permute-start | bytes 294920 | tf_op jit(solution)/shard_map/ppermute | solution.py:98
  88.0 10.9 %collective-permute-start.19 = (bf16[64,768]{1,0:T(8,128)(2,1)S(1)}, bf16[64,768]{1,0:T(8,128)(2,1)S(1)}, u32[]{:S(2)}, u32[]{:S(2)}) collective-permute-start(bf16[64,768]{1,0:T(8,128)(2,1)S(1)} %get-tuple-element.46), channel_id=1, source_target_pairs={{0,8},{1,11},{2,10},{3,9},{4,12},{5,15},{6,14},{7,13},{8,0},{9,3},... | collective-permute-start | bytes 294920 | tf_op jit(solution)/shard_map/ppermute | solution.py:98
  91.2 9.5 %collective-permute-start.25 = (bf16[64,768]{1,0:T(8,128)(2,1)S(1)}, bf16[64,768]{1,0:T(8,128)(2,1)S(1)}, u32[]{:S(2)}, u32[]{:S(2)}) collective-permute-start(bf16[64,768]{1,0:T(8,128)(2,1)S(1)} %collective-permute-done.23), channel_id=1, source_target_pairs={{0,4},{4,0},{8,12},{12,8},{1,5},{5,1},{9,13},{13,9},{2,6},{6,2},{1... | collective-permute-start | bytes 294920 | tf_op jit(solution)/shard_map/ppermute | solution.py:84
  94.3 10.2 %collective-permute-start.22 = (bf16[128,768]{1,0:T(8,128)(2,1)S(1)}, bf16[128,768]{1,0:T(8,128)(2,1)S(1)}, u32[]{:S(2)}, u32[]{:S(2)}) collective-permute-start(bf16[128,768]{1,0:T(8,128)(2,1)S(1)} %collective-permute-done.18.refs_1_), channel_id=1, source_target_pairs={{0,1},{1,0},{2,3},{3,2},{4,5},{5,4},{6,7},{7,6},{8,9},{9,8},{10,11... | collective-permute-start | bytes 589832 | tf_op jit(solution)/shard_map/ppermute | solution.py:84
  98.4 6.0 %collective-permute-start.21 = (bf16[128,768]{1,0:T(8,128)(2,1)S(1)}, bf16[128,768]{1,0:T(8,128)(2,1)S(1)}, u32[]{:S(2)}, u32[]{:S(2)}) collective-permute-start(bf16[128,768]{1,0:T(8,128)(2,1)S(1)} %collective-permute-done.17.refs_0_), channel_id=1, source_target_pairs={{0,1},{1,0},{2,3},{3,2},{4,5},{5,4},{6,7},{7,6},{8,9},{9,8},{10,11... | collective-permute-start | bytes 589832 | tf_op jit(solution)/shard_map/ppermute | solution.py:84
  98.5 5.9 %collective-permute-start.24 = (bf16[64,768]{1,0:T(8,128)(2,1)S(1)}, bf16[64,768]{1,0:T(8,128)(2,1)S(1)}, u32[]{:S(2)}, u32[]{:S(2)}) collective-permute-start(bf16[64,768]{1,0:T(8,128)(2,1)S(1)} %collective-permute-done.23), channel_id=1, source_target_pairs={{0,1},{1,0},{2,3},{3,2},{4,5},{5,4},{6,7},{7,6},{8,9},{9,8},{10,11... | collective-permute-start | bytes 294920 | tf_op jit(solution)/shard_map/ppermute | solution.py:84
  98.9 5.5 %collective-permute-start.20 = (bf16[64,768]{1,0:T(8,128)(2,1)S(1)}, bf16[64,768]{1,0:T(8,128)(2,1)S(1)}, u32[]{:S(2)}, u32[]{:S(2)}) collective-permute-start(bf16[64,768]{1,0:T(8,128)(2,1)S(1)} %collective-permute-done.19.refs_2_), channel_id=1, source_target_pairs={{0,4},{4,0},{8,12},{12,8},{1,5},{5,1},{9,13},{13,9},{2,6},{6,2},{1... | collective-permute-start | bytes 294920 | tf_op jit(solution)/shard_map/ppermute | solution.py:84
  100.7 3.7 %collective-permute-start.26 = (bf16[64,768]{1,0:T(8,128)(2,1)S(1)}, bf16[64,768]{1,0:T(8,128)(2,1)S(1)}, u32[]{:S(2)}, u32[]{:S(2)}) collective-permute-start(bf16[64,768]{1,0:T(8,128)(2,1)S(1)} %collective-permute-done.25), channel_id=1, source_target_pairs={{0,1},{1,0},{2,3},{3,2},{4,5},{5,4},{6,7},{7,6},{8,9},{9,8},{10,11... | collective-permute-start | bytes 294920 | tf_op jit(solution)/shard_map/ppermute | solution.py:84

commit v9 on v8

--- a/solution.py
+++ b/solution.py
@@ -110,33 +110,34 @@
         c.wait()
 
 
-def give_kernel(dps, idx, norm, grad, attn, hand, sk_q, sk_o, give, sems):
+def give_thin_kernel(idx, grad, attn, give, sems):
+    for which, ref in ((0, attn), (1, grad)):
+
+        @pl.when(idx[3] == which)
+        def _():
+            move([(ref, give)], sems)
+
+
+def give_wide_kernel(dps, idx, norm, hand, sk_q, sk_o, give, sems):
     z, kind = idx[0], idx[3]
-    wide, narrow = norm.shape[1], grad.shape[1]
-    big_w, small_w = wide // dps, narrow // dps
-    rows = RANK // dps
-
-    def sketch(ref, width, start):
+    rows, fold = RANK // dps, give.shape[1] // dps
+    small_w = sk_q.shape[1] // dps
+
+    def sketch(ref, width):
         part = ref.at[:, pl.ds(pl.multiple_of(z * width, width), width)]
         return [
-            (
-                part.at[i * rows : (i + 1) * rows],
-                give.at[BLK:, i * (big_w + small_w) + start : i * (big_w + small_w) + start + width],
-            )
+            (part.at[i * rows : (i + 1) * rows], give.at[BLK:, i * fold : i * fold + width])
             for i in range(dps)
         ]
 
-    give[BLK:, :] = jnp.zeros((rows, wide + narrow), bf16)
-
     @pl.when(kind == 0)
     def _():
-        pairs = [(hand, give.at[:BLK, :wide]), (attn, give.at[:BLK, wide:])]
-        move(pairs + sketch(sk_o, big_w, 0), sems)
+        move([(hand, give.at[:BLK])] + sketch(sk_o, fold), sems)
 
     @pl.when(kind == 1)
     def _():
-        pairs = [(norm, give.at[:BLK, :wide]), (grad, give.at[:BLK, wide:])]
-        move(pairs + sketch(sk_q, small_w, big_w), sems)
+        give[BLK:, :] = jnp.zeros((rows, give.shape[1]), bf16)
+        move([(norm, give.at[:BLK])] + sketch(sk_q, small_w), sems)
 
 
 def merge_kernel(dps, kind, fill, pairs, sems):
@@ -158,12 +159,11 @@
 def merge_thin_kernel(dps, idx, grad, attn, got, *refs):
     z, kind, smalls, sems = idx[0], idx[3], refs[:dps], refs[-1]
     small_w = smalls[0].shape[1] // 2
-    wide = got.shape[1] - grad.shape[1]
 
     def fill(_):
         for d in range(dps):
-            at = pl.multiple_of(wide + (z ^ d) * small_w, small_w)
-            smalls[d][:, small_w:] = got[:BLK, pl.ds(at, small_w)]
+            at = pl.multiple_of((z ^ d) * small_w, small_w)
+            smalls[d][:, small_w:] = got[:, pl.ds(at, small_w)]
 
     def keep(ref):
         return [
@@ -183,10 +183,14 @@
             at = pl.multiple_of((z ^ d) * big_w, big_w)
             bigs[d][:, big_w:] = got[:BLK, pl.ds(at, big_w)]
         for i in range(dps):
-            at = i * (big_w + small_w)
-            sk[RANK + i * rows : RANK + (i + 1) * rows, :] = got[BLK:, at : at + big_w]
-            below = slice(2 * RANK + i * rows, 2 * RANK + (i + 1) * rows)
-            sk[below, small_w:] = got[BLK:, at + big_w : at + big_w + small_w]
+            part = got[BLK:, i * big_w : (i + 1) * big_w]
+            one, two = RANK + i * rows, 2 * RANK + i * rows
+            if which == 0:
+                sk[one : one + rows, :] = jnp.zeros_like(part)
+                sk[two : two + rows, small_w:] = part[:, :small_w]
+            else:
+                sk[one : one + rows, :] = part
+                sk[two : two + rows, small_w:] = jnp.zeros_like(part[:, :small_w])
         if which == 0:
             sk[:RANK, :] = jnp.zeros((RANK, big_w), bf16)
         else:
@@ -491,21 +495,31 @@
         for v in (norm_in, query_grad, attn_out, handed, sketch_q, sketch_o)
     )
 
+    give_thin = call(
+        give_thin_kernel,
+        shape(BLK, narrow),
+        (idx, grad, attn),
+        [pltpu.SemaphoreType.DMA((1,))],
+        [SMEM] + [hbm] * 2,
+    )
+    after, give_thin = lax.optimization_barrier((idx, give_thin))
+    got_thin = swap(give_thin, "tensor", 1)
     give = call(
-        functools.partial(give_kernel, dps),
-        shape(BLK + RANK // dps, wide + narrow),
-        (idx, norm, grad, attn, hand, sk_q, sk_o),
-        [pltpu.SemaphoreType.DMA((2 + dps,))],
-        [SMEM] + [hbm] * 6,
-    )
-    got = swap(give, "tensor", 1)
+        functools.partial(give_wide_kernel, dps),
+        shape(BLK + RANK // dps, wide),
+        (after, norm, hand, sk_q, sk_o),
+        [pltpu.SemaphoreType.DMA((1 + dps,))],
+        [SMEM] + [hbm] * 4,
+    )
+    give, got_thin = lax.optimization_barrier((give, got_thin))
     smalls = call(
         functools.partial(merge_thin_kernel, dps),
         [shape(BLK, 2 * small_w)] * dps,
-        (idx, grad, attn, got),
+        (idx, grad, attn, got_thin),
         [pltpu.SemaphoreType.DMA((dps,))],
         [SMEM, hbm, hbm, VMEM],
     )
+    got = swap(give, "tensor", 1)
     packed = call(
         functools.partial(merge_wide_kernel, dps),
         [shape(BLK, 2 * big_w)] * dps + [shape(3 * RANK, 2 * small_w)],
@@ -563,6 +577,7 @@
     leaves, stays = routed(leaves, sizes, 2, False), routed(stays, sizes, 2, False)
     near, here = routed(whole, sizes, 1, False), routed(whole, sizes, 0, False)
     leaves_on, stays_on = swap(leaves, "dp", 1), swap(stays, "dp", 1)
+    here, near, stays = lax.optimization_barrier((here, near, stays))
     mine = (here, near, stays, stays_on)
     theirs = [swap(v, "tensor", 1) for v in (here, near, leaves, leaves_on)]
     outs = call(

time: 106 us -> 107 us (level)
  starting transfers between devices: 38.9 us -> 34.6 us
  waiting for transfers between devices: 44.7 us -> 48 us
  Pallas kernels: 21.6 us -> 23 us
    ppermute x13, waiting for transfers between devices: 20.7 us -> 25 us  [routed(): return lax.ppermute(value, ('section', 'dp', 'tensor'), pairs)]
    ppermute x14 -> x15, starting transfers between devices: 21.1 us -> 16.8 us  [swap(): return lax.ppermute(value, axis, [(i, i ^ bit) for i in range(count)])]
    pallas_call x10 -> x11, Pallas kernels: 21.6 us -> 23 us  [call(): pl.pallas_call(kernel, out_shape=out_shapes, in_specs=spaces, out_specs=j...]
    ppermute x14 -> x15, waiting for transfers between devices: 24.1 us -> 22.9 us  [swap(): return lax.ppermute(value, axis, [(i, i ^ bit) for i in range(count)])]
  transfers between devices with their start and end apart: 27 -> 28, of which waited for: 11 -> 11; matrix products, arithmetic and copies ran while one was open for 0% -> 0% of each run, Pallas kernels for 3% -> 6%
where the time goes in v9:
time: 107 us
  waiting for transfers between devices  48 us (45%)
  starting transfers between devices  34.6 us (32%)
  Pallas kernels  23 us (21%)
    ppermute x13, waiting for transfers between devices, routed(): return lax.ppermute(value, ('section', 'dp', 'tensor'), pairs)  25 us
    pallas_call x11, Pallas kernels, call(): pl.pallas_call(kernel, out_shape=out_shapes, in_specs=spaces, out_specs=j...  23 us
    ppermute x15, waiting for transfers between devices, swap(): return lax.ppermute(value, axis, [(i, i ^ bit) for i in range(count)])  22.9 us
    ppermute x13, starting transfers between devices, routed(): return lax.ppermute(value, ('section', 'dp', 'tensor'), pairs)  17.8 us
    ppermute x15, starting transfers between devices, swap(): return lax.ppermute(value, axis, [(i, i ^ bit) for i in range(count)])  16.8 us
  transfers between devices with their start and end apart: 28, of which 11 were waited for; matrix products, arithmetic and copies ran while one was open for 0% of the time, Pallas kernels for 6%

profile of v9, /device:TPU:0, one launch (start us, length us, event | category | flops | bytes accessed | tf_op | source)
XLA Modules:
  0.0 106.5 jit_solution(3040650630087508970)
XLA Ops:
  0.6 0.1 pad_add_fusion.idx
  0.7 1.5 %shard_map.93 = bf16[128,1024]{1,0:T(8,128)(2,1)S(1)} custom-call(s32[4]{0:T(128)S(1)} %pad_add_fusion.idx, bf16[128,1024]{1,0:T(8,128)(2,1)} %bitcast.20, bf16[128,1024]{1,0:T(8,128)(2,1)} %bitcast.22), custom_call_target="tpu_custom_call" | custom-call | tf_op jit(solution)/shard_map/pallas_call | solution.py:469
  2.2 0.5 collective-permute-start
  2.8 1.6 %shard_map.94 = bf16[144,2048]{1,0:T(8,128)(2,1)S(1)} custom-call(s32[4]{0:T(128)S(1)} %pad_add_fusion.idx, bf16[128,2048]{1,0:T(8,128)(2,1)} %bitcast.14, bf16[128,2048]{1,0:T(8,128)(2,1)} %bitcast.16, bf16[64,1024]{1,0:T(8,128)(2,1)} %bitcast.24, bf16[64,2048]{1,0:T(8,128)(2,1)} %bitcast.18), custom_call_target="tpu_custom_call" | custom-call | tf_op jit(solution)/shard_map/pallas_call | solution.py:469
  4.4 0.1 collective-permute-start.6
  4.5 1.5 %shard_map.95 = (bf16[128,512]{1,0:T(8,128)(2,1)S(1)}, bf16[128,512]{1,0:T(8,128)(2,1)S(1)}, bf16[128,512]{1,0:T(8,128)(2,1)S(1)}, bf16[128,512]{1,0:T(8,128)(2,1)S(1)}) custom-call(s32[4]{0:T(128)S(1)} %pad_add_fusion.idx, bf16[128,1024]{1,0:T(8,128)(2,1)} %bitcast.21, bf16[128,1024]{1,0:T(8,128)(2,1)} %bitcast.23, ...), custom_call_target="tpu_custom_call" | custom-call | tf_op jit(solution)/shard_map/pallas_call | solution.py:469
  6.1 4.1 %collective-permute-start.1 = (bf16[128,512]{1,0:T(8,128)(2,1)S(1)}, bf16[128,512]{1,0:T(8,128)(2,1)S(1)}, u32[]{:S(2)}, u32[]{:S(2)}) collective-permute-start(bf16[128,512]{1,0:T(8,128)(2,1)S(1)} %get-tuple-element.38), channel_id=1, source_target_pairs={{0,8},{1,11},{2,10},{3,9},{4,12},{5,15},{6,14},{7,13},{8,0},{9,3},... | collective-permute-start | bytes 393224 | tf_op jit(solution)/shard_map/ppermute | solution.py:98
  10.2 1.6 %collective-permute-start.2 = (bf16[128,512]{1,0:T(8,128)(2,1)S(1)}, bf16[128,512]{1,0:T(8,128)(2,1)S(1)}, u32[]{:S(2)}, u32[]{:S(2)}) collective-permute-start(bf16[128,512]{1,0:T(8,128)(2,1)S(1)} %get-tuple-element.39), channel_id=1, source_target_pairs={{0,4},{1,7},{2,6},{3,5},{4,0},{5,3},{6,2},{7,1},{8,12},{9,15},{10,... | collective-permute-start | bytes 393224 | tf_op jit(solution)/shard_map/ppermute | solution.py:98
  11.8 0.7 collective-permute-start.3
  12.4 0.1 collective-permute-start.4
  12.5 0.0 collective-permute-done.6.got
  12.5 1.7 %shard_map.97 = (bf16[128,1024]{1,0:T(8,128)(2,1)S(1)}, bf16[128,1024]{1,0:T(8,128)(2,1)S(1)}, bf16[128,1024]{1,0:T(8,128)(2,1)S(1)}, bf16[128,1024]{1,0:T(8,128)(2,1)S(1)}, bf16[192,512]{1,0:T(8,128)(2,1)S(1)}) custom-call(s32[4]{0:T(128)S(1)} %pad_add_fusion.idx, bf16[128,2048]{1,0:T(8,128)(2,1)} %bitcast.15, bf16[128,2048]{1,0:T(8,128)(2,1)} %bitcast.17, ...), custom_call_target="tpu_custom_call" | custom-call | tf_op jit(solution)/shard_map/pallas_call | solution.py:469
  14.2 1.9 %collective-permute-start.8 = (bf16[128,1024]{1,0:T(8,128)(2,1)S(1)}, bf16[128,1024]{1,0:T(8,128)(2,1)S(1)}, u32[]{:S(2)}, u32[]{:S(2)}) collective-permute-start(bf16[128,1024]{1,0:T(8,128)(2,1)S(1)} %get-tuple-element.46), channel_id=1, source_target_pairs={{0,8},{1,27},{2,26},{3,9},{4,12},{5,31},{6,30},{7,13},{8,0},{9,19}... | collective-permute-start | bytes 786440 | tf_op jit(solution)/shard_map/ppermute | solution.py:98
  16.2 0.9 collective-permute-done.1.refs_0_
  17.1 4.1 %collective-permute-start.9 = (bf16[128,1024]{1,0:T(8,128)(2,1)S(1)}, bf16[128,1024]{1,0:T(8,128)(2,1)S(1)}, u32[]{:S(2)}, u32[]{:S(2)}) collective-permute-start(bf16[128,1024]{1,0:T(8,128)(2,1)S(1)} %get-tuple-element.47), channel_id=1, source_target_pairs={{0,12},{1,31},{2,30},{3,13},{4,8},{5,27},{6,26},{7,9},{8,4},{9,23}... | collective-permute-start | bytes 786440 | tf_op jit(solution)/shard_map/ppermute | solution.py:98
  21.2 0.7 collective-permute-start.11
  21.9 0.7 collective-permute-start.7
  22.5 1.1 %shard_map.96 = (bf16[512,512]{1,0:T(8,128)(2,1)S(1)}, bf16[528,128]{1,0:T(8,128)(2,1)S(1)}, bf16[528,128]{1,0:T(8,128)(2,1)S(1)}) custom-call(s32[4]{0:T(128)S(1)} %pad_add_fusion.idx, bf16[128,512]{1,0:T(8,128)(2,1)S(1)} %collective-permute-done.1.refs_0_, bf16[128,512]{1,0:T(8,128)(2,1)S(1)} %collective-permute-done.2.refs_1_, ...), custom_call_target="tpu_custom_call" | custom-call | tf_op jit(solution)/shard_map/pallas_call | solution.py:469
  23.7 15.7 %collective-permute-done.8.refs_1_ = bf16[128,1024]{1,0:T(8,128)(2,1)S(1)} collective-permute-done((bf16[128,1024]{1,0:T(8,128)(2,1)S(1)}, bf16[128,1024]{1,0:T(8,128)(2,1)S(1)}, u32[]{:S(2)}, u32[]{:S(2)}) %collective-permute-start.8) | collective-permute-done | bytes 262176 | tf_op jit(solution)/shard_map/ppermute | solution.py:98
  39.4 1.4 %collective-permute-done.10.refs_3_ = bf16[128,1024]{1,0:T(8,128)(2,1)S(1)} collective-permute-done((bf16[128,1024]{1,0:T(8,128)(2,1)S(1)}, bf16[128,1024]{1,0:T(8,128)(2,1)S(1)}, u32[]{:S(2)}, u32[]{:S(2)}) %collective-permute-start.10) | collective-permute-done | bytes 262176 | tf_op jit(solution)/shard_map/ppermute | solution.py:98
  40.9 2.0 %shard_map.98 = (bf16[512,1024]{1,0:T(8,128)(2,1)S(1)}, bf16[656,128]{1,0:T(8,128)(2,1)S(1)}, bf16[656,128]{1,0:T(8,128)(2,1)S(1)}) custom-call(s32[4]{0:T(128)S(1)} %pad_add_fusion.idx, bf16[192,512]{1,0:T(8,128)(2,1)S(1)} %collective-permute-done.7.refs_0_, bf16[128,1024]{1,0:T(8,128)(2,1)S(1)} %collective-permute-done.8.refs_1_, ...), custom_call_target="tpu_custom_call" | custom-call | tf_op jit(solution)/shard_map/pallas_call | solution.py:469
  42.9 1.8 %collective-permute-start.12 = (bf16[656,128]{1,0:T(8,128)(2,1)S(1)}, bf16[656,128]{1,0:T(8,128)(2,1)S(1)}, u32[]{:S(2)}, u32[]{:S(2)}) collective-permute-start(bf16[656,128]{1,0:T(8,128)(2,1)S(1)} %get-tuple-element.52), channel_id=1, source_target_pairs={{0,1},{1,0},{2,3},{3,2},{4,5},{5,4},{6,7},{7,6},{8,9},{9,8},{10,11... | collective-permute-start | bytes 503816 | tf_op jit(solution)/shard_map/ppermute | solution.py:84
  44.7 0.1 collective-permute-start.5
  44.8 1.3 %collective-permute-done.5.thin_got = bf16[528,128]{1,0:T(8,128)(2,1)S(1)} collective-permute-done((bf16[528,128]{1,0:T(8,128)(2,1)S(1)}, bf16[528,128]{1,0:T(8,128)(2,1)S(1)}, u32[]{:S(2)}, u32[]{:S(2)}) %collective-permute-start.5) | collective-permute-done | bytes 135200 | tf_op jit(solution)/shard_map/ppermute | solution.py:84
  46.1 0.7 shard_map.99
  46.8 4.1 %collective-permute-start.13 = (bf16[592,128]{1,0:T(8,128)(2,1)S(1)}, bf16[592,128]{1,0:T(8,128)(2,1)S(1)}, u32[]{:S(2)}, u32[]{:S(2)}) collective-permute-start(bf16[592,128]{1,0:T(8,128)(2,1)S(1)} %get-tuple-element.54), channel_id=1, source_target_pairs={{0,4},{4,0},{8,12},{12,8},{1,5},{5,1},{9,13},{13,9},{2,6},{6,2},{1... | collective-permute-start | bytes 454664 | tf_op jit(solution)/shard_map/ppermute | solution.py:84
  50.9 4.4 %collective-permute-done.13.got = bf16[592,128]{1,0:T(8,128)(2,1)S(1)} collective-permute-done((bf16[592,128]{1,0:T(8,128)(2,1)S(1)}, bf16[592,128]{1,0:T(8,128)(2,1)S(1)}, u32[]{:S(2)}, u32[]{:S(2)}) %collective-permute-start.13) | collective-permute-done | bytes 151584 | tf_op jit(solution)/shard_map/ppermute | solution.py:84
  55.3 3.7 %collective-permute-start.14 = (bf16[592,128]{1,0:T(8,128)(2,1)S(1)}, bf16[592,128]{1,0:T(8,128)(2,1)S(1)}, u32[]{:S(2)}, u32[]{:S(2)}) collective-permute-start(bf16[592,128]{1,0:T(8,128)(2,1)S(1)} %shard_map.100.mine), channel_id=1, source_target_pairs={{0,8},{4,12},{8,0},{12,4},{1,9},{5,13},{9,1},{13,5},{2,10},{6,14},... | collective-permute-start | bytes 454664 | tf_op jit(solution)/shard_map/ppermute | solution.py:84
  59.0 6.8 %collective-permute-done.14.got = bf16[592,128]{1,0:T(8,128)(2,1)S(1)} collective-permute-done((bf16[592,128]{1,0:T(8,128)(2,1)S(1)}, bf16[592,128]{1,0:T(8,128)(2,1)S(1)}, u32[]{:S(2)}, u32[]{:S(2)}) %collective-permute-start.14) | collective-permute-done | bytes 151584 | tf_op jit(solution)/shard_map/ppermute | solution.py:84
  65.9 0.1 collective-permute-start.15
  65.9 0.1 collective-permute-start.16
  66.0 5.6 %collective-permute-done.15.refs_1_ = bf16[592,128]{1,0:T(8,128)(2,1)S(1)} collective-permute-done((bf16[592,128]{1,0:T(8,128)(2,1)S(1)}, bf16[592,128]{1,0:T(8,128)(2,1)S(1)}, u32[]{:S(2)}, u32[]{:S(2)}) %collective-permute-start.15) | collective-permute-done | bytes 151584 | tf_op jit(solution)/shard_map/ppermute | solution.py:84
  71.6 1.4 %collective-permute-done.17.refs_3_ = bf16[592,128]{1,0:T(8,128)(2,1)S(1)} collective-permute-done((bf16[592,128]{1,0:T(8,128)(2,1)S(1)}, bf16[592,128]{1,0:T(8,128)(2,1)S(1)}, u32[]{:S(2)}, u32[]{:S(2)}) %collective-permute-start.17) | collective-permute-done | bytes 151584 | tf_op jit(solution)/shard_map/ppermute | solution.py:84
  73.0 11.1 %shard_map.102 = (bf16[128,768]{1,0:T(8,128)(2,1)S(1)}, bf16[64,768]{1,0:T(8,128)(2,1)S(1)}, bf16[64,768]{1,0:T(8,128)(2,1)S(1)}) custom-call(s32[4]{0:T(128)S(1)} %pad_add_fusion.idx, bf16[592,128]{1,0:T(8,128)(2,1)S(1)} %shard_map.101.refs_0_, bf16[592,128]{1,0:T(8,128)(2,1)S(1)} %collective-permute-done.15.refs_1_, ...), custom_call_target="tpu_custom_call" | custom-call | tf_op jit(solution)/shard_map/pallas_call | solution.py:469
  84.1 0.4 collective-permute-start.19
  84.5 0.7 collective-permute-start.18
  85.1 2.5 %collective-permute-start.24 = (bf16[64,768]{1,0:T(8,128)(2,1)S(1)}, bf16[64,768]{1,0:T(8,128)(2,1)S(1)}, u32[]{:S(2)}, u32[]{:S(2)}) collective-permute-start(bf16[64,768]{1,0:T(8,128)(2,1)S(1)} %get-tuple-element.61), channel_id=1, source_target_pairs={{0,8},{1,11},{2,10},{3,9},{4,12},{5,15},{6,14},{7,13},{8,0},{9,3},... | collective-permute-start | bytes 294920 | tf_op jit(solution)/shard_map/ppermute | solution.py:98
  87.6 0.5 collective-permute-start.20
  88.1 2.7 %collective-permute-done.24 = bf16[64,768]{1,0:T(8,128)(2,1)S(1)} collective-permute-done((bf16[64,768]{1,0:T(8,128)(2,1)S(1)}, bf16[64,768]{1,0:T(8,128)(2,1)S(1)}, u32[]{:S(2)}, u32[]{:S(2)}) %collective-permute-start.24) | collective-permute-done | bytes 98336 | tf_op jit(solution)/shard_map/ppermute | solution.py:98
  90.8 3.1 %collective-permute-start.26 = (bf16[64,768]{1,0:T(8,128)(2,1)S(1)}, bf16[64,768]{1,0:T(8,128)(2,1)S(1)}, u32[]{:S(2)}, u32[]{:S(2)}) collective-permute-start(bf16[64,768]{1,0:T(8,128)(2,1)S(1)} %collective-permute-done.24), channel_id=1, source_target_pairs={{0,4},{4,0},{8,12},{12,8},{1,5},{5,1},{9,13},{13,9},{2,6},{6,2},{1... | collective-permute-start | bytes 294920 | tf_op jit(solution)/shard_map/ppermute | solution.py:84
  93.9 4.2 %collective-permute-done.20.refs_2_ = bf16[64,768]{1,0:T(8,128)(2,1)S(1)} collective-permute-done((bf16[64,768]{1,0:T(8,128)(2,1)S(1)}, bf16[64,768]{1,0:T(8,128)(2,1)S(1)}, u32[]{:S(2)}, u32[]{:S(2)}) %collective-permute-start.20) | collective-permute-done | bytes 98336 | tf_op jit(solution)/shard_map/ppermute | solution.py:98
  98.1 1.5 %collective-permute-start.22 = (bf16[128,768]{1,0:T(8,128)(2,1)S(1)}, bf16[128,768]{1,0:T(8,128)(2,1)S(1)}, u32[]{:S(2)}, u32[]{:S(2)}) collective-permute-start(bf16[128,768]{1,0:T(8,128)(2,1)S(1)} %collective-permute-done.18.refs_0_), channel_id=1, source_target_pairs={{0,1},{1,0},{2,3},{3,2},{4,5},{5,4},{6,7},{7,6},{8,9},{9,8},{10,11... | collective-permute-start | bytes 589832 | tf_op jit(solution)/shard_map/ppermute | solution.py:84
  99.6 0.1 collective-permute-start.23
  99.7 0.1 collective-permute-start.21
  99.8 0.3 collective-permute-start.25
  100.2 1.2 %collective-permute-start.27 = (bf16[64,768]{1,0:T(8,128)(2,1)S(1)}, bf16[64,768]{1,0:T(8,128)(2,1)S(1)}, u32[]{:S(2)}, u32[]{:S(2)}) collective-permute-start(bf16[64,768]{1,0:T(8,128)(2,1)S(1)} %collective-permute-done.26), channel_id=1, source_target_pairs={{0,1},{1,0},{2,3},{3,2},{4,5},{5,4},{6,7},{7,6},{8,9},{9,8},{10,11... | collective-permute-start | bytes 294920 | tf_op jit(solution)/shard_map/ppermute | solution.py:84
  101.4 3.5 %collective-permute-done.21.refs_3_ = bf16[64,768]{1,0:T(8,128)(2,1)S(1)} collective-permute-done((bf16[64,768]{1,0:T(8,128)(2,1)S(1)}, bf16[64,768]{1,0:T(8,128)(2,1)S(1)}, u32[]{:S(2)}, u32[]{:S(2)}) %collective-permute-start.21) | collective-permute-done | bytes 98336 | tf_op jit(solution)/shard_map/ppermute | solution.py:84
  104.9 1.7 %shard_map.103 = (bf16[64,2048]{1,0:T(8,128)(2,1)}, f32[64,1024]{1,0:T(8,128)}, bf16[64,1024]{1,0:T(8,128)(2,1)}, f32[64,2048]{1,0:T(8,128)}) custom-call(s32[4]{0:T(128)S(1)} %pad_add_fusion.idx, bf16[128,768]{1,0:T(8,128)(2,1)S(1)} %collective-permute-done.18.refs_0_, bf16[128,768]{1,0:T(8,128)(2,1)S(1)} %collective-permute-done.19.refs_1_, ...), custom_call_target="tpu_custom_call" | custom-call | tf_op jit(solution)/shard_map/pallas_call | solution.py:469
  (20 shorter events, 0.1 us)
Async XLA Ops:
  2.2 2.2 %collective-permute-start = (bf16[128,1024]{1,0:T(8,128)(2,1)S(1)}, bf16[128,1024]{1,0:T(8,128)(2,1)S(1)}, u32[]{:S(2)}, u32[]{:S(2)}) collective-permute-start(bf16[128,1024]{1,0:T(8,128)(2,1)S(1)} %shard_map.93), channel_id=1, source_target_pairs={{0,1},{1,0},{2,3},{3,2},{4,5},{5,4},{6,7},{7,6},{8,9},{9,8},{10,11... | collective-permute-start | bytes 786440 | tf_op jit(solution)/shard_map/ppermute | solution.py:84
  4.4 8.1 %collective-permute-start.6 = (bf16[144,2048]{1,0:T(8,128)(2,1)S(1)}, bf16[144,2048]{1,0:T(8,128)(2,1)S(1)}, u32[]{:S(2)}, u32[]{:S(2)}) collective-permute-start(bf16[144,2048]{1,0:T(8,128)(2,1)S(1)} %shard_map.94), channel_id=1, source_target_pairs={{0,1},{1,0},{2,3},{3,2},{4,5},{5,4},{6,7},{7,6},{8,9},{9,8},{10,11... | collective-permute-start | bytes 1769480 | tf_op jit(solution)/shard_map/ppermute | solution.py:84
  6.1 11.0 %collective-permute-start.1 = (bf16[128,512]{1,0:T(8,128)(2,1)S(1)}, bf16[128,512]{1,0:T(8,128)(2,1)S(1)}, u32[]{:S(2)}, u32[]{:S(2)}) collective-permute-start(bf16[128,512]{1,0:T(8,128)(2,1)S(1)} %get-tuple-element.38), channel_id=1, source_target_pairs={{0,8},{1,11},{2,10},{3,9},{4,12},{5,15},{6,14},{7,13},{8,0},{9,3},... | collective-permute-start | bytes 393224 | tf_op jit(solution)/shard_map/ppermute | solution.py:98
  10.2 11.0 %collective-permute-start.2 = (bf16[128,512]{1,0:T(8,128)(2,1)S(1)}, bf16[128,512]{1,0:T(8,128)(2,1)S(1)}, u32[]{:S(2)}, u32[]{:S(2)}) collective-permute-start(bf16[128,512]{1,0:T(8,128)(2,1)S(1)} %get-tuple-element.39), channel_id=1, source_target_pairs={{0,4},{1,7},{2,6},{3,5},{4,0},{5,3},{6,2},{7,1},{8,12},{9,15},{10,... | collective-permute-start | bytes 393224 | tf_op jit(solution)/shard_map/ppermute | solution.py:98
  11.8 9.4 %collective-permute-start.3 = (bf16[128,512]{1,0:T(8,128)(2,1)S(1)}, bf16[128,512]{1,0:T(8,128)(2,1)S(1)}, u32[]{:S(2)}, u32[]{:S(2)}) collective-permute-start(bf16[128,512]{1,0:T(8,128)(2,1)S(1)} %get-tuple-element.40), channel_id=1, source_target_pairs={{0,0},{1,3},{2,2},{3,1},{4,4},{5,7},{6,6},{7,5},{8,8},{9,11},{10,1... | collective-permute-start | bytes 393224 | tf_op jit(solution)/shard_map/ppermute | solution.py:98
  12.4 9.4 %collective-permute-start.4 = (bf16[128,512]{1,0:T(8,128)(2,1)S(1)}, bf16[128,512]{1,0:T(8,128)(2,1)S(1)}, u32[]{:S(2)}, u32[]{:S(2)}) collective-permute-start(bf16[128,512]{1,0:T(8,128)(2,1)S(1)} %get-tuple-element.41), channel_id=1, source_target_pairs={{0,12},{1,15},{2,14},{3,13},{4,8},{5,11},{6,10},{7,9},{8,4},{9,7},... | collective-permute-start | bytes 393224 | tf_op jit(solution)/shard_map/ppermute | solution.py:98
  14.2 25.2 %collective-permute-start.8 = (bf16[128,1024]{1,0:T(8,128)(2,1)S(1)}, bf16[128,1024]{1,0:T(8,128)(2,1)S(1)}, u32[]{:S(2)}, u32[]{:S(2)}) collective-permute-start(bf16[128,1024]{1,0:T(8,128)(2,1)S(1)} %get-tuple-element.46), channel_id=1, source_target_pairs={{0,8},{1,27},{2,26},{3,9},{4,12},{5,31},{6,30},{7,13},{8,0},{9,19}... | collective-permute-start | bytes 786440 | tf_op jit(solution)/shard_map/ppermute | solution.py:98
  17.1 22.3 %collective-permute-start.9 = (bf16[128,1024]{1,0:T(8,128)(2,1)S(1)}, bf16[128,1024]{1,0:T(8,128)(2,1)S(1)}, u32[]{:S(2)}, u32[]{:S(2)}) collective-permute-start(bf16[128,1024]{1,0:T(8,128)(2,1)S(1)} %get-tuple-element.47), channel_id=1, source_target_pairs={{0,12},{1,31},{2,30},{3,13},{4,8},{5,27},{6,26},{7,9},{8,4},{9,23}... | collective-permute-start | bytes 786440 | tf_op jit(solution)/shard_map/ppermute | solution.py:98
  21.2 19.7 %collective-permute-start.10 = (bf16[128,1024]{1,0:T(8,128)(2,1)S(1)}, bf16[128,1024]{1,0:T(8,128)(2,1)S(1)}, u32[]{:S(2)}, u32[]{:S(2)}) collective-permute-start(bf16[128,1024]{1,0:T(8,128)(2,1)S(1)} %get-tuple-element.48), channel_id=1, source_target_pairs={{0,4},{1,23},{2,22},{3,5},{4,0},{5,19},{6,18},{7,1},{8,12},{9,31},... | collective-permute-start | bytes 786440 | tf_op jit(solution)/shard_map/ppermute | solution.py:98
  21.2 19.7 %collective-permute-start.11 = (bf16[128,1024]{1,0:T(8,128)(2,1)S(1)}, bf16[128,1024]{1,0:T(8,128)(2,1)S(1)}, u32[]{:S(2)}, u32[]{:S(2)}) collective-permute-start(bf16[128,1024]{1,0:T(8,128)(2,1)S(1)} %get-tuple-element.49), channel_id=1, source_target_pairs={{0,0},{1,19},{2,18},{3,1},{4,4},{5,23},{6,22},{7,5},{8,8},{9,27},{... | collective-permute-start | bytes 786440 | tf_op jit(solution)/shard_map/ppermute | solution.py:98
  21.9 1.8 %collective-permute-start.7 = (bf16[192,512]{1,0:T(8,128)(2,1)S(1)}, bf16[192,512]{1,0:T(8,128)(2,1)S(1)}, u32[]{:S(2)}, u32[]{:S(2)}) collective-permute-start(bf16[192,512]{1,0:T(8,128)(2,1)S(1)} %get-tuple-element.45), channel_id=1, source_target_pairs={{0,0},{1,3},{2,2},{3,1},{4,4},{5,7},{6,6},{7,5},{8,8},{9,11},{10,1... | collective-permute-start | bytes 589832 | tf_op jit(solution)/shard_map/ppermute | solution.py:98
  42.9 3.2 %collective-permute-start.12 = (bf16[656,128]{1,0:T(8,128)(2,1)S(1)}, bf16[656,128]{1,0:T(8,128)(2,1)S(1)}, u32[]{:S(2)}, u32[]{:S(2)}) collective-permute-start(bf16[656,128]{1,0:T(8,128)(2,1)S(1)} %get-tuple-element.52), channel_id=1, source_target_pairs={{0,1},{1,0},{2,3},{3,2},{4,5},{5,4},{6,7},{7,6},{8,9},{9,8},{10,11... | collective-permute-start | bytes 503816 | tf_op jit(solution)/shard_map/ppermute | solution.py:84
  44.7 1.4 %collective-permute-start.5 = (bf16[528,128]{1,0:T(8,128)(2,1)S(1)}, bf16[528,128]{1,0:T(8,128)(2,1)S(1)}, u32[]{:S(2)}, u32[]{:S(2)}) collective-permute-start(bf16[528,128]{1,0:T(8,128)(2,1)S(1)} %get-tuple-element.43), channel_id=1, source_target_pairs={{0,1},{1,0},{2,3},{3,2},{4,5},{5,4},{6,7},{7,6},{8,9},{9,8},{10,11... | collective-permute-start | bytes 405512 | tf_op jit(solution)/shard_map/ppermute | solution.py:84
  46.8 8.5 %collective-permute-start.13 = (bf16[592,128]{1,0:T(8,128)(2,1)S(1)}, bf16[592,128]{1,0:T(8,128)(2,1)S(1)}, u32[]{:S(2)}, u32[]{:S(2)}) collective-permute-start(bf16[592,128]{1,0:T(8,128)(2,1)S(1)} %get-tuple-element.54), channel_id=1, source_target_pairs={{0,4},{4,0},{8,12},{12,8},{1,5},{5,1},{9,13},{13,9},{2,6},{6,2},{1... | collective-permute-start | bytes 454664 | tf_op jit(solution)/shard_map/ppermute | solution.py:84
  55.3 10.5 %collective-permute-start.14 = (bf16[592,128]{1,0:T(8,128)(2,1)S(1)}, bf16[592,128]{1,0:T(8,128)(2,1)S(1)}, u32[]{:S(2)}, u32[]{:S(2)}) collective-permute-start(bf16[592,128]{1,0:T(8,128)(2,1)S(1)} %shard_map.100.mine), channel_id=1, source_target_pairs={{0,8},{4,12},{8,0},{12,4},{1,9},{5,13},{9,1},{13,5},{2,10},{6,14},... | collective-permute-start | bytes 454664 | tf_op jit(solution)/shard_map/ppermute | solution.py:84
  65.9 5.8 %collective-permute-start.15 = (bf16[592,128]{1,0:T(8,128)(2,1)S(1)}, bf16[592,128]{1,0:T(8,128)(2,1)S(1)}, u32[]{:S(2)}, u32[]{:S(2)}) collective-permute-start(bf16[592,128]{1,0:T(8,128)(2,1)S(1)} %shard_map.101.refs_0_), channel_id=1, source_target_pairs={{0,4},{4,0},{8,12},{12,8},{1,5},{5,1},{9,13},{13,9},{2,6},{6,2},{1... | collective-permute-start | bytes 454664 | tf_op jit(solution)/shard_map/ppermute | solution.py:84
  65.9 5.7 %collective-permute-start.16 = (bf16[592,128]{1,0:T(8,128)(2,1)S(1)}, bf16[592,128]{1,0:T(8,128)(2,1)S(1)}, u32[]{:S(2)}, u32[]{:S(2)}) collective-permute-start(bf16[592,128]{1,0:T(8,128)(2,1)S(1)} %shard_map.101.refs_0_), channel_id=1, source_target_pairs={{0,1},{1,0},{2,3},{3,2},{4,5},{5,4},{6,7},{7,6},{8,9},{9,8},{10,11... | collective-permute-start | bytes 454664 | tf_op jit(solution)/shard_map/ppermute | solution.py:84
  71.6 1.4 %collective-permute-start.17 = (bf16[592,128]{1,0:T(8,128)(2,1)S(1)}, bf16[592,128]{1,0:T(8,128)(2,1)S(1)}, u32[]{:S(2)}, u32[]{:S(2)}) collective-permute-start(bf16[592,128]{1,0:T(8,128)(2,1)S(1)} %collective-permute-done.15.refs_1_), channel_id=1, source_target_pairs={{0,1},{1,0},{2,3},{3,2},{4,5},{5,4},{6,7},{7,6},{8,9},{9,8},{10,11... | collective-permute-start | bytes 454664 | tf_op jit(solution)/shard_map/ppermute | solution.py:84
  84.1 14.0 %collective-permute-start.19 = (bf16[128,768]{1,0:T(8,128)(2,1)S(1)}, bf16[128,768]{1,0:T(8,128)(2,1)S(1)}, u32[]{:S(2)}, u32[]{:S(2)}) collective-permute-start(bf16[128,768]{1,0:T(8,128)(2,1)S(1)} %get-tuple-element.56), channel_id=1, source_target_pairs={{0,4},{1,7},{2,6},{3,5},{4,0},{5,3},{6,2},{7,1},{8,12},{9,15},{10,... | collective-permute-start | bytes 589832 | tf_op jit(solution)/shard_map/ppermute | solution.py:98
  84.5 13.7 %collective-permute-start.18 = (bf16[128,768]{1,0:T(8,128)(2,1)S(1)}, bf16[128,768]{1,0:T(8,128)(2,1)S(1)}, u32[]{:S(2)}, u32[]{:S(2)}) collective-permute-start(bf16[128,768]{1,0:T(8,128)(2,1)S(1)} %get-tuple-element.56), channel_id=1, source_target_pairs={{0,0},{1,3},{2,2},{3,1},{4,4},{5,7},{6,6},{7,5},{8,8},{9,11},{10,1... | collective-permute-start | bytes 589832 | tf_op jit(solution)/shard_map/ppermute | solution.py:98
  85.1 5.7 %collective-permute-start.24 = (bf16[64,768]{1,0:T(8,128)(2,1)S(1)}, bf16[64,768]{1,0:T(8,128)(2,1)S(1)}, u32[]{:S(2)}, u32[]{:S(2)}) collective-permute-start(bf16[64,768]{1,0:T(8,128)(2,1)S(1)} %get-tuple-element.61), channel_id=1, source_target_pairs={{0,8},{1,11},{2,10},{3,9},{4,12},{5,15},{6,14},{7,13},{8,0},{9,3},... | collective-permute-start | bytes 294920 | tf_op jit(solution)/shard_map/ppermute | solution.py:98
  87.6 10.5 %collective-permute-start.20 = (bf16[64,768]{1,0:T(8,128)(2,1)S(1)}, bf16[64,768]{1,0:T(8,128)(2,1)S(1)}, u32[]{:S(2)}, u32[]{:S(2)}) collective-permute-start(bf16[64,768]{1,0:T(8,128)(2,1)S(1)} %get-tuple-element.57), channel_id=1, source_target_pairs={{0,8},{1,11},{2,10},{3,9},{4,12},{5,15},{6,14},{7,13},{8,0},{9,3},... | collective-permute-start | bytes 294920 | tf_op jit(solution)/shard_map/ppermute | solution.py:98
  90.8 9.3 %collective-permute-start.26 = (bf16[64,768]{1,0:T(8,128)(2,1)S(1)}, bf16[64,768]{1,0:T(8,128)(2,1)S(1)}, u32[]{:S(2)}, u32[]{:S(2)}) collective-permute-start(bf16[64,768]{1,0:T(8,128)(2,1)S(1)} %collective-permute-done.24), channel_id=1, source_target_pairs={{0,4},{4,0},{8,12},{12,8},{1,5},{5,1},{9,13},{13,9},{2,6},{6,2},{1... | collective-permute-start | bytes 294920 | tf_op jit(solution)/shard_map/ppermute | solution.py:84
  98.1 6.7 %collective-permute-start.22 = (bf16[128,768]{1,0:T(8,128)(2,1)S(1)}, bf16[128,768]{1,0:T(8,128)(2,1)S(1)}, u32[]{:S(2)}, u32[]{:S(2)}) collective-permute-start(bf16[128,768]{1,0:T(8,128)(2,1)S(1)} %collective-permute-done.18.refs_0_), channel_id=1, source_target_pairs={{0,1},{1,0},{2,3},{3,2},{4,5},{5,4},{6,7},{7,6},{8,9},{9,8},{10,11... | collective-permute-start | bytes 589832 | tf_op jit(solution)/shard_map/ppermute | solution.py:84
  99.6 5.2 %collective-permute-start.23 = (bf16[128,768]{1,0:T(8,128)(2,1)S(1)}, bf16[128,768]{1,0:T(8,128)(2,1)S(1)}, u32[]{:S(2)}, u32[]{:S(2)}) collective-permute-start(bf16[128,768]{1,0:T(8,128)(2,1)S(1)} %collective-permute-done.19.refs_1_), channel_id=1, source_target_pairs={{0,1},{1,0},{2,3},{3,2},{4,5},{5,4},{6,7},{7,6},{8,9},{9,8},{10,11... | collective-permute-start | bytes 589832 | tf_op jit(solution)/shard_map/ppermute | solution.py:84
  99.7 5.1 %collective-permute-start.21 = (bf16[64,768]{1,0:T(8,128)(2,1)S(1)}, bf16[64,768]{1,0:T(8,128)(2,1)S(1)}, u32[]{:S(2)}, u32[]{:S(2)}) collective-permute-start(bf16[64,768]{1,0:T(8,128)(2,1)S(1)} %collective-permute-done.20.refs_2_), channel_id=1, source_target_pairs={{0,4},{4,0},{8,12},{12,8},{1,5},{5,1},{9,13},{13,9},{2,6},{6,2},{1... | collective-permute-start | bytes 294920 | tf_op jit(solution)/shard_map/ppermute | solution.py:84
  99.8 5.0 %collective-permute-start.25 = (bf16[64,768]{1,0:T(8,128)(2,1)S(1)}, bf16[64,768]{1,0:T(8,128)(2,1)S(1)}, u32[]{:S(2)}, u32[]{:S(2)}) collective-permute-start(bf16[64,768]{1,0:T(8,128)(2,1)S(1)} %collective-permute-done.24), channel_id=1, source_target_pairs={{0,1},{1,0},{2,3},{3,2},{4,5},{5,4},{6,7},{7,6},{8,9},{9,8},{10,11... | collective-permute-start | bytes 294920 | tf_op jit(solution)/shard_map/ppermute | solution.py:84
  100.2 4.7 %collective-permute-start.27 = (bf16[64,768]{1,0:T(8,128)(2,1)S(1)}, bf16[64,768]{1,0:T(8,128)(2,1)S(1)}, u32[]{:S(2)}, u32[]{:S(2)}) collective-permute-start(bf16[64,768]{1,0:T(8,128)(2,1)S(1)} %collective-permute-done.26), channel_id=1, source_target_pairs={{0,1},{1,0},{2,3},{3,2},{4,5},{5,4},{6,7},{7,6},{8,9},{9,8},{10,11... | collective-permute-start | bytes 294920 | tf_op jit(solution)/shard_map/ppermute | solution.py:84

commit v10 on v8

--- a/solution.py
+++ b/solution.py
@@ -563,6 +563,8 @@
     leaves, stays = routed(leaves, sizes, 2, False), routed(stays, sizes, 2, False)
     near, here = routed(whole, sizes, 1, False), routed(whole, sizes, 0, False)
     leaves_on, stays_on = swap(leaves, "dp", 1), swap(stays, "dp", 1)
+    here, near, stays = lax.optimization_barrier((here, near, stays))
+    leaves_on, stays_on = lax.optimization_barrier((leaves_on, stays_on))
     mine = (here, near, stays, stays_on)
     theirs = [swap(v, "tensor", 1) for v in (here, near, leaves, leaves_on)]
     outs = call(

time: 106 us -> 107 us (level)
  waiting for transfers between devices: 44.7 us -> 50.2 us
  starting transfers between devices: 38.9 us -> 33.9 us
    ppermute x14, starting transfers between devices: 21.1 us -> 16.1 us  [swap(): return lax.ppermute(value, axis, [(i, i ^ bit) for i in range(count)])]
    ppermute x13, waiting for transfers between devices: 20.7 us -> 24.9 us  [routed(): return lax.ppermute(value, ('section', 'dp', 'tensor'), pairs)]
    ppermute x14, waiting for transfers between devices: 24.1 us -> 25.4 us  [swap(): return lax.ppermute(value, axis, [(i, i ^ bit) for i in range(count)])]
  transfers between devices with their start and end apart: 27 -> 27, of which waited for: 11 -> 13; matrix products, arithmetic and copies ran while one was open for 0% -> 0% of each run, Pallas kernels for 3% -> 3%
where the time goes in v10:
time: 107 us
  waiting for transfers between devices  50.2 us (47%)
  starting transfers between devices  33.9 us (32%)
  Pallas kernels  21.6 us (20%)
    ppermute x14, waiting for transfers between devices, swap(): return lax.ppermute(value, axis, [(i, i ^ bit) for i in range(count)])  25.4 us
    ppermute x13, waiting for transfers between devices, routed(): return lax.ppermute(value, ('section', 'dp', 'tensor'), pairs)  24.9 us
    pallas_call x10, Pallas kernels, call(): pl.pallas_call(kernel, out_shape=out_shapes, in_specs=spaces, out_specs=j...  21.6 us
    ppermute x13, starting transfers between devices, routed(): return lax.ppermute(value, ('section', 'dp', 'tensor'), pairs)  17.8 us
    ppermute x14, starting transfers between devices, swap(): return lax.ppermute(value, axis, [(i, i ^ bit) for i in range(count)])  16.1 us
  transfers between devices with their start and end apart: 27, of which 13 were waited for; matrix products, arithmetic and copies ran while one was open for 0% of the time, Pallas kernels for 3%

profile of v10, /device:TPU:0, one launch (start us, length us, event | category | flops | bytes accessed | tf_op | source)
XLA Modules:
  0.0 106.6 jit_solution(7270307966118223593)
XLA Ops:
  0.6 0.1 pad_add_fusion.idx
  0.7 1.7 %shard_map.93 = bf16[144,3072]{1,0:T(8,128)(2,1)S(1)} custom-call(s32[4]{0:T(128)S(1)} %pad_add_fusion.idx, bf16[128,2048]{1,0:T(8,128)(2,1)} %bitcast.14, bf16[128,1024]{1,0:T(8,128)(2,1)} %bitcast.18, bf16[128,1024]{1,0:T(8,128)(2,1)} %bitcast.20, bf16[128,2048]{1,0:T(8,128)(2,1)} %bitcast.16, bf16[64,1024]{1,0:T(8,128)(2,1)} %bitcast.24, ...), custom_call_target="tpu_custom_call" | custom-call | tf_op jit(solution)/shard_map/pallas_call | solution.py:465
  2.4 0.5 collective-permute-start
  3.0 2.1 %collective-permute-done.got = bf16[144,3072]{1,0:T(8,128)(2,1)S(1)} collective-permute-done((bf16[144,3072]{1,0:T(8,128)(2,1)S(1)}, bf16[144,3072]{1,0:T(8,128)(2,1)S(1)}, u32[]{:S(2)}, u32[]{:S(2)}) %collective-permute-start) | collective-permute-done | bytes 884768 | tf_op jit(solution)/shard_map/ppermute | solution.py:84
  5.0 1.5 %shard_map.94 = (bf16[128,512]{1,0:T(8,128)(2,1)S(1)}, bf16[128,512]{1,0:T(8,128)(2,1)S(1)}, bf16[128,512]{1,0:T(8,128)(2,1)S(1)}, bf16[128,512]{1,0:T(8,128)(2,1)S(1)}) custom-call(s32[4]{0:T(128)S(1)} %pad_add_fusion.idx, bf16[128,1024]{1,0:T(8,128)(2,1)} %bitcast.19, bf16[128,1024]{1,0:T(8,128)(2,1)} %bitcast.21, ...), custom_call_target="tpu_custom_call" | custom-call | tf_op jit(solution)/shard_map/pallas_call | solution.py:465
  6.6 4.0 %collective-permute-start.1 = (bf16[128,512]{1,0:T(8,128)(2,1)S(1)}, bf16[128,512]{1,0:T(8,128)(2,1)S(1)}, u32[]{:S(2)}, u32[]{:S(2)}) collective-permute-start(bf16[128,512]{1,0:T(8,128)(2,1)S(1)} %get-tuple-element.33), channel_id=1, source_target_pairs={{0,8},{1,11},{2,10},{3,9},{4,12},{5,15},{6,14},{7,13},{8,0},{9,3},... | collective-permute-start | bytes 393224 | tf_op jit(solution)/shard_map/ppermute | solution.py:98
  10.6 1.6 %collective-permute-start.2 = (bf16[128,512]{1,0:T(8,128)(2,1)S(1)}, bf16[128,512]{1,0:T(8,128)(2,1)S(1)}, u32[]{:S(2)}, u32[]{:S(2)}) collective-permute-start(bf16[128,512]{1,0:T(8,128)(2,1)S(1)} %get-tuple-element.34), channel_id=1, source_target_pairs={{0,4},{1,7},{2,6},{3,5},{4,0},{5,3},{6,2},{7,1},{8,12},{9,15},{10,... | collective-permute-start | bytes 393224 | tf_op jit(solution)/shard_map/ppermute | solution.py:98
  12.1 0.7 collective-permute-start.3
  12.8 0.1 collective-permute-start.4
  12.9 1.7 %shard_map.96 = (bf16[128,1024]{1,0:T(8,128)(2,1)S(1)}, bf16[128,1024]{1,0:T(8,128)(2,1)S(1)}, bf16[128,1024]{1,0:T(8,128)(2,1)S(1)}, bf16[128,1024]{1,0:T(8,128)(2,1)S(1)}, bf16[192,512]{1,0:T(8,128)(2,1)S(1)}) custom-call(s32[4]{0:T(128)S(1)} %pad_add_fusion.idx, bf16[128,2048]{1,0:T(8,128)(2,1)} %bitcast.15, bf16[128,2048]{1,0:T(8,128)(2,1)} %bitcast.17, ...), custom_call_target="tpu_custom_call" | custom-call | tf_op jit(solution)/shard_map/pallas_call | solution.py:465
  14.6 1.9 %collective-permute-start.7 = (bf16[128,1024]{1,0:T(8,128)(2,1)S(1)}, bf16[128,1024]{1,0:T(8,128)(2,1)S(1)}, u32[]{:S(2)}, u32[]{:S(2)}) collective-permute-start(bf16[128,1024]{1,0:T(8,128)(2,1)S(1)} %get-tuple-element.40), channel_id=1, source_target_pairs={{0,8},{1,27},{2,26},{3,9},{4,12},{5,31},{6,30},{7,13},{8,0},{9,19}... | collective-permute-start | bytes 786440 | tf_op jit(solution)/shard_map/ppermute | solution.py:98
  16.6 0.9 collective-permute-done.1.refs_0_
  17.4 4.2 %collective-permute-start.8 = (bf16[128,1024]{1,0:T(8,128)(2,1)S(1)}, bf16[128,1024]{1,0:T(8,128)(2,1)S(1)}, u32[]{:S(2)}, u32[]{:S(2)}) collective-permute-start(bf16[128,1024]{1,0:T(8,128)(2,1)S(1)} %get-tuple-element.41), channel_id=1, source_target_pairs={{0,12},{1,31},{2,30},{3,13},{4,8},{5,27},{6,26},{7,9},{8,4},{9,23}... | collective-permute-start | bytes 786440 | tf_op jit(solution)/shard_map/ppermute | solution.py:98
  21.6 0.0 collective-permute-done.2.refs_1_
  21.6 0.7 collective-permute-start.10
  22.3 0.0 collective-permute-done.4.refs_3_
  22.3 0.7 collective-permute-start.6
  23.0 1.1 %shard_map.95 = (bf16[512,512]{1,0:T(8,128)(2,1)S(1)}, bf16[528,128]{1,0:T(8,128)(2,1)S(1)}, bf16[528,128]{1,0:T(8,128)(2,1)S(1)}) custom-call(s32[4]{0:T(128)S(1)} %pad_add_fusion.idx, bf16[128,512]{1,0:T(8,128)(2,1)S(1)} %collective-permute-done.1.refs_0_, bf16[128,512]{1,0:T(8,128)(2,1)S(1)} %collective-permute-done.2.refs_1_, ...), custom_call_target="tpu_custom_call" | custom-call | tf_op jit(solution)/shard_map/pallas_call | solution.py:465
  24.2 15.4 %collective-permute-done.7.refs_1_ = bf16[128,1024]{1,0:T(8,128)(2,1)S(1)} collective-permute-done((bf16[128,1024]{1,0:T(8,128)(2,1)S(1)}, bf16[128,1024]{1,0:T(8,128)(2,1)S(1)}, u32[]{:S(2)}, u32[]{:S(2)}) %collective-permute-start.7) | collective-permute-done | bytes 262176 | tf_op jit(solution)/shard_map/ppermute | solution.py:98
  39.6 1.6 %collective-permute-done.9.refs_3_ = bf16[128,1024]{1,0:T(8,128)(2,1)S(1)} collective-permute-done((bf16[128,1024]{1,0:T(8,128)(2,1)S(1)}, bf16[128,1024]{1,0:T(8,128)(2,1)S(1)}, u32[]{:S(2)}, u32[]{:S(2)}) %collective-permute-start.9) | collective-permute-done | bytes 262176 | tf_op jit(solution)/shard_map/ppermute | solution.py:98
  41.3 2.0 %shard_map.97 = (bf16[512,1024]{1,0:T(8,128)(2,1)S(1)}, bf16[656,128]{1,0:T(8,128)(2,1)S(1)}, bf16[656,128]{1,0:T(8,128)(2,1)S(1)}) custom-call(s32[4]{0:T(128)S(1)} %pad_add_fusion.idx, bf16[192,512]{1,0:T(8,128)(2,1)S(1)} %collective-permute-done.6.refs_0_, bf16[128,1024]{1,0:T(8,128)(2,1)S(1)} %collective-permute-done.7.refs_1_, ...), custom_call_target="tpu_custom_call" | custom-call | tf_op jit(solution)/shard_map/pallas_call | solution.py:465
  43.3 2.0 %collective-permute-start.11 = (bf16[656,128]{1,0:T(8,128)(2,1)S(1)}, bf16[656,128]{1,0:T(8,128)(2,1)S(1)}, u32[]{:S(2)}, u32[]{:S(2)}) collective-permute-start(bf16[656,128]{1,0:T(8,128)(2,1)S(1)} %get-tuple-element.46), channel_id=1, source_target_pairs={{0,1},{1,0},{2,3},{3,2},{4,5},{5,4},{6,7},{7,6},{8,9},{9,8},{10,11... | collective-permute-start | bytes 503816 | tf_op jit(solution)/shard_map/ppermute | solution.py:84
  45.2 0.1 collective-permute-start.5
  45.3 1.3 %collective-permute-done.5.thin_got = bf16[528,128]{1,0:T(8,128)(2,1)S(1)} collective-permute-done((bf16[528,128]{1,0:T(8,128)(2,1)S(1)}, bf16[528,128]{1,0:T(8,128)(2,1)S(1)}, u32[]{:S(2)}, u32[]{:S(2)}) %collective-permute-start.5) | collective-permute-done | bytes 135200 | tf_op jit(solution)/shard_map/ppermute | solution.py:84
  46.6 0.7 shard_map.98
  47.3 4.0 %collective-permute-start.12 = (bf16[592,128]{1,0:T(8,128)(2,1)S(1)}, bf16[592,128]{1,0:T(8,128)(2,1)S(1)}, u32[]{:S(2)}, u32[]{:S(2)}) collective-permute-start(bf16[592,128]{1,0:T(8,128)(2,1)S(1)} %get-tuple-element.48), channel_id=1, source_target_pairs={{0,4},{4,0},{8,12},{12,8},{1,5},{5,1},{9,13},{13,9},{2,6},{6,2},{1... | collective-permute-start | bytes 454664 | tf_op jit(solution)/shard_map/ppermute | solution.py:84
  51.2 4.4 %collective-permute-done.12.got = bf16[592,128]{1,0:T(8,128)(2,1)S(1)} collective-permute-done((bf16[592,128]{1,0:T(8,128)(2,1)S(1)}, bf16[592,128]{1,0:T(8,128)(2,1)S(1)}, u32[]{:S(2)}, u32[]{:S(2)}) %collective-permute-start.12) | collective-permute-done | bytes 151584 | tf_op jit(solution)/shard_map/ppermute | solution.py:84
  55.7 3.7 %collective-permute-start.13 = (bf16[592,128]{1,0:T(8,128)(2,1)S(1)}, bf16[592,128]{1,0:T(8,128)(2,1)S(1)}, u32[]{:S(2)}, u32[]{:S(2)}) collective-permute-start(bf16[592,128]{1,0:T(8,128)(2,1)S(1)} %shard_map.99.mine), channel_id=1, source_target_pairs={{0,8},{4,12},{8,0},{12,4},{1,9},{5,13},{9,1},{13,5},{2,10},{6,14},... | collective-permute-start | bytes 454664 | tf_op jit(solution)/shard_map/ppermute | solution.py:84
  59.4 6.8 %collective-permute-done.13.got = bf16[592,128]{1,0:T(8,128)(2,1)S(1)} collective-permute-done((bf16[592,128]{1,0:T(8,128)(2,1)S(1)}, bf16[592,128]{1,0:T(8,128)(2,1)S(1)}, u32[]{:S(2)}, u32[]{:S(2)}) %collective-permute-start.13) | collective-permute-done | bytes 151584 | tf_op jit(solution)/shard_map/ppermute | solution.py:84
  66.2 0.1 collective-permute-start.14
  66.3 0.1 collective-permute-start.15
  66.4 5.6 %collective-permute-done.14.refs_1_ = bf16[592,128]{1,0:T(8,128)(2,1)S(1)} collective-permute-done((bf16[592,128]{1,0:T(8,128)(2,1)S(1)}, bf16[592,128]{1,0:T(8,128)(2,1)S(1)}, u32[]{:S(2)}, u32[]{:S(2)}) %collective-permute-start.14) | collective-permute-done | bytes 151584 | tf_op jit(solution)/shard_map/ppermute | solution.py:84
  72.0 1.4 %collective-permute-done.16.refs_3_ = bf16[592,128]{1,0:T(8,128)(2,1)S(1)} collective-permute-done((bf16[592,128]{1,0:T(8,128)(2,1)S(1)}, bf16[592,128]{1,0:T(8,128)(2,1)S(1)}, u32[]{:S(2)}, u32[]{:S(2)}) %collective-permute-start.16) | collective-permute-done | bytes 151584 | tf_op jit(solution)/shard_map/ppermute | solution.py:84
  73.4 11.1 %shard_map.101 = (bf16[128,768]{1,0:T(8,128)(2,1)S(1)}, bf16[64,768]{1,0:T(8,128)(2,1)S(1)}, bf16[64,768]{1,0:T(8,128)(2,1)S(1)}) custom-call(s32[4]{0:T(128)S(1)} %pad_add_fusion.idx, bf16[592,128]{1,0:T(8,128)(2,1)S(1)} %shard_map.100.refs_0_, bf16[592,128]{1,0:T(8,128)(2,1)S(1)} %collective-permute-done.14.refs_1_, ...), custom_call_target="tpu_custom_call" | custom-call | tf_op jit(solution)/shard_map/pallas_call | solution.py:465
  84.5 0.4 collective-permute-start.18
  84.8 0.7 collective-permute-start.17
  85.5 2.5 %collective-permute-start.19 = (bf16[64,768]{1,0:T(8,128)(2,1)S(1)}, bf16[64,768]{1,0:T(8,128)(2,1)S(1)}, u32[]{:S(2)}, u32[]{:S(2)}) collective-permute-start(bf16[64,768]{1,0:T(8,128)(2,1)S(1)} %get-tuple-element.51), channel_id=1, source_target_pairs={{0,8},{1,11},{2,10},{3,9},{4,12},{5,15},{6,14},{7,13},{8,0},{9,3},... | collective-permute-start | bytes 294920 | tf_op jit(solution)/shard_map/ppermute | solution.py:98
  88.0 0.5 collective-permute-start.20
  88.5 2.7 %collective-permute-done.19.refs_2_ = bf16[64,768]{1,0:T(8,128)(2,1)S(1)} collective-permute-done((bf16[64,768]{1,0:T(8,128)(2,1)S(1)}, bf16[64,768]{1,0:T(8,128)(2,1)S(1)}, u32[]{:S(2)}, u32[]{:S(2)}) %collective-permute-start.19) | collective-permute-done | bytes 98336 | tf_op jit(solution)/shard_map/ppermute | solution.py:98
  91.2 3.1 %collective-permute-start.22 = (bf16[64,768]{1,0:T(8,128)(2,1)S(1)}, bf16[64,768]{1,0:T(8,128)(2,1)S(1)}, u32[]{:S(2)}, u32[]{:S(2)}) collective-permute-start(bf16[64,768]{1,0:T(8,128)(2,1)S(1)} %collective-permute-done.19.refs_2_), channel_id=1, source_target_pairs={{0,4},{4,0},{8,12},{12,8},{1,5},{5,1},{9,13},{13,9},{2,6},{6,2},{1... | collective-permute-start | bytes 294920 | tf_op jit(solution)/shard_map/ppermute | solution.py:84
  94.2 4.2 %collective-permute-done.20 = bf16[64,768]{1,0:T(8,128)(2,1)S(1)} collective-permute-done((bf16[64,768]{1,0:T(8,128)(2,1)S(1)}, bf16[64,768]{1,0:T(8,128)(2,1)S(1)}, u32[]{:S(2)}, u32[]{:S(2)}) %collective-permute-start.20) | collective-permute-done | bytes 98336 | tf_op jit(solution)/shard_map/ppermute | solution.py:98
  98.5 1.7 %collective-permute-start.23 = (bf16[128,768]{1,0:T(8,128)(2,1)S(1)}, bf16[128,768]{1,0:T(8,128)(2,1)S(1)}, u32[]{:S(2)}, u32[]{:S(2)}) collective-permute-start(bf16[128,768]{1,0:T(8,128)(2,1)S(1)} %collective-permute-done.17.refs_0_), channel_id=1, source_target_pairs={{0,1},{1,0},{2,3},{3,2},{4,5},{5,4},{6,7},{7,6},{8,9},{9,8},{10,11... | collective-permute-start | bytes 589832 | tf_op jit(solution)/shard_map/ppermute | solution.py:84
  100.2 0.1 collective-permute-start.24
  100.2 0.4 collective-permute-start.25
  100.7 2.9 %collective-permute-done.21 = bf16[64,768]{1,0:T(8,128)(2,1)S(1)} collective-permute-done((bf16[64,768]{1,0:T(8,128)(2,1)S(1)}, bf16[64,768]{1,0:T(8,128)(2,1)S(1)}, u32[]{:S(2)}, u32[]{:S(2)}) %collective-permute-start.21) | collective-permute-done | bytes 98336 | tf_op jit(solution)/shard_map/ppermute | solution.py:84
  103.6 0.4 collective-permute-start.26
  104.0 0.9 collective-permute-done.26.refs_7_
  104.9 1.7 %shard_map.102 = (bf16[64,2048]{1,0:T(8,128)(2,1)}, f32[64,1024]{1,0:T(8,128)}, bf16[64,1024]{1,0:T(8,128)(2,1)}, f32[64,2048]{1,0:T(8,128)}) custom-call(s32[4]{0:T(128)S(1)} %pad_add_fusion.idx, bf16[128,768]{1,0:T(8,128)(2,1)S(1)} %collective-permute-done.17.refs_0_, bf16[128,768]{1,0:T(8,128)(2,1)S(1)} %collective-permute-done.18.refs_1_, ...), custom_call_target="tpu_custom_call" | custom-call | tf_op jit(solution)/shard_map/pallas_call | solution.py:465
  (17 shorter events, 0.1 us)
Async XLA Ops:
  2.4 2.6 %collective-permute-start = (bf16[144,3072]{1,0:T(8,128)(2,1)S(1)}, bf16[144,3072]{1,0:T(8,128)(2,1)S(1)}, u32[]{:S(2)}, u32[]{:S(2)}) collective-permute-start(bf16[144,3072]{1,0:T(8,128)(2,1)S(1)} %shard_map.93), channel_id=1, source_target_pairs={{0,1},{1,0},{2,3},{3,2},{4,5},{5,4},{6,7},{7,6},{8,9},{9,8},{10,11... | collective-permute-start | bytes 2654216 | tf_op jit(solution)/shard_map/ppermute | solution.py:84
  6.6 10.9 %collective-permute-start.1 = (bf16[128,512]{1,0:T(8,128)(2,1)S(1)}, bf16[128,512]{1,0:T(8,128)(2,1)S(1)}, u32[]{:S(2)}, u32[]{:S(2)}) collective-permute-start(bf16[128,512]{1,0:T(8,128)(2,1)S(1)} %get-tuple-element.33), channel_id=1, source_target_pairs={{0,8},{1,11},{2,10},{3,9},{4,12},{5,15},{6,14},{7,13},{8,0},{9,3},... | collective-permute-start | bytes 393224 | tf_op jit(solution)/shard_map/ppermute | solution.py:98
  10.6 11.0 %collective-permute-start.2 = (bf16[128,512]{1,0:T(8,128)(2,1)S(1)}, bf16[128,512]{1,0:T(8,128)(2,1)S(1)}, u32[]{:S(2)}, u32[]{:S(2)}) collective-permute-start(bf16[128,512]{1,0:T(8,128)(2,1)S(1)} %get-tuple-element.34), channel_id=1, source_target_pairs={{0,4},{1,7},{2,6},{3,5},{4,0},{5,3},{6,2},{7,1},{8,12},{9,15},{10,... | collective-permute-start | bytes 393224 | tf_op jit(solution)/shard_map/ppermute | solution.py:98
  12.1 9.5 %collective-permute-start.3 = (bf16[128,512]{1,0:T(8,128)(2,1)S(1)}, bf16[128,512]{1,0:T(8,128)(2,1)S(1)}, u32[]{:S(2)}, u32[]{:S(2)}) collective-permute-start(bf16[128,512]{1,0:T(8,128)(2,1)S(1)} %get-tuple-element.35), channel_id=1, source_target_pairs={{0,0},{1,3},{2,2},{3,1},{4,4},{5,7},{6,6},{7,5},{8,8},{9,11},{10,1... | collective-permute-start | bytes 393224 | tf_op jit(solution)/shard_map/ppermute | solution.py:98
  12.8 9.5 %collective-permute-start.4 = (bf16[128,512]{1,0:T(8,128)(2,1)S(1)}, bf16[128,512]{1,0:T(8,128)(2,1)S(1)}, u32[]{:S(2)}, u32[]{:S(2)}) collective-permute-start(bf16[128,512]{1,0:T(8,128)(2,1)S(1)} %get-tuple-element.36), channel_id=1, source_target_pairs={{0,12},{1,15},{2,14},{3,13},{4,8},{5,11},{6,10},{7,9},{8,4},{9,7},... | collective-permute-start | bytes 393224 | tf_op jit(solution)/shard_map/ppermute | solution.py:98
  14.6 25.0 %collective-permute-start.7 = (bf16[128,1024]{1,0:T(8,128)(2,1)S(1)}, bf16[128,1024]{1,0:T(8,128)(2,1)S(1)}, u32[]{:S(2)}, u32[]{:S(2)}) collective-permute-start(bf16[128,1024]{1,0:T(8,128)(2,1)S(1)} %get-tuple-element.40), channel_id=1, source_target_pairs={{0,8},{1,27},{2,26},{3,9},{4,12},{5,31},{6,30},{7,13},{8,0},{9,19}... | collective-permute-start | bytes 786440 | tf_op jit(solution)/shard_map/ppermute | solution.py:98
  17.4 22.2 %collective-permute-start.8 = (bf16[128,1024]{1,0:T(8,128)(2,1)S(1)}, bf16[128,1024]{1,0:T(8,128)(2,1)S(1)}, u32[]{:S(2)}, u32[]{:S(2)}) collective-permute-start(bf16[128,1024]{1,0:T(8,128)(2,1)S(1)} %get-tuple-element.41), channel_id=1, source_target_pairs={{0,12},{1,31},{2,30},{3,13},{4,8},{5,27},{6,26},{7,9},{8,4},{9,23}... | collective-permute-start | bytes 786440 | tf_op jit(solution)/shard_map/ppermute | solution.py:98
  21.6 19.6 %collective-permute-start.9 = (bf16[128,1024]{1,0:T(8,128)(2,1)S(1)}, bf16[128,1024]{1,0:T(8,128)(2,1)S(1)}, u32[]{:S(2)}, u32[]{:S(2)}) collective-permute-start(bf16[128,1024]{1,0:T(8,128)(2,1)S(1)} %get-tuple-element.42), channel_id=1, source_target_pairs={{0,4},{1,23},{2,22},{3,5},{4,0},{5,19},{6,18},{7,1},{8,12},{9,31},... | collective-permute-start | bytes 786440 | tf_op jit(solution)/shard_map/ppermute | solution.py:98
  21.6 19.6 %collective-permute-start.10 = (bf16[128,1024]{1,0:T(8,128)(2,1)S(1)}, bf16[128,1024]{1,0:T(8,128)(2,1)S(1)}, u32[]{:S(2)}, u32[]{:S(2)}) collective-permute-start(bf16[128,1024]{1,0:T(8,128)(2,1)S(1)} %get-tuple-element.43), channel_id=1, source_target_pairs={{0,0},{1,19},{2,18},{3,1},{4,4},{5,23},{6,22},{7,5},{8,8},{9,27},{... | collective-permute-start | bytes 786440 | tf_op jit(solution)/shard_map/ppermute | solution.py:98
  22.3 1.8 %collective-permute-start.6 = (bf16[192,512]{1,0:T(8,128)(2,1)S(1)}, bf16[192,512]{1,0:T(8,128)(2,1)S(1)}, u32[]{:S(2)}, u32[]{:S(2)}) collective-permute-start(bf16[192,512]{1,0:T(8,128)(2,1)S(1)} %get-tuple-element.39), channel_id=1, source_target_pairs={{0,0},{1,3},{2,2},{3,1},{4,4},{5,7},{6,6},{7,5},{8,8},{9,11},{10,1... | collective-permute-start | bytes 589832 | tf_op jit(solution)/shard_map/ppermute | solution.py:98
  43.3 3.3 %collective-permute-start.11 = (bf16[656,128]{1,0:T(8,128)(2,1)S(1)}, bf16[656,128]{1,0:T(8,128)(2,1)S(1)}, u32[]{:S(2)}, u32[]{:S(2)}) collective-permute-start(bf16[656,128]{1,0:T(8,128)(2,1)S(1)} %get-tuple-element.46), channel_id=1, source_target_pairs={{0,1},{1,0},{2,3},{3,2},{4,5},{5,4},{6,7},{7,6},{8,9},{9,8},{10,11... | collective-permute-start | bytes 503816 | tf_op jit(solution)/shard_map/ppermute | solution.py:84
  45.2 1.4 %collective-permute-start.5 = (bf16[528,128]{1,0:T(8,128)(2,1)S(1)}, bf16[528,128]{1,0:T(8,128)(2,1)S(1)}, u32[]{:S(2)}, u32[]{:S(2)}) collective-permute-start(bf16[528,128]{1,0:T(8,128)(2,1)S(1)} %get-tuple-element.38), channel_id=1, source_target_pairs={{0,1},{1,0},{2,3},{3,2},{4,5},{5,4},{6,7},{7,6},{8,9},{9,8},{10,11... | collective-permute-start | bytes 405512 | tf_op jit(solution)/shard_map/ppermute | solution.py:84
  47.3 8.3 %collective-permute-start.12 = (bf16[592,128]{1,0:T(8,128)(2,1)S(1)}, bf16[592,128]{1,0:T(8,128)(2,1)S(1)}, u32[]{:S(2)}, u32[]{:S(2)}) collective-permute-start(bf16[592,128]{1,0:T(8,128)(2,1)S(1)} %get-tuple-element.48), channel_id=1, source_target_pairs={{0,4},{4,0},{8,12},{12,8},{1,5},{5,1},{9,13},{13,9},{2,6},{6,2},{1... | collective-permute-start | bytes 454664 | tf_op jit(solution)/shard_map/ppermute | solution.py:84
  55.7 10.5 %collective-permute-start.13 = (bf16[592,128]{1,0:T(8,128)(2,1)S(1)}, bf16[592,128]{1,0:T(8,128)(2,1)S(1)}, u32[]{:S(2)}, u32[]{:S(2)}) collective-permute-start(bf16[592,128]{1,0:T(8,128)(2,1)S(1)} %shard_map.99.mine), channel_id=1, source_target_pairs={{0,8},{4,12},{8,0},{12,4},{1,9},{5,13},{9,1},{13,5},{2,10},{6,14},... | collective-permute-start | bytes 454664 | tf_op jit(solution)/shard_map/ppermute | solution.py:84
  66.2 5.8 %collective-permute-start.14 = (bf16[592,128]{1,0:T(8,128)(2,1)S(1)}, bf16[592,128]{1,0:T(8,128)(2,1)S(1)}, u32[]{:S(2)}, u32[]{:S(2)}) collective-permute-start(bf16[592,128]{1,0:T(8,128)(2,1)S(1)} %shard_map.100.refs_0_), channel_id=1, source_target_pairs={{0,4},{4,0},{8,12},{12,8},{1,5},{5,1},{9,13},{13,9},{2,6},{6,2},{1... | collective-permute-start | bytes 454664 | tf_op jit(solution)/shard_map/ppermute | solution.py:84
  66.3 5.7 %collective-permute-start.15 = (bf16[592,128]{1,0:T(8,128)(2,1)S(1)}, bf16[592,128]{1,0:T(8,128)(2,1)S(1)}, u32[]{:S(2)}, u32[]{:S(2)}) collective-permute-start(bf16[592,128]{1,0:T(8,128)(2,1)S(1)} %shard_map.100.refs_0_), channel_id=1, source_target_pairs={{0,1},{1,0},{2,3},{3,2},{4,5},{5,4},{6,7},{7,6},{8,9},{9,8},{10,11... | collective-permute-start | bytes 454664 | tf_op jit(solution)/shard_map/ppermute | solution.py:84
  72.0 1.4 %collective-permute-start.16 = (bf16[592,128]{1,0:T(8,128)(2,1)S(1)}, bf16[592,128]{1,0:T(8,128)(2,1)S(1)}, u32[]{:S(2)}, u32[]{:S(2)}) collective-permute-start(bf16[592,128]{1,0:T(8,128)(2,1)S(1)} %collective-permute-done.14.refs_1_), channel_id=1, source_target_pairs={{0,1},{1,0},{2,3},{3,2},{4,5},{5,4},{6,7},{7,6},{8,9},{9,8},{10,11... | collective-permute-start | bytes 454664 | tf_op jit(solution)/shard_map/ppermute | solution.py:84
  84.5 14.0 %collective-permute-start.18 = (bf16[128,768]{1,0:T(8,128)(2,1)S(1)}, bf16[128,768]{1,0:T(8,128)(2,1)S(1)}, u32[]{:S(2)}, u32[]{:S(2)}) collective-permute-start(bf16[128,768]{1,0:T(8,128)(2,1)S(1)} %get-tuple-element.50), channel_id=1, source_target_pairs={{0,4},{1,7},{2,6},{3,5},{4,0},{5,3},{6,2},{7,1},{8,12},{9,15},{10,... | collective-permute-start | bytes 589832 | tf_op jit(solution)/shard_map/ppermute | solution.py:98
  84.8 13.6 %collective-permute-start.17 = (bf16[128,768]{1,0:T(8,128)(2,1)S(1)}, bf16[128,768]{1,0:T(8,128)(2,1)S(1)}, u32[]{:S(2)}, u32[]{:S(2)}) collective-permute-start(bf16[128,768]{1,0:T(8,128)(2,1)S(1)} %get-tuple-element.50), channel_id=1, source_target_pairs={{0,0},{1,3},{2,2},{3,1},{4,4},{5,7},{6,6},{7,5},{8,8},{9,11},{10,1... | collective-permute-start | bytes 589832 | tf_op jit(solution)/shard_map/ppermute | solution.py:98
  85.5 5.7 %collective-permute-start.19 = (bf16[64,768]{1,0:T(8,128)(2,1)S(1)}, bf16[64,768]{1,0:T(8,128)(2,1)S(1)}, u32[]{:S(2)}, u32[]{:S(2)}) collective-permute-start(bf16[64,768]{1,0:T(8,128)(2,1)S(1)} %get-tuple-element.51), channel_id=1, source_target_pairs={{0,8},{1,11},{2,10},{3,9},{4,12},{5,15},{6,14},{7,13},{8,0},{9,3},... | collective-permute-start | bytes 294920 | tf_op jit(solution)/shard_map/ppermute | solution.py:98
  88.0 10.4 %collective-permute-start.20 = (bf16[64,768]{1,0:T(8,128)(2,1)S(1)}, bf16[64,768]{1,0:T(8,128)(2,1)S(1)}, u32[]{:S(2)}, u32[]{:S(2)}) collective-permute-start(bf16[64,768]{1,0:T(8,128)(2,1)S(1)} %get-tuple-element.55), channel_id=1, source_target_pairs={{0,8},{1,11},{2,10},{3,9},{4,12},{5,15},{6,14},{7,13},{8,0},{9,3},... | collective-permute-start | bytes 294920 | tf_op jit(solution)/shard_map/ppermute | solution.py:98
  91.2 9.5 %collective-permute-start.22 = (bf16[64,768]{1,0:T(8,128)(2,1)S(1)}, bf16[64,768]{1,0:T(8,128)(2,1)S(1)}, u32[]{:S(2)}, u32[]{:S(2)}) collective-permute-start(bf16[64,768]{1,0:T(8,128)(2,1)S(1)} %collective-permute-done.19.refs_2_), channel_id=1, source_target_pairs={{0,4},{4,0},{8,12},{12,8},{1,5},{5,1},{9,13},{13,9},{2,6},{6,2},{1... | collective-permute-start | bytes 294920 | tf_op jit(solution)/shard_map/ppermute | solution.py:84
  98.5 5.1 %collective-permute-start.21 = (bf16[64,768]{1,0:T(8,128)(2,1)S(1)}, bf16[64,768]{1,0:T(8,128)(2,1)S(1)}, u32[]{:S(2)}, u32[]{:S(2)}) collective-permute-start(bf16[64,768]{1,0:T(8,128)(2,1)S(1)} %collective-permute-done.20), channel_id=1, source_target_pairs={{0,4},{4,0},{8,12},{12,8},{1,5},{5,1},{9,13},{13,9},{2,6},{6,2},{1... | collective-permute-start | bytes 294920 | tf_op jit(solution)/shard_map/ppermute | solution.py:84
  98.5 6.5 %collective-permute-start.23 = (bf16[128,768]{1,0:T(8,128)(2,1)S(1)}, bf16[128,768]{1,0:T(8,128)(2,1)S(1)}, u32[]{:S(2)}, u32[]{:S(2)}) collective-permute-start(bf16[128,768]{1,0:T(8,128)(2,1)S(1)} %collective-permute-done.17.refs_0_), channel_id=1, source_target_pairs={{0,1},{1,0},{2,3},{3,2},{4,5},{5,4},{6,7},{7,6},{8,9},{9,8},{10,11... | collective-permute-start | bytes 589832 | tf_op jit(solution)/shard_map/ppermute | solution.py:84
  100.2 4.8 %collective-permute-start.24 = (bf16[128,768]{1,0:T(8,128)(2,1)S(1)}, bf16[128,768]{1,0:T(8,128)(2,1)S(1)}, u32[]{:S(2)}, u32[]{:S(2)}) collective-permute-start(bf16[128,768]{1,0:T(8,128)(2,1)S(1)} %collective-permute-done.18.refs_1_), channel_id=1, source_target_pairs={{0,1},{1,0},{2,3},{3,2},{4,5},{5,4},{6,7},{7,6},{8,9},{9,8},{10,11... | collective-permute-start | bytes 589832 | tf_op jit(solution)/shard_map/ppermute | solution.py:84
  100.2 3.7 %collective-permute-start.25 = (bf16[64,768]{1,0:T(8,128)(2,1)S(1)}, bf16[64,768]{1,0:T(8,128)(2,1)S(1)}, u32[]{:S(2)}, u32[]{:S(2)}) collective-permute-start(bf16[64,768]{1,0:T(8,128)(2,1)S(1)} %collective-permute-done.20), channel_id=1, source_target_pairs={{0,1},{1,0},{2,3},{3,2},{4,5},{5,4},{6,7},{7,6},{8,9},{9,8},{10,11... | collective-permute-start | bytes 294920 | tf_op jit(solution)/shard_map/ppermute | solution.py:84
  103.6 1.3 %collective-permute-start.26 = (bf16[64,768]{1,0:T(8,128)(2,1)S(1)}, bf16[64,768]{1,0:T(8,128)(2,1)S(1)}, u32[]{:S(2)}, u32[]{:S(2)}) collective-permute-start(bf16[64,768]{1,0:T(8,128)(2,1)S(1)} %collective-permute-done.21), channel_id=1, source_target_pairs={{0,1},{1,0},{2,3},{3,2},{4,5},{5,4},{6,7},{7,6},{8,9},{9,8},{10,11... | collective-permute-start | bytes 294920 | tf_op jit(solution)/shard_map/ppermute | solution.py:84

commit v11 on v9

--- a/solution.py
+++ b/solution.py
@@ -110,14 +110,6 @@
         c.wait()
 
 
-def give_thin_kernel(idx, grad, attn, give, sems):
-    for which, ref in ((0, attn), (1, grad)):
-
-        @pl.when(idx[3] == which)
-        def _():
-            move([(ref, give)], sems)
-
-
 def give_wide_kernel(dps, idx, norm, hand, sk_q, sk_o, give, sems):
     z, kind = idx[0], idx[3]
     rows, fold = RANK // dps, give.shape[1] // dps
@@ -156,21 +148,17 @@
                 c.wait()
 
 
-def merge_thin_kernel(dps, idx, grad, attn, got, *refs):
-    z, kind, smalls, sems = idx[0], idx[3], refs[:dps], refs[-1]
+def merge_thin_kernel(dps, idx, grad, attn, got_grad, got_attn, *smalls):
+    z, kind = idx[0], idx[3]
     small_w = smalls[0].shape[1] // 2
-
-    def fill(_):
-        for d in range(dps):
-            at = pl.multiple_of((z ^ d) * small_w, small_w)
-            smalls[d][:, small_w:] = got[:, pl.ds(at, small_w)]
-
-    def keep(ref):
-        return [
-            (window(ref, small_w, z ^ d), smalls[d].at[:, :small_w]) for d in range(dps)
-        ]
-
-    merge_kernel(dps, kind, fill, (keep(grad), keep(attn)), sems)
+    for which, keep, got in ((0, grad, got_grad), (1, attn, got_attn)):
+
+        @pl.when(kind == which)
+        def _():
+            for d in range(dps):
+                part = pl.ds(pl.multiple_of((z ^ d) * small_w, small_w), small_w)
+                smalls[d][:, :small_w] = keep[:, part]
+                smalls[d][:, small_w:] = got[:, part]
 
 
 def merge_wide_kernel(dps, idx, norm, hand, sk_q, sk_o, got, *refs):
@@ -490,35 +478,26 @@
     big_w, small_w = wide // dps, narrow // dps
     tokens = dps * BLK
     hbm = pl.BlockSpec(memory_space=pltpu.HBM)
-    norm, grad, attn, hand, sk_q, sk_o = (
+    norm, hand, sk_q, sk_o = (
         pltpu.with_memory_space_constraint(v[0], pltpu.HBM)
-        for v in (norm_in, query_grad, attn_out, handed, sketch_q, sketch_o)
-    )
-
-    give_thin = call(
-        give_thin_kernel,
-        shape(BLK, narrow),
-        (idx, grad, attn),
-        [pltpu.SemaphoreType.DMA((1,))],
-        [SMEM] + [hbm] * 2,
-    )
-    after, give_thin = lax.optimization_barrier((idx, give_thin))
-    got_thin = swap(give_thin, "tensor", 1)
+        for v in (norm_in, handed, sketch_q, sketch_o)
+    )
+
+    got_grad, got_attn = swap(query_grad[0], "tensor", 1), swap(attn_out[0], "tensor", 1)
     give = call(
         functools.partial(give_wide_kernel, dps),
         shape(BLK + RANK // dps, wide),
-        (after, norm, hand, sk_q, sk_o),
+        (idx, norm, hand, sk_q, sk_o),
         [pltpu.SemaphoreType.DMA((1 + dps,))],
         [SMEM] + [hbm] * 4,
     )
-    give, got_thin = lax.optimization_barrier((give, got_thin))
+    give, got_grad, got_attn = lax.optimization_barrier((give, got_grad, got_attn))
     smalls = call(
         functools.partial(merge_thin_kernel, dps),
         [shape(BLK, 2 * small_w)] * dps,
-        (idx, grad, attn, got_thin),
-        [pltpu.SemaphoreType.DMA((dps,))],
-        [SMEM, hbm, hbm, VMEM],
-    )
+        (idx, query_grad[0], attn_out[0], got_grad, got_attn),
+    )
+    smalls = list(smalls)
     got = swap(give, "tensor", 1)
     packed = call(
         functools.partial(merge_wide_kernel, dps),
@@ -577,7 +556,6 @@
     leaves, stays = routed(leaves, sizes, 2, False), routed(stays, sizes, 2, False)
     near, here = routed(whole, sizes, 1, False), routed(whole, sizes, 0, False)
     leaves_on, stays_on = swap(leaves, "dp", 1), swap(stays, "dp", 1)
-    here, near, stays = lax.optimization_barrier((here, near, stays))
     mine = (here, near, stays, stays_on)
     theirs = [swap(v, "tensor", 1) for v in (here, near, leaves, leaves_on)]
     outs = call(

time: 107 us -> 104 us (0.972)
  waiting for transfers between devices: 48 us -> 42.2 us
  starting transfers between devices: 34.6 us -> 39.7 us
  Pallas kernels: 23 us -> 20.6 us
    ppermute x15 -> x16, starting transfers between devices: 16.8 us -> 21.7 us  [swap(): return lax.ppermute(value, axis, [(i, i ^ bit) for i in range(count)])]
    ppermute x13, waiting for transfers between devices: 25 us -> 20.2 us  [routed(): return lax.ppermute(value, ('section', 'dp', 'tensor'), pairs)]
    pallas_call x11 -> x10, Pallas kernels: 23 us -> 20.6 us  [call(): pl.pallas_call(kernel, out_shape=out_shapes, in_specs=spaces, out_specs=j...]
    ppermute x15 -> x16, waiting for transfers between devices: 22.9 us -> 22 us  [swap(): return lax.ppermute(value, axis, [(i, i ^ bit) for i in range(count)])]
  transfers between devices with their start and end apart: 28 -> 29, of which waited for: 11 -> 10; matrix products, arithmetic and copies ran while one was open for 0% -> 0% of each run, Pallas kernels for 6% -> 5%
where the time goes in v11:
time: 104 us; the launch traced here: 103 us
  waiting for transfers between devices  42.2 us (41%)
  starting transfers between devices  39.7 us (38%)
  Pallas kernels  20.6 us (20%)
    ppermute x16, waiting for transfers between devices, swap(): return lax.ppermute(value, axis, [(i, i ^ bit) for i in range(count)])  22 us
    ppermute x16, starting transfers between devices, swap(): return lax.ppermute(value, axis, [(i, i ^ bit) for i in range(count)])  21.7 us
    pallas_call x10, Pallas kernels, call(): pl.pallas_call(kernel, out_shape=out_shapes, in_specs=spaces, out_specs=j...  20.6 us
    ppermute x13, waiting for transfers between devices, routed(): return lax.ppermute(value, ('section', 'dp', 'tensor'), pairs)  20.2 us
    ppermute x13, starting transfers between devices, routed(): return lax.ppermute(value, ('section', 'dp', 'tensor'), pairs)  18 us
  transfers between devices with their start and end apart: 29, of which 10 were waited for; matrix products, arithmetic and copies ran while one was open for 0% of the time, Pallas kernels for 5%

profile of v11, /device:TPU:0, one launch (start us, length us, event | category | flops | bytes accessed | tf_op | source)
XLA Modules:
  0.0 103.4 jit_solution(2763602314577614093)
XLA Ops:
  0.6 0.5 collective-permute-start
  1.1 0.1 collective-permute-start.1
  1.2 0.1 pad_add_fusion.idx
  1.3 1.6 %shard_map.93 = bf16[144,2048]{1,0:T(8,128)(2,1)S(1)} custom-call(s32[4]{0:T(128)S(1)} %pad_add_fusion.idx, bf16[128,2048]{1,0:T(8,128)(2,1)} %bitcast.18, bf16[128,2048]{1,0:T(8,128)(2,1)} %bitcast.20, bf16[64,1024]{1,0:T(8,128)(2,1)} %bitcast.24, bf16[64,2048]{1,0:T(8,128)(2,1)} %bitcast.22), custom_call_target="tpu_custom_call" | custom-call | tf_op jit(solution)/shard_map/pallas_call | solution.py:457
  3.0 0.5 collective-permute-start.7
  3.5 0.6 shard_map.94
  4.1 3.7 %collective-permute-start.2 = (bf16[128,512]{1,0:T(8,128)(2,1)S(1)}, bf16[128,512]{1,0:T(8,128)(2,1)S(1)}, u32[]{:S(2)}, u32[]{:S(2)}) collective-permute-start(bf16[128,512]{1,0:T(8,128)(2,1)S(1)} %get-tuple-element.33), channel_id=1, source_target_pairs={{0,8},{1,11},{2,10},{3,9},{4,12},{5,15},{6,14},{7,13},{8,0},{9,3},... | collective-permute-start | bytes 393224 | tf_op jit(solution)/shard_map/ppermute | solution.py:98
  7.8 1.6 %collective-permute-start.3 = (bf16[128,512]{1,0:T(8,128)(2,1)S(1)}, bf16[128,512]{1,0:T(8,128)(2,1)S(1)}, u32[]{:S(2)}, u32[]{:S(2)}) collective-permute-start(bf16[128,512]{1,0:T(8,128)(2,1)S(1)} %get-tuple-element.34), channel_id=1, source_target_pairs={{0,4},{1,7},{2,6},{3,5},{4,0},{5,3},{6,2},{7,1},{8,12},{9,15},{10,... | collective-permute-start | bytes 393224 | tf_op jit(solution)/shard_map/ppermute | solution.py:98
  9.4 0.7 collective-permute-start.4
  10.1 0.1 collective-permute-start.5
  10.2 0.0 collective-permute-done.7.got
  10.2 1.7 %shard_map.96 = (bf16[128,1024]{1,0:T(8,128)(2,1)S(1)}, bf16[128,1024]{1,0:T(8,128)(2,1)S(1)}, bf16[128,1024]{1,0:T(8,128)(2,1)S(1)}, bf16[128,1024]{1,0:T(8,128)(2,1)S(1)}, bf16[192,512]{1,0:T(8,128)(2,1)S(1)}) custom-call(s32[4]{0:T(128)S(1)} %pad_add_fusion.idx, bf16[128,2048]{1,0:T(8,128)(2,1)} %bitcast.19, bf16[128,2048]{1,0:T(8,128)(2,1)} %bitcast.21, ...), custom_call_target="tpu_custom_call" | custom-call | tf_op jit(solution)/shard_map/pallas_call | solution.py:457
  11.9 1.9 %collective-permute-start.9 = (bf16[128,1024]{1,0:T(8,128)(2,1)S(1)}, bf16[128,1024]{1,0:T(8,128)(2,1)S(1)}, u32[]{:S(2)}, u32[]{:S(2)}) collective-permute-start(bf16[128,1024]{1,0:T(8,128)(2,1)S(1)} %get-tuple-element.41), channel_id=1, source_target_pairs={{0,8},{1,27},{2,26},{3,9},{4,12},{5,31},{6,30},{7,13},{8,0},{9,19}... | collective-permute-start | bytes 786440 | tf_op jit(solution)/shard_map/ppermute | solution.py:98
  13.8 0.6 collective-permute-done.2.refs_0_
  14.4 4.6 %collective-permute-start.10 = (bf16[128,1024]{1,0:T(8,128)(2,1)S(1)}, bf16[128,1024]{1,0:T(8,128)(2,1)S(1)}, u32[]{:S(2)}, u32[]{:S(2)}) collective-permute-start(bf16[128,1024]{1,0:T(8,128)(2,1)S(1)} %get-tuple-element.42), channel_id=1, source_target_pairs={{0,12},{1,31},{2,30},{3,13},{4,8},{5,27},{6,26},{7,9},{8,4},{9,23}... | collective-permute-start | bytes 786440 | tf_op jit(solution)/shard_map/ppermute | solution.py:98
  19.0 0.0 collective-permute-done.3.refs_1_
  19.0 0.7 collective-permute-start.12
  19.7 0.7 collective-permute-start.8
  20.4 1.1 %shard_map.95 = (bf16[512,512]{1,0:T(8,128)(2,1)S(1)}, bf16[528,128]{1,0:T(8,128)(2,1)S(1)}, bf16[528,128]{1,0:T(8,128)(2,1)S(1)}) custom-call(s32[4]{0:T(128)S(1)} %pad_add_fusion.idx, bf16[128,512]{1,0:T(8,128)(2,1)S(1)} %collective-permute-done.2.refs_0_, bf16[128,512]{1,0:T(8,128)(2,1)S(1)} %collective-permute-done.3.refs_1_, ...), custom_call_target="tpu_custom_call" | custom-call | tf_op jit(solution)/shard_map/pallas_call | solution.py:457
  21.6 15.0 %collective-permute-done.9.refs_1_ = bf16[128,1024]{1,0:T(8,128)(2,1)S(1)} collective-permute-done((bf16[128,1024]{1,0:T(8,128)(2,1)S(1)}, bf16[128,1024]{1,0:T(8,128)(2,1)S(1)}, u32[]{:S(2)}, u32[]{:S(2)}) %collective-permute-start.9) | collective-permute-done | bytes 262176 | tf_op jit(solution)/shard_map/ppermute | solution.py:98
  36.6 1.9 %collective-permute-done.11.refs_3_ = bf16[128,1024]{1,0:T(8,128)(2,1)S(1)} collective-permute-done((bf16[128,1024]{1,0:T(8,128)(2,1)S(1)}, bf16[128,1024]{1,0:T(8,128)(2,1)S(1)}, u32[]{:S(2)}, u32[]{:S(2)}) %collective-permute-start.11) | collective-permute-done | bytes 262176 | tf_op jit(solution)/shard_map/ppermute | solution.py:98
  38.5 2.0 %shard_map.97 = (bf16[512,1024]{1,0:T(8,128)(2,1)S(1)}, bf16[656,128]{1,0:T(8,128)(2,1)S(1)}, bf16[656,128]{1,0:T(8,128)(2,1)S(1)}) custom-call(s32[4]{0:T(128)S(1)} %pad_add_fusion.idx, bf16[192,512]{1,0:T(8,128)(2,1)S(1)} %collective-permute-done.8.refs_0_, bf16[128,1024]{1,0:T(8,128)(2,1)S(1)} %collective-permute-done.9.refs_1_, ...), custom_call_target="tpu_custom_call" | custom-call | tf_op jit(solution)/shard_map/pallas_call | solution.py:457
  40.5 2.2 %collective-permute-start.13 = (bf16[656,128]{1,0:T(8,128)(2,1)S(1)}, bf16[656,128]{1,0:T(8,128)(2,1)S(1)}, u32[]{:S(2)}, u32[]{:S(2)}) collective-permute-start(bf16[656,128]{1,0:T(8,128)(2,1)S(1)} %get-tuple-element.47), channel_id=1, source_target_pairs={{0,1},{1,0},{2,3},{3,2},{4,5},{5,4},{6,7},{7,6},{8,9},{9,8},{10,11... | collective-permute-start | bytes 503816 | tf_op jit(solution)/shard_map/ppermute | solution.py:84
  42.7 0.1 collective-permute-start.6
  42.8 1.3 %collective-permute-done.6.thin_got = bf16[528,128]{1,0:T(8,128)(2,1)S(1)} collective-permute-done((bf16[528,128]{1,0:T(8,128)(2,1)S(1)}, bf16[528,128]{1,0:T(8,128)(2,1)S(1)}, u32[]{:S(2)}, u32[]{:S(2)}) %collective-permute-start.6) | collective-permute-done | bytes 135200 | tf_op jit(solution)/shard_map/ppermute | solution.py:84
  44.1 0.7 shard_map.98
  44.8 3.7 %collective-permute-start.14 = (bf16[592,128]{1,0:T(8,128)(2,1)S(1)}, bf16[592,128]{1,0:T(8,128)(2,1)S(1)}, u32[]{:S(2)}, u32[]{:S(2)}) collective-permute-start(bf16[592,128]{1,0:T(8,128)(2,1)S(1)} %get-tuple-element.49), channel_id=1, source_target_pairs={{0,4},{4,0},{8,12},{12,8},{1,5},{5,1},{9,13},{13,9},{2,6},{6,2},{1... | collective-permute-start | bytes 454664 | tf_op jit(solution)/shard_map/ppermute | solution.py:84
  48.5 4.4 %collective-permute-done.14.got = bf16[592,128]{1,0:T(8,128)(2,1)S(1)} collective-permute-done((bf16[592,128]{1,0:T(8,128)(2,1)S(1)}, bf16[592,128]{1,0:T(8,128)(2,1)S(1)}, u32[]{:S(2)}, u32[]{:S(2)}) %collective-permute-start.14) | collective-permute-done | bytes 151584 | tf_op jit(solution)/shard_map/ppermute | solution.py:84
  52.9 3.7 %collective-permute-start.15 = (bf16[592,128]{1,0:T(8,128)(2,1)S(1)}, bf16[592,128]{1,0:T(8,128)(2,1)S(1)}, u32[]{:S(2)}, u32[]{:S(2)}) collective-permute-start(bf16[592,128]{1,0:T(8,128)(2,1)S(1)} %shard_map.99.mine), channel_id=1, source_target_pairs={{0,8},{4,12},{8,0},{12,4},{1,9},{5,13},{9,1},{13,5},{2,10},{6,14},... | collective-permute-start | bytes 454664 | tf_op jit(solution)/shard_map/ppermute | solution.py:84
  56.6 6.8 %collective-permute-done.15.got = bf16[592,128]{1,0:T(8,128)(2,1)S(1)} collective-permute-done((bf16[592,128]{1,0:T(8,128)(2,1)S(1)}, bf16[592,128]{1,0:T(8,128)(2,1)S(1)}, u32[]{:S(2)}, u32[]{:S(2)}) %collective-permute-start.15) | collective-permute-done | bytes 151584 | tf_op jit(solution)/shard_map/ppermute | solution.py:84
  63.5 0.1 collective-permute-start.16
  63.6 0.1 collective-permute-start.17
  63.6 5.6 %collective-permute-done.16.refs_1_ = bf16[592,128]{1,0:T(8,128)(2,1)S(1)} collective-permute-done((bf16[592,128]{1,0:T(8,128)(2,1)S(1)}, bf16[592,128]{1,0:T(8,128)(2,1)S(1)}, u32[]{:S(2)}, u32[]{:S(2)}) %collective-permute-start.16) | collective-permute-done | bytes 151584 | tf_op jit(solution)/shard_map/ppermute | solution.py:84
  69.2 1.4 %collective-permute-done.18.refs_3_ = bf16[592,128]{1,0:T(8,128)(2,1)S(1)} collective-permute-done((bf16[592,128]{1,0:T(8,128)(2,1)S(1)}, bf16[592,128]{1,0:T(8,128)(2,1)S(1)}, u32[]{:S(2)}, u32[]{:S(2)}) %collective-permute-start.18) | collective-permute-done | bytes 151584 | tf_op jit(solution)/shard_map/ppermute | solution.py:84
  70.6 11.1 %shard_map.101 = (bf16[128,768]{1,0:T(8,128)(2,1)S(1)}, bf16[64,768]{1,0:T(8,128)(2,1)S(1)}, bf16[64,768]{1,0:T(8,128)(2,1)S(1)}) custom-call(s32[4]{0:T(128)S(1)} %pad_add_fusion.idx, bf16[592,128]{1,0:T(8,128)(2,1)S(1)} %shard_map.100.refs_0_, bf16[592,128]{1,0:T(8,128)(2,1)S(1)} %collective-permute-done.16.refs_1_, ...), custom_call_target="tpu_custom_call" | custom-call | tf_op jit(solution)/shard_map/pallas_call | solution.py:457
  81.7 0.4 collective-permute-start.20
  82.1 0.7 collective-permute-start.19
  82.7 2.5 %collective-permute-start.25 = (bf16[64,768]{1,0:T(8,128)(2,1)S(1)}, bf16[64,768]{1,0:T(8,128)(2,1)S(1)}, u32[]{:S(2)}, u32[]{:S(2)}) collective-permute-start(bf16[64,768]{1,0:T(8,128)(2,1)S(1)} %get-tuple-element.53), channel_id=1, source_target_pairs={{0,8},{1,11},{2,10},{3,9},{4,12},{5,15},{6,14},{7,13},{8,0},{9,3},... | collective-permute-start | bytes 294920 | tf_op jit(solution)/shard_map/ppermute | solution.py:98
  85.3 0.5 collective-permute-start.21
  85.7 2.7 %collective-permute-done.25 = bf16[64,768]{1,0:T(8,128)(2,1)S(1)} collective-permute-done((bf16[64,768]{1,0:T(8,128)(2,1)S(1)}, bf16[64,768]{1,0:T(8,128)(2,1)S(1)}, u32[]{:S(2)}, u32[]{:S(2)}) %collective-permute-start.25) | collective-permute-done | bytes 98336 | tf_op jit(solution)/shard_map/ppermute | solution.py:98
  88.4 3.1 %collective-permute-start.27 = (bf16[64,768]{1,0:T(8,128)(2,1)S(1)}, bf16[64,768]{1,0:T(8,128)(2,1)S(1)}, u32[]{:S(2)}, u32[]{:S(2)}) collective-permute-start(bf16[64,768]{1,0:T(8,128)(2,1)S(1)} %collective-permute-done.25), channel_id=1, source_target_pairs={{0,4},{4,0},{8,12},{12,8},{1,5},{5,1},{9,13},{13,9},{2,6},{6,2},{1... | collective-permute-start | bytes 294920 | tf_op jit(solution)/shard_map/ppermute | solution.py:84
  91.5 4.2 %collective-permute-start.24 = (bf16[128,768]{1,0:T(8,128)(2,1)S(1)}, bf16[128,768]{1,0:T(8,128)(2,1)S(1)}, u32[]{:S(2)}, u32[]{:S(2)}) collective-permute-start(bf16[128,768]{1,0:T(8,128)(2,1)S(1)} %collective-permute-done.20.refs_1_), channel_id=1, source_target_pairs={{0,1},{1,0},{2,3},{3,2},{4,5},{5,4},{6,7},{7,6},{8,9},{9,8},{10,11... | collective-permute-start | bytes 589832 | tf_op jit(solution)/shard_map/ppermute | solution.py:84
  95.7 0.1 collective-permute-start.23
  95.8 0.4 collective-permute-start.26
  96.2 1.7 %collective-permute-start.22 = (bf16[64,768]{1,0:T(8,128)(2,1)S(1)}, bf16[64,768]{1,0:T(8,128)(2,1)S(1)}, u32[]{:S(2)}, u32[]{:S(2)}) collective-permute-start(bf16[64,768]{1,0:T(8,128)(2,1)S(1)} %collective-permute-done.21.refs_2_), channel_id=1, source_target_pairs={{0,4},{4,0},{8,12},{12,8},{1,5},{5,1},{9,13},{13,9},{2,6},{6,2},{1... | collective-permute-start | bytes 294920 | tf_op jit(solution)/shard_map/ppermute | solution.py:84
  98.0 1.2 %collective-permute-start.28 = (bf16[64,768]{1,0:T(8,128)(2,1)S(1)}, bf16[64,768]{1,0:T(8,128)(2,1)S(1)}, u32[]{:S(2)}, u32[]{:S(2)}) collective-permute-start(bf16[64,768]{1,0:T(8,128)(2,1)S(1)} %collective-permute-done.27), channel_id=1, source_target_pairs={{0,1},{1,0},{2,3},{3,2},{4,5},{5,4},{6,7},{7,6},{8,9},{9,8},{10,11... | collective-permute-start | bytes 294920 | tf_op jit(solution)/shard_map/ppermute | solution.py:84
  99.2 2.5 %collective-permute-done.22.refs_3_ = bf16[64,768]{1,0:T(8,128)(2,1)S(1)} collective-permute-done((bf16[64,768]{1,0:T(8,128)(2,1)S(1)}, bf16[64,768]{1,0:T(8,128)(2,1)S(1)}, u32[]{:S(2)}, u32[]{:S(2)}) %collective-permute-start.22) | collective-permute-done | bytes 98336 | tf_op jit(solution)/shard_map/ppermute | solution.py:84
  101.7 1.7 %shard_map.102 = (bf16[64,2048]{1,0:T(8,128)(2,1)}, f32[64,1024]{1,0:T(8,128)}, bf16[64,1024]{1,0:T(8,128)(2,1)}, f32[64,2048]{1,0:T(8,128)}) custom-call(s32[4]{0:T(128)S(1)} %pad_add_fusion.idx, bf16[128,768]{1,0:T(8,128)(2,1)S(1)} %collective-permute-done.19.refs_0_, bf16[128,768]{1,0:T(8,128)(2,1)S(1)} %collective-permute-done.20.refs_1_, ...), custom_call_target="tpu_custom_call" | custom-call | tf_op jit(solution)/shard_map/pallas_call | solution.py:457
  (25 shorter events, 0.1 us)
Async XLA Ops:
  0.6 2.3 %collective-permute-start = (bf16[128,1024]{1,0:T(8,128)(2,1)}, bf16[128,1024]{1,0:T(8,128)(2,1)S(1)}, u32[]{:S(2)}, u32[]{:S(2)}) collective-permute-start(bf16[128,1024]{1,0:T(8,128)(2,1)} %bitcast.14), channel_id=1, source_target_pairs={{0,1},{1,0},{2,3},{3,2},{4,5},{5,4},{6,7},{7,6},{8,9},{9,8},{10,11... | collective-permute-start | bytes 786440 | tf_op jit(solution)/shard_map/ppermute | solution.py:84
  1.1 1.8 %collective-permute-start.1 = (bf16[128,1024]{1,0:T(8,128)(2,1)}, bf16[128,1024]{1,0:T(8,128)(2,1)S(1)}, u32[]{:S(2)}, u32[]{:S(2)}) collective-permute-start(bf16[128,1024]{1,0:T(8,128)(2,1)} %bitcast.16), channel_id=1, source_target_pairs={{0,1},{1,0},{2,3},{3,2},{4,5},{5,4},{6,7},{7,6},{8,9},{9,8},{10,11... | collective-permute-start | bytes 786440 | tf_op jit(solution)/shard_map/ppermute | solution.py:84
  1.3 2.2 %copy-start = (bf16[1,128,1024]{2,1,0:T(8,128)(2,1)S(1)}, bf16[1,128,1024]{2,1,0:T(8,128)(2,1)}, u32[]{:S(2)}) copy-start(bf16[1,128,1024]{2,1,0:T(8,128)(2,1)} %param.7) | copy-start | bytes 786436
  1.3 2.2 %copy-start.1 = (bf16[1,128,1024]{2,1,0:T(8,128)(2,1)S(1)}, bf16[1,128,1024]{2,1,0:T(8,128)(2,1)}, u32[]{:S(2)}) copy-start(bf16[1,128,1024]{2,1,0:T(8,128)(2,1)} %param.8) | copy-start | bytes 786436
  3.0 7.2 %collective-permute-start.7 = (bf16[144,2048]{1,0:T(8,128)(2,1)S(1)}, bf16[144,2048]{1,0:T(8,128)(2,1)S(1)}, u32[]{:S(2)}, u32[]{:S(2)}) collective-permute-start(bf16[144,2048]{1,0:T(8,128)(2,1)S(1)} %shard_map.93), channel_id=1, source_target_pairs={{0,1},{1,0},{2,3},{3,2},{4,5},{5,4},{6,7},{7,6},{8,9},{9,8},{10,11... | collective-permute-start | bytes 1769480 | tf_op jit(solution)/shard_map/ppermute | solution.py:84
  4.1 10.3 %collective-permute-start.2 = (bf16[128,512]{1,0:T(8,128)(2,1)S(1)}, bf16[128,512]{1,0:T(8,128)(2,1)S(1)}, u32[]{:S(2)}, u32[]{:S(2)}) collective-permute-start(bf16[128,512]{1,0:T(8,128)(2,1)S(1)} %get-tuple-element.33), channel_id=1, source_target_pairs={{0,8},{1,11},{2,10},{3,9},{4,12},{5,15},{6,14},{7,13},{8,0},{9,3},... | collective-permute-start | bytes 393224 | tf_op jit(solution)/shard_map/ppermute | solution.py:98
  7.8 11.2 %collective-permute-start.3 = (bf16[128,512]{1,0:T(8,128)(2,1)S(1)}, bf16[128,512]{1,0:T(8,128)(2,1)S(1)}, u32[]{:S(2)}, u32[]{:S(2)}) collective-permute-start(bf16[128,512]{1,0:T(8,128)(2,1)S(1)} %get-tuple-element.34), channel_id=1, source_target_pairs={{0,4},{1,7},{2,6},{3,5},{4,0},{5,3},{6,2},{7,1},{8,12},{9,15},{10,... | collective-permute-start | bytes 393224 | tf_op jit(solution)/shard_map/ppermute | solution.py:98
  9.4 9.6 %collective-permute-start.4 = (bf16[128,512]{1,0:T(8,128)(2,1)S(1)}, bf16[128,512]{1,0:T(8,128)(2,1)S(1)}, u32[]{:S(2)}, u32[]{:S(2)}) collective-permute-start(bf16[128,512]{1,0:T(8,128)(2,1)S(1)} %get-tuple-element.35), channel_id=1, source_target_pairs={{0,0},{1,3},{2,2},{3,1},{4,4},{5,7},{6,6},{7,5},{8,8},{9,11},{10,1... | collective-permute-start | bytes 393224 | tf_op jit(solution)/shard_map/ppermute | solution.py:98
  10.1 9.6 %collective-permute-start.5 = (bf16[128,512]{1,0:T(8,128)(2,1)S(1)}, bf16[128,512]{1,0:T(8,128)(2,1)S(1)}, u32[]{:S(2)}, u32[]{:S(2)}) collective-permute-start(bf16[128,512]{1,0:T(8,128)(2,1)S(1)} %get-tuple-element.36), channel_id=1, source_target_pairs={{0,12},{1,15},{2,14},{3,13},{4,8},{5,11},{6,10},{7,9},{8,4},{9,7},... | collective-permute-start | bytes 393224 | tf_op jit(solution)/shard_map/ppermute | solution.py:98
  11.9 24.7 %collective-permute-start.9 = (bf16[128,1024]{1,0:T(8,128)(2,1)S(1)}, bf16[128,1024]{1,0:T(8,128)(2,1)S(1)}, u32[]{:S(2)}, u32[]{:S(2)}) collective-permute-start(bf16[128,1024]{1,0:T(8,128)(2,1)S(1)} %get-tuple-element.41), channel_id=1, source_target_pairs={{0,8},{1,27},{2,26},{3,9},{4,12},{5,31},{6,30},{7,13},{8,0},{9,19}... | collective-permute-start | bytes 786440 | tf_op jit(solution)/shard_map/ppermute | solution.py:98
  14.4 22.2 %collective-permute-start.10 = (bf16[128,1024]{1,0:T(8,128)(2,1)S(1)}, bf16[128,1024]{1,0:T(8,128)(2,1)S(1)}, u32[]{:S(2)}, u32[]{:S(2)}) collective-permute-start(bf16[128,1024]{1,0:T(8,128)(2,1)S(1)} %get-tuple-element.42), channel_id=1, source_target_pairs={{0,12},{1,31},{2,30},{3,13},{4,8},{5,27},{6,26},{7,9},{8,4},{9,23}... | collective-permute-start | bytes 786440 | tf_op jit(solution)/shard_map/ppermute | solution.py:98
  19.0 19.4 %collective-permute-start.11 = (bf16[128,1024]{1,0:T(8,128)(2,1)S(1)}, bf16[128,1024]{1,0:T(8,128)(2,1)S(1)}, u32[]{:S(2)}, u32[]{:S(2)}) collective-permute-start(bf16[128,1024]{1,0:T(8,128)(2,1)S(1)} %get-tuple-element.43), channel_id=1, source_target_pairs={{0,4},{1,23},{2,22},{3,5},{4,0},{5,19},{6,18},{7,1},{8,12},{9,31},... | collective-permute-start | bytes 786440 | tf_op jit(solution)/shard_map/ppermute | solution.py:98
  19.0 19.4 %collective-permute-start.12 = (bf16[128,1024]{1,0:T(8,128)(2,1)S(1)}, bf16[128,1024]{1,0:T(8,128)(2,1)S(1)}, u32[]{:S(2)}, u32[]{:S(2)}) collective-permute-start(bf16[128,1024]{1,0:T(8,128)(2,1)S(1)} %get-tuple-element.44), channel_id=1, source_target_pairs={{0,0},{1,19},{2,18},{3,1},{4,4},{5,23},{6,22},{7,5},{8,8},{9,27},{... | collective-permute-start | bytes 786440 | tf_op jit(solution)/shard_map/ppermute | solution.py:98
  19.7 1.8 %collective-permute-start.8 = (bf16[192,512]{1,0:T(8,128)(2,1)S(1)}, bf16[192,512]{1,0:T(8,128)(2,1)S(1)}, u32[]{:S(2)}, u32[]{:S(2)}) collective-permute-start(bf16[192,512]{1,0:T(8,128)(2,1)S(1)} %get-tuple-element.40), channel_id=1, source_target_pairs={{0,0},{1,3},{2,2},{3,1},{4,4},{5,7},{6,6},{7,5},{8,8},{9,11},{10,1... | collective-permute-start | bytes 589832 | tf_op jit(solution)/shard_map/ppermute | solution.py:98
  40.5 3.6 %collective-permute-start.13 = (bf16[656,128]{1,0:T(8,128)(2,1)S(1)}, bf16[656,128]{1,0:T(8,128)(2,1)S(1)}, u32[]{:S(2)}, u32[]{:S(2)}) collective-permute-start(bf16[656,128]{1,0:T(8,128)(2,1)S(1)} %get-tuple-element.47), channel_id=1, source_target_pairs={{0,1},{1,0},{2,3},{3,2},{4,5},{5,4},{6,7},{7,6},{8,9},{9,8},{10,11... | collective-permute-start | bytes 503816 | tf_op jit(solution)/shard_map/ppermute | solution.py:84
  42.7 1.4 %collective-permute-start.6 = (bf16[528,128]{1,0:T(8,128)(2,1)S(1)}, bf16[528,128]{1,0:T(8,128)(2,1)S(1)}, u32[]{:S(2)}, u32[]{:S(2)}) collective-permute-start(bf16[528,128]{1,0:T(8,128)(2,1)S(1)} %get-tuple-element.38), channel_id=1, source_target_pairs={{0,1},{1,0},{2,3},{3,2},{4,5},{5,4},{6,7},{7,6},{8,9},{9,8},{10,11... | collective-permute-start | bytes 405512 | tf_op jit(solution)/shard_map/ppermute | solution.py:84
  44.8 8.1 %collective-permute-start.14 = (bf16[592,128]{1,0:T(8,128)(2,1)S(1)}, bf16[592,128]{1,0:T(8,128)(2,1)S(1)}, u32[]{:S(2)}, u32[]{:S(2)}) collective-permute-start(bf16[592,128]{1,0:T(8,128)(2,1)S(1)} %get-tuple-element.49), channel_id=1, source_target_pairs={{0,4},{4,0},{8,12},{12,8},{1,5},{5,1},{9,13},{13,9},{2,6},{6,2},{1... | collective-permute-start | bytes 454664 | tf_op jit(solution)/shard_map/ppermute | solution.py:84
  52.9 10.5 %collective-permute-start.15 = (bf16[592,128]{1,0:T(8,128)(2,1)S(1)}, bf16[592,128]{1,0:T(8,128)(2,1)S(1)}, u32[]{:S(2)}, u32[]{:S(2)}) collective-permute-start(bf16[592,128]{1,0:T(8,128)(2,1)S(1)} %shard_map.99.mine), channel_id=1, source_target_pairs={{0,8},{4,12},{8,0},{12,4},{1,9},{5,13},{9,1},{13,5},{2,10},{6,14},... | collective-permute-start | bytes 454664 | tf_op jit(solution)/shard_map/ppermute | solution.py:84
  63.5 5.8 %collective-permute-start.16 = (bf16[592,128]{1,0:T(8,128)(2,1)S(1)}, bf16[592,128]{1,0:T(8,128)(2,1)S(1)}, u32[]{:S(2)}, u32[]{:S(2)}) collective-permute-start(bf16[592,128]{1,0:T(8,128)(2,1)S(1)} %shard_map.100.refs_0_), channel_id=1, source_target_pairs={{0,4},{4,0},{8,12},{12,8},{1,5},{5,1},{9,13},{13,9},{2,6},{6,2},{1... | collective-permute-start | bytes 454664 | tf_op jit(solution)/shard_map/ppermute | solution.py:84
  63.6 5.7 %collective-permute-start.17 = (bf16[592,128]{1,0:T(8,128)(2,1)S(1)}, bf16[592,128]{1,0:T(8,128)(2,1)S(1)}, u32[]{:S(2)}, u32[]{:S(2)}) collective-permute-start(bf16[592,128]{1,0:T(8,128)(2,1)S(1)} %shard_map.100.refs_0_), channel_id=1, source_target_pairs={{0,1},{1,0},{2,3},{3,2},{4,5},{5,4},{6,7},{7,6},{8,9},{9,8},{10,11... | collective-permute-start | bytes 454664 | tf_op jit(solution)/shard_map/ppermute | solution.py:84
  69.2 1.4 %collective-permute-start.18 = (bf16[592,128]{1,0:T(8,128)(2,1)S(1)}, bf16[592,128]{1,0:T(8,128)(2,1)S(1)}, u32[]{:S(2)}, u32[]{:S(2)}) collective-permute-start(bf16[592,128]{1,0:T(8,128)(2,1)S(1)} %collective-permute-done.16.refs_1_), channel_id=1, source_target_pairs={{0,1},{1,0},{2,3},{3,2},{4,5},{5,4},{6,7},{7,6},{8,9},{9,8},{10,11... | collective-permute-start | bytes 454664 | tf_op jit(solution)/shard_map/ppermute | solution.py:84
  81.7 9.8 %collective-permute-start.20 = (bf16[128,768]{1,0:T(8,128)(2,1)S(1)}, bf16[128,768]{1,0:T(8,128)(2,1)S(1)}, u32[]{:S(2)}, u32[]{:S(2)}) collective-permute-start(bf16[128,768]{1,0:T(8,128)(2,1)S(1)} %get-tuple-element.51), channel_id=1, source_target_pairs={{0,4},{1,7},{2,6},{3,5},{4,0},{5,3},{6,2},{7,1},{8,12},{9,15},{10,... | collective-permute-start | bytes 589832 | tf_op jit(solution)/shard_map/ppermute | solution.py:98
  82.1 13.6 %collective-permute-start.19 = (bf16[128,768]{1,0:T(8,128)(2,1)S(1)}, bf16[128,768]{1,0:T(8,128)(2,1)S(1)}, u32[]{:S(2)}, u32[]{:S(2)}) collective-permute-start(bf16[128,768]{1,0:T(8,128)(2,1)S(1)} %get-tuple-element.51), channel_id=1, source_target_pairs={{0,0},{1,3},{2,2},{3,1},{4,4},{5,7},{6,6},{7,5},{8,8},{9,11},{10,1... | collective-permute-start | bytes 589832 | tf_op jit(solution)/shard_map/ppermute | solution.py:98
  82.7 5.7 %collective-permute-start.25 = (bf16[64,768]{1,0:T(8,128)(2,1)S(1)}, bf16[64,768]{1,0:T(8,128)(2,1)S(1)}, u32[]{:S(2)}, u32[]{:S(2)}) collective-permute-start(bf16[64,768]{1,0:T(8,128)(2,1)S(1)} %get-tuple-element.53), channel_id=1, source_target_pairs={{0,8},{1,11},{2,10},{3,9},{4,12},{5,15},{6,14},{7,13},{8,0},{9,3},... | collective-permute-start | bytes 294920 | tf_op jit(solution)/shard_map/ppermute | solution.py:98
  85.3 10.9 %collective-permute-start.21 = (bf16[64,768]{1,0:T(8,128)(2,1)S(1)}, bf16[64,768]{1,0:T(8,128)(2,1)S(1)}, u32[]{:S(2)}, u32[]{:S(2)}) collective-permute-start(bf16[64,768]{1,0:T(8,128)(2,1)S(1)} %get-tuple-element.52), channel_id=1, source_target_pairs={{0,8},{1,11},{2,10},{3,9},{4,12},{5,15},{6,14},{7,13},{8,0},{9,3},... | collective-permute-start | bytes 294920 | tf_op jit(solution)/shard_map/ppermute | solution.py:98
  88.4 9.5 %collective-permute-start.27 = (bf16[64,768]{1,0:T(8,128)(2,1)S(1)}, bf16[64,768]{1,0:T(8,128)(2,1)S(1)}, u32[]{:S(2)}, u32[]{:S(2)}) collective-permute-start(bf16[64,768]{1,0:T(8,128)(2,1)S(1)} %collective-permute-done.25), channel_id=1, source_target_pairs={{0,4},{4,0},{8,12},{12,8},{1,5},{5,1},{9,13},{13,9},{2,6},{6,2},{1... | collective-permute-start | bytes 294920 | tf_op jit(solution)/shard_map/ppermute | solution.py:84
  91.5 10.2 %collective-permute-start.24 = (bf16[128,768]{1,0:T(8,128)(2,1)S(1)}, bf16[128,768]{1,0:T(8,128)(2,1)S(1)}, u32[]{:S(2)}, u32[]{:S(2)}) collective-permute-start(bf16[128,768]{1,0:T(8,128)(2,1)S(1)} %collective-permute-done.20.refs_1_), channel_id=1, source_target_pairs={{0,1},{1,0},{2,3},{3,2},{4,5},{5,4},{6,7},{7,6},{8,9},{9,8},{10,11... | collective-permute-start | bytes 589832 | tf_op jit(solution)/shard_map/ppermute | solution.py:84
  95.7 6.0 %collective-permute-start.23 = (bf16[128,768]{1,0:T(8,128)(2,1)S(1)}, bf16[128,768]{1,0:T(8,128)(2,1)S(1)}, u32[]{:S(2)}, u32[]{:S(2)}) collective-permute-start(bf16[128,768]{1,0:T(8,128)(2,1)S(1)} %collective-permute-done.19.refs_0_), channel_id=1, source_target_pairs={{0,1},{1,0},{2,3},{3,2},{4,5},{5,4},{6,7},{7,6},{8,9},{9,8},{10,11... | collective-permute-start | bytes 589832 | tf_op jit(solution)/shard_map/ppermute | solution.py:84
  95.8 5.9 %collective-permute-start.26 = (bf16[64,768]{1,0:T(8,128)(2,1)S(1)}, bf16[64,768]{1,0:T(8,128)(2,1)S(1)}, u32[]{:S(2)}, u32[]{:S(2)}) collective-permute-start(bf16[64,768]{1,0:T(8,128)(2,1)S(1)} %collective-permute-done.25), channel_id=1, source_target_pairs={{0,1},{1,0},{2,3},{3,2},{4,5},{5,4},{6,7},{7,6},{8,9},{9,8},{10,11... | collective-permute-start | bytes 294920 | tf_op jit(solution)/shard_map/ppermute | solution.py:84
  96.2 5.5 %collective-permute-start.22 = (bf16[64,768]{1,0:T(8,128)(2,1)S(1)}, bf16[64,768]{1,0:T(8,128)(2,1)S(1)}, u32[]{:S(2)}, u32[]{:S(2)}) collective-permute-start(bf16[64,768]{1,0:T(8,128)(2,1)S(1)} %collective-permute-done.21.refs_2_), channel_id=1, source_target_pairs={{0,4},{4,0},{8,12},{12,8},{1,5},{5,1},{9,13},{13,9},{2,6},{6,2},{1... | collective-permute-start | bytes 294920 | tf_op jit(solution)/shard_map/ppermute | solution.py:84
  98.0 3.7 %collective-permute-start.28 = (bf16[64,768]{1,0:T(8,128)(2,1)S(1)}, bf16[64,768]{1,0:T(8,128)(2,1)S(1)}, u32[]{:S(2)}, u32[]{:S(2)}) collective-permute-start(bf16[64,768]{1,0:T(8,128)(2,1)S(1)} %collective-permute-done.27), channel_id=1, source_target_pairs={{0,1},{1,0},{2,3},{3,2},{4,5},{5,4},{6,7},{7,6},{8,9},{9,8},{10,11... | collective-permute-start | bytes 294920 | tf_op jit(solution)/shard_map/ppermute | solution.py:84

commit v12 on v11

--- a/solution.py
+++ b/solution.py
@@ -433,23 +433,44 @@
         out[n * RANK : (n + 1) * RANK, :] = half[...]
 
 
-def place_kernel(dps, idx, *refs):
-    z, kind = idx[0], idx[3]
-    mine, theirs = refs[:dps], refs[dps : 2 * dps]
-    b_q, a_q, b_o, a_o = refs[2 * dps :]
-    big_w, small_w = b_q.shape[1] // dps, a_q.shape[1] // dps
-    for d in range(dps):
-        bigs = pl.ds(pl.multiple_of((z ^ d) * big_w, big_w), big_w)
-        smalls = pl.ds(pl.multiple_of((z ^ d) * small_w, small_w), small_w)
-        here, there = mine[d].at[:RANK], theirs[d].at[theirs[d].shape[0] - RANK :]
-        for which, query, output in ((0, here, there), (1, there, here)):
-
-            @pl.when(kind == which)
+def place_kernel(which, idx, *refs):
+    z, kind, n = idx[0], idx[3], len(which)
+    mine, theirs = refs[:n], refs[n : 2 * n]
+    outs, held, sems = refs[-9:-5], refs[-5:-1], refs[-1]
+    for i in range(n):
+        here, there = mine[i].at[:RANK], theirs[i].at[theirs[i].shape[0] - RANK :]
+        b_q, a_q, b_o, a_o = (h.at[i] for h in held)
+        big_w = b_q.shape[1]
+        for half, query, output in ((0, here, there), (1, there, here)):
+
+            @pl.when(kind == half)
             def _():
-                b_q[:, bigs] = query[:, :big_w]
-                a_q[:, smalls] = query[:, big_w:].astype(f32)
-                a_o[:, bigs] = output[:, :big_w].astype(f32)
-                b_o[:, smalls] = output[:, big_w:]
+                b_q[...] = query[:, :big_w]
+                a_q[...] = query[:, big_w:].astype(f32)
+                a_o[...] = output[:, :big_w].astype(f32)
+                b_o[...] = output[:, big_w:]
+
+    pairs = [
+        (h.at[i], window(out, h.shape[2], z ^ d))
+        for i, d in enumerate(which)
+        for h, out in zip(held, outs)
+    ]
+    move(pairs, sems)
+
+
+def place(which, idx, mine, theirs, shapes, widths, outs=()):
+    n = len(which)
+    hbm = pl.BlockSpec(memory_space=pl.ANY)
+    return pl.pallas_call(
+        functools.partial(place_kernel, which),
+        out_shape=shapes,
+        in_specs=[SMEM] + [VMEM] * (2 * n) + [hbm] * len(outs),
+        out_specs=[hbm] * len(shapes),
+        scratch_shapes=[pltpu.VMEM((n, RANK, w), s.dtype) for w, s in zip(widths, shapes)]
+        + [pltpu.SemaphoreType.DMA((n * len(shapes),))],
+        input_output_aliases={2 * n + 1 + i: i for i in range(len(outs))},
+        compiler_params=pltpu.CompilerParams(vmem_limit_bytes=48 * 2**20),
+    )(idx, *mine, *theirs, *outs)
 
 
 def call(kernel, out_shapes, args, scratch=(), spaces=()):
@@ -558,16 +579,15 @@
     leaves_on, stays_on = swap(leaves, "dp", 1), swap(stays, "dp", 1)
     mine = (here, near, stays, stays_on)
     theirs = [swap(v, "tensor", 1) for v in (here, near, leaves, leaves_on)]
-    outs = call(
-        functools.partial(place_kernel, dps),
-        [
-            shape(RANK, wide),
-            shape(RANK, narrow, dtype=f32),
-            shape(RANK, narrow),
-            shape(RANK, wide, dtype=f32),
-        ],
-        (idx, *mine, *theirs),
-    )
+    shapes = [
+        shape(RANK, wide),
+        shape(RANK, narrow, dtype=f32),
+        shape(RANK, narrow),
+        shape(RANK, wide, dtype=f32),
+    ]
+    widths = (big_w, small_w, small_w, big_w)
+    outs = place((0, 1, 2), idx, mine[:3], theirs[:3], shapes, widths)
+    outs = place((3,), idx, mine[3:], theirs[3:], shapes, widths, outs)
     return tuple(o[None] for o in outs)
 
 

time: 104 us -> 102 us (0.981)
  starting transfers between devices: 39.7 us -> 37 us
  Pallas kernels: 20.6 us -> 21.9 us
    pallas_call x0 -> x2, Pallas kernels: none -> 2.94 us  [place(): pl.pallas_call(functools.partial(place_kernel, which), out_shape=shapes,...]
    ppermute x16, starting transfers between devices: 21.7 us -> 19.1 us  [swap(): return lax.ppermute(value, axis, [(i, i ^ bit) for i in range(count)])]
    ppermute x13, waiting for transfers between devices: 20.2 us -> 22.2 us  [routed(): return lax.ppermute(value, ('section', 'dp', 'tensor'), pairs)]
    ppermute x16, waiting for transfers between devices: 22 us -> 20.1 us  [swap(): return lax.ppermute(value, axis, [(i, i ^ bit) for i in range(count)])]
    pallas_call x10 -> x9, Pallas kernels: 20.6 us -> 19 us  [call(): pl.pallas_call(kernel, out_shape=out_shapes, in_specs=spaces, out_specs=j...]
  transfers between devices with their start and end apart: 29 -> 29, of which waited for: 10 -> 12; matrix products, arithmetic and copies ran while one was open for 0% -> 0% of each run, Pallas kernels for 5% -> 7%
where the time goes in v12:
time: 102 us
  waiting for transfers between devices  42.4 us (42%)
  starting transfers between devices  37 us (36%)
  Pallas kernels  21.9 us (21%)
    ppermute x13, waiting for transfers between devices, routed(): return lax.ppermute(value, ('section', 'dp', 'tensor'), pairs)  22.2 us
    ppermute x16, waiting for transfers between devices, swap(): return lax.ppermute(value, axis, [(i, i ^ bit) for i in range(count)])  20.1 us
    ppermute x16, starting transfers between devices, swap(): return lax.ppermute(value, axis, [(i, i ^ bit) for i in range(count)])  19.1 us
    pallas_call x9, Pallas kernels, call(): pl.pallas_call(kernel, out_shape=out_shapes, in_specs=spaces, out_specs=j...  19 us
    ppermute x13, starting transfers between devices, routed(): return lax.ppermute(value, ('section', 'dp', 'tensor'), pairs)  18 us
    pallas_call x2, Pallas kernels, place(): pl.pallas_call(functools.partial(place_kernel, which), out_shape=shapes,...  2.94 us
  transfers between devices with their start and end apart: 29, of which 12 were waited for; matrix products, arithmetic and copies ran while one was open for 0% of the time, Pallas kernels for 7%

profile of v12, /device:TPU:0, one launch (start us, length us, event | category | flops | bytes accessed | tf_op | source)
XLA Modules:
  0.0 102.2 jit_solution(3803524286477248927)
XLA Ops:
  0.6 0.5 collective-permute-start
  1.1 0.1 collective-permute-start.1
  1.2 0.1 pad_add_fusion.idx
  1.3 1.6 %shard_map.93 = bf16[144,2048]{1,0:T(8,128)(2,1)S(1)} custom-call(s32[4]{0:T(128)S(1)} %pad_add_fusion.idx, bf16[128,2048]{1,0:T(8,128)(2,1)} %bitcast.18, bf16[128,2048]{1,0:T(8,128)(2,1)} %bitcast.20, bf16[64,1024]{1,0:T(8,128)(2,1)} %bitcast.25, bf16[64,2048]{1,0:T(8,128)(2,1)} %bitcast.22), custom_call_target="tpu_custom_call" | custom-call | tf_op jit(solution)/shard_map/pallas_call | solution.py:478
  3.0 0.5 collective-permute-start.7
  3.5 0.6 shard_map.94
  4.1 3.7 %collective-permute-start.2 = (bf16[128,512]{1,0:T(8,128)(2,1)S(1)}, bf16[128,512]{1,0:T(8,128)(2,1)S(1)}, u32[]{:S(2)}, u32[]{:S(2)}) collective-permute-start(bf16[128,512]{1,0:T(8,128)(2,1)S(1)} %get-tuple-element.37), channel_id=1, source_target_pairs={{0,8},{1,11},{2,10},{3,9},{4,12},{5,15},{6,14},{7,13},{8,0},{9,3},... | collective-permute-start | bytes 393224 | tf_op jit(solution)/shard_map/ppermute | solution.py:98
  7.8 1.6 %collective-permute-start.3 = (bf16[128,512]{1,0:T(8,128)(2,1)S(1)}, bf16[128,512]{1,0:T(8,128)(2,1)S(1)}, u32[]{:S(2)}, u32[]{:S(2)}) collective-permute-start(bf16[128,512]{1,0:T(8,128)(2,1)S(1)} %get-tuple-element.38), channel_id=1, source_target_pairs={{0,4},{1,7},{2,6},{3,5},{4,0},{5,3},{6,2},{7,1},{8,12},{9,15},{10,... | collective-permute-start | bytes 393224 | tf_op jit(solution)/shard_map/ppermute | solution.py:98
  9.4 0.7 collective-permute-start.4
  10.1 0.1 collective-permute-start.5
  10.2 1.7 %shard_map.96 = (bf16[128,1024]{1,0:T(8,128)(2,1)S(1)}, bf16[128,1024]{1,0:T(8,128)(2,1)S(1)}, bf16[128,1024]{1,0:T(8,128)(2,1)S(1)}, bf16[128,1024]{1,0:T(8,128)(2,1)S(1)}, bf16[192,512]{1,0:T(8,128)(2,1)S(1)}) custom-call(s32[4]{0:T(128)S(1)} %pad_add_fusion.idx, bf16[128,2048]{1,0:T(8,128)(2,1)} %bitcast.19, bf16[128,2048]{1,0:T(8,128)(2,1)} %bitcast.21, ...), custom_call_target="tpu_custom_call" | custom-call | tf_op jit(solution)/shard_map/pallas_call | solution.py:478
  11.9 1.9 %collective-permute-start.9 = (bf16[128,1024]{1,0:T(8,128)(2,1)S(1)}, bf16[128,1024]{1,0:T(8,128)(2,1)S(1)}, u32[]{:S(2)}, u32[]{:S(2)}) collective-permute-start(bf16[128,1024]{1,0:T(8,128)(2,1)S(1)} %get-tuple-element.45), channel_id=1, source_target_pairs={{0,8},{1,27},{2,26},{3,9},{4,12},{5,31},{6,30},{7,13},{8,0},{9,19}... | collective-permute-start | bytes 786440 | tf_op jit(solution)/shard_map/ppermute | solution.py:98
  13.8 0.6 collective-permute-done.2.refs_0_
  14.4 4.6 %collective-permute-start.10 = (bf16[128,1024]{1,0:T(8,128)(2,1)S(1)}, bf16[128,1024]{1,0:T(8,128)(2,1)S(1)}, u32[]{:S(2)}, u32[]{:S(2)}) collective-permute-start(bf16[128,1024]{1,0:T(8,128)(2,1)S(1)} %get-tuple-element.46), channel_id=1, source_target_pairs={{0,12},{1,31},{2,30},{3,13},{4,8},{5,27},{6,26},{7,9},{8,4},{9,23}... | collective-permute-start | bytes 786440 | tf_op jit(solution)/shard_map/ppermute | solution.py:98
  19.0 0.7 collective-permute-start.12
  19.7 0.7 collective-permute-start.8
  20.4 1.1 %shard_map.95 = (bf16[512,512]{1,0:T(8,128)(2,1)S(1)}, bf16[528,128]{1,0:T(8,128)(2,1)S(1)}, bf16[528,128]{1,0:T(8,128)(2,1)S(1)}) custom-call(s32[4]{0:T(128)S(1)} %pad_add_fusion.idx, bf16[128,512]{1,0:T(8,128)(2,1)S(1)} %collective-permute-done.2.refs_0_, bf16[128,512]{1,0:T(8,128)(2,1)S(1)} %collective-permute-done.3.refs_1_, ...), custom_call_target="tpu_custom_call" | custom-call | tf_op jit(solution)/shard_map/pallas_call | solution.py:478
  21.6 15.0 %collective-permute-done.9.refs_1_ = bf16[128,1024]{1,0:T(8,128)(2,1)S(1)} collective-permute-done((bf16[128,1024]{1,0:T(8,128)(2,1)S(1)}, bf16[128,1024]{1,0:T(8,128)(2,1)S(1)}, u32[]{:S(2)}, u32[]{:S(2)}) %collective-permute-start.9) | collective-permute-done | bytes 262176 | tf_op jit(solution)/shard_map/ppermute | solution.py:98
  36.6 1.9 %collective-permute-done.11.refs_3_ = bf16[128,1024]{1,0:T(8,128)(2,1)S(1)} collective-permute-done((bf16[128,1024]{1,0:T(8,128)(2,1)S(1)}, bf16[128,1024]{1,0:T(8,128)(2,1)S(1)}, u32[]{:S(2)}, u32[]{:S(2)}) %collective-permute-start.11) | collective-permute-done | bytes 262176 | tf_op jit(solution)/shard_map/ppermute | solution.py:98
  38.5 2.0 %shard_map.97 = (bf16[512,1024]{1,0:T(8,128)(2,1)S(1)}, bf16[656,128]{1,0:T(8,128)(2,1)S(1)}, bf16[656,128]{1,0:T(8,128)(2,1)S(1)}) custom-call(s32[4]{0:T(128)S(1)} %pad_add_fusion.idx, bf16[192,512]{1,0:T(8,128)(2,1)S(1)} %collective-permute-done.8.refs_0_, bf16[128,1024]{1,0:T(8,128)(2,1)S(1)} %collective-permute-done.9.refs_1_, ...), custom_call_target="tpu_custom_call" | custom-call | tf_op jit(solution)/shard_map/pallas_call | solution.py:478
  40.5 2.2 %collective-permute-start.13 = (bf16[656,128]{1,0:T(8,128)(2,1)S(1)}, bf16[656,128]{1,0:T(8,128)(2,1)S(1)}, u32[]{:S(2)}, u32[]{:S(2)}) collective-permute-start(bf16[656,128]{1,0:T(8,128)(2,1)S(1)} %get-tuple-element.51), channel_id=1, source_target_pairs={{0,1},{1,0},{2,3},{3,2},{4,5},{5,4},{6,7},{7,6},{8,9},{9,8},{10,11... | collective-permute-start | bytes 503816 | tf_op jit(solution)/shard_map/ppermute | solution.py:84
  42.7 0.1 collective-permute-start.6
  42.8 1.3 %collective-permute-done.6.thin_got = bf16[528,128]{1,0:T(8,128)(2,1)S(1)} collective-permute-done((bf16[528,128]{1,0:T(8,128)(2,1)S(1)}, bf16[528,128]{1,0:T(8,128)(2,1)S(1)}, u32[]{:S(2)}, u32[]{:S(2)}) %collective-permute-start.6) | collective-permute-done | bytes 135200 | tf_op jit(solution)/shard_map/ppermute | solution.py:84
  44.1 0.7 shard_map.98
  44.8 3.7 %collective-permute-start.14 = (bf16[592,128]{1,0:T(8,128)(2,1)S(1)}, bf16[592,128]{1,0:T(8,128)(2,1)S(1)}, u32[]{:S(2)}, u32[]{:S(2)}) collective-permute-start(bf16[592,128]{1,0:T(8,128)(2,1)S(1)} %get-tuple-element.53), channel_id=1, source_target_pairs={{0,4},{4,0},{8,12},{12,8},{1,5},{5,1},{9,13},{13,9},{2,6},{6,2},{1... | collective-permute-start | bytes 454664 | tf_op jit(solution)/shard_map/ppermute | solution.py:84
  48.5 4.4 %collective-permute-done.14.got = bf16[592,128]{1,0:T(8,128)(2,1)S(1)} collective-permute-done((bf16[592,128]{1,0:T(8,128)(2,1)S(1)}, bf16[592,128]{1,0:T(8,128)(2,1)S(1)}, u32[]{:S(2)}, u32[]{:S(2)}) %collective-permute-start.14) | collective-permute-done | bytes 151584 | tf_op jit(solution)/shard_map/ppermute | solution.py:84
  52.9 3.7 %collective-permute-start.15 = (bf16[592,128]{1,0:T(8,128)(2,1)S(1)}, bf16[592,128]{1,0:T(8,128)(2,1)S(1)}, u32[]{:S(2)}, u32[]{:S(2)}) collective-permute-start(bf16[592,128]{1,0:T(8,128)(2,1)S(1)} %shard_map.99.mine), channel_id=1, source_target_pairs={{0,8},{4,12},{8,0},{12,4},{1,9},{5,13},{9,1},{13,5},{2,10},{6,14},... | collective-permute-start | bytes 454664 | tf_op jit(solution)/shard_map/ppermute | solution.py:84
  56.6 6.8 %collective-permute-done.15.got = bf16[592,128]{1,0:T(8,128)(2,1)S(1)} collective-permute-done((bf16[592,128]{1,0:T(8,128)(2,1)S(1)}, bf16[592,128]{1,0:T(8,128)(2,1)S(1)}, u32[]{:S(2)}, u32[]{:S(2)}) %collective-permute-start.15) | collective-permute-done | bytes 151584 | tf_op jit(solution)/shard_map/ppermute | solution.py:84
  63.5 0.1 collective-permute-start.16
  63.6 0.1 collective-permute-start.17
  63.6 5.6 %collective-permute-done.16.refs_1_ = bf16[592,128]{1,0:T(8,128)(2,1)S(1)} collective-permute-done((bf16[592,128]{1,0:T(8,128)(2,1)S(1)}, bf16[592,128]{1,0:T(8,128)(2,1)S(1)}, u32[]{:S(2)}, u32[]{:S(2)}) %collective-permute-start.16) | collective-permute-done | bytes 151584 | tf_op jit(solution)/shard_map/ppermute | solution.py:84
  69.2 1.4 %collective-permute-done.18.refs_3_ = bf16[592,128]{1,0:T(8,128)(2,1)S(1)} collective-permute-done((bf16[592,128]{1,0:T(8,128)(2,1)S(1)}, bf16[592,128]{1,0:T(8,128)(2,1)S(1)}, u32[]{:S(2)}, u32[]{:S(2)}) %collective-permute-start.18) | collective-permute-done | bytes 151584 | tf_op jit(solution)/shard_map/ppermute | solution.py:84
  70.6 11.1 %shard_map.101 = (bf16[128,768]{1,0:T(8,128)(2,1)S(1)}, bf16[64,768]{1,0:T(8,128)(2,1)S(1)}, bf16[64,768]{1,0:T(8,128)(2,1)S(1)}) custom-call(s32[4]{0:T(128)S(1)} %pad_add_fusion.idx, bf16[592,128]{1,0:T(8,128)(2,1)S(1)} %shard_map.100.refs_0_, bf16[592,128]{1,0:T(8,128)(2,1)S(1)} %collective-permute-done.16.refs_1_, ...), custom_call_target="tpu_custom_call" | custom-call | tf_op jit(solution)/shard_map/pallas_call | solution.py:478
  81.7 0.4 collective-permute-start.25
  82.1 0.7 collective-permute-start.24
  82.7 2.5 %collective-permute-start.21 = (bf16[64,768]{1,0:T(8,128)(2,1)S(1)}, bf16[64,768]{1,0:T(8,128)(2,1)S(1)}, u32[]{:S(2)}, u32[]{:S(2)}) collective-permute-start(bf16[64,768]{1,0:T(8,128)(2,1)S(1)} %get-tuple-element.56), channel_id=1, source_target_pairs={{0,8},{1,11},{2,10},{3,9},{4,12},{5,15},{6,14},{7,13},{8,0},{9,3},... | collective-permute-start | bytes 294920 | tf_op jit(solution)/shard_map/ppermute | solution.py:98
  85.3 0.5 collective-permute-start.19
  85.7 4.6 %collective-permute-done.25.refs_1_ = bf16[128,768]{1,0:T(8,128)(2,1)S(1)} collective-permute-done((bf16[128,768]{1,0:T(8,128)(2,1)S(1)}, bf16[128,768]{1,0:T(8,128)(2,1)S(1)}, u32[]{:S(2)}, u32[]{:S(2)}) %collective-permute-start.25) | collective-permute-done | bytes 196640 | tf_op jit(solution)/shard_map/ppermute | solution.py:98
  90.3 0.5 collective-permute-start.26
  90.8 1.1 %collective-permute-start.22 = (bf16[64,768]{1,0:T(8,128)(2,1)S(1)}, bf16[64,768]{1,0:T(8,128)(2,1)S(1)}, u32[]{:S(2)}, u32[]{:S(2)}) collective-permute-start(bf16[64,768]{1,0:T(8,128)(2,1)S(1)} %collective-permute-done.21), channel_id=1, source_target_pairs={{0,4},{4,0},{8,12},{12,8},{1,5},{5,1},{9,13},{13,9},{2,6},{6,2},{1... | collective-permute-start | bytes 294920 | tf_op jit(solution)/shard_map/ppermute | solution.py:84
  91.9 3.7 %collective-permute-start.28 = (bf16[64,768]{1,0:T(8,128)(2,1)S(1)}, bf16[64,768]{1,0:T(8,128)(2,1)S(1)}, u32[]{:S(2)}, u32[]{:S(2)}) collective-permute-start(bf16[64,768]{1,0:T(8,128)(2,1)S(1)} %collective-permute-done.21), channel_id=1, source_target_pairs={{0,1},{1,0},{2,3},{3,2},{4,5},{5,4},{6,7},{7,6},{8,9},{9,8},{10,11... | collective-permute-start | bytes 294920 | tf_op jit(solution)/shard_map/ppermute | solution.py:84
  95.6 0.1 collective-permute-done.19.refs_2_
  95.8 1.6 %collective-permute-start.20 = (bf16[64,768]{1,0:T(8,128)(2,1)S(1)}, bf16[64,768]{1,0:T(8,128)(2,1)S(1)}, u32[]{:S(2)}, u32[]{:S(2)}) collective-permute-start(bf16[64,768]{1,0:T(8,128)(2,1)S(1)} %collective-permute-done.19.refs_2_), channel_id=1, source_target_pairs={{0,4},{4,0},{8,12},{12,8},{1,5},{5,1},{9,13},{13,9},{2,6},{6,2},{1... | collective-permute-start | bytes 294920 | tf_op jit(solution)/shard_map/ppermute | solution.py:84
  97.4 0.6 collective-permute-done.22
  97.9 1.2 %collective-permute-start.23 = (bf16[64,768]{1,0:T(8,128)(2,1)S(1)}, bf16[64,768]{1,0:T(8,128)(2,1)S(1)}, u32[]{:S(2)}, u32[]{:S(2)}) collective-permute-start(bf16[64,768]{1,0:T(8,128)(2,1)S(1)} %collective-permute-done.22), channel_id=1, source_target_pairs={{0,1},{1,0},{2,3},{3,2},{4,5},{5,4},{6,7},{7,6},{8,9},{9,8},{10,11... | collective-permute-start | bytes 294920 | tf_op jit(solution)/shard_map/ppermute | solution.py:84
  99.1 1.6 %shard_map.102 = (bf16[64,2048]{1,0:T(8,128)(2,1)}, f32[64,1024]{1,0:T(8,128)}, bf16[64,1024]{1,0:T(8,128)(2,1)}, f32[64,2048]{1,0:T(8,128)}) custom-call(s32[4]{0:T(128)S(1)} %pad_add_fusion.idx, bf16[128,768]{1,0:T(8,128)(2,1)S(1)} %collective-permute-done.24.refs_0_, bf16[128,768]{1,0:T(8,128)(2,1)S(1)} %collective-permute-done.25.refs_1_, ...), custom_call_target="tpu_custom_call" | custom-call | tf_op jit(solution)/shard_map/pallas_call | solution.py:464
  100.7 0.1 collective-permute-done.20.refs_0_
  100.9 1.3 %shard_map.103 = (bf16[64,2048]{1,0:T(8,128)(2,1)}, f32[64,1024]{1,0:T(8,128)}, bf16[64,1024]{1,0:T(8,128)(2,1)}, f32[64,2048]{1,0:T(8,128)}) custom-call(s32[4]{0:T(128)S(1)} %pad_add_fusion.idx, bf16[64,768]{1,0:T(8,128)(2,1)S(1)} %collective-permute-done.20.refs_0_, ...), custom_call_target="tpu_custom_call", output_to_operand_aliasing={{0}: (3, {}), {1}: (4, {}), {2}: (5, {}), {3}: (6, {})} | custom-call | tf_op jit(solution)/shard_map/pallas_call | solution.py:464
  (26 shorter events, 0.1 us)
Async XLA Ops:
  0.6 2.3 %collective-permute-start = (bf16[128,1024]{1,0:T(8,128)(2,1)}, bf16[128,1024]{1,0:T(8,128)(2,1)S(1)}, u32[]{:S(2)}, u32[]{:S(2)}) collective-permute-start(bf16[128,1024]{1,0:T(8,128)(2,1)} %bitcast.14), channel_id=1, source_target_pairs={{0,1},{1,0},{2,3},{3,2},{4,5},{5,4},{6,7},{7,6},{8,9},{9,8},{10,11... | collective-permute-start | bytes 786440 | tf_op jit(solution)/shard_map/ppermute | solution.py:84
  1.1 1.8 %collective-permute-start.1 = (bf16[128,1024]{1,0:T(8,128)(2,1)}, bf16[128,1024]{1,0:T(8,128)(2,1)S(1)}, u32[]{:S(2)}, u32[]{:S(2)}) collective-permute-start(bf16[128,1024]{1,0:T(8,128)(2,1)} %bitcast.16), channel_id=1, source_target_pairs={{0,1},{1,0},{2,3},{3,2},{4,5},{5,4},{6,7},{7,6},{8,9},{9,8},{10,11... | collective-permute-start | bytes 786440 | tf_op jit(solution)/shard_map/ppermute | solution.py:84
  1.3 2.2 %copy-start = (bf16[1,128,1024]{2,1,0:T(8,128)(2,1)S(1)}, bf16[1,128,1024]{2,1,0:T(8,128)(2,1)}, u32[]{:S(2)}) copy-start(bf16[1,128,1024]{2,1,0:T(8,128)(2,1)} %param.7) | copy-start | bytes 786436
  1.3 2.2 %copy-start.1 = (bf16[1,128,1024]{2,1,0:T(8,128)(2,1)S(1)}, bf16[1,128,1024]{2,1,0:T(8,128)(2,1)}, u32[]{:S(2)}) copy-start(bf16[1,128,1024]{2,1,0:T(8,128)(2,1)} %param.8) | copy-start | bytes 786436
  3.0 7.2 %collective-permute-start.7 = (bf16[144,2048]{1,0:T(8,128)(2,1)S(1)}, bf16[144,2048]{1,0:T(8,128)(2,1)S(1)}, u32[]{:S(2)}, u32[]{:S(2)}) collective-permute-start(bf16[144,2048]{1,0:T(8,128)(2,1)S(1)} %shard_map.93), channel_id=1, source_target_pairs={{0,1},{1,0},{2,3},{3,2},{4,5},{5,4},{6,7},{7,6},{8,9},{9,8},{10,11... | collective-permute-start | bytes 1769480 | tf_op jit(solution)/shard_map/ppermute | solution.py:84
  4.1 10.3 %collective-permute-start.2 = (bf16[128,512]{1,0:T(8,128)(2,1)S(1)}, bf16[128,512]{1,0:T(8,128)(2,1)S(1)}, u32[]{:S(2)}, u32[]{:S(2)}) collective-permute-start(bf16[128,512]{1,0:T(8,128)(2,1)S(1)} %get-tuple-element.37), channel_id=1, source_target_pairs={{0,8},{1,11},{2,10},{3,9},{4,12},{5,15},{6,14},{7,13},{8,0},{9,3},... | collective-permute-start | bytes 393224 | tf_op jit(solution)/shard_map/ppermute | solution.py:98
  7.8 11.2 %collective-permute-start.3 = (bf16[128,512]{1,0:T(8,128)(2,1)S(1)}, bf16[128,512]{1,0:T(8,128)(2,1)S(1)}, u32[]{:S(2)}, u32[]{:S(2)}) collective-permute-start(bf16[128,512]{1,0:T(8,128)(2,1)S(1)} %get-tuple-element.38), channel_id=1, source_target_pairs={{0,4},{1,7},{2,6},{3,5},{4,0},{5,3},{6,2},{7,1},{8,12},{9,15},{10,... | collective-permute-start | bytes 393224 | tf_op jit(solution)/shard_map/ppermute | solution.py:98
  9.4 9.6 %collective-permute-start.4 = (bf16[128,512]{1,0:T(8,128)(2,1)S(1)}, bf16[128,512]{1,0:T(8,128)(2,1)S(1)}, u32[]{:S(2)}, u32[]{:S(2)}) collective-permute-start(bf16[128,512]{1,0:T(8,128)(2,1)S(1)} %get-tuple-element.39), channel_id=1, source_target_pairs={{0,0},{1,3},{2,2},{3,1},{4,4},{5,7},{6,6},{7,5},{8,8},{9,11},{10,1... | collective-permute-start | bytes 393224 | tf_op jit(solution)/shard_map/ppermute | solution.py:98
  10.1 9.6 %collective-permute-start.5 = (bf16[128,512]{1,0:T(8,128)(2,1)S(1)}, bf16[128,512]{1,0:T(8,128)(2,1)S(1)}, u32[]{:S(2)}, u32[]{:S(2)}) collective-permute-start(bf16[128,512]{1,0:T(8,128)(2,1)S(1)} %get-tuple-element.40), channel_id=1, source_target_pairs={{0,12},{1,15},{2,14},{3,13},{4,8},{5,11},{6,10},{7,9},{8,4},{9,7},... | collective-permute-start | bytes 393224 | tf_op jit(solution)/shard_map/ppermute | solution.py:98
  11.9 24.7 %collective-permute-start.9 = (bf16[128,1024]{1,0:T(8,128)(2,1)S(1)}, bf16[128,1024]{1,0:T(8,128)(2,1)S(1)}, u32[]{:S(2)}, u32[]{:S(2)}) collective-permute-start(bf16[128,1024]{1,0:T(8,128)(2,1)S(1)} %get-tuple-element.45), channel_id=1, source_target_pairs={{0,8},{1,27},{2,26},{3,9},{4,12},{5,31},{6,30},{7,13},{8,0},{9,19}... | collective-permute-start | bytes 786440 | tf_op jit(solution)/shard_map/ppermute | solution.py:98
  14.4 22.2 %collective-permute-start.10 = (bf16[128,1024]{1,0:T(8,128)(2,1)S(1)}, bf16[128,1024]{1,0:T(8,128)(2,1)S(1)}, u32[]{:S(2)}, u32[]{:S(2)}) collective-permute-start(bf16[128,1024]{1,0:T(8,128)(2,1)S(1)} %get-tuple-element.46), channel_id=1, source_target_pairs={{0,12},{1,31},{2,30},{3,13},{4,8},{5,27},{6,26},{7,9},{8,4},{9,23}... | collective-permute-start | bytes 786440 | tf_op jit(solution)/shard_map/ppermute | solution.py:98
  19.0 19.4 %collective-permute-start.11 = (bf16[128,1024]{1,0:T(8,128)(2,1)S(1)}, bf16[128,1024]{1,0:T(8,128)(2,1)S(1)}, u32[]{:S(2)}, u32[]{:S(2)}) collective-permute-start(bf16[128,1024]{1,0:T(8,128)(2,1)S(1)} %get-tuple-element.47), channel_id=1, source_target_pairs={{0,4},{1,23},{2,22},{3,5},{4,0},{5,19},{6,18},{7,1},{8,12},{9,31},... | collective-permute-start | bytes 786440 | tf_op jit(solution)/shard_map/ppermute | solution.py:98
  19.0 19.4 %collective-permute-start.12 = (bf16[128,1024]{1,0:T(8,128)(2,1)S(1)}, bf16[128,1024]{1,0:T(8,128)(2,1)S(1)}, u32[]{:S(2)}, u32[]{:S(2)}) collective-permute-start(bf16[128,1024]{1,0:T(8,128)(2,1)S(1)} %get-tuple-element.48), channel_id=1, source_target_pairs={{0,0},{1,19},{2,18},{3,1},{4,4},{5,23},{6,22},{7,5},{8,8},{9,27},{... | collective-permute-start | bytes 786440 | tf_op jit(solution)/shard_map/ppermute | solution.py:98
  19.7 1.8 %collective-permute-start.8 = (bf16[192,512]{1,0:T(8,128)(2,1)S(1)}, bf16[192,512]{1,0:T(8,128)(2,1)S(1)}, u32[]{:S(2)}, u32[]{:S(2)}) collective-permute-start(bf16[192,512]{1,0:T(8,128)(2,1)S(1)} %get-tuple-element.44), channel_id=1, source_target_pairs={{0,0},{1,3},{2,2},{3,1},{4,4},{5,7},{6,6},{7,5},{8,8},{9,11},{10,1... | collective-permute-start | bytes 589832 | tf_op jit(solution)/shard_map/ppermute | solution.py:98
  40.5 3.6 %collective-permute-start.13 = (bf16[656,128]{1,0:T(8,128)(2,1)S(1)}, bf16[656,128]{1,0:T(8,128)(2,1)S(1)}, u32[]{:S(2)}, u32[]{:S(2)}) collective-permute-start(bf16[656,128]{1,0:T(8,128)(2,1)S(1)} %get-tuple-element.51), channel_id=1, source_target_pairs={{0,1},{1,0},{2,3},{3,2},{4,5},{5,4},{6,7},{7,6},{8,9},{9,8},{10,11... | collective-permute-start | bytes 503816 | tf_op jit(solution)/shard_map/ppermute | solution.py:84
  42.7 1.4 %collective-permute-start.6 = (bf16[528,128]{1,0:T(8,128)(2,1)S(1)}, bf16[528,128]{1,0:T(8,128)(2,1)S(1)}, u32[]{:S(2)}, u32[]{:S(2)}) collective-permute-start(bf16[528,128]{1,0:T(8,128)(2,1)S(1)} %get-tuple-element.42), channel_id=1, source_target_pairs={{0,1},{1,0},{2,3},{3,2},{4,5},{5,4},{6,7},{7,6},{8,9},{9,8},{10,11... | collective-permute-start | bytes 405512 | tf_op jit(solution)/shard_map/ppermute | solution.py:84
  44.8 8.1 %collective-permute-start.14 = (bf16[592,128]{1,0:T(8,128)(2,1)S(1)}, bf16[592,128]{1,0:T(8,128)(2,1)S(1)}, u32[]{:S(2)}, u32[]{:S(2)}) collective-permute-start(bf16[592,128]{1,0:T(8,128)(2,1)S(1)} %get-tuple-element.53), channel_id=1, source_target_pairs={{0,4},{4,0},{8,12},{12,8},{1,5},{5,1},{9,13},{13,9},{2,6},{6,2},{1... | collective-permute-start | bytes 454664 | tf_op jit(solution)/shard_map/ppermute | solution.py:84
  52.9 10.5 %collective-permute-start.15 = (bf16[592,128]{1,0:T(8,128)(2,1)S(1)}, bf16[592,128]{1,0:T(8,128)(2,1)S(1)}, u32[]{:S(2)}, u32[]{:S(2)}) collective-permute-start(bf16[592,128]{1,0:T(8,128)(2,1)S(1)} %shard_map.99.mine), channel_id=1, source_target_pairs={{0,8},{4,12},{8,0},{12,4},{1,9},{5,13},{9,1},{13,5},{2,10},{6,14},... | collective-permute-start | bytes 454664 | tf_op jit(solution)/shard_map/ppermute | solution.py:84
  63.5 5.8 %collective-permute-start.16 = (bf16[592,128]{1,0:T(8,128)(2,1)S(1)}, bf16[592,128]{1,0:T(8,128)(2,1)S(1)}, u32[]{:S(2)}, u32[]{:S(2)}) collective-permute-start(bf16[592,128]{1,0:T(8,128)(2,1)S(1)} %shard_map.100.refs_0_), channel_id=1, source_target_pairs={{0,4},{4,0},{8,12},{12,8},{1,5},{5,1},{9,13},{13,9},{2,6},{6,2},{1... | collective-permute-start | bytes 454664 | tf_op jit(solution)/shard_map/ppermute | solution.py:84
  63.6 5.7 %collective-permute-start.17 = (bf16[592,128]{1,0:T(8,128)(2,1)S(1)}, bf16[592,128]{1,0:T(8,128)(2,1)S(1)}, u32[]{:S(2)}, u32[]{:S(2)}) collective-permute-start(bf16[592,128]{1,0:T(8,128)(2,1)S(1)} %shard_map.100.refs_0_), channel_id=1, source_target_pairs={{0,1},{1,0},{2,3},{3,2},{4,5},{5,4},{6,7},{7,6},{8,9},{9,8},{10,11... | collective-permute-start | bytes 454664 | tf_op jit(solution)/shard_map/ppermute | solution.py:84
  69.2 1.4 %collective-permute-start.18 = (bf16[592,128]{1,0:T(8,128)(2,1)S(1)}, bf16[592,128]{1,0:T(8,128)(2,1)S(1)}, u32[]{:S(2)}, u32[]{:S(2)}) collective-permute-start(bf16[592,128]{1,0:T(8,128)(2,1)S(1)} %collective-permute-done.16.refs_1_), channel_id=1, source_target_pairs={{0,1},{1,0},{2,3},{3,2},{4,5},{5,4},{6,7},{7,6},{8,9},{9,8},{10,11... | collective-permute-start | bytes 454664 | tf_op jit(solution)/shard_map/ppermute | solution.py:84
  81.7 8.6 %collective-permute-start.25 = (bf16[128,768]{1,0:T(8,128)(2,1)S(1)}, bf16[128,768]{1,0:T(8,128)(2,1)S(1)}, u32[]{:S(2)}, u32[]{:S(2)}) collective-permute-start(bf16[128,768]{1,0:T(8,128)(2,1)S(1)} %get-tuple-element.57), channel_id=1, source_target_pairs={{0,4},{1,7},{2,6},{3,5},{4,0},{5,3},{6,2},{7,1},{8,12},{9,15},{10,... | collective-permute-start | bytes 589832 | tf_op jit(solution)/shard_map/ppermute | solution.py:98
  82.1 8.3 %collective-permute-start.24 = (bf16[128,768]{1,0:T(8,128)(2,1)S(1)}, bf16[128,768]{1,0:T(8,128)(2,1)S(1)}, u32[]{:S(2)}, u32[]{:S(2)}) collective-permute-start(bf16[128,768]{1,0:T(8,128)(2,1)S(1)} %get-tuple-element.57), channel_id=1, source_target_pairs={{0,0},{1,3},{2,2},{3,1},{4,4},{5,7},{6,6},{7,5},{8,8},{9,11},{10,1... | collective-permute-start | bytes 589832 | tf_op jit(solution)/shard_map/ppermute | solution.py:98
  82.7 8.1 %collective-permute-start.21 = (bf16[64,768]{1,0:T(8,128)(2,1)S(1)}, bf16[64,768]{1,0:T(8,128)(2,1)S(1)}, u32[]{:S(2)}, u32[]{:S(2)}) collective-permute-start(bf16[64,768]{1,0:T(8,128)(2,1)S(1)} %get-tuple-element.56), channel_id=1, source_target_pairs={{0,8},{1,11},{2,10},{3,9},{4,12},{5,15},{6,14},{7,13},{8,0},{9,3},... | collective-permute-start | bytes 294920 | tf_op jit(solution)/shard_map/ppermute | solution.py:98
  85.3 10.5 %collective-permute-start.19 = (bf16[64,768]{1,0:T(8,128)(2,1)S(1)}, bf16[64,768]{1,0:T(8,128)(2,1)S(1)}, u32[]{:S(2)}, u32[]{:S(2)}) collective-permute-start(bf16[64,768]{1,0:T(8,128)(2,1)S(1)} %get-tuple-element.55), channel_id=1, source_target_pairs={{0,8},{1,11},{2,10},{3,9},{4,12},{5,15},{6,14},{7,13},{8,0},{9,3},... | collective-permute-start | bytes 294920 | tf_op jit(solution)/shard_map/ppermute | solution.py:98
  90.3 8.8 %collective-permute-start.27 = (bf16[128,768]{1,0:T(8,128)(2,1)S(1)}, bf16[128,768]{1,0:T(8,128)(2,1)S(1)}, u32[]{:S(2)}, u32[]{:S(2)}) collective-permute-start(bf16[128,768]{1,0:T(8,128)(2,1)S(1)} %collective-permute-done.25.refs_1_), channel_id=1, source_target_pairs={{0,1},{1,0},{2,3},{3,2},{4,5},{5,4},{6,7},{7,6},{8,9},{9,8},{10,11... | collective-permute-start | bytes 589832 | tf_op jit(solution)/shard_map/ppermute | solution.py:84
  90.3 8.8 %collective-permute-start.26 = (bf16[128,768]{1,0:T(8,128)(2,1)S(1)}, bf16[128,768]{1,0:T(8,128)(2,1)S(1)}, u32[]{:S(2)}, u32[]{:S(2)}) collective-permute-start(bf16[128,768]{1,0:T(8,128)(2,1)S(1)} %collective-permute-done.24.refs_0_), channel_id=1, source_target_pairs={{0,1},{1,0},{2,3},{3,2},{4,5},{5,4},{6,7},{7,6},{8,9},{9,8},{10,11... | collective-permute-start | bytes 589832 | tf_op jit(solution)/shard_map/ppermute | solution.py:84
  90.8 7.1 %collective-permute-start.22 = (bf16[64,768]{1,0:T(8,128)(2,1)S(1)}, bf16[64,768]{1,0:T(8,128)(2,1)S(1)}, u32[]{:S(2)}, u32[]{:S(2)}) collective-permute-start(bf16[64,768]{1,0:T(8,128)(2,1)S(1)} %collective-permute-done.21), channel_id=1, source_target_pairs={{0,4},{4,0},{8,12},{12,8},{1,5},{5,1},{9,13},{13,9},{2,6},{6,2},{1... | collective-permute-start | bytes 294920 | tf_op jit(solution)/shard_map/ppermute | solution.py:84
  91.9 7.1 %collective-permute-start.28 = (bf16[64,768]{1,0:T(8,128)(2,1)S(1)}, bf16[64,768]{1,0:T(8,128)(2,1)S(1)}, u32[]{:S(2)}, u32[]{:S(2)}) collective-permute-start(bf16[64,768]{1,0:T(8,128)(2,1)S(1)} %collective-permute-done.21), channel_id=1, source_target_pairs={{0,1},{1,0},{2,3},{3,2},{4,5},{5,4},{6,7},{7,6},{8,9},{9,8},{10,11... | collective-permute-start | bytes 294920 | tf_op jit(solution)/shard_map/ppermute | solution.py:84
  95.8 5.1 %collective-permute-start.20 = (bf16[64,768]{1,0:T(8,128)(2,1)S(1)}, bf16[64,768]{1,0:T(8,128)(2,1)S(1)}, u32[]{:S(2)}, u32[]{:S(2)}) collective-permute-start(bf16[64,768]{1,0:T(8,128)(2,1)S(1)} %collective-permute-done.19.refs_2_), channel_id=1, source_target_pairs={{0,4},{4,0},{8,12},{12,8},{1,5},{5,1},{9,13},{13,9},{2,6},{6,2},{1... | collective-permute-start | bytes 294920 | tf_op jit(solution)/shard_map/ppermute | solution.py:84
  97.9 2.9 %collective-permute-start.23 = (bf16[64,768]{1,0:T(8,128)(2,1)S(1)}, bf16[64,768]{1,0:T(8,128)(2,1)S(1)}, u32[]{:S(2)}, u32[]{:S(2)}) collective-permute-start(bf16[64,768]{1,0:T(8,128)(2,1)S(1)} %collective-permute-done.22), channel_id=1, source_target_pairs={{0,1},{1,0},{2,3},{3,2},{4,5},{5,4},{6,7},{7,6},{8,9},{9,8},{10,11... | collective-permute-start | bytes 294920 | tf_op jit(solution)/shard_map/ppermute | solution.py:84

commit v13 on v12

--- a/solution.py
+++ b/solution.py
@@ -167,9 +167,11 @@
     rows = RANK // dps
 
     def fill(which):
+        own = hand if which else norm
         for d in range(dps):
-            at = pl.multiple_of((z ^ d) * big_w, big_w)
-            bigs[d][:, big_w:] = got[:BLK, pl.ds(at, big_w)]
+            part = pl.ds(pl.multiple_of((z ^ d) * big_w, big_w), big_w)
+            bigs[d][:, :big_w] = own[:, part]
+            bigs[d][:, big_w:] = got[:BLK, part]
         for i in range(dps):
             part = got[BLK:, i * big_w : (i + 1) * big_w]
             one, two = RANK + i * rows, 2 * RANK + i * rows
@@ -184,14 +186,9 @@
         else:
             sk[2 * RANK :, :small_w] = jnp.zeros((RANK, small_w), bf16)
 
-    def keep(ref, sketch):
-        return [sketch] + [
-            (window(ref, big_w, z ^ d), bigs[d].at[:, :big_w]) for d in range(dps)
-        ]
-
     pairs = (
-        keep(norm, (window(sk_q, small_w, z), sk.at[2 * RANK :, :small_w])),
-        keep(hand, (window(sk_o, big_w, z), sk.at[:RANK, :])),
+        [(window(sk_q, small_w, z), sk.at[2 * RANK :, :small_w])],
+        [(window(sk_o, big_w, z), sk.at[:RANK, :])],
     )
     merge_kernel(dps, kind, fill, pairs, sems)
 
@@ -405,12 +402,8 @@
         inner = product_nt(beyond, ahead)
         low_inv = inverse_factor(gram, spread)
         rows = product(low_inv, ahead)
-        if step < 2 * POWER - 1:
-            gram = product_nt(product(low_inv, inner), low_inv)
-            ahead = product(low_inv, beyond)
-        else:
-            ahead = times(rows, following)
-            gram = product_nt(ahead, rows)
+        gram = product_nt(product(low_inv, inner), low_inv)
+        ahead = product(low_inv, beyond)
     low_inv = inverse_factor(gram, spread)
     basis = product(low_inv, rows)
     rows = product(low_inv, ahead)
@@ -523,9 +516,9 @@
     packed = call(
         functools.partial(merge_wide_kernel, dps),
         [shape(BLK, 2 * big_w)] * dps + [shape(3 * RANK, 2 * small_w)],
-        (idx, norm, hand, sk_q, sk_o, got),
-        [pltpu.SemaphoreType.DMA((dps + 1,))],
-        [SMEM, hbm, hbm, hbm, hbm, VMEM],
+        (idx, norm_in[0], handed[0], sk_q, sk_o, got),
+        [pltpu.SemaphoreType.DMA((1,))],
+        [SMEM, VMEM, VMEM, hbm, hbm, VMEM],
     )
     smalls = [routed(smalls[d], sizes, d, False) for d in THIN_ORDER]
     sketch = routed(packed[dps], sizes, 0, False)

time: 102 us -> 102 us (level)
  transfers between devices with their start and end apart: 29 -> 29, of which waited for: 12 -> 12; matrix products, arithmetic and copies ran while one was open for 0% -> 0% of each run, Pallas kernels for 7% -> 6%
where the time goes in v13:
time: 102 us
  waiting for transfers between devices  42.8 us (42%)
  starting transfers between devices  37 us (36%)
  Pallas kernels  21.4 us (21%)
    ppermute x13, waiting for transfers between devices, routed(): return lax.ppermute(value, ('section', 'dp', 'tensor'), pairs)  22.6 us
    ppermute x16, waiting for transfers between devices, swap(): return lax.ppermute(value, axis, [(i, i ^ bit) for i in range(count)])  20.2 us
    ppermute x16, starting transfers between devices, swap(): return lax.ppermute(value, axis, [(i, i ^ bit) for i in range(count)])  19 us
    pallas_call x9, Pallas kernels, call(): pl.pallas_call(kernel, out_shape=out_shapes, in_specs=spaces, out_specs=j...  18.5 us
    ppermute x13, starting transfers between devices, routed(): return lax.ppermute(value, ('section', 'dp', 'tensor'), pairs)  18 us
    pallas_call x2, Pallas kernels, place(): pl.pallas_call(functools.partial(place_kernel, which), out_shape=shapes,...  2.94 us
  transfers between devices with their start and end apart: 29, of which 12 were waited for; matrix products, arithmetic and copies ran while one was open for 0% of the time, Pallas kernels for 6%

profile of v13, /device:TPU:0, one launch (start us, length us, event | category | flops | bytes accessed | tf_op | source)
XLA Modules:
  0.0 102.1 jit_solution(17229058169270731711)
XLA Ops:
  0.6 0.5 collective-permute-start
  1.1 0.1 collective-permute-start.1
  1.2 0.1 pad_add_fusion.idx
  1.3 1.6 %shard_map.93 = bf16[144,2048]{1,0:T(8,128)(2,1)S(1)} custom-call(s32[4]{0:T(128)S(1)} %pad_add_fusion.idx, bf16[128,2048]{1,0:T(8,128)(2,1)} %bitcast.14, bf16[128,2048]{1,0:T(8,128)(2,1)} %bitcast.16, bf16[64,1024]{1,0:T(8,128)(2,1)} %bitcast.25, bf16[64,2048]{1,0:T(8,128)(2,1)} %bitcast.22), custom_call_target="tpu_custom_call" | custom-call | tf_op jit(solution)/shard_map/pallas_call | solution.py:471
  3.0 0.5 collective-permute-start.7
  3.5 0.6 shard_map.94
  4.1 3.7 %collective-permute-start.2 = (bf16[128,512]{1,0:T(8,128)(2,1)S(1)}, bf16[128,512]{1,0:T(8,128)(2,1)S(1)}, u32[]{:S(2)}, u32[]{:S(2)}) collective-permute-start(bf16[128,512]{1,0:T(8,128)(2,1)S(1)} %get-tuple-element.37), channel_id=1, source_target_pairs={{0,8},{1,11},{2,10},{3,9},{4,12},{5,15},{6,14},{7,13},{8,0},{9,3},... | collective-permute-start | bytes 393224 | tf_op jit(solution)/shard_map/ppermute | solution.py:98
  7.9 1.6 %collective-permute-start.3 = (bf16[128,512]{1,0:T(8,128)(2,1)S(1)}, bf16[128,512]{1,0:T(8,128)(2,1)S(1)}, u32[]{:S(2)}, u32[]{:S(2)}) collective-permute-start(bf16[128,512]{1,0:T(8,128)(2,1)S(1)} %get-tuple-element.38), channel_id=1, source_target_pairs={{0,4},{1,7},{2,6},{3,5},{4,0},{5,3},{6,2},{7,1},{8,12},{9,15},{10,... | collective-permute-start | bytes 393224 | tf_op jit(solution)/shard_map/ppermute | solution.py:98
  9.5 0.7 collective-permute-start.4
  10.1 0.1 collective-permute-start.5
  10.2 1.3 %shard_map.96 = (bf16[128,1024]{1,0:T(8,128)(2,1)S(1)}, bf16[128,1024]{1,0:T(8,128)(2,1)S(1)}, bf16[128,1024]{1,0:T(8,128)(2,1)S(1)}, bf16[128,1024]{1,0:T(8,128)(2,1)S(1)}, bf16[192,512]{1,0:T(8,128)(2,1)S(1)}) custom-call(s32[4]{0:T(128)S(1)} %pad_add_fusion.idx, bf16[128,2048]{1,0:T(8,128)(2,1)S(1)} %bitcast.15, bf16[128,2048]{1,0:T(8,128)(2,1)S(1)} %bitcast.17, ...), custom_call_target="tpu_custom_call" | custom-call | tf_op jit(solution)/shard_map/pallas_call | solution.py:471
  11.5 1.9 %collective-permute-start.9 = (bf16[128,1024]{1,0:T(8,128)(2,1)S(1)}, bf16[128,1024]{1,0:T(8,128)(2,1)S(1)}, u32[]{:S(2)}, u32[]{:S(2)}) collective-permute-start(bf16[128,1024]{1,0:T(8,128)(2,1)S(1)} %get-tuple-element.45), channel_id=1, source_target_pairs={{0,8},{1,27},{2,26},{3,9},{4,12},{5,31},{6,30},{7,13},{8,0},{9,19}... | collective-permute-start | bytes 786440 | tf_op jit(solution)/shard_map/ppermute | solution.py:98
  13.5 0.9 collective-permute-done.2.refs_0_
  14.4 4.6 %collective-permute-start.10 = (bf16[128,1024]{1,0:T(8,128)(2,1)S(1)}, bf16[128,1024]{1,0:T(8,128)(2,1)S(1)}, u32[]{:S(2)}, u32[]{:S(2)}) collective-permute-start(bf16[128,1024]{1,0:T(8,128)(2,1)S(1)} %get-tuple-element.46), channel_id=1, source_target_pairs={{0,12},{1,31},{2,30},{3,13},{4,8},{5,27},{6,26},{7,9},{8,4},{9,23}... | collective-permute-start | bytes 786440 | tf_op jit(solution)/shard_map/ppermute | solution.py:98
  19.1 0.7 collective-permute-start.12
  19.8 0.7 collective-permute-start.8
  20.5 1.1 %shard_map.95 = (bf16[512,512]{1,0:T(8,128)(2,1)S(1)}, bf16[528,128]{1,0:T(8,128)(2,1)S(1)}, bf16[528,128]{1,0:T(8,128)(2,1)S(1)}) custom-call(s32[4]{0:T(128)S(1)} %pad_add_fusion.idx, bf16[128,512]{1,0:T(8,128)(2,1)S(1)} %collective-permute-done.2.refs_0_, bf16[128,512]{1,0:T(8,128)(2,1)S(1)} %collective-permute-done.3.refs_1_, ...), custom_call_target="tpu_custom_call" | custom-call | tf_op jit(solution)/shard_map/pallas_call | solution.py:471
  21.6 15.0 %collective-permute-done.9.refs_1_ = bf16[128,1024]{1,0:T(8,128)(2,1)S(1)} collective-permute-done((bf16[128,1024]{1,0:T(8,128)(2,1)S(1)}, bf16[128,1024]{1,0:T(8,128)(2,1)S(1)}, u32[]{:S(2)}, u32[]{:S(2)}) %collective-permute-start.9) | collective-permute-done | bytes 262176 | tf_op jit(solution)/shard_map/ppermute | solution.py:98
  36.6 1.9 %collective-permute-done.11.refs_3_ = bf16[128,1024]{1,0:T(8,128)(2,1)S(1)} collective-permute-done((bf16[128,1024]{1,0:T(8,128)(2,1)S(1)}, bf16[128,1024]{1,0:T(8,128)(2,1)S(1)}, u32[]{:S(2)}, u32[]{:S(2)}) %collective-permute-start.11) | collective-permute-done | bytes 262176 | tf_op jit(solution)/shard_map/ppermute | solution.py:98
  38.5 2.0 %shard_map.97 = (bf16[512,1024]{1,0:T(8,128)(2,1)S(1)}, bf16[656,128]{1,0:T(8,128)(2,1)S(1)}, bf16[656,128]{1,0:T(8,128)(2,1)S(1)}) custom-call(s32[4]{0:T(128)S(1)} %pad_add_fusion.idx, bf16[192,512]{1,0:T(8,128)(2,1)S(1)} %collective-permute-done.8.refs_0_, bf16[128,1024]{1,0:T(8,128)(2,1)S(1)} %collective-permute-done.9.refs_1_, ...), custom_call_target="tpu_custom_call" | custom-call | tf_op jit(solution)/shard_map/pallas_call | solution.py:471
  40.5 2.0 %collective-permute-start.13 = (bf16[656,128]{1,0:T(8,128)(2,1)S(1)}, bf16[656,128]{1,0:T(8,128)(2,1)S(1)}, u32[]{:S(2)}, u32[]{:S(2)}) collective-permute-start(bf16[656,128]{1,0:T(8,128)(2,1)S(1)} %get-tuple-element.51), channel_id=1, source_target_pairs={{0,1},{1,0},{2,3},{3,2},{4,5},{5,4},{6,7},{7,6},{8,9},{9,8},{10,11... | collective-permute-start | bytes 503816 | tf_op jit(solution)/shard_map/ppermute | solution.py:84
  42.6 0.1 collective-permute-start.6
  42.7 1.3 %collective-permute-done.6.thin_got = bf16[528,128]{1,0:T(8,128)(2,1)S(1)} collective-permute-done((bf16[528,128]{1,0:T(8,128)(2,1)S(1)}, bf16[528,128]{1,0:T(8,128)(2,1)S(1)}, u32[]{:S(2)}, u32[]{:S(2)}) %collective-permute-start.6) | collective-permute-done | bytes 135200 | tf_op jit(solution)/shard_map/ppermute | solution.py:84
  43.9 0.7 shard_map.98
  44.6 3.9 %collective-permute-start.14 = (bf16[592,128]{1,0:T(8,128)(2,1)S(1)}, bf16[592,128]{1,0:T(8,128)(2,1)S(1)}, u32[]{:S(2)}, u32[]{:S(2)}) collective-permute-start(bf16[592,128]{1,0:T(8,128)(2,1)S(1)} %get-tuple-element.53), channel_id=1, source_target_pairs={{0,4},{4,0},{8,12},{12,8},{1,5},{5,1},{9,13},{13,9},{2,6},{6,2},{1... | collective-permute-start | bytes 454664 | tf_op jit(solution)/shard_map/ppermute | solution.py:84
  48.5 4.4 %collective-permute-done.14.got = bf16[592,128]{1,0:T(8,128)(2,1)S(1)} collective-permute-done((bf16[592,128]{1,0:T(8,128)(2,1)S(1)}, bf16[592,128]{1,0:T(8,128)(2,1)S(1)}, u32[]{:S(2)}, u32[]{:S(2)}) %collective-permute-start.14) | collective-permute-done | bytes 151584 | tf_op jit(solution)/shard_map/ppermute | solution.py:84
  52.9 3.7 %collective-permute-start.15 = (bf16[592,128]{1,0:T(8,128)(2,1)S(1)}, bf16[592,128]{1,0:T(8,128)(2,1)S(1)}, u32[]{:S(2)}, u32[]{:S(2)}) collective-permute-start(bf16[592,128]{1,0:T(8,128)(2,1)S(1)} %shard_map.99.mine), channel_id=1, source_target_pairs={{0,8},{4,12},{8,0},{12,4},{1,9},{5,13},{9,1},{13,5},{2,10},{6,14},... | collective-permute-start | bytes 454664 | tf_op jit(solution)/shard_map/ppermute | solution.py:84
  56.7 6.8 %collective-permute-done.15.got = bf16[592,128]{1,0:T(8,128)(2,1)S(1)} collective-permute-done((bf16[592,128]{1,0:T(8,128)(2,1)S(1)}, bf16[592,128]{1,0:T(8,128)(2,1)S(1)}, u32[]{:S(2)}, u32[]{:S(2)}) %collective-permute-start.15) | collective-permute-done | bytes 151584 | tf_op jit(solution)/shard_map/ppermute | solution.py:84
  63.5 0.1 collective-permute-start.16
  63.6 0.1 collective-permute-start.17
  63.7 5.6 %collective-permute-done.16.refs_1_ = bf16[592,128]{1,0:T(8,128)(2,1)S(1)} collective-permute-done((bf16[592,128]{1,0:T(8,128)(2,1)S(1)}, bf16[592,128]{1,0:T(8,128)(2,1)S(1)}, u32[]{:S(2)}, u32[]{:S(2)}) %collective-permute-start.16) | collective-permute-done | bytes 151584 | tf_op jit(solution)/shard_map/ppermute | solution.py:84
  69.3 1.4 %collective-permute-done.18.refs_3_ = bf16[592,128]{1,0:T(8,128)(2,1)S(1)} collective-permute-done((bf16[592,128]{1,0:T(8,128)(2,1)S(1)}, bf16[592,128]{1,0:T(8,128)(2,1)S(1)}, u32[]{:S(2)}, u32[]{:S(2)}) %collective-permute-start.18) | collective-permute-done | bytes 151584 | tf_op jit(solution)/shard_map/ppermute | solution.py:84
  70.6 11.0 %shard_map.101 = (bf16[128,768]{1,0:T(8,128)(2,1)S(1)}, bf16[64,768]{1,0:T(8,128)(2,1)S(1)}, bf16[64,768]{1,0:T(8,128)(2,1)S(1)}) custom-call(s32[4]{0:T(128)S(1)} %pad_add_fusion.idx, bf16[592,128]{1,0:T(8,128)(2,1)S(1)} %shard_map.100.refs_0_, bf16[592,128]{1,0:T(8,128)(2,1)S(1)} %collective-permute-done.16.refs_1_, ...), custom_call_target="tpu_custom_call" | custom-call | tf_op jit(solution)/shard_map/pallas_call | solution.py:471
  81.6 0.4 collective-permute-start.25
  82.0 0.7 collective-permute-start.24
  82.6 2.5 %collective-permute-start.21 = (bf16[64,768]{1,0:T(8,128)(2,1)S(1)}, bf16[64,768]{1,0:T(8,128)(2,1)S(1)}, u32[]{:S(2)}, u32[]{:S(2)}) collective-permute-start(bf16[64,768]{1,0:T(8,128)(2,1)S(1)} %get-tuple-element.56), channel_id=1, source_target_pairs={{0,8},{1,11},{2,10},{3,9},{4,12},{5,15},{6,14},{7,13},{8,0},{9,3},... | collective-permute-start | bytes 294920 | tf_op jit(solution)/shard_map/ppermute | solution.py:98
  85.2 0.5 collective-permute-start.19
  85.6 4.6 %collective-permute-done.25.refs_1_ = bf16[128,768]{1,0:T(8,128)(2,1)S(1)} collective-permute-done((bf16[128,768]{1,0:T(8,128)(2,1)S(1)}, bf16[128,768]{1,0:T(8,128)(2,1)S(1)}, u32[]{:S(2)}, u32[]{:S(2)}) %collective-permute-start.25) | collective-permute-done | bytes 196640 | tf_op jit(solution)/shard_map/ppermute | solution.py:98
  90.2 0.5 collective-permute-start.26
  90.7 1.1 %collective-permute-start.22 = (bf16[64,768]{1,0:T(8,128)(2,1)S(1)}, bf16[64,768]{1,0:T(8,128)(2,1)S(1)}, u32[]{:S(2)}, u32[]{:S(2)}) collective-permute-start(bf16[64,768]{1,0:T(8,128)(2,1)S(1)} %collective-permute-done.21), channel_id=1, source_target_pairs={{0,4},{4,0},{8,12},{12,8},{1,5},{5,1},{9,13},{13,9},{2,6},{6,2},{1... | collective-permute-start | bytes 294920 | tf_op jit(solution)/shard_map/ppermute | solution.py:84
  91.8 3.7 %collective-permute-start.28 = (bf16[64,768]{1,0:T(8,128)(2,1)S(1)}, bf16[64,768]{1,0:T(8,128)(2,1)S(1)}, u32[]{:S(2)}, u32[]{:S(2)}) collective-permute-start(bf16[64,768]{1,0:T(8,128)(2,1)S(1)} %collective-permute-done.21), channel_id=1, source_target_pairs={{0,1},{1,0},{2,3},{3,2},{4,5},{5,4},{6,7},{7,6},{8,9},{9,8},{10,11... | collective-permute-start | bytes 294920 | tf_op jit(solution)/shard_map/ppermute | solution.py:84
  95.5 0.1 collective-permute-done.19.refs_2_
  95.7 1.6 %collective-permute-start.20 = (bf16[64,768]{1,0:T(8,128)(2,1)S(1)}, bf16[64,768]{1,0:T(8,128)(2,1)S(1)}, u32[]{:S(2)}, u32[]{:S(2)}) collective-permute-start(bf16[64,768]{1,0:T(8,128)(2,1)S(1)} %collective-permute-done.19.refs_2_), channel_id=1, source_target_pairs={{0,4},{4,0},{8,12},{12,8},{1,5},{5,1},{9,13},{13,9},{2,6},{6,2},{1... | collective-permute-start | bytes 294920 | tf_op jit(solution)/shard_map/ppermute | solution.py:84
  97.3 0.6 collective-permute-done.22
  97.8 1.1 %collective-permute-start.23 = (bf16[64,768]{1,0:T(8,128)(2,1)S(1)}, bf16[64,768]{1,0:T(8,128)(2,1)S(1)}, u32[]{:S(2)}, u32[]{:S(2)}) collective-permute-start(bf16[64,768]{1,0:T(8,128)(2,1)S(1)} %collective-permute-done.22), channel_id=1, source_target_pairs={{0,1},{1,0},{2,3},{3,2},{4,5},{5,4},{6,7},{7,6},{8,9},{9,8},{10,11... | collective-permute-start | bytes 294920 | tf_op jit(solution)/shard_map/ppermute | solution.py:84
  99.0 1.6 %shard_map.102 = (bf16[64,2048]{1,0:T(8,128)(2,1)}, f32[64,1024]{1,0:T(8,128)}, bf16[64,1024]{1,0:T(8,128)(2,1)}, f32[64,2048]{1,0:T(8,128)}) custom-call(s32[4]{0:T(128)S(1)} %pad_add_fusion.idx, bf16[128,768]{1,0:T(8,128)(2,1)S(1)} %collective-permute-done.24.refs_0_, bf16[128,768]{1,0:T(8,128)(2,1)S(1)} %collective-permute-done.25.refs_1_, ...), custom_call_target="tpu_custom_call" | custom-call | tf_op jit(solution)/shard_map/pallas_call | solution.py:457
  100.6 0.1 collective-permute-done.20.refs_0_
  100.8 1.3 %shard_map.103 = (bf16[64,2048]{1,0:T(8,128)(2,1)}, f32[64,1024]{1,0:T(8,128)}, bf16[64,1024]{1,0:T(8,128)(2,1)}, f32[64,2048]{1,0:T(8,128)}) custom-call(s32[4]{0:T(128)S(1)} %pad_add_fusion.idx, bf16[64,768]{1,0:T(8,128)(2,1)S(1)} %collective-permute-done.20.refs_0_, ...), custom_call_target="tpu_custom_call", output_to_operand_aliasing={{0}: (3, {}), {1}: (4, {}), {2}: (5, {}), {3}: (6, {})} | custom-call | tf_op jit(solution)/shard_map/pallas_call | solution.py:457
  (30 shorter events, 0.2 us)
Async XLA Ops:
  0.6 2.4 %collective-permute-start = (bf16[128,1024]{1,0:T(8,128)(2,1)}, bf16[128,1024]{1,0:T(8,128)(2,1)S(1)}, u32[]{:S(2)}, u32[]{:S(2)}) collective-permute-start(bf16[128,1024]{1,0:T(8,128)(2,1)} %bitcast.18), channel_id=1, source_target_pairs={{0,1},{1,0},{2,3},{3,2},{4,5},{5,4},{6,7},{7,6},{8,9},{9,8},{10,11... | collective-permute-start | bytes 786440 | tf_op jit(solution)/shard_map/ppermute | solution.py:84
  1.1 1.8 %collective-permute-start.1 = (bf16[128,1024]{1,0:T(8,128)(2,1)}, bf16[128,1024]{1,0:T(8,128)(2,1)S(1)}, u32[]{:S(2)}, u32[]{:S(2)}) collective-permute-start(bf16[128,1024]{1,0:T(8,128)(2,1)} %bitcast.20), channel_id=1, source_target_pairs={{0,1},{1,0},{2,3},{3,2},{4,5},{5,4},{6,7},{7,6},{8,9},{9,8},{10,11... | collective-permute-start | bytes 786440 | tf_op jit(solution)/shard_map/ppermute | solution.py:84
  1.3 2.2 %copy-start.2 = (bf16[1,128,1024]{2,1,0:T(8,128)(2,1)S(1)}, bf16[1,128,1024]{2,1,0:T(8,128)(2,1)}, u32[]{:S(2)}) copy-start(bf16[1,128,1024]{2,1,0:T(8,128)(2,1)} %param.7) | copy-start | bytes 786436
  1.3 2.2 %copy-start.3 = (bf16[1,128,1024]{2,1,0:T(8,128)(2,1)S(1)}, bf16[1,128,1024]{2,1,0:T(8,128)(2,1)}, u32[]{:S(2)}) copy-start(bf16[1,128,1024]{2,1,0:T(8,128)(2,1)} %param.8) | copy-start | bytes 786436
  3.0 7.3 %copy-start = (bf16[1,128,2048]{2,1,0:T(8,128)(2,1)S(1)}, bf16[1,128,2048]{2,1,0:T(8,128)(2,1)}, u32[]{:S(2)}) copy-start(bf16[1,128,2048]{2,1,0:T(8,128)(2,1)} %param.6) | copy-start | bytes 1572868
  3.0 7.3 %copy-start.1 = (bf16[1,128,2048]{2,1,0:T(8,128)(2,1)S(1)}, bf16[1,128,2048]{2,1,0:T(8,128)(2,1)}, u32[]{:S(2)}) copy-start(bf16[1,128,2048]{2,1,0:T(8,128)(2,1)} %param.9) | copy-start | bytes 1572868
  3.0 7.2 %collective-permute-start.7 = (bf16[144,2048]{1,0:T(8,128)(2,1)S(1)}, bf16[144,2048]{1,0:T(8,128)(2,1)S(1)}, u32[]{:S(2)}, u32[]{:S(2)}) collective-permute-start(bf16[144,2048]{1,0:T(8,128)(2,1)S(1)} %shard_map.93), channel_id=1, source_target_pairs={{0,1},{1,0},{2,3},{3,2},{4,5},{5,4},{6,7},{7,6},{8,9},{9,8},{10,11... | collective-permute-start | bytes 1769480 | tf_op jit(solution)/shard_map/ppermute | solution.py:84
  4.1 10.3 %collective-permute-start.2 = (bf16[128,512]{1,0:T(8,128)(2,1)S(1)}, bf16[128,512]{1,0:T(8,128)(2,1)S(1)}, u32[]{:S(2)}, u32[]{:S(2)}) collective-permute-start(bf16[128,512]{1,0:T(8,128)(2,1)S(1)} %get-tuple-element.37), channel_id=1, source_target_pairs={{0,8},{1,11},{2,10},{3,9},{4,12},{5,15},{6,14},{7,13},{8,0},{9,3},... | collective-permute-start | bytes 393224 | tf_op jit(solution)/shard_map/ppermute | solution.py:98
  7.9 11.2 %collective-permute-start.3 = (bf16[128,512]{1,0:T(8,128)(2,1)S(1)}, bf16[128,512]{1,0:T(8,128)(2,1)S(1)}, u32[]{:S(2)}, u32[]{:S(2)}) collective-permute-start(bf16[128,512]{1,0:T(8,128)(2,1)S(1)} %get-tuple-element.38), channel_id=1, source_target_pairs={{0,4},{1,7},{2,6},{3,5},{4,0},{5,3},{6,2},{7,1},{8,12},{9,15},{10,... | collective-permute-start | bytes 393224 | tf_op jit(solution)/shard_map/ppermute | solution.py:98
  9.5 9.6 %collective-permute-start.4 = (bf16[128,512]{1,0:T(8,128)(2,1)S(1)}, bf16[128,512]{1,0:T(8,128)(2,1)S(1)}, u32[]{:S(2)}, u32[]{:S(2)}) collective-permute-start(bf16[128,512]{1,0:T(8,128)(2,1)S(1)} %get-tuple-element.39), channel_id=1, source_target_pairs={{0,0},{1,3},{2,2},{3,1},{4,4},{5,7},{6,6},{7,5},{8,8},{9,11},{10,1... | collective-permute-start | bytes 393224 | tf_op jit(solution)/shard_map/ppermute | solution.py:98
  10.1 9.6 %collective-permute-start.5 = (bf16[128,512]{1,0:T(8,128)(2,1)S(1)}, bf16[128,512]{1,0:T(8,128)(2,1)S(1)}, u32[]{:S(2)}, u32[]{:S(2)}) collective-permute-start(bf16[128,512]{1,0:T(8,128)(2,1)S(1)} %get-tuple-element.40), channel_id=1, source_target_pairs={{0,12},{1,15},{2,14},{3,13},{4,8},{5,11},{6,10},{7,9},{8,4},{9,7},... | collective-permute-start | bytes 393224 | tf_op jit(solution)/shard_map/ppermute | solution.py:98
  11.5 25.1 %collective-permute-start.9 = (bf16[128,1024]{1,0:T(8,128)(2,1)S(1)}, bf16[128,1024]{1,0:T(8,128)(2,1)S(1)}, u32[]{:S(2)}, u32[]{:S(2)}) collective-permute-start(bf16[128,1024]{1,0:T(8,128)(2,1)S(1)} %get-tuple-element.45), channel_id=1, source_target_pairs={{0,8},{1,27},{2,26},{3,9},{4,12},{5,31},{6,30},{7,13},{8,0},{9,19}... | collective-permute-start | bytes 786440 | tf_op jit(solution)/shard_map/ppermute | solution.py:98
  14.4 22.2 %collective-permute-start.10 = (bf16[128,1024]{1,0:T(8,128)(2,1)S(1)}, bf16[128,1024]{1,0:T(8,128)(2,1)S(1)}, u32[]{:S(2)}, u32[]{:S(2)}) collective-permute-start(bf16[128,1024]{1,0:T(8,128)(2,1)S(1)} %get-tuple-element.46), channel_id=1, source_target_pairs={{0,12},{1,31},{2,30},{3,13},{4,8},{5,27},{6,26},{7,9},{8,4},{9,23}... | collective-permute-start | bytes 786440 | tf_op jit(solution)/shard_map/ppermute | solution.py:98
  19.1 19.4 %collective-permute-start.11 = (bf16[128,1024]{1,0:T(8,128)(2,1)S(1)}, bf16[128,1024]{1,0:T(8,128)(2,1)S(1)}, u32[]{:S(2)}, u32[]{:S(2)}) collective-permute-start(bf16[128,1024]{1,0:T(8,128)(2,1)S(1)} %get-tuple-element.47), channel_id=1, source_target_pairs={{0,4},{1,23},{2,22},{3,5},{4,0},{5,19},{6,18},{7,1},{8,12},{9,31},... | collective-permute-start | bytes 786440 | tf_op jit(solution)/shard_map/ppermute | solution.py:98
  19.1 19.4 %collective-permute-start.12 = (bf16[128,1024]{1,0:T(8,128)(2,1)S(1)}, bf16[128,1024]{1,0:T(8,128)(2,1)S(1)}, u32[]{:S(2)}, u32[]{:S(2)}) collective-permute-start(bf16[128,1024]{1,0:T(8,128)(2,1)S(1)} %get-tuple-element.48), channel_id=1, source_target_pairs={{0,0},{1,19},{2,18},{3,1},{4,4},{5,23},{6,22},{7,5},{8,8},{9,27},{... | collective-permute-start | bytes 786440 | tf_op jit(solution)/shard_map/ppermute | solution.py:98
  19.8 1.8 %collective-permute-start.8 = (bf16[192,512]{1,0:T(8,128)(2,1)S(1)}, bf16[192,512]{1,0:T(8,128)(2,1)S(1)}, u32[]{:S(2)}, u32[]{:S(2)}) collective-permute-start(bf16[192,512]{1,0:T(8,128)(2,1)S(1)} %get-tuple-element.44), channel_id=1, source_target_pairs={{0,0},{1,3},{2,2},{3,1},{4,4},{5,7},{6,6},{7,5},{8,8},{9,11},{10,1... | collective-permute-start | bytes 589832 | tf_op jit(solution)/shard_map/ppermute | solution.py:98
  40.5 3.4 %collective-permute-start.13 = (bf16[656,128]{1,0:T(8,128)(2,1)S(1)}, bf16[656,128]{1,0:T(8,128)(2,1)S(1)}, u32[]{:S(2)}, u32[]{:S(2)}) collective-permute-start(bf16[656,128]{1,0:T(8,128)(2,1)S(1)} %get-tuple-element.51), channel_id=1, source_target_pairs={{0,1},{1,0},{2,3},{3,2},{4,5},{5,4},{6,7},{7,6},{8,9},{9,8},{10,11... | collective-permute-start | bytes 503816 | tf_op jit(solution)/shard_map/ppermute | solution.py:84
  42.6 1.4 %collective-permute-start.6 = (bf16[528,128]{1,0:T(8,128)(2,1)S(1)}, bf16[528,128]{1,0:T(8,128)(2,1)S(1)}, u32[]{:S(2)}, u32[]{:S(2)}) collective-permute-start(bf16[528,128]{1,0:T(8,128)(2,1)S(1)} %get-tuple-element.42), channel_id=1, source_target_pairs={{0,1},{1,0},{2,3},{3,2},{4,5},{5,4},{6,7},{7,6},{8,9},{9,8},{10,11... | collective-permute-start | bytes 405512 | tf_op jit(solution)/shard_map/ppermute | solution.py:84
  44.6 8.3 %collective-permute-start.14 = (bf16[592,128]{1,0:T(8,128)(2,1)S(1)}, bf16[592,128]{1,0:T(8,128)(2,1)S(1)}, u32[]{:S(2)}, u32[]{:S(2)}) collective-permute-start(bf16[592,128]{1,0:T(8,128)(2,1)S(1)} %get-tuple-element.53), channel_id=1, source_target_pairs={{0,4},{4,0},{8,12},{12,8},{1,5},{5,1},{9,13},{13,9},{2,6},{6,2},{1... | collective-permute-start | bytes 454664 | tf_op jit(solution)/shard_map/ppermute | solution.py:84
  52.9 10.5 %collective-permute-start.15 = (bf16[592,128]{1,0:T(8,128)(2,1)S(1)}, bf16[592,128]{1,0:T(8,128)(2,1)S(1)}, u32[]{:S(2)}, u32[]{:S(2)}) collective-permute-start(bf16[592,128]{1,0:T(8,128)(2,1)S(1)} %shard_map.99.mine), channel_id=1, source_target_pairs={{0,8},{4,12},{8,0},{12,4},{1,9},{5,13},{9,1},{13,5},{2,10},{6,14},... | collective-permute-start | bytes 454664 | tf_op jit(solution)/shard_map/ppermute | solution.py:84
  63.5 5.8 %collective-permute-start.16 = (bf16[592,128]{1,0:T(8,128)(2,1)S(1)}, bf16[592,128]{1,0:T(8,128)(2,1)S(1)}, u32[]{:S(2)}, u32[]{:S(2)}) collective-permute-start(bf16[592,128]{1,0:T(8,128)(2,1)S(1)} %shard_map.100.refs_0_), channel_id=1, source_target_pairs={{0,4},{4,0},{8,12},{12,8},{1,5},{5,1},{9,13},{13,9},{2,6},{6,2},{1... | collective-permute-start | bytes 454664 | tf_op jit(solution)/shard_map/ppermute | solution.py:84
  63.6 5.7 %collective-permute-start.17 = (bf16[592,128]{1,0:T(8,128)(2,1)S(1)}, bf16[592,128]{1,0:T(8,128)(2,1)S(1)}, u32[]{:S(2)}, u32[]{:S(2)}) collective-permute-start(bf16[592,128]{1,0:T(8,128)(2,1)S(1)} %shard_map.100.refs_0_), channel_id=1, source_target_pairs={{0,1},{1,0},{2,3},{3,2},{4,5},{5,4},{6,7},{7,6},{8,9},{9,8},{10,11... | collective-permute-start | bytes 454664 | tf_op jit(solution)/shard_map/ppermute | solution.py:84
  69.3 1.4 %collective-permute-start.18 = (bf16[592,128]{1,0:T(8,128)(2,1)S(1)}, bf16[592,128]{1,0:T(8,128)(2,1)S(1)}, u32[]{:S(2)}, u32[]{:S(2)}) collective-permute-start(bf16[592,128]{1,0:T(8,128)(2,1)S(1)} %collective-permute-done.16.refs_1_), channel_id=1, source_target_pairs={{0,1},{1,0},{2,3},{3,2},{4,5},{5,4},{6,7},{7,6},{8,9},{9,8},{10,11... | collective-permute-start | bytes 454664 | tf_op jit(solution)/shard_map/ppermute | solution.py:84
  81.6 8.6 %collective-permute-start.25 = (bf16[128,768]{1,0:T(8,128)(2,1)S(1)}, bf16[128,768]{1,0:T(8,128)(2,1)S(1)}, u32[]{:S(2)}, u32[]{:S(2)}) collective-permute-start(bf16[128,768]{1,0:T(8,128)(2,1)S(1)} %get-tuple-element.57), channel_id=1, source_target_pairs={{0,4},{1,7},{2,6},{3,5},{4,0},{5,3},{6,2},{7,1},{8,12},{9,15},{10,... | collective-permute-start | bytes 589832 | tf_op jit(solution)/shard_map/ppermute | solution.py:98
  82.0 8.3 %collective-permute-start.24 = (bf16[128,768]{1,0:T(8,128)(2,1)S(1)}, bf16[128,768]{1,0:T(8,128)(2,1)S(1)}, u32[]{:S(2)}, u32[]{:S(2)}) collective-permute-start(bf16[128,768]{1,0:T(8,128)(2,1)S(1)} %get-tuple-element.57), channel_id=1, source_target_pairs={{0,0},{1,3},{2,2},{3,1},{4,4},{5,7},{6,6},{7,5},{8,8},{9,11},{10,1... | collective-permute-start | bytes 589832 | tf_op jit(solution)/shard_map/ppermute | solution.py:98
  82.6 8.1 %collective-permute-start.21 = (bf16[64,768]{1,0:T(8,128)(2,1)S(1)}, bf16[64,768]{1,0:T(8,128)(2,1)S(1)}, u32[]{:S(2)}, u32[]{:S(2)}) collective-permute-start(bf16[64,768]{1,0:T(8,128)(2,1)S(1)} %get-tuple-element.56), channel_id=1, source_target_pairs={{0,8},{1,11},{2,10},{3,9},{4,12},{5,15},{6,14},{7,13},{8,0},{9,3},... | collective-permute-start | bytes 294920 | tf_op jit(solution)/shard_map/ppermute | solution.py:98
  85.2 10.5 %collective-permute-start.19 = (bf16[64,768]{1,0:T(8,128)(2,1)S(1)}, bf16[64,768]{1,0:T(8,128)(2,1)S(1)}, u32[]{:S(2)}, u32[]{:S(2)}) collective-permute-start(bf16[64,768]{1,0:T(8,128)(2,1)S(1)} %get-tuple-element.55), channel_id=1, source_target_pairs={{0,8},{1,11},{2,10},{3,9},{4,12},{5,15},{6,14},{7,13},{8,0},{9,3},... | collective-permute-start | bytes 294920 | tf_op jit(solution)/shard_map/ppermute | solution.py:98
  90.2 8.8 %collective-permute-start.27 = (bf16[128,768]{1,0:T(8,128)(2,1)S(1)}, bf16[128,768]{1,0:T(8,128)(2,1)S(1)}, u32[]{:S(2)}, u32[]{:S(2)}) collective-permute-start(bf16[128,768]{1,0:T(8,128)(2,1)S(1)} %collective-permute-done.25.refs_1_), channel_id=1, source_target_pairs={{0,1},{1,0},{2,3},{3,2},{4,5},{5,4},{6,7},{7,6},{8,9},{9,8},{10,11... | collective-permute-start | bytes 589832 | tf_op jit(solution)/shard_map/ppermute | solution.py:84
  90.2 8.8 %collective-permute-start.26 = (bf16[128,768]{1,0:T(8,128)(2,1)S(1)}, bf16[128,768]{1,0:T(8,128)(2,1)S(1)}, u32[]{:S(2)}, u32[]{:S(2)}) collective-permute-start(bf16[128,768]{1,0:T(8,128)(2,1)S(1)} %collective-permute-done.24.refs_0_), channel_id=1, source_target_pairs={{0,1},{1,0},{2,3},{3,2},{4,5},{5,4},{6,7},{7,6},{8,9},{9,8},{10,11... | collective-permute-start | bytes 589832 | tf_op jit(solution)/shard_map/ppermute | solution.py:84
  90.7 7.1 %collective-permute-start.22 = (bf16[64,768]{1,0:T(8,128)(2,1)S(1)}, bf16[64,768]{1,0:T(8,128)(2,1)S(1)}, u32[]{:S(2)}, u32[]{:S(2)}) collective-permute-start(bf16[64,768]{1,0:T(8,128)(2,1)S(1)} %collective-permute-done.21), channel_id=1, source_target_pairs={{0,4},{4,0},{8,12},{12,8},{1,5},{5,1},{9,13},{13,9},{2,6},{6,2},{1... | collective-permute-start | bytes 294920 | tf_op jit(solution)/shard_map/ppermute | solution.py:84
  91.8 7.2 %collective-permute-start.28 = (bf16[64,768]{1,0:T(8,128)(2,1)S(1)}, bf16[64,768]{1,0:T(8,128)(2,1)S(1)}, u32[]{:S(2)}, u32[]{:S(2)}) collective-permute-start(bf16[64,768]{1,0:T(8,128)(2,1)S(1)} %collective-permute-done.21), channel_id=1, source_target_pairs={{0,1},{1,0},{2,3},{3,2},{4,5},{5,4},{6,7},{7,6},{8,9},{9,8},{10,11... | collective-permute-start | bytes 294920 | tf_op jit(solution)/shard_map/ppermute | solution.py:84
  95.7 5.1 %collective-permute-start.20 = (bf16[64,768]{1,0:T(8,128)(2,1)S(1)}, bf16[64,768]{1,0:T(8,128)(2,1)S(1)}, u32[]{:S(2)}, u32[]{:S(2)}) collective-permute-start(bf16[64,768]{1,0:T(8,128)(2,1)S(1)} %collective-permute-done.19.refs_2_), channel_id=1, source_target_pairs={{0,4},{4,0},{8,12},{12,8},{1,5},{5,1},{9,13},{13,9},{2,6},{6,2},{1... | collective-permute-start | bytes 294920 | tf_op jit(solution)/shard_map/ppermute | solution.py:84
  97.8 2.9 %collective-permute-start.23 = (bf16[64,768]{1,0:T(8,128)(2,1)S(1)}, bf16[64,768]{1,0:T(8,128)(2,1)S(1)}, u32[]{:S(2)}, u32[]{:S(2)}) collective-permute-start(bf16[64,768]{1,0:T(8,128)(2,1)S(1)} %collective-permute-done.22), channel_id=1, source_target_pairs={{0,1},{1,0},{2,3},{3,2},{4,5},{5,4},{6,7},{7,6},{8,9},{9,8},{10,11... | collective-permute-start | bytes 294920 | tf_op jit(solution)/shard_map/ppermute | solution.py:84
